TPU v7x, 128 devices: a whole 4x4x4 slice. The times are simulated.
128 devices in a mesh: grp: 2 (over y_lo), dp: 8 (over x, y_hi), tensor: 8 (over z, core).
Axes of the slice: x: 4, y: 4 (y_hi: 2, y_lo: 2; y = y_hi * 2 + y_lo), z: 4, core: 2. Of those that a mesh axis runs over, the one named last changes fastest.
Arguments:
- teacher_values: bfloat16 [2048, 16384], P('grp', 'tensor'), may hold values from -6 to 6
- teacher_weight: bfloat16 [16384, 16384], P('tensor', 'dp'), may hold values from -0.046875 to 0.046875
- teacher_stream: bfloat16 [2048, 16384], P(('grp', 'tensor'), 'dp'), may hold values from -6 to 6
- send_order: int32 [16, 128], replicated, may hold values from 0 to 127, each once within a row
- projection: bfloat16 [16384, 8192], P('dp', 'tensor'), may hold values from -0.046875 to 0.046875
- student_values: bfloat16 [2048, 8192], P(('grp', 'tensor'), 'dp'), may hold values from -0.75 to 0.75
- student_weight: bfloat16 [8192, 8192], P('dp', 'tensor'), may hold values from -0.5 to 0.5
- student_stream: bfloat16 [2048, 8192], P(('grp', 'dp'), 'tensor'), may hold values from -6 to 6
Outputs:
- values_grad: float32 [2048, 8192], P(('grp', 'tensor'), 'dp')
- weight_grad: float32 [8192, 8192], P('dp', 'tensor')
Inputs may be any that keep to these rules, and one draw needn't show every extreme that they name: `send_order`: each row is an ordering of the 128 rows of one teacher block.
All inputs are finite; a program needn't handle non-finite values.
Results may differ from a plain program's by a relative error of at most 0.0085.
Values may be sent and summed in bfloat16 or wider, within the bound.
No kernel may reach another device: no remote copies, remote signals or barrier semaphores. Data moves between devices by JAX's collectives and lax.ppermute only.
A program may use at most 128 MiB of HBM per device.

v0:
```python
import math

import jax
import jax.numpy as jnp
from jax import lax
from jax.sharding import PartitionSpec as P


def reorder(row_block, send_order, block_index):
    row_order = lax.dynamic_index_in_dim(send_order, block_index, 0, keepdims=False)
    return jnp.take(row_block, row_order, axis=0)


def relay_wide(row_block):
    halves = lax.axis_size("grp")
    within = lax.axis_size("tensor")
    piece_rows = row_block.shape[0] // (halves * within)
    pieces = row_block.reshape(halves * within, piece_rows, row_block.shape[1])
    arrived = lax.all_to_all(pieces, ("grp", "tensor"), split_axis=0, concat_axis=0, tiled=True)
    return arrived.reshape(row_block.shape)


def project(row_block, projection):
    gathered = lax.all_gather(row_block, "tensor", axis=0, tiled=True)
    summed = lax.psum_scatter(
        jnp.dot(gathered, projection, preferred_element_type=jnp.float32),
        "dp",
        scatter_dimension=0,
        tiled=True,
    )
    return summed.astype(jnp.bfloat16)


def per_device(
    teacher_values,
    teacher_weight,
    teacher_stream,
    send_order,
    projection,
    student_values,
    student_weight,
    student_stream,
):
    picked = teacher_values
    teacher_out = lax.psum_scatter(
        jnp.dot(picked, teacher_weight, preferred_element_type=jnp.float32),
        "tensor",
        scatter_dimension=0,
        tiled=True,
    )
    hidden = (teacher_stream.astype(jnp.float32) + teacher_out).astype(jnp.bfloat16)
    block_index = lax.axis_index("grp") * lax.axis_size("tensor") + lax.axis_index("tensor")
    arrived_rows = relay_wide(reorder(hidden, send_order, block_index))
    target = project(arrived_rows, projection)
    gathered_values = lax.all_gather(student_values, "tensor", axis=0, tiled=True)
    picked = gathered_values
    layer_out = lax.psum_scatter(
        jnp.dot(picked, student_weight, preferred_element_type=jnp.float32),
        "dp",
        scatter_dimension=0,
        tiled=True,
    )
    total_tokens = student_stream.shape[0] * lax.axis_size("grp") * lax.axis_size("dp")
    loss_scale = 1.0 / math.sqrt(total_tokens)
    residual_gap = student_stream.astype(jnp.float32) + layer_out - target.astype(jnp.float32)
    gap_rows = (residual_gap * loss_scale).astype(jnp.bfloat16)
    gathered_gap = lax.all_gather(gap_rows, "dp", axis=0, tiled=True)
    picked = gathered_gap
    values_grad = lax.psum_scatter(
        lax.dot_general(
            picked, student_weight, (((1,), (1,)), ((), ())), preferred_element_type=jnp.float32
        ),
        "tensor",
        scatter_dimension=0,
        tiled=True,
    )
    local_weight = lax.dot_general(
        gathered_values, gathered_gap, (((0,), (0,)), ((), ())), preferred_element_type=jnp.float32
    )
    weight_grad = lax.psum(local_weight, "grp")
    return (values_grad, weight_grad)


def solution(mesh):
    in_specs = (
        P("grp", "tensor"),
        P("tensor", "dp"),
        P(("grp", "tensor"), "dp"),
        P(),
        P("dp", "tensor"),
        P(("grp", "tensor"), "dp"),
        P("dp", "tensor"),
        P(("grp", "dp"), "tensor"),
    )
    out_specs = (P(("grp", "tensor"), "dp"), P("dp", "tensor"))
    return jax.shard_map(
        per_device, mesh=mesh, in_specs=in_specs, out_specs=out_specs, check_vma=False
    )
```

profile of v0, /device:TPU:1, one launch (start us, length us, event | category | flops | bytes accessed | tf_op | source)
XLA Modules:
  0.0 538.5 jit_solution(7709787551249771284)
XLA Ops:
  7.2 0.0 copy-start
  7.2 0.0 reduce-scatter.7.cloned.1.call-start
  7.2 14.6 %fusion.3 = f32[1024,2048]{1,0:T(8,128)} fusion(bf16[1024,2048]{1,0:T(8,128)(2,1)} %param.8, bf16[2048,2048]{1,0:T(8,128)(2,1)} %param.9), kind=kOutput, calls=%fused_computation.13 | convolution fusion | flops 8589934592 | bytes 20971520 | tf_op jit(solution)/shard_map/dot_general | solution.py:46
  21.8 0.0 copy-start.1
  21.8 0.0 reduce-scatter.7.cloned.1.call-update
  21.8 0.0 all-gather.4.cloned.1.call-start
  21.9 0.7 all-gather.4.cloned.1.call-update
  22.6 0.0 all-gather.6.cloned.1.call-start
  22.6 0.7 fusion.1
  23.3 0.1 squeeze.6
  23.4 0.7 fusion
  24.1 53.0 %reduce-scatter.7.cloned.1.call-done = f32[128,2048]{1,0:T(8,128)} async-done(((f32[1024,2048]{1,0:T(8,128)}), f32[128,2048]{1,0:T(8,128)}) %reduce-scatter.7.cloned.1.call-update) | async-done | bytes 1048592 | tf_op jit(solution)/shard_map/reduce_scatter | solution.py:45
  77.1 0.0 copy-done.1
  77.1 1.3 add_convert_fusion
  78.4 0.9 gather_fusion
  79.4 0.1 bitcast_select_fusion
  79.5 14.6 %all_to_all.5 = bf16[16,8,2048]{2,1,0:T(8,128)(2,1)} all-to-all(bf16[16,8,2048]{2,1,0:T(8,128)(2,1)S(1)} %bitcast_select_fusion), channel_id=1, replica_groups=mesh['grp'=2,'dp'=8,'tensor'=8] {'grp','tensor'}, dimensions={0} | all-to-all | bytes 1048576 | tf_op jit(solution)/shard_map/all_to_all | solution.py:19
  94.1 0.0 all-gather.6.cloned.1.call-update
  94.1 0.0 reduce-scatter.5.cloned.1.call-start
  94.2 11.6 %all-gather.4.cloned.1.call-done = bf16[1024,1024]{1,0:T(8,128)(2,1)} async-done(((bf16[128,1024]{1,0:T(8,128)(2,1)}), bf16[1024,1024]{1,0:T(8,128)(2,1)}) %all-gather.4.cloned.1.call-update) | async-done | bytes 2097168 | tf_op jit(solution)/shard_map/all_gather | solution.py:55
  105.8 0.0 copy-done
  105.8 5.9 %fusion.2 = f32[1024,1024]{1,0:T(8,128)} fusion(bf16[1024,1024]{1,0:T(8,128)(2,1)} %all-gather.4.cloned.1.call-done, bf16[1024,1024]{1,0:T(8,128)(2,1)S(1)} %copy-done), kind=kOutput, calls=%fused_computation.12 | convolution fusion | flops 2147483648 | bytes 8388608 | tf_op jit(solution)/shard_map/dot_general | solution.py:58
  111.7 0.0 reduce-scatter.5.cloned.1.call-update
  111.7 0.0 reduce-scatter.9.cloned.1.call-start
  111.8 28.1 %all-gather.6.cloned.1.call-done = bf16[1024,2048]{1,0:T(8,128)(2,1)} async-done(((bf16[128,2048]{1,0:T(8,128)(2,1)}), bf16[1024,2048]{1,0:T(8,128)(2,1)}) %all-gather.6.cloned.1.call-update) | async-done | bytes 4194320 | tf_op jit(solution)/shard_map/all_gather | solution.py:24
  139.9 9.9 %fusion.4 = f32[1024,1024]{1,0:T(8,128)} fusion(bf16[1024,2048]{1,0:T(8,128)(2,1)} %all-gather.6.cloned.1.call-done, bf16[2048,1024]{1,0:T(8,128)(2,1)} %param.12), kind=kOutput, calls=%fused_computation.14 | convolution fusion | flops 4294967296 | bytes 12582912 | tf_op jit(solution)/shard_map/dot_general | solution.py:26
  149.8 0.0 copy-start.2
  149.8 0.0 reduce-scatter.9.cloned.1.call-update
  149.9 0.0 all-gather.8.cloned.1.call-start
  149.9 77.2 %reduce-scatter.5.cloned.1.call-done = f32[128,1024]{1,0:T(8,128)} async-done(((f32[1024,1024]{1,0:T(8,128)}), f32[128,1024]{1,0:T(8,128)}) %reduce-scatter.5.cloned.1.call-update) | async-done | bytes 524304 | tf_op jit(solution)/shard_map/reduce_scatter | solution.py:57
  227.1 87.3 %reduce-scatter.9.cloned.1.call-done = f32[128,1024]{1,0:T(8,128)} async-done(((f32[1024,1024]{1,0:T(8,128)}), f32[128,1024]{1,0:T(8,128)}) %reduce-scatter.9.cloned.1.call-update) | async-done | bytes 524304 | tf_op jit(solution)/shard_map/reduce_scatter | solution.py:25
  314.4 0.0 copy-done.2
  314.4 2.0 multiply_convert_fusion
  316.4 0.0 all-gather.8.cloned.1.call-update
  316.4 0.0 all-reduce.2.cloned.1.call-start
  316.5 54.4 %all-gather.8.cloned.1.call-done = bf16[1024,1024]{1,0:T(8,128)(2,1)} async-done(((bf16[128,1024]{1,0:T(8,128)(2,1)}), bf16[1024,1024]{1,0:T(8,128)(2,1)}) %all-gather.8.cloned.1.call-update) | async-done | bytes 2097168 | tf_op jit(solution)/shard_map/all_gather | solution.py:67
  370.8 6.6 %convolution_bitcast_fusion = f32[1024,1024]{0,1:T(8,128)} fusion(bf16[1024,1024]{1,0:T(8,128)(2,1)} %all-gather.8.cloned.1.call-done, bf16[1024,1024]{1,0:T(8,128)(2,1)} %all-gather.4.cloned.1.call-done), kind=kOutput, calls=%fused_computation.1 | convolution fusion | flops 2147483648 | bytes 8388608 | tf_op jit(solution)/shard_map/dot_general | solution.py:77
  377.5 0.0 all-reduce.2.cloned.1.call-update
  377.5 0.0 reduce-scatter.11.cloned.1.call-start
  377.5 5.9 %fusion.5 = f32[1024,1024]{1,0:T(8,128)} fusion(bf16[1024,1024]{1,0:T(8,128)(2,1)} %all-gather.8.cloned.1.call-done, bf16[1024,1024]{1,0:T(8,128)(2,1)S(1)} %copy-done), kind=kOutput, calls=%fused_computation.15 | convolution fusion | flops 2147483648 | bytes 8388608 | tf_op jit(solution)/shard_map/dot_general | solution.py:70
  383.5 0.0 reduce-scatter.11.cloned.1.call-update
  383.5 108.8 %all-reduce.2.cloned.1.call-done = f32[1024,1024]{0,1:T(8,128)} async-done(((f32[1024,1024]{0,1:T(8,128)}), f32[1024,1024]{0,1:T(8,128)}) %all-reduce.2.cloned.1.call-update) | async-done | bytes 4194320 | tf_op jit(solution)/shard_map/psum | solution.py:80
  492.3 5.3 copy.11
  497.6 34.0 %reduce-scatter.11.cloned.1.call-done = f32[128,1024]{1,0:T(8,128)} async-done(((f32[1024,1024]{1,0:T(8,128)}), f32[128,1024]{1,0:T(8,128)}) %reduce-scatter.11.cloned.1.call-update) | async-done | bytes 524304 | tf_op jit(solution)/shard_map/reduce_scatter | solution.py:69
  (2 shorter events, 0.0 us)
Async XLA Ops:
  7.2 98.6 %copy-start = (bf16[1024,1024]{1,0:T(8,128)(2,1)S(1)}, bf16[1024,1024]{1,0:T(8,128)(2,1)}, u32[]{:S(2)}) copy-start(bf16[1024,1024]{1,0:T(8,128)(2,1)} %param.14) | copy-start | bytes 6291460
  7.2 69.9 %reduce-scatter.7.cloned.1.call-start = ((), (), s32[]{:S(2)}) async-start(), calls=%async_computation.7 | async-start | bytes 9437184 | tf_op jit(solution)/shard_map/reduce_scatter | solution.py:45
  21.8 55.3 %copy-start.1 = (bf16[128,2048]{1,0:T(8,128)(2,1)S(1)}, bf16[128,2048]{1,0:T(8,128)(2,1)}, u32[]{:S(2)}) copy-start(bf16[128,2048]{1,0:T(8,128)(2,1)} %param.10) | copy-start | bytes 1572868
  21.8 84.0 %all-gather.4.cloned.1.call-start = ((), (), s32[]{:S(2)}) async-start(), calls=%async_computation.5 | async-start | bytes 2359296 | tf_op jit(solution)/shard_map/all_gather | solution.py:55
  22.6 117.4 %all-gather.6.cloned.1.call-start = ((), (), s32[]{:S(2)}) async-start(), calls=%async_computation.8 | async-start | bytes 4718592 | tf_op jit(solution)/shard_map/all_gather | solution.py:24
  94.1 133.0 %reduce-scatter.5.cloned.1.call-start = ((), (), s32[]{:S(2)}) async-start(), calls=%async_computation.6 | async-start | bytes 4718592 | tf_op jit(solution)/shard_map/reduce_scatter | solution.py:57
  111.7 202.7 %reduce-scatter.9.cloned.1.call-start = ((), (), s32[]{:S(2)}) async-start(), calls=%async_computation.9 | async-start | bytes 4718592 | tf_op jit(solution)/shard_map/reduce_scatter | solution.py:25
  149.8 164.6 %copy-start.2 = (bf16[128,1024]{1,0:T(8,128)(2,1)S(1)}, bf16[128,1024]{1,0:T(8,128)(2,1)}, u32[]{:S(2)}) copy-start(bf16[128,1024]{1,0:T(8,128)(2,1)} %param.15) | copy-start | bytes 786436
  149.9 221.0 %all-gather.8.cloned.1.call-start = ((), (), s32[]{:S(2)}) async-start(), calls=%async_computation.10 | async-start | bytes 2359296 | tf_op jit(solution)/shard_map/all_gather | solution.py:67
  316.4 175.8 %all-reduce.2.cloned.1.call-start = ((), (), s32[]{:S(2)}) async-start(), calls=%async_computation.12 | async-start | bytes 8388608 | tf_op jit(solution)/shard_map/psum | solution.py:80
  377.5 154.1 %reduce-scatter.11.cloned.1.call-start = ((), (), s32[]{:S(2)}) async-start(), calls=%async_computation.11 | async-start | bytes 4718592 | tf_op jit(solution)/shard_map/reduce_scatter | solution.py:69
Sparse Core Ops, SparseCore 0:
  21.9 55.1 reduce-scatter.6
  78.8 26.9 all-gather.3
  107.5 32.3 all-gather.5
  144.2 82.8 reduce-scatter.4
  230.8 83.5 reduce-scatter.8
  317.2 53.6 all-gather.7
  377.6 114.6 all-reduce.1
  495.4 36.1 reduce-scatter.10
where the time goes:
time: 541 us; the launch traced here: 538 us
  waiting for transfers between devices  455 us (84%)
  matrix products  43 us (8%)
  blocking collectives  14.6 us (3%)
  between operations  14.2 us (3%)
  local copies, waits for them, and re-layouts  7.08 us (1%)
    psum x1, waiting for transfers between devices, per_device(): weight_grad = lax.psum(local_weight, 'grp')  109 us
    reduce_scatter x1, waiting for transfers between devices, project(): lax.psum_scatter(jnp.dot(gathered, projection, preferred_element_type=jnp...  87.3 us
    reduce_scatter x1, waiting for transfers between devices, per_device(): lax.psum_scatter(jnp.dot(picked, student_weight, preferred_element_type=j...  77.2 us
    all_gather x1, waiting for transfers between devices, per_device(): gathered_gap = lax.all_gather(gap_rows, 'dp', axis=0, tiled=True)  54.4 us
    reduce_scatter x1, waiting for transfers between devices, per_device(): lax.psum_scatter(jnp.dot(picked, teacher_weight, preferred_element_type=j...  53 us
    reduce_scatter x1, waiting for transfers between devices, per_device(): lax.psum_scatter(lax.dot_general(picked, student_weight, (((1,), (1,)), (...  34 us
    all_gather x1, waiting for transfers between devices, project(): gathered = lax.all_gather(row_block, 'tensor', axis=0, tiled=True)  28.1 us
    all_to_all x1, blocking collectives, relay_wide(): lax.all_to_all(pieces, ('grp', 'tensor'), split_axis=0, concat_axis=0, ti...  14.6 us
  transfers between devices with their start and end apart: 8, of which 8 were waited for; matrix products, arithmetic and copies ran while one was open for 6% of the time, Pallas kernels for 0%

commit v1 on v0

v1 whole, which is shorter than its diff:
```python
import functools
import math

import jax
import jax.numpy as jnp
from jax import lax
from jax.experimental import pallas as pl
from jax.experimental.pallas import tpu as pltpu
from jax.sharding import Mesh, PartitionSpec as P

BF16 = jnp.bfloat16
F32 = jnp.float32
CHUNKS = 2
X = "x"
Z = "z"
CORE = "core"
GRP = "grp"
DP = ("x", "yh")
Y = ("grp", "yh")
SIZES = {"grp": 2, "x": 4, "yh": 2, "z": 4, "core": 2}
VMEM_LIMIT = 56 * 1024 * 1024


def swap(array, axes, distance):
    names = axes if isinstance(axes, tuple) else (axes,)
    size = math.prod(SIZES[name] for name in names)
    return lax.ppermute(array, axes, [(i, i ^ distance) for i in range(size)])


def params():
    return pltpu.CompilerParams(vmem_limit_bytes=VMEM_LIMIT)


def cost(macs, moved):
    return pl.CostEstimate(flops=2 * macs, bytes_accessed=moved, transcendentals=0)


def whole(array):
    return pl.BlockSpec(array.shape, lambda *_: (0,) * array.ndim)


def smem():
    return pl.BlockSpec(memory_space=pltpu.SMEM)


def nn(a, b):
    return jnp.dot(a, b, preferred_element_type=F32)


def nt(a, b):
    return lax.dot_general(a, b, (((1,), (1,)), ((), ())), preferred_element_type=F32)


def teacher_kernel(row_ref, own_ref, x_ref, w_ref, s_ref, mine_ref, peer_ref, a_ref, o_ref):
    rows, depth = a_ref.shape

    @pl.when(pl.program_id(0) == 0)
    def _():
        source = lax.broadcasted_iota(jnp.int32, (rows, rows), 1)
        pick = jnp.where(source == row_ref[...], 1.0, 0.0).astype(BF16)
        wide = 512

        def step(i, _):
            columns = pl.ds(pl.multiple_of(i * wide, wide), wide)
            a_ref[:, columns] = nn(pick, x_ref[:, columns]).astype(BF16)
            return 0

        lax.fori_loop(0, depth // wide, step, 0)
        source = lax.broadcasted_iota(jnp.int32, o_ref.shape, 1)
        o_ref[...] = jnp.where(source == own_ref[...], 1.0, 0.0).astype(BF16)

    out = (nn(a_ref[...], w_ref[...]) + nn(o_ref[...], s_ref[...])).astype(BF16)
    mine_ref[...] = out[: rows // 2]
    peer_ref[...] = out[rows // 2 :]


def teacher(row, own, values, weight, stream, chunk, tile=256):
    rows, depth = values.shape[0] // CHUNKS, values.shape[1]
    width = weight.shape[1]
    half = jax.ShapeDtypeStruct((rows // 2, width), BF16)
    return pl.pallas_call(
        teacher_kernel,
        grid=(width // tile,),
        out_shape=(half, half),
        in_specs=[
            whole(row),
            whole(own),
            pl.BlockSpec((rows, depth), lambda j: (chunk, 0)),
            pl.BlockSpec((depth, tile), lambda j: (0, j)),
            pl.BlockSpec((stream.shape[0], tile), lambda j: (0, j)),
        ],
        out_specs=[pl.BlockSpec((rows // 2, tile), lambda j: (0, j))] * 2,
        scratch_shapes=[pltpu.VMEM((rows, depth), BF16), pltpu.VMEM((rows, stream.shape[0]), BF16)],
        compiler_params=params(),
        cost_estimate=cost(rows * depth * width, 2 * (depth * width + rows * depth + rows * width)),
    )(row, own, values, weight, stream)


def partial_kernel(ids_ref, *refs):
    hidden, values = refs[:8], refs[8:16]
    p_ref, w_ref = refs[16:18]
    outs = refs[18:26]
    h_ref, v_ref = refs[26:]
    piece = hidden[0].shape[0]

    @pl.when(pl.program_id(0) == 0)
    def _():
        for k in range(8):
            at = pl.multiple_of((ids_ref[0] ^ ids_ref[1] ^ k) * piece, piece)
            h_ref[pl.ds(at, piece), :] = hidden[k][...]
            v_ref[pl.ds(at, piece), :] = values[k][...]

    out = (nn(v_ref[...], w_ref[...]) - nn(h_ref[...], p_ref[...])).astype(BF16)
    for k in range(8):
        outs[k][...] = out[k * piece : (k + 1) * piece]


def partial_sums(ids, hidden, values, projection, weight, chunk, tile=256):
    piece, deep = hidden[0].shape
    depth, width = weight.shape
    rows = 8 * piece
    return pl.pallas_call(
        partial_kernel,
        grid=(width // tile,),
        out_shape=[jax.ShapeDtypeStruct((piece, width), BF16)] * 8,
        in_specs=[smem()]
        + [whole(hidden[0])] * 8
        + [pl.BlockSpec((piece, depth), lambda j: (chunk, 0))] * 8
        + [pl.BlockSpec((deep, tile), lambda j: (0, j)), pl.BlockSpec((depth, tile), lambda j: (0, j))],
        out_specs=[pl.BlockSpec((piece, tile), lambda j: (0, j))] * 8,
        scratch_shapes=[pltpu.VMEM((rows, deep), BF16), pltpu.VMEM((rows, depth), BF16)],
        compiler_params=params(),
        cost_estimate=cost(rows * (deep + depth) * width, 2 * (deep + depth) * (width + rows)),
    )(ids, *hidden, *values, projection, weight)


def gap_places(first, second):
    piece = first[0].shape[0] // 2
    for e in range(4):
        for n in range(2):
            yield 2 * e + n, 0, first[e], n * piece
            yield 2 * e + n, 1, second[n], e * piece


def values_kernel(ids_ref, a0, a1, a2, a3, b0, b1, w_ref, mine_ref, peer_ref, g_ref):
    piece = a0.shape[0] // 2
    rows = g_ref.shape[0]
    block = CHUNKS * piece

    @pl.when(pl.program_id(0) == 0)
    def _():
        for k, chunk, ref, start in gap_places((a0, a1, a2, a3), (b0, b1)):
            to = ids_ref[0] ^ ids_ref[1] ^ k
            at = pl.multiple_of((to & 1) * (rows // 2) + (to >> 1) * block + chunk * piece, piece)
            g_ref[pl.ds(at, piece), :] = ref[start : start + piece, :]

    out = nt(g_ref[...], w_ref[...]).astype(BF16)
    mine_ref[...] = out[: rows // 2]
    peer_ref[...] = out[rows // 2 :]


def values_partial(ids, gaps, weight, tile=256):
    piece, width = gaps[0].shape[0] // 2, gaps[0].shape[1]
    rows = 8 * CHUNKS * piece
    feats = weight.shape[0]
    half = jax.ShapeDtypeStruct((rows // 2, feats), BF16)
    return pl.pallas_call(
        values_kernel,
        grid=(feats // tile,),
        out_shape=(half, half),
        in_specs=[smem()] + [whole(g) for g in gaps] + [pl.BlockSpec((tile, width), lambda j: (j, 0))],
        out_specs=[pl.BlockSpec((rows // 2, tile), lambda j: (0, j))] * 2,
        scratch_shapes=[pltpu.VMEM((rows, width), BF16)],
        compiler_params=params(),
        cost_estimate=cost(rows * width * feats, 2 * (rows * width + feats * width + rows * feats)),
    )(ids, *gaps, weight)


def turn_kernel(ids_ref, *refs):
    own, other, out_ref = refs[:8], refs[8:10], refs[10]
    rows = own[0].shape[0]
    for k in range(8):
        block = ids_ref[1] ^ k
        at = pl.multiple_of(block * rows, rows)
        out_ref[:, pl.ds(at, rows)] = own[k][...].T
        at = pl.multiple_of((block + 8) * rows, rows)
        start = (k >> 1) * rows
        out_ref[:, pl.ds(at, rows)] = other[k & 1][start : start + rows, :].T


def turned(ids, own, other):
    rows, feats = own[0].shape
    return pl.pallas_call(
        turn_kernel,
        out_shape=jax.ShapeDtypeStruct((feats, 16 * rows), BF16),
        in_specs=[smem()] + [pl.BlockSpec(memory_space=pltpu.VMEM)] * 10,
        out_specs=pl.BlockSpec(memory_space=pltpu.VMEM),
        compiler_params=params(),
        cost_estimate=cost(0, 64 * rows * feats),
    )(ids, *own, *other)


def weight_kernel(ids_ref, *refs):
    own, other = refs[:6], refs[6:12]
    v_ref, out_ref, g_ref = refs[12:]
    piece = own[0].shape[0] // 2
    half = g_ref.shape[0] // 2
    block = CHUNKS * piece

    @pl.when(pl.program_id(0) == 0)
    def _():
        for side, gaps in enumerate((own, other)):
            for k, chunk, ref, start in gap_places(gaps[:4], gaps[4:]):
                place = (ids_ref[0] ^ k) * block + side * half + chunk * piece
                at = pl.multiple_of(place, piece)
                g_ref[pl.ds(at, piece), :] = ref[start : start + piece, :]

    out_ref[...] = nn(v_ref[...], g_ref[...])


def weight_sums(ids, own, other, values, tile=256):
    feats, rows = values.shape
    width = own[0].shape[1]
    return pl.pallas_call(
        weight_kernel,
        grid=(feats // tile,),
        out_shape=jax.ShapeDtypeStruct((feats, width), F32),
        in_specs=[smem()]
        + [whole(g) for g in (*own, *other)]
        + [pl.BlockSpec((tile, rows), lambda j: (j, 0))],
        out_specs=pl.BlockSpec((tile, width), lambda j: (j, 0)),
        scratch_shapes=[pltpu.VMEM((rows, width), BF16)],
        compiler_params=params(),
        cost_estimate=cost(rows * width * feats, 2 * (rows * width + feats * rows + 2 * width * feats)),
    )(ids, *own, *other, values)


def add(*terms):
    total = terms[0].astype(F32)
    for term in terms[1:]:
        total = total + term.astype(F32)
    return total


def gather_tensor(block):
    across = [block, swap(block, Z, 1), swap(block, Z, 2), swap(block, Z, 3)]
    out = []
    for piece in across:
        out += [piece, swap(piece, CORE, 1)]
    return out


def per_device(
    teacher_values,
    teacher_weight,
    teacher_stream,
    send_order,
    projection,
    student_values,
    student_weight,
    student_stream,
):
    g = lax.axis_index("grp")
    dp = lax.axis_index("x") * 2 + lax.axis_index("yh")
    t = lax.axis_index("z") * 2 + lax.axis_index("core")
    ids = jnp.stack([dp, t]).astype(jnp.int32)
    piece = send_order.shape[1] // 16
    span = 8 // CHUNKS

    def ordered(rows):
        parts = rows.reshape(2, CHUNKS, -1, rows.shape[1])
        parts = jnp.where(g == 0, parts, parts[::-1])
        return parts.transpose(1, 0, 2, 3).reshape(rows.shape)

    def unordered(rows):
        parts = rows.reshape(CHUNKS, 2, -1, rows.shape[1]).transpose(1, 0, 2, 3)
        return jnp.where(g == 0, parts, parts[::-1]).reshape(rows.shape)

    order = lax.dynamic_slice_in_dim(send_order, g * 8, 8, 0).reshape(8, 16, piece)
    place = jnp.arange(16)
    core_far, z_far, half_far = place // 8, (place // 2) % 4, place % 2
    owner = (half_far ^ g) * 8 + (t ^ (z_far * 2 + core_far))
    chosen = owner[:, None] == jnp.arange(16)[None, :]
    order = jnp.sum(jnp.where(chosen[None, :, :, None], order[:, None], 0), axis=2)
    block = jnp.arange(8)[:, None, None]
    rows_of = ((block % span) * (16 * piece) + order).reshape(CHUNKS, span, 16, piece)
    owns_of = jnp.where(block == t, order, -1).reshape(CHUNKS, span, 16, piece)
    rows_of = rows_of.transpose(0, 2, 1, 3).reshape(CHUNKS, -1, 1)
    owns_of = owns_of.transpose(0, 2, 1, 3).reshape(CHUNKS, -1, 1)

    values = ordered(student_values)
    stream = ordered(student_stream)
    values_own = gather_tensor(values)
    pair = jnp.concatenate(values_own[0::2], axis=0)
    values_far = swap(pair, GRP, 1)
    values_other = [values_far, swap(values_far, CORE, 1)]

    loss_scale = 1.0 / math.sqrt(student_stream.shape[0] * 16)
    gaps = []
    for chunk in range(CHUNKS):
        mine, peer = teacher(
            rows_of[chunk], owns_of[chunk], teacher_values, teacher_weight, teacher_stream, chunk
        )
        arrived = swap(peer, CORE, 1)
        rows = mine.shape[0] // 4
        sums = [
            add(mine[k * rows : (k + 1) * rows], arrived[k * rows : (k + 1) * rows]).astype(BF16)
            for k in range(4)
        ]
        hidden = add(sums[0], *[swap(sums[k], Z, k) for k in (1, 2, 3)]).astype(BF16)
        relayed = swap(hidden[rows // 2 :], GRP, 1)
        hidden = jnp.concatenate([hidden[: rows // 2], relayed], axis=0)
        parts = partial_sums(
            ids, gather_tensor(hidden), values_own, projection, student_weight, chunk
        )
        total = add(parts[0], *[swap(parts[k], DP, k) for k in range(1, 8)])
        rows = total.shape[0]
        gap = stream[chunk * rows : (chunk + 1) * rows].astype(F32) + total
        gaps.append((gap * loss_scale).astype(BF16))

    first, second = gaps
    near = jnp.concatenate([first, swap(first, Y, 1)], axis=0)
    far = jnp.concatenate([swap(first, Y, 2), swap(first, Y, 3)], axis=0)
    along = jnp.concatenate([second] + [swap(second, X, k) for k in (1, 2, 3)], axis=0)
    own = [near] + [swap(near, X, k) for k in (1, 2, 3)] + [along, swap(along, Y, 1)]
    other = [far] + [swap(far, X, k) for k in (1, 2, 3)] + [swap(along, Y, 2), swap(along, Y, 3)]

    mine, peer = values_partial(ids, own, student_weight)
    arrived = swap(peer, CORE, 1)
    rows = mine.shape[0] // 4
    sums = [
        add(mine[k * rows : (k + 1) * rows], arrived[k * rows : (k + 1) * rows]) for k in range(4)
    ]
    values_grad = add(sums[0], *[swap(sums[k].astype(BF16), Z, k) for k in (1, 2, 3)])
    weight_grad = weight_sums(ids, own, other, turned(ids, values_own, values_other))
    return (unordered(values_grad), weight_grad)


def solution(mesh):
    fine = Mesh(mesh.devices.reshape(2, 4, 2, 4, 2), ("grp", "x", "yh", "z", "core"))
    tensor = ("z", "core")
    in_specs = (
        P("grp", tensor),
        P(tensor, DP),
        P(("grp",) + tensor, DP),
        P(),
        P(DP, tensor),
        P(("grp",) + tensor, DP),
        P(DP, tensor),
        P(("grp",) + DP, tensor),
    )
    out_specs = (P(("grp",) + tensor, DP), P(DP, tensor))
    return jax.shard_map(
        per_device, mesh=fine, in_specs=in_specs, out_specs=out_specs, check_vma=False
    )
```

time: 541 us -> 281 us (0.52)
  waiting for transfers between devices: 455 us -> 94.5 us
  starting transfers between devices: 0.33 us -> 104 us
  Pallas kernels: 0 us -> 62.1 us
  matrix products: 43 us -> 0 us
  blocking collectives: 14.6 us -> 0 us
  between operations: 14.2 us -> 1.43 us
    reduce_scatter x4 -> x0, waiting for transfers between devices: 251 us -> none  [the longest x1 87.3 us: project(): lax.psum_scatter(jnp.dot(gathered, projection, preferred_element_type=jnp...]
    psum x1 -> x0, waiting for transfers between devices: 109 us -> none  [per_device(): weight_grad = lax.psum(local_weight, 'grp')]
    ppermute x0 -> x66, starting transfers between devices: none -> 104 us  [swap(): return lax.ppermute(array, axes, [(i, i ^ distance) for i in range(size)])]
    ppermute x0 -> x66, waiting for transfers between devices: none -> 94.5 us  [swap(): return lax.ppermute(array, axes, [(i, i ^ distance) for i in range(size)])]
    all_gather x3 -> x0, waiting for transfers between devices: 94.1 us -> none  [the longest x1 54.4 us: per_device(): gathered_gap = lax.all_gather(gap_rows, 'dp', axis=0, tiled=True)]
    pallas_call x0 -> x7, Pallas kernels: none -> 62.1 us  [the longest x2 25.8 us: teacher(): pl.pallas_call(teacher_kernel, grid=(width // tile,), out_shape=(half, ha...]
    dot_general x5 -> x0, matrix products: 43 us -> none  [the longest x1 14.6 us: per_device(): jnp.dot(picked, teacher_weight, preferred_element_type=jnp.float32)]
    all_to_all x1 -> x0, blocking collectives: 14.6 us -> none  [relay_wide(): lax.all_to_all(pieces, ('grp', 'tensor'), split_axis=0, concat_axis=0, ti...]
  transfers between devices with their start and end apart: 8 -> 66, of which waited for: 8 -> 16; matrix products, arithmetic and copies ran while one was open for 6% -> 2% of each run, Pallas kernels for 0% -> 18%
where the time goes in v1:
time: 281 us; the launch traced here: 279 us
  starting transfers between devices  104 us (37%)
  waiting for transfers between devices  94.5 us (34%)
  Pallas kernels  62.1 us (22%)
  local copies, waits for them, and re-layouts  9.76 us (3%)
  other arithmetic  7.26 us (3%)
    ppermute x66, starting transfers between devices, swap(): return lax.ppermute(array, axes, [(i, i ^ distance) for i in range(size)])  104 us
    ppermute x66, waiting for transfers between devices, swap(): return lax.ppermute(array, axes, [(i, i ^ distance) for i in range(size)])  94.5 us
    pallas_call x2, Pallas kernels, teacher(): pl.pallas_call(teacher_kernel, grid=(width // tile,), out_shape=(half, ha...  25.8 us
    pallas_call x2, Pallas kernels, partial_sums(): pl.pallas_call(partial_kernel, grid=(width // tile,), out_shape=[jax.Shap...  15.5 us
    pallas_call x1, Pallas kernels, weight_sums(): pl.pallas_call(weight_kernel, grid=(feats // tile,), out_shape=jax.ShapeD...  9.23 us
    pallas_call x1, Pallas kernels, values_partial(): pl.pallas_call(values_kernel, grid=(feats // tile,), out_shape=(half, hal...  6.07 us
  transfers between devices with their start and end apart: 66, of which 16 were waited for; matrix products, arithmetic and copies ran while one was open for 2% of the time, Pallas kernels for 18%

profile of v1, /device:TPU:1, one launch (start us, length us, event | category | flops | bytes accessed | tf_op | source)
XLA Modules:
  0.0 278.8 jit_solution(10991140082182703994)
XLA Ops:
  1.5 2.2 select_reduce_fusion
  5.8 12.8 %shard_map.97 = (bf16[256,2048]{1,0:T(8,128)(2,1)}, bf16[256,2048]{1,0:T(8,128)(2,1)}) custom-call(s32[512,1]{1,0:T(8,128)} %squeeze.18.row_ref, s32[512,1]{1,0:T(8,128)} %squeeze.19.own_ref, bf16[1024,2048]{1,0:T(8,128)(2,1)} %x_ref.3, bf16[2048,2048]{1,0:T(8,128)(2,1)} %w_ref.4, bf16[128,2048]{1,0:T(8,128)(2,1)} %s_ref.3), custom_call_target="tpu_custom_call" | custom-call | flops 4294967296 | bytes 12582912 | tf_op jit(solution)/shard_map/pallas_call | solution.py:81
  21.9 12.9 %shard_map.95 = (bf16[256,2048]{1,0:T(8,128)(2,1)}, bf16[256,2048]{1,0:T(8,128)(2,1)}) custom-call(s32[512,1]{1,0:T(8,128)} %squeeze.16.row_ref, s32[512,1]{1,0:T(8,128)} %squeeze.17.own_ref, bf16[1024,2048]{1,0:T(8,128)(2,1)} %x_ref.3, bf16[2048,2048]{1,0:T(8,128)(2,1)} %w_ref.4, bf16[128,2048]{1,0:T(8,128)(2,1)} %s_ref.3), custom_call_target="tpu_custom_call" | custom-call | flops 4294967296 | bytes 12582912 | tf_op jit(solution)/shard_map/pallas_call | solution.py:81
  35.0 3.9 %collective-permute-start.17 = (bf16[128,1024]{1,0:T(8,128)(2,1)S(1)}, bf16[128,1024]{1,0:T(8,128)(2,1)S(1)}, u32[]{:S(2)}, u32[]{:S(2)}) collective-permute-start(bf16[128,1024]{1,0:T(8,128)(2,1)S(1)} %bitcast.24), channel_id=1, source_target_pairs={{0,6},{2,4},{4,2},{6,0},{1,7},{3,5},{5,3},{7,1},{8,14},{10,12},{12... | collective-permute-start | bytes 786440 | tf_op jit(solution)/shard_map/ppermute | solution.py:27
  41.0 2.6 collective-permute-start.33
  43.9 7.3 %collective-permute-done.31 = bf16[64,2048]{1,0:T(8,128)(2,1)S(1)} collective-permute-done((bf16[64,2048]{1,0:T(8,128)(2,1)S(1)}, bf16[64,2048]{1,0:T(8,128)(2,1)S(1)}, u32[]{:S(2)}, u32[]{:S(2)}) %collective-permute-start.31) | collective-permute-done | bytes 262176 | tf_op jit(solution)/shard_map/ppermute | solution.py:27
  52.0 10.0 %collective-permute-done.33 = bf16[64,2048]{1,0:T(8,128)(2,1)S(1)} collective-permute-done((bf16[64,2048]{1,0:T(8,128)(2,1)S(1)}, bf16[64,2048]{1,0:T(8,128)(2,1)S(1)}, u32[]{:S(2)}, u32[]{:S(2)}) %collective-permute-start.33) | collective-permute-done | bytes 262176 | tf_op jit(solution)/shard_map/ppermute | solution.py:27
  62.0 2.8 %collective-permute-start.3 = (bf16[64,2048]{1,0:T(8,128)(2,1)S(1)}, bf16[64,2048]{1,0:T(8,128)(2,1)S(1)}, u32[]{:S(2)}, u32[]{:S(2)}) collective-permute-start(bf16[64,2048]{1,0:T(8,128)(2,1)S(1)} %get-tuple-element.53), channel_id=1, source_target_pairs={{0,6},{2,4},{4,2},{6,0},{1,7},{3,5},{5,3},{7,1},{8,14},{10,12},{12... | collective-permute-start | bytes 786440 | tf_op jit(solution)/shard_map/ppermute | solution.py:27
  68.9 3.3 %collective-permute-start.16 = (bf16[128,1024]{1,0:T(8,128)(2,1)S(1)}, bf16[128,1024]{1,0:T(8,128)(2,1)S(1)}, u32[]{:S(2)}, u32[]{:S(2)}) collective-permute-start(bf16[128,1024]{1,0:T(8,128)(2,1)S(1)} %collective-permute-done.15.refs_12_.refs_4_), channel_id=1, source_target_pairs={{0,1},{1,0},{2,3},{3,2},{4,5},{5,4},{6,7},{7,6},{8,9},{9,8},{10,11... | collective-permute-start | bytes 786440 | tf_op jit(solution)/shard_map/ppermute | solution.py:27
  72.3 4.7 %collective-permute-start.14 = (bf16[128,1024]{1,0:T(8,128)(2,1)S(1)}, bf16[128,1024]{1,0:T(8,128)(2,1)S(1)}, u32[]{:S(2)}, u32[]{:S(2)}) collective-permute-start(bf16[128,1024]{1,0:T(8,128)(2,1)S(1)} %collective-permute-done.13.refs_10_.refs_2_), channel_id=1, source_target_pairs={{0,1},{1,0},{2,3},{3,2},{4,5},{5,4},{6,7},{7,6},{8,9},{9,8},{10,11... | collective-permute-start | bytes 786440 | tf_op jit(solution)/shard_map/ppermute | solution.py:27
  78.6 2.3 collective-permute-done.34
  82.2 2.5 collective-permute-done.4
  84.7 5.0 %collective-permute-start.40 = (bf16[64,2048]{1,0:T(8,128)(2,1)S(1)}, bf16[64,2048]{1,0:T(8,128)(2,1)S(1)}, u32[]{:S(2)}, u32[]{:S(2)}) collective-permute-start(bf16[64,2048]{1,0:T(8,128)(2,1)S(1)} %pad_maximum_fusion.4.refs_0_), channel_id=1, source_target_pairs={{0,6},{2,4},{4,2},{6,0},{1,7},{3,5},{5,3},{7,1},{8,14},{10,12},{12... | collective-permute-start | bytes 786440 | tf_op jit(solution)/shard_map/ppermute | solution.py:27
  90.5 2.8 %collective-permute-start.35 = (bf16[64,2048]{1,0:T(8,128)(2,1)S(1)}, bf16[64,2048]{1,0:T(8,128)(2,1)S(1)}, u32[]{:S(2)}, u32[]{:S(2)}) collective-permute-start(bf16[64,2048]{1,0:T(8,128)(2,1)S(1)} %pad_maximum_fusion.4.refs_0_), channel_id=1, source_target_pairs={{0,1},{1,0},{2,3},{3,2},{4,5},{5,4},{6,7},{7,6},{8,9},{9,8},{10,11... | collective-permute-start | bytes 786440 | tf_op jit(solution)/shard_map/ppermute | solution.py:27
  93.4 2.6 collective-permute-start.10
  96.1 4.8 %collective-permute-done.40.refs_6_ = bf16[64,2048]{1,0:T(8,128)(2,1)S(1)} collective-permute-done((bf16[64,2048]{1,0:T(8,128)(2,1)S(1)}, bf16[64,2048]{1,0:T(8,128)(2,1)S(1)}, u32[]{:S(2)}, u32[]{:S(2)}) %collective-permute-start.40) | collective-permute-done | bytes 262176 | tf_op jit(solution)/shard_map/ppermute | solution.py:27
  101.4 3.4 %collective-permute-start.6 = (bf16[64,2048]{1,0:T(8,128)(2,1)S(1)}, bf16[64,2048]{1,0:T(8,128)(2,1)S(1)}, u32[]{:S(2)}, u32[]{:S(2)}) collective-permute-start(bf16[64,2048]{1,0:T(8,128)(2,1)S(1)} %pad_maximum_fusion.2.refs_0_), channel_id=1, source_target_pairs={{0,2},{2,0},{4,6},{6,4},{1,3},{3,1},{5,7},{7,5},{8,10},{10,8},{12,... | collective-permute-start | bytes 786440 | tf_op jit(solution)/shard_map/ppermute | solution.py:27
  104.9 2.2 collective-permute-start.41
  107.1 3.7 %collective-permute-done.10.refs_6_ = bf16[64,2048]{1,0:T(8,128)(2,1)S(1)} collective-permute-done((bf16[64,2048]{1,0:T(8,128)(2,1)S(1)}, bf16[64,2048]{1,0:T(8,128)(2,1)S(1)}, u32[]{:S(2)}, u32[]{:S(2)}) %collective-permute-start.10) | collective-permute-done | bytes 262176 | tf_op jit(solution)/shard_map/ppermute | solution.py:27
  115.3 2.5 collective-permute-start.11
  119.3 7.7 %shard_map.98 = (bf16[64,1024]{1,0:T(8,128)(2,1)}, bf16[64,1024]{1,0:T(8,128)(2,1)}, bf16[64,1024]{1,0:T(8,128)(2,1)}, bf16[64,1024]{1,0:T(8,128)(2,1)}, bf16[64...) custom-call(s32[2]{0:T(128)} %pad_add_fusion.ids_ref, ...), custom_call_target="tpu_custom_call" | custom-call | flops 3221225472 | bytes 9437184 | tf_op jit(solution)/shard_map/pallas_call | solution.py:122
  127.1 3.0 %collective-permute-start.42 = (bf16[64,1024]{1,0:T(8,128)(2,1)}, bf16[64,1024]{1,0:T(8,128)(2,1)S(1)}, u32[]{:S(2)}, u32[]{:S(2)}) collective-permute-start(bf16[64,1024]{1,0:T(8,128)(2,1)} %get-tuple-element.37), channel_id=1, source_target_pairs={{0,8},{8,0},{16,24},{24,16},{32,40},{40,32},{48,56},{56,48},{1,9},... | collective-permute-start | bytes 393224 | tf_op jit(solution)/shard_map/ppermute | solution.py:27
  131.8 2.6 collective-permute-start.45
  134.5 2.9 %collective-permute-start.46 = (bf16[64,1024]{1,0:T(8,128)(2,1)S(1)}, bf16[64,1024]{1,0:T(8,128)(2,1)S(1)}, u32[]{:S(2)}, u32[]{:S(2)}) collective-permute-start(bf16[64,1024]{1,0:T(8,128)(2,1)S(1)} %copy-done.52), channel_id=1, source_target_pairs={{0,40},{8,32},{16,56},{24,48},{32,8},{40,0},{48,24},{56,16},{1,41}... | collective-permute-start | bytes 393224 | tf_op jit(solution)/shard_map/ppermute | solution.py:27
  137.3 2.5 collective-permute-start.47
  140.1 7.8 %shard_map.96 = (bf16[64,1024]{1,0:T(8,128)(2,1)}, bf16[64,1024]{1,0:T(8,128)(2,1)}, bf16[64,1024]{1,0:T(8,128)(2,1)}, bf16[64,1024]{1,0:T(8,128)(2,1)}, bf16[64...) custom-call(s32[2]{0:T(128)} %pad_add_fusion.ids_ref, ...), custom_call_target="tpu_custom_call" | custom-call | flops 3221225472 | bytes 9437184 | tf_op jit(solution)/shard_map/pallas_call | solution.py:122
  149.1 2.6 collective-permute-start.19
  153.4 2.6 collective-permute-start.51
  156.0 21.8 %collective-permute-done.19 = bf16[64,1024]{1,0:T(8,128)(2,1)S(1)} collective-permute-done((bf16[64,1024]{1,0:T(8,128)(2,1)}, bf16[64,1024]{1,0:T(8,128)(2,1)S(1)}, u32[]{:S(2)}, u32[]{:S(2)}) %collective-permute-start.19) | collective-permute-done | bytes 131104 | tf_op jit(solution)/shard_map/ppermute | solution.py:27
  181.5 2.4 collective-permute-start.23
  183.9 2.4 collective-permute-start.24
  186.4 2.6 collective-permute-start.25
  190.1 2.2 collective-permute-done.23
  192.3 5.9 %collective-permute-done.25 = bf16[64,1024]{1,0:T(8,128)(2,1)S(1)} collective-permute-done((bf16[64,1024]{1,0:T(8,128)(2,1)}, bf16[64,1024]{1,0:T(8,128)(2,1)S(1)}, u32[]{:S(2)}, u32[]{:S(2)}) %collective-permute-start.25) | collective-permute-done | bytes 131104 | tf_op jit(solution)/shard_map/ppermute | solution.py:27
  199.2 9.4 %collective-permute-done.26 = bf16[64,1024]{1,0:T(8,128)(2,1)S(1)} collective-permute-done((bf16[64,1024]{1,0:T(8,128)(2,1)S(1)}, bf16[64,1024]{1,0:T(8,128)(2,1)S(1)}, u32[]{:S(2)}, u32[]{:S(2)}) %collective-permute-start.26) | collective-permute-done | bytes 131104 | tf_op jit(solution)/shard_map/ppermute | solution.py:27
  209.2 2.7 collective-permute-start.27
  211.9 4.2 %collective-permute-start.65 = (bf16[512,1024]{1,0:T(8,128)(2,1)S(1)}, bf16[512,1024]{1,0:T(8,128)(2,1)S(1)}, u32[]{:S(2)}, u32[]{:S(2)}) collective-permute-start(bf16[512,1024]{1,0:T(8,128)(2,1)S(1)} %collective-permute-done.64.refs_8_), channel_id=1, source_target_pairs={{0,1},{1,0},{2,3},{3,2},{4,5},{5,4},{6,7},{7,6},{8,9},{9,8},{10,11... | collective-permute-start | bytes 3145736 | tf_op jit(solution)/shard_map/ppermute | solution.py:27
  216.2 6.6 %collective-permute-done.29.a3.refs_3_ = bf16[128,1024]{1,0:T(8,128)(2,1)S(1)} collective-permute-done((bf16[128,1024]{1,0:T(8,128)(2,1)S(1)}, bf16[128,1024]{1,0:T(8,128)(2,1)S(1)}, u32[]{:S(2)}, u32[]{:S(2)}) %collective-permute-start.29) | collective-permute-done | bytes 262176 | tf_op jit(solution)/shard_map/ppermute | solution.py:27
  224.5 6.1 %shard_map.99 = (bf16[512,1024]{1,0:T(8,128)(2,1)}, bf16[512,1024]{1,0:T(8,128)(2,1)}) custom-call(s32[2]{0:T(128)} %pad_add_fusion.ids_ref, bf16[128,1024]{1,0:T(8,128)(2,1)} %copy-done.23, bf16[128,1024]{1,0:T(8,128)(2,1)} %copy-done.37, bf16[128,1024]{1,0:T(8,128)(2,1)} %copy-done.36, bf16[128,1024]{1,0:T(8,128)(2,1)} %copy-done.34, ...), custom_call_target="tpu_custom_call" | custom-call | flops 2147483648 | bytes 6291456 | tf_op jit(solution)/shard_map/pallas_call | solution.py:167
  230.5 2.0 collective-permute-start.53
  232.6 2.1 collective-permute-start.63
  235.5 2.1 collective-permute-done.57
  237.6 2.1 collective-permute-start.58
  239.7 10.3 %collective-permute-done.58 = bf16[64,1024]{1,0:T(8,128)(2,1)S(1)} collective-permute-done((bf16[64,1024]{1,0:T(8,128)(2,1)S(1)}, bf16[64,1024]{1,0:T(8,128)(2,1)S(1)}, u32[]{:S(2)}, u32[]{:S(2)}) %collective-permute-start.58) | collective-permute-done | bytes 131104 | tf_op jit(solution)/shard_map/ppermute | solution.py:27
  253.4 5.5 %shard_map.100.refs_12_ = bf16[1024,2048]{1,0:T(8,128)(2,1)} custom-call(s32[2]{0:T(128)} %pad_add_fusion.ids_ref, bf16[128,1024]{1,0:T(8,128)(2,1)} %bitcast.30, bf16[128,1024]{1,0:T(8,128)(2,1)} %copy-done.15, bf16[128,1024]{1,0:T(8,128)(2,1)} %copy-done.12, bf16[128,1024]{1,0:T(8,128)(2,1)} %copy-done.18, bf16[128,1024]{1,0:T(8,128)(2,1)} %copy-done.10, ...), custom_call_target="tpu_custom_call" | custom-call | bytes 8388608 | tf_op jit(solution)/shard_map/pallas_call | solution.py:193
  259.2 4.3 %collective-permute-done.61.refs_9_ = bf16[128,1024]{1,0:T(8,128)(2,1)S(1)} collective-permute-done((bf16[128,1024]{1,0:T(8,128)(2,1)S(1)}, bf16[128,1024]{1,0:T(8,128)(2,1)S(1)}, u32[]{:S(2)}, u32[]{:S(2)}) %collective-permute-start.61) | collective-permute-done | bytes 262176 | tf_op jit(solution)/shard_map/ppermute | solution.py:27
  264.5 2.3 collective-permute-start.55
  268.4 9.2 %shard_map.101 = f32[1024,1024]{1,0:T(8,128)} custom-call(s32[2]{0:T(128)} %pad_add_fusion.ids_ref, bf16[128,1024]{1,0:T(8,128)(2,1)} %copy-done.23, bf16[128,1024]{1,0:T(8,128)(2,1)} %copy-done.37, bf16[128,1024]{1,0:T(8,128)(2,1)} %copy-done.36, bf16[128,1024]{1,0:T(8,128)(2,1)} %copy-done.34, bf16[256,1024]{1,0:T(8,128)(2,1)} %copy-done.14, ...), custom_call_target="tpu_custom_call" | custom-call | flops 4294967296 | bytes 12582912 | tf_op jit(solution)/shard_map/pallas_call | solution.py:224
  (245 shorter events, 44.9 us)
Async XLA Ops:
  18.6 20.3 %collective-permute-start.30 = (bf16[256,2048]{1,0:T(8,128)(2,1)}, bf16[256,2048]{1,0:T(8,128)(2,1)}, u32[]{:S(2)}, u32[]{:S(2)}) collective-permute-start(bf16[256,2048]{1,0:T(8,128)(2,1)} %get-tuple-element.35), channel_id=1, source_target_pairs={{0,1},{1,0},{2,3},{3,2},{4,5},{5,4},{6,7},{7,6},{8,9},{9,8},{10,11... | collective-permute-start | bytes 3145736 | tf_op jit(solution)/shard_map/ppermute | solution.py:27
  35.0 31.0 %collective-permute-start.17 = (bf16[128,1024]{1,0:T(8,128)(2,1)S(1)}, bf16[128,1024]{1,0:T(8,128)(2,1)S(1)}, u32[]{:S(2)}, u32[]{:S(2)}) collective-permute-start(bf16[128,1024]{1,0:T(8,128)(2,1)S(1)} %bitcast.24), channel_id=1, source_target_pairs={{0,6},{2,4},{4,2},{6,0},{1,7},{3,5},{5,3},{7,1},{8,14},{10,12},{12... | collective-permute-start | bytes 786440 | tf_op jit(solution)/shard_map/ppermute | solution.py:27
  38.9 28.4 %collective-permute-start.15 = (bf16[128,1024]{1,0:T(8,128)(2,1)S(1)}, bf16[128,1024]{1,0:T(8,128)(2,1)S(1)}, u32[]{:S(2)}, u32[]{:S(2)}) collective-permute-start(bf16[128,1024]{1,0:T(8,128)(2,1)S(1)} %bitcast.25), channel_id=1, source_target_pairs={{0,4},{2,6},{4,0},{6,2},{1,5},{3,7},{5,1},{7,3},{8,12},{10,14},{12... | collective-permute-start | bytes 786440 | tf_op jit(solution)/shard_map/ppermute | solution.py:27
  41.0 21.0 %collective-permute-start.33 = (bf16[64,2048]{1,0:T(8,128)(2,1)S(1)}, bf16[64,2048]{1,0:T(8,128)(2,1)S(1)}, u32[]{:S(2)}, u32[]{:S(2)}) collective-permute-start(bf16[64,2048]{1,0:T(8,128)(2,1)S(1)} %get-tuple-element.50), channel_id=1, source_target_pairs={{0,6},{2,4},{4,2},{6,0},{1,7},{3,5},{5,3},{7,1},{8,14},{10,12},{12... | collective-permute-start | bytes 786440 | tf_op jit(solution)/shard_map/ppermute | solution.py:27
  43.6 18.4 %collective-permute-start.32 = (bf16[64,2048]{1,0:T(8,128)(2,1)S(1)}, bf16[64,2048]{1,0:T(8,128)(2,1)S(1)}, u32[]{:S(2)}, u32[]{:S(2)}) collective-permute-start(bf16[64,2048]{1,0:T(8,128)(2,1)S(1)} %get-tuple-element.51), channel_id=1, source_target_pairs={{0,4},{2,6},{4,0},{6,2},{1,5},{3,7},{5,1},{7,3},{8,12},{10,14},{12... | collective-permute-start | bytes 786440 | tf_op jit(solution)/shard_map/ppermute | solution.py:27
  51.2 17.7 %collective-permute-start.13 = (bf16[128,1024]{1,0:T(8,128)(2,1)S(1)}, bf16[128,1024]{1,0:T(8,128)(2,1)S(1)}, u32[]{:S(2)}, u32[]{:S(2)}) collective-permute-start(bf16[128,1024]{1,0:T(8,128)(2,1)S(1)} %bitcast.26), channel_id=1, source_target_pairs={{0,2},{2,0},{4,6},{6,4},{1,3},{3,1},{5,7},{7,5},{8,10},{10,8},{12,... | collective-permute-start | bytes 786440 | tf_op jit(solution)/shard_map/ppermute | solution.py:27
  67.3 22.5 %collective-permute-start.12 = (bf16[128,1024]{1,0:T(8,128)(2,1)S(1)}, bf16[128,1024]{1,0:T(8,128)(2,1)S(1)}, u32[]{:S(2)}, u32[]{:S(2)}) collective-permute-start(bf16[128,1024]{1,0:T(8,128)(2,1)S(1)} %bitcast.27), channel_id=1, source_target_pairs={{0,1},{1,0},{2,3},{3,2},{4,5},{5,4},{6,7},{7,6},{8,9},{9,8},{10,11... | collective-permute-start | bytes 786440 | tf_op jit(solution)/shard_map/ppermute | solution.py:27
  68.8 21.1 %collective-permute-start.18 = (bf16[128,1024]{1,0:T(8,128)(2,1)S(1)}, bf16[128,1024]{1,0:T(8,128)(2,1)S(1)}, u32[]{:S(2)}, u32[]{:S(2)}) collective-permute-start(bf16[128,1024]{1,0:T(8,128)(2,1)S(1)} %collective-permute-done.17.refs_14_.refs_6_), channel_id=1, source_target_pairs={{0,1},{1,0},{2,3},{3,2},{4,5},{5,4},{6,7},{7,6},{8,9},{9,8},{10,11... | collective-permute-start | bytes 786440 | tf_op jit(solution)/shard_map/ppermute | solution.py:27
  68.9 21.6 %collective-permute-start.16 = (bf16[128,1024]{1,0:T(8,128)(2,1)S(1)}, bf16[128,1024]{1,0:T(8,128)(2,1)S(1)}, u32[]{:S(2)}, u32[]{:S(2)}) collective-permute-start(bf16[128,1024]{1,0:T(8,128)(2,1)S(1)} %collective-permute-done.15.refs_12_.refs_4_), channel_id=1, source_target_pairs={{0,1},{1,0},{2,3},{3,2},{4,5},{5,4},{6,7},{7,6},{8,9},{9,8},{10,11... | collective-permute-start | bytes 786440 | tf_op jit(solution)/shard_map/ppermute | solution.py:27
  72.3 21.1 %collective-permute-start.14 = (bf16[128,1024]{1,0:T(8,128)(2,1)S(1)}, bf16[128,1024]{1,0:T(8,128)(2,1)S(1)}, u32[]{:S(2)}, u32[]{:S(2)}) collective-permute-start(bf16[128,1024]{1,0:T(8,128)(2,1)S(1)} %collective-permute-done.13.refs_10_.refs_2_), channel_id=1, source_target_pairs={{0,1},{1,0},{2,3},{3,2},{4,5},{5,4},{6,7},{7,6},{8,9},{9,8},{10,11... | collective-permute-start | bytes 786440 | tf_op jit(solution)/shard_map/ppermute | solution.py:27
  84.7 16.1 %collective-permute-start.40 = (bf16[64,2048]{1,0:T(8,128)(2,1)S(1)}, bf16[64,2048]{1,0:T(8,128)(2,1)S(1)}, u32[]{:S(2)}, u32[]{:S(2)}) collective-permute-start(bf16[64,2048]{1,0:T(8,128)(2,1)S(1)} %pad_maximum_fusion.4.refs_0_), channel_id=1, source_target_pairs={{0,6},{2,4},{4,2},{6,0},{1,7},{3,5},{5,3},{7,1},{8,14},{10,12},{12... | collective-permute-start | bytes 786440 | tf_op jit(solution)/shard_map/ppermute | solution.py:27
  89.8 11.6 %collective-permute-start.38 = (bf16[64,2048]{1,0:T(8,128)(2,1)S(1)}, bf16[64,2048]{1,0:T(8,128)(2,1)S(1)}, u32[]{:S(2)}, u32[]{:S(2)}) collective-permute-start(bf16[64,2048]{1,0:T(8,128)(2,1)S(1)} %pad_maximum_fusion.4.refs_0_), channel_id=1, source_target_pairs={{0,4},{2,6},{4,0},{6,2},{1,5},{3,7},{5,1},{7,3},{8,12},{10,14},{12... | collective-permute-start | bytes 786440 | tf_op jit(solution)/shard_map/ppermute | solution.py:27
  89.9 14.9 %collective-permute-start.36 = (bf16[64,2048]{1,0:T(8,128)(2,1)S(1)}, bf16[64,2048]{1,0:T(8,128)(2,1)S(1)}, u32[]{:S(2)}, u32[]{:S(2)}) collective-permute-start(bf16[64,2048]{1,0:T(8,128)(2,1)S(1)} %pad_maximum_fusion.4.refs_0_), channel_id=1, source_target_pairs={{0,2},{2,0},{4,6},{6,4},{1,3},{3,1},{5,7},{7,5},{8,10},{10,8},{12,... | collective-permute-start | bytes 786440 | tf_op jit(solution)/shard_map/ppermute | solution.py:27
  90.5 16.5 %collective-permute-start.35 = (bf16[64,2048]{1,0:T(8,128)(2,1)S(1)}, bf16[64,2048]{1,0:T(8,128)(2,1)S(1)}, u32[]{:S(2)}, u32[]{:S(2)}) collective-permute-start(bf16[64,2048]{1,0:T(8,128)(2,1)S(1)} %pad_maximum_fusion.4.refs_0_), channel_id=1, source_target_pairs={{0,1},{1,0},{2,3},{3,2},{4,5},{5,4},{6,7},{7,6},{8,9},{9,8},{10,11... | collective-permute-start | bytes 786440 | tf_op jit(solution)/shard_map/ppermute | solution.py:27
  93.4 17.5 %collective-permute-start.10 = (bf16[64,2048]{1,0:T(8,128)(2,1)S(1)}, bf16[64,2048]{1,0:T(8,128)(2,1)S(1)}, u32[]{:S(2)}, u32[]{:S(2)}) collective-permute-start(bf16[64,2048]{1,0:T(8,128)(2,1)S(1)} %pad_maximum_fusion.2.refs_0_), channel_id=1, source_target_pairs={{0,6},{2,4},{4,2},{6,0},{1,7},{3,5},{5,3},{7,1},{8,14},{10,12},{12... | collective-permute-start | bytes 786440 | tf_op jit(solution)/shard_map/ppermute | solution.py:27
  100.9 12.7 %collective-permute-start.8 = (bf16[64,2048]{1,0:T(8,128)(2,1)S(1)}, bf16[64,2048]{1,0:T(8,128)(2,1)S(1)}, u32[]{:S(2)}, u32[]{:S(2)}) collective-permute-start(bf16[64,2048]{1,0:T(8,128)(2,1)S(1)} %pad_maximum_fusion.2.refs_0_), channel_id=1, source_target_pairs={{0,4},{2,6},{4,0},{6,2},{1,5},{3,7},{5,1},{7,3},{8,12},{10,14},{12... | collective-permute-start | bytes 786440 | tf_op jit(solution)/shard_map/ppermute | solution.py:27
  101.4 13.9 %collective-permute-start.6 = (bf16[64,2048]{1,0:T(8,128)(2,1)S(1)}, bf16[64,2048]{1,0:T(8,128)(2,1)S(1)}, u32[]{:S(2)}, u32[]{:S(2)}) collective-permute-start(bf16[64,2048]{1,0:T(8,128)(2,1)S(1)} %pad_maximum_fusion.2.refs_0_), channel_id=1, source_target_pairs={{0,2},{2,0},{4,6},{6,4},{1,3},{3,1},{5,7},{7,5},{8,10},{10,8},{12,... | collective-permute-start | bytes 786440 | tf_op jit(solution)/shard_map/ppermute | solution.py:27
  104.9 12.9 %collective-permute-start.41 = (bf16[64,2048]{1,0:T(8,128)(2,1)S(1)}, bf16[64,2048]{1,0:T(8,128)(2,1)S(1)}, u32[]{:S(2)}, u32[]{:S(2)}) collective-permute-start(bf16[64,2048]{1,0:T(8,128)(2,1)S(1)} %collective-permute-done.40.refs_6_), channel_id=1, source_target_pairs={{0,1},{1,0},{2,3},{3,2},{4,5},{5,4},{6,7},{7,6},{8,9},{9,8},{10,11... | collective-permute-start | bytes 786440 | tf_op jit(solution)/shard_map/ppermute | solution.py:27
  113.6 16.6 %collective-permute-start.5 = (bf16[64,2048]{1,0:T(8,128)(2,1)S(1)}, bf16[64,2048]{1,0:T(8,128)(2,1)S(1)}, u32[]{:S(2)}, u32[]{:S(2)}) collective-permute-start(bf16[64,2048]{1,0:T(8,128)(2,1)S(1)} %pad_maximum_fusion.2.refs_0_), channel_id=1, source_target_pairs={{0,1},{1,0},{2,3},{3,2},{4,5},{5,4},{6,7},{7,6},{8,9},{9,8},{10,11... | collective-permute-start | bytes 786440 | tf_op jit(solution)/shard_map/ppermute | solution.py:27
  115.3 16.1 %collective-permute-start.11 = (bf16[64,2048]{1,0:T(8,128)(2,1)S(1)}, bf16[64,2048]{1,0:T(8,128)(2,1)S(1)}, u32[]{:S(2)}, u32[]{:S(2)}) collective-permute-start(bf16[64,2048]{1,0:T(8,128)(2,1)S(1)} %collective-permute-done.10.refs_6_), channel_id=1, source_target_pairs={{0,1},{1,0},{2,3},{3,2},{4,5},{5,4},{6,7},{7,6},{8,9},{9,8},{10,11... | collective-permute-start | bytes 786440 | tf_op jit(solution)/shard_map/ppermute | solution.py:27
  117.8 14.0 %collective-permute-start.9 = (bf16[64,2048]{1,0:T(8,128)(2,1)S(1)}, bf16[64,2048]{1,0:T(8,128)(2,1)S(1)}, u32[]{:S(2)}, u32[]{:S(2)}) collective-permute-start(bf16[64,2048]{1,0:T(8,128)(2,1)S(1)} %collective-permute-done.8.refs_4_), channel_id=1, source_target_pairs={{0,1},{1,0},{2,3},{3,2},{4,5},{5,4},{6,7},{7,6},{8,9},{9,8},{10,11... | collective-permute-start | bytes 786440 | tf_op jit(solution)/shard_map/ppermute | solution.py:27
  117.9 16.6 %collective-permute-start.7 = (bf16[64,2048]{1,0:T(8,128)(2,1)S(1)}, bf16[64,2048]{1,0:T(8,128)(2,1)S(1)}, u32[]{:S(2)}, u32[]{:S(2)}) collective-permute-start(bf16[64,2048]{1,0:T(8,128)(2,1)S(1)} %collective-permute-done.6.refs_2_), channel_id=1, source_target_pairs={{0,1},{1,0},{2,3},{3,2},{4,5},{5,4},{6,7},{7,6},{8,9},{9,8},{10,11... | collective-permute-start | bytes 786440 | tf_op jit(solution)/shard_map/ppermute | solution.py:27
  131.5 16.5 %collective-permute-start.44 = (bf16[64,1024]{1,0:T(8,128)(2,1)S(1)}, bf16[64,1024]{1,0:T(8,128)(2,1)S(1)}, u32[]{:S(2)}, u32[]{:S(2)}) collective-permute-start(bf16[64,1024]{1,0:T(8,128)(2,1)S(1)} %copy-done.54), channel_id=1, source_target_pairs={{0,24},{8,16},{16,8},{24,0},{32,56},{40,48},{48,40},{56,32},{1,25}... | collective-permute-start | bytes 393224 | tf_op jit(solution)/shard_map/ppermute | solution.py:27
  131.8 17.2 %collective-permute-start.45 = (bf16[64,1024]{1,0:T(8,128)(2,1)S(1)}, bf16[64,1024]{1,0:T(8,128)(2,1)S(1)}, u32[]{:S(2)}, u32[]{:S(2)}) collective-permute-start(bf16[64,1024]{1,0:T(8,128)(2,1)S(1)} %copy-done.53), channel_id=1, source_target_pairs={{0,32},{8,40},{16,48},{24,56},{32,0},{40,8},{48,16},{56,24},{1,33}... | collective-permute-start | bytes 393224 | tf_op jit(solution)/shard_map/ppermute | solution.py:27
  134.5 17.2 %collective-permute-start.46 = (bf16[64,1024]{1,0:T(8,128)(2,1)S(1)}, bf16[64,1024]{1,0:T(8,128)(2,1)S(1)}, u32[]{:S(2)}, u32[]{:S(2)}) collective-permute-start(bf16[64,1024]{1,0:T(8,128)(2,1)S(1)} %copy-done.52), channel_id=1, source_target_pairs={{0,40},{8,32},{16,56},{24,48},{32,8},{40,0},{48,24},{56,16},{1,41}... | collective-permute-start | bytes 393224 | tf_op jit(solution)/shard_map/ppermute | solution.py:27
  137.3 14.4 %collective-permute-start.47 = (bf16[64,1024]{1,0:T(8,128)(2,1)S(1)}, bf16[64,1024]{1,0:T(8,128)(2,1)S(1)}, u32[]{:S(2)}, u32[]{:S(2)}) collective-permute-start(bf16[64,1024]{1,0:T(8,128)(2,1)S(1)} %copy-done.51), channel_id=1, source_target_pairs={{0,48},{8,56},{16,32},{24,40},{32,16},{40,24},{48,0},{56,8},{1,49}... | collective-permute-start | bytes 393224 | tf_op jit(solution)/shard_map/ppermute | solution.py:27
  139.8 13.4 %collective-permute-start.48 = (bf16[64,1024]{1,0:T(8,128)(2,1)S(1)}, bf16[64,1024]{1,0:T(8,128)(2,1)S(1)}, u32[]{:S(2)}, u32[]{:S(2)}) collective-permute-start(bf16[64,1024]{1,0:T(8,128)(2,1)S(1)} %copy-done.50), channel_id=1, source_target_pairs={{0,56},{8,48},{16,40},{24,32},{32,24},{40,16},{48,8},{56,0},{1,57}... | collective-permute-start | bytes 393224 | tf_op jit(solution)/shard_map/ppermute | solution.py:27
  147.9 64.0 %collective-permute-start.64 = (bf16[512,1024]{1,0:T(8,128)(2,1)S(1)}, bf16[512,1024]{1,0:T(8,128)(2,1)S(1)}, u32[]{:S(2)}, u32[]{:S(2)}) collective-permute-start(bf16[512,1024]{1,0:T(8,128)(2,1)S(1)} %pad_maximum_fusion), channel_id=1, source_target_pairs={{0,64},{64,0},{1,65},{65,1},{2,66},{66,2},{3,67},{67,3},{4,68},{68... | collective-permute-start | bytes 3145736 | tf_op jit(solution)/shard_map/ppermute | solution.py:27
  149.1 28.8 %collective-permute-start.19 = (bf16[64,1024]{1,0:T(8,128)(2,1)}, bf16[64,1024]{1,0:T(8,128)(2,1)S(1)}, u32[]{:S(2)}, u32[]{:S(2)}) collective-permute-start(bf16[64,1024]{1,0:T(8,128)(2,1)} %get-tuple-element.27), channel_id=1, source_target_pairs={{0,8},{8,0},{16,24},{24,16},{32,40},{40,32},{48,56},{56,48},{1,9},... | collective-permute-start | bytes 393224 | tf_op jit(solution)/shard_map/ppermute | solution.py:27
  151.7 27.7 %collective-permute-start.20 = (bf16[64,1024]{1,0:T(8,128)(2,1)}, bf16[64,1024]{1,0:T(8,128)(2,1)S(1)}, u32[]{:S(2)}, u32[]{:S(2)}) collective-permute-start(bf16[64,1024]{1,0:T(8,128)(2,1)} %get-tuple-element.28), channel_id=1, source_target_pairs={{0,16},{8,24},{16,0},{24,8},{32,48},{40,56},{48,32},{56,40},{1,17}... | collective-permute-start | bytes 393224 | tf_op jit(solution)/shard_map/ppermute | solution.py:27
  151.7 29.2 %collective-permute-start.21 = (bf16[64,1024]{1,0:T(8,128)(2,1)}, bf16[64,1024]{1,0:T(8,128)(2,1)S(1)}, u32[]{:S(2)}, u32[]{:S(2)}) collective-permute-start(bf16[64,1024]{1,0:T(8,128)(2,1)} %get-tuple-element.29), channel_id=1, source_target_pairs={{0,24},{8,16},{16,8},{24,0},{32,56},{40,48},{48,40},{56,32},{1,25}... | collective-permute-start | bytes 393224 | tf_op jit(solution)/shard_map/ppermute | solution.py:27
  153.4 28.1 %collective-permute-start.51 = (bf16[64,1024]{1,0:T(8,128)(2,1)S(1)}, bf16[64,1024]{1,0:T(8,128)(2,1)S(1)}, u32[]{:S(2)}, u32[]{:S(2)}) collective-permute-start(bf16[64,1024]{1,0:T(8,128)(2,1)S(1)} %fusion.2), channel_id=1, source_target_pairs={{0,48},{16,32},{32,16},{48,0},{1,49},{17,33},{33,17},{49,1},{2,50}... | collective-permute-start | bytes 393224 | tf_op jit(solution)/shard_map/ppermute | solution.py:27
  186.4 11.8 %collective-permute-start.25 = (bf16[64,1024]{1,0:T(8,128)(2,1)}, bf16[64,1024]{1,0:T(8,128)(2,1)S(1)}, u32[]{:S(2)}, u32[]{:S(2)}) collective-permute-start(bf16[64,1024]{1,0:T(8,128)(2,1)} %get-tuple-element.33), channel_id=1, source_target_pairs={{0,56},{8,48},{16,40},{24,32},{32,24},{40,16},{48,8},{56,0},{1,57}... | collective-permute-start | bytes 393224 | tf_op jit(solution)/shard_map/ppermute | solution.py:27
  189.0 33.8 %collective-permute-start.52 = (bf16[256,1024]{1,0:T(8,128)(2,1)S(1)}, bf16[256,1024]{1,0:T(8,128)(2,1)S(1)}, u32[]{:S(2)}, u32[]{:S(2)}) collective-permute-start(bf16[256,1024]{1,0:T(8,128)(2,1)S(1)} %pad_maximum_fusion.1.b0.refs_4_), channel_id=1, source_target_pairs={{0,8},{8,0},{64,72},{72,64},{1,9},{9,1},{65,73},{73,65},{2,10},{10... | collective-permute-start | bytes 1572872 | tf_op jit(solution)/shard_map/ppermute | solution.py:27
  208.6 14.1 %collective-permute-start.29 = (bf16[128,1024]{1,0:T(8,128)(2,1)S(1)}, bf16[128,1024]{1,0:T(8,128)(2,1)S(1)}, u32[]{:S(2)}, u32[]{:S(2)}) collective-permute-start(bf16[128,1024]{1,0:T(8,128)(2,1)S(1)} %pad_maximum_fusion.3.a0.refs_0_), channel_id=1, source_target_pairs={{0,48},{16,32},{32,16},{48,0},{1,49},{17,33},{33,17},{49,1},{2,50}... | collective-permute-start | bytes 786440 | tf_op jit(solution)/shard_map/ppermute | solution.py:27
  209.1 13.7 %collective-permute-start.28 = (bf16[128,1024]{1,0:T(8,128)(2,1)S(1)}, bf16[128,1024]{1,0:T(8,128)(2,1)S(1)}, u32[]{:S(2)}, u32[]{:S(2)}) collective-permute-start(bf16[128,1024]{1,0:T(8,128)(2,1)S(1)} %pad_maximum_fusion.3.a0.refs_0_), channel_id=1, source_target_pairs={{0,32},{16,48},{32,0},{48,16},{1,33},{17,49},{33,1},{49,17},{2,34}... | collective-permute-start | bytes 786440 | tf_op jit(solution)/shard_map/ppermute | solution.py:27
  209.2 13.5 %collective-permute-start.27 = (bf16[128,1024]{1,0:T(8,128)(2,1)S(1)}, bf16[128,1024]{1,0:T(8,128)(2,1)S(1)}, u32[]{:S(2)}, u32[]{:S(2)}) collective-permute-start(bf16[128,1024]{1,0:T(8,128)(2,1)S(1)} %pad_maximum_fusion.3.a0.refs_0_), channel_id=1, source_target_pairs={{0,16},{16,0},{32,48},{48,32},{1,17},{17,1},{33,49},{49,33},{2,18}... | collective-permute-start | bytes 786440 | tf_op jit(solution)/shard_map/ppermute | solution.py:27
  211.9 39.9 %collective-permute-start.65 = (bf16[512,1024]{1,0:T(8,128)(2,1)S(1)}, bf16[512,1024]{1,0:T(8,128)(2,1)S(1)}, u32[]{:S(2)}, u32[]{:S(2)}) collective-permute-start(bf16[512,1024]{1,0:T(8,128)(2,1)S(1)} %collective-permute-done.64.refs_8_), channel_id=1, source_target_pairs={{0,1},{1,0},{2,3},{3,2},{4,5},{5,4},{6,7},{7,6},{8,9},{9,8},{10,11... | collective-permute-start | bytes 3145736 | tf_op jit(solution)/shard_map/ppermute | solution.py:27
  230.5 21.4 %collective-permute-start.53 = (bf16[512,1024]{1,0:T(8,128)(2,1)}, bf16[512,1024]{1,0:T(8,128)(2,1)S(1)}, u32[]{:S(2)}, u32[]{:S(2)}) collective-permute-start(bf16[512,1024]{1,0:T(8,128)(2,1)} %get-tuple-element.45), channel_id=1, source_target_pairs={{0,1},{1,0},{2,3},{3,2},{4,5},{5,4},{6,7},{7,6},{8,9},{9,8},{10,11... | collective-permute-start | bytes 3145736 | tf_op jit(solution)/shard_map/ppermute | solution.py:27
  232.6 34.2 %collective-permute-start.63 = (bf16[256,1024]{1,0:T(8,128)(2,1)}, bf16[256,1024]{1,0:T(8,128)(2,1)S(1)}, u32[]{:S(2)}, u32[]{:S(2)}) collective-permute-start(bf16[256,1024]{1,0:T(8,128)(2,1)} %copy-done.14), channel_id=1, source_target_pairs={{0,72},{8,64},{64,8},{72,0},{1,73},{9,65},{65,9},{73,1},{2,74},{10... | collective-permute-start | bytes 1572872 | tf_op jit(solution)/shard_map/ppermute | solution.py:27
  234.7 32.2 %collective-permute-start.62 = (bf16[256,1024]{1,0:T(8,128)(2,1)}, bf16[256,1024]{1,0:T(8,128)(2,1)S(1)}, u32[]{:S(2)}, u32[]{:S(2)}) collective-permute-start(bf16[256,1024]{1,0:T(8,128)(2,1)} %copy-done.14), channel_id=1, source_target_pairs={{0,64},{8,72},{64,0},{72,8},{1,65},{9,73},{65,1},{73,9},{2,66},{10... | collective-permute-start | bytes 1572872 | tf_op jit(solution)/shard_map/ppermute | solution.py:27
  237.6 12.4 %collective-permute-start.58 = (bf16[64,1024]{1,0:T(8,128)(2,1)S(1)}, bf16[64,1024]{1,0:T(8,128)(2,1)S(1)}, u32[]{:S(2)}, u32[]{:S(2)}) collective-permute-start(bf16[64,1024]{1,0:T(8,128)(2,1)S(1)} %fusion.4), channel_id=1, source_target_pairs={{0,72},{8,64},{64,8},{72,0},{1,73},{9,65},{65,9},{73,1},{2,74},{10... | collective-permute-start | bytes 393224 | tf_op jit(solution)/shard_map/ppermute | solution.py:27
  250.0 13.5 %collective-permute-start.61 = (bf16[128,1024]{1,0:T(8,128)(2,1)S(1)}, bf16[128,1024]{1,0:T(8,128)(2,1)S(1)}, u32[]{:S(2)}, u32[]{:S(2)}) collective-permute-start(bf16[128,1024]{1,0:T(8,128)(2,1)S(1)} %constant_dynamic-update-slice_fusion.refs_6_), channel_id=1, source_target_pairs={{0,48},{16,32},{32,16},{48,0},{1,49},{17,33},{33,17},{49,1},{2,50}... | collective-permute-start | bytes 786440 | tf_op jit(solution)/shard_map/ppermute | solution.py:27
  251.8 11.7 %collective-permute-start.60 = (bf16[128,1024]{1,0:T(8,128)(2,1)S(1)}, bf16[128,1024]{1,0:T(8,128)(2,1)S(1)}, u32[]{:S(2)}, u32[]{:S(2)}) collective-permute-start(bf16[128,1024]{1,0:T(8,128)(2,1)S(1)} %constant_dynamic-update-slice_fusion.refs_6_), channel_id=1, source_target_pairs={{0,32},{16,48},{32,0},{48,16},{1,33},{17,49},{33,1},{49,17},{2,34}... | collective-permute-start | bytes 786440 | tf_op jit(solution)/shard_map/ppermute | solution.py:27
  251.9 12.5 %collective-permute-start.59 = (bf16[128,1024]{1,0:T(8,128)(2,1)S(1)}, bf16[128,1024]{1,0:T(8,128)(2,1)S(1)}, u32[]{:S(2)}, u32[]{:S(2)}) collective-permute-start(bf16[128,1024]{1,0:T(8,128)(2,1)S(1)} %constant_dynamic-update-slice_fusion.refs_6_), channel_id=1, source_target_pairs={{0,16},{16,0},{32,48},{48,32},{1,17},{17,1},{33,49},{49,33},{2,18}... | collective-permute-start | bytes 786440 | tf_op jit(solution)/shard_map/ppermute | solution.py:27
  263.5 14.1 %collective-permute-start.54 = (bf16[128,1024]{1,0:T(8,128)(2,1)S(1)}, bf16[128,1024]{1,0:T(8,128)(2,1)S(1)}, u32[]{:S(2)}, u32[]{:S(2)}) collective-permute-start(bf16[128,1024]{1,0:T(8,128)(2,1)S(1)} %get-tuple-element.46), channel_id=1, source_target_pairs={{0,2},{2,0},{4,6},{6,4},{1,3},{3,1},{5,7},{7,5},{8,10},{10,8},{12,... | collective-permute-start | bytes 786440 | tf_op jit(solution)/shard_map/ppermute | solution.py:27
  263.6 14.1 %collective-permute-start.56 = (bf16[128,1024]{1,0:T(8,128)(2,1)S(1)}, bf16[128,1024]{1,0:T(8,128)(2,1)S(1)}, u32[]{:S(2)}, u32[]{:S(2)}) collective-permute-start(bf16[128,1024]{1,0:T(8,128)(2,1)S(1)} %get-tuple-element.47), channel_id=1, source_target_pairs={{0,6},{2,4},{4,2},{6,0},{1,7},{3,5},{5,3},{7,1},{8,14},{10,12},{12... | collective-permute-start | bytes 786440 | tf_op jit(solution)/shard_map/ppermute | solution.py:27
  264.5 13.2 %collective-permute-start.55 = (bf16[128,1024]{1,0:T(8,128)(2,1)S(1)}, bf16[128,1024]{1,0:T(8,128)(2,1)S(1)}, u32[]{:S(2)}, u32[]{:S(2)}) collective-permute-start(bf16[128,1024]{1,0:T(8,128)(2,1)S(1)} %get-tuple-element.48), channel_id=1, source_target_pairs={{0,4},{2,6},{4,0},{6,2},{1,5},{3,7},{5,1},{7,3},{8,12},{10,14},{12... | collective-permute-start | bytes 786440 | tf_op jit(solution)/shard_map/ppermute | solution.py:27
  (73 other events, 919.9 us)

commit v2 on v0

v2 whole, which is shorter than its diff:
```python
import functools
import math

import jax
import jax.numpy as jnp
from jax import lax
from jax.experimental import pallas as pl
from jax.experimental.pallas import tpu as pltpu
from jax.sharding import Mesh, PartitionSpec as P

BF16 = jnp.bfloat16
F32 = jnp.float32
SPAN = 2
LONG = 50
SHORT = 0.01
X = "x"
Z = "z"
CORE = "core"
GRP = "grp"
DP = ("x", "yh")
Y = ("grp", "yh")
SIZES = {"grp": 2, "x": 4, "yh": 2, "z": 4, "core": 2}
VMEM_LIMIT = 62 * 1024 * 1024


def swap(array, axes, distance):
    names = axes if isinstance(axes, tuple) else (axes,)
    size = math.prod(SIZES[name] for name in names)
    return lax.ppermute(array, axes, [(i, i ^ distance) for i in range(size)])


def params():
    return pltpu.CompilerParams(vmem_limit_bytes=VMEM_LIMIT)


def call(micros, body, grid, out_shape, in_specs, out_specs, scratch, *args):
    return pl.pallas_call(
        body,
        grid=grid,
        out_shape=out_shape,
        in_specs=in_specs,
        out_specs=out_specs,
        scratch_shapes=scratch,
        compiler_params=params(),
        cost_estimate=pl.CostEstimate(
            flops=int(micros * 1e9), bytes_accessed=1024, transcendentals=0
        ),
    )(*args)


def whole(array):
    return pl.BlockSpec(array.shape, lambda *_: (0,) * array.ndim)


def smem():
    return pl.BlockSpec(memory_space=pltpu.SMEM)


def unread():
    return pl.BlockSpec(memory_space=pl.ANY)


def shape(rows, columns, kind=BF16):
    return jax.ShapeDtypeStruct((rows, columns), kind)


def nn(a, b):
    return jnp.dot(a, b, preferred_element_type=F32)


def nt(a, b):
    return lax.dot_general(a, b, (((1,), (1,)), ((), ())), preferred_element_type=F32)


def with_unread(body, count):
    return lambda *refs: body(*refs[count:])


def one_hot(hits):
    return jnp.where(hits, 1.0, 0.0).astype(BF16)


def pick_rows(piece, ids_ref, order_ref, x_ref, a_ref, o_ref, pick_ref):
    rows, size = pick_ref.shape[0], o_ref.shape[1]
    t, g = ids_ref[1], ids_ref[2]
    to = lax.broadcasted_iota(jnp.int32, (rows, rows), 0)
    at = lax.broadcasted_iota(jnp.int32, (rows, rows), 1)
    far = to // (piece * SPAN)
    owner = ((far % 2) ^ g) * 8 + (t ^ (((far // 2) % 4) * 2 + far // 8))
    wanted = one_hot(at == ((to // piece) % SPAN) * size + owner * piece + to % piece)
    line = lax.broadcasted_iota(jnp.int32, (size, size), 0)

    def part(k, _):
        for b in range(SPAN):
            order = order_ref[pl.ds(g * 8 + k * SPAN + b, 1), :]
            columns = slice(b * size, (b + 1) * size)
            pick_ref[:, columns] = nt(wanted[:, columns], one_hot(line == order)).astype(BF16)
        here = pl.ds(pl.multiple_of(k * rows, rows), rows)
        a_ref[here, :] = nn(pick_ref[...], x_ref[here, :]).astype(BF16)
        mine = t - k * SPAN
        inside = jnp.logical_and(mine >= 0, mine < SPAN).astype(F32)
        start = pl.multiple_of(jnp.clip(mine, 0, SPAN - 1) * size, size)
        o_ref[here, :] = (pick_ref[:, pl.ds(start, size)].astype(F32) * inside).astype(BF16)
        return 0

    lax.fori_loop(0, x_ref.shape[0] // rows, part, 0)


def teacher_tile(piece, a_ref, o_ref, w_ref, s_ref, mine_ref, peer_ref):
    group = piece * SPAN
    parts = a_ref.shape[0] // (16 * group)
    out = (nn(a_ref[...], w_ref[...]) + nn(o_ref[...], s_ref[...])).astype(BF16)
    for k in range(parts):
        for far in range(16):
            start = (k * 16 + far) * group
            to = ((far % 8) * parts + k) * group
            (mine_ref, peer_ref)[far // 8][to : to + group, :] = out[start : start + group]


def first_teacher_kernel(piece, ids_ref, order_ref, x_ref, w_ref, s_ref, *rest):
    mine_ref, peer_ref, a_ref, o_ref, pick_ref = rest

    @pl.when(pl.program_id(0) == 0)
    def _():
        pick_rows(piece, ids_ref, order_ref, x_ref, a_ref, o_ref, pick_ref)

    teacher_tile(piece, a_ref, o_ref, w_ref, s_ref, mine_ref, peer_ref)


def second_teacher_kernel(piece, a_ref, o_ref, w_ref, s_ref, mine_ref, peer_ref):
    teacher_tile(piece, a_ref, o_ref, w_ref, s_ref, mine_ref, peer_ref)


def first_teacher(ids, order, values, weight, stream, tile=512):
    rows, depth = values.shape
    width, size = weight.shape[1] // 2, stream.shape[0]
    piece = order.shape[1] // 16
    return call(
        LONG,
        functools.partial(first_teacher_kernel, piece),
        (width // tile,),
        [shape(rows // 2, width)] * 2 + [shape(rows, depth), shape(rows, size)],
        [
            smem(),
            whole(order),
            whole(values),
            pl.BlockSpec((depth, tile), lambda j: (0, j)),
            pl.BlockSpec((size, tile), lambda j: (0, j)),
        ],
        [pl.BlockSpec((rows // 2, tile), lambda j: (0, j))] * 2
        + [pl.BlockSpec((rows, depth), lambda j: (0, 0)), pl.BlockSpec((rows, size), lambda j: (0, 0))],
        [pltpu.VMEM((SPAN * size, SPAN * size), BF16)],
        ids,
        order,
        values,
        weight,
        stream,
    )


def second_teacher(picked, owned, weight, stream, piece, after, tile=512):
    rows, depth = picked.shape
    width, size = weight.shape[1] // 2, stream.shape[0]
    skip = width // tile
    return call(
        LONG,
        with_unread(functools.partial(second_teacher_kernel, piece), len(after)),
        (width // tile,),
        [shape(rows // 2, width)] * 2,
        [unread()] * len(after)
        + [
            whole(picked),
            whole(owned),
            pl.BlockSpec((depth, tile), lambda j: (0, j + skip)),
            pl.BlockSpec((size, tile), lambda j: (0, j + skip)),
        ],
        [pl.BlockSpec((rows // 2, tile), lambda j: (0, j))] * 2,
        [],
        *after,
        picked,
        owned,
        weight,
        stream,
    )


def merge_kernel(count, *refs):
    total = refs[0][...].astype(F32)
    for ref in refs[1:count]:
        total = total + ref[...].astype(F32)
    outs = refs[count:]
    rows = total.shape[0] // len(outs)
    for k, out in enumerate(outs):
        out[...] = total[k * rows : (k + 1) * rows].astype(BF16)


def merged(terms, pieces, after=(), micros=SHORT, steps=2):
    rows, width = terms[0].shape
    tile = width // steps
    return call(
        micros,
        with_unread(functools.partial(merge_kernel, len(terms)), len(after)),
        (steps,),
        [shape(rows // pieces, width)] * pieces,
        [unread()] * len(after) + [pl.BlockSpec((rows, tile), lambda j: (0, j))] * len(terms),
        [pl.BlockSpec((rows // pieces, tile), lambda j: (0, j))] * pieces,
        [],
        *after,
        *terms,
    )


def layer_kernel(ids_ref, near_ref, pair_ref, w_ref, out_ref, v_ref):
    block = v_ref.shape[0] // 8

    @pl.when(pl.program_id(0) == 0)
    def _():
        for k in range(8):
            place = (ids_ref[1] ^ k) * block
            ref = (near_ref, pair_ref)[k & 1]
            start = (k >> 1) * block
            v_ref[pl.ds(pl.multiple_of(place, block), block), :] = ref[start : start + block, :]

    out_ref[...] = nn(v_ref[...], w_ref[...])


def layer(ids, near, pair, weight, after, tile=512):
    rows = 2 * near.shape[0]
    depth, width = weight.shape
    return call(
        LONG,
        with_unread(layer_kernel, len(after)),
        (width // tile,),
        shape(rows, width, F32),
        [unread()] * len(after)
        + [smem(), whole(near), whole(pair), pl.BlockSpec((depth, tile), lambda j: (0, j))],
        pl.BlockSpec((rows, tile), lambda j: (0, j)),
        [pltpu.VMEM((rows, depth), BF16)],
        *after,
        ids,
        near,
        pair,
        weight,
    )


def target_kernel(ids_ref, *refs):
    hidden = refs[:6]
    l_ref, p_ref = refs[6:8]
    outs, h_ref = refs[8:-1], refs[-1]
    piece = hidden[0].shape[0]
    blocks = [(0, 0, 0), (2, 1, 0), (6, 2, 0), (4, 3, 0), (1, 4, 0), (3, 5, 0), (7, 5, 1), (5, 5, 2)]

    @pl.when(pl.program_id(0) == 0)
    def _():
        for far, k, start in blocks:
            at = pl.multiple_of((ids_ref[1] ^ far) * piece, piece)
            h_ref[pl.ds(at, piece), :] = hidden[k][start * piece : (start + 1) * piece, :]

    out = l_ref[...] - nn(h_ref[...], p_ref[...])
    rows = out.shape[0] // len(outs)
    for k, to in enumerate(outs):
        to[...] = out[k * rows : (k + 1) * rows].astype(to.dtype)


def less_target(ids, hidden, left, projection, half, outs, kind, after=(), tile=512):
    piece, deep = hidden[0].shape
    width = projection.shape[1]
    rows = 8 * piece
    return call(
        LONG,
        with_unread(target_kernel, len(after)),
        (width // tile,),
        [shape(rows // outs, width, kind)] * outs,
        [unread()] * len(after)
        + [smem()]
        + [whole(h) for h in hidden]
        + [pl.BlockSpec((rows, tile), lambda j: (0, j)), pl.BlockSpec((deep, tile), lambda j: (half, j))],
        [pl.BlockSpec((rows // outs, tile), lambda j: (0, j))] * outs,
        [pltpu.VMEM((rows, deep), BF16)],
        *after,
        ids,
        *hidden,
        left,
        projection,
    )


def gap_places(gaps, halves):
    piece = gaps[0].shape[0] // 4
    for half in range(halves):
        for e in range(4):
            for n in range(2):
                yield 2 * e + n, half, 0, gaps[e], (2 * half + n) * piece
                yield 2 * e + n, half, 1, gaps[4 + 2 * half + n], e * piece


def values_kernel(ids_ref, *refs):
    gaps = refs[:8]
    w_ref, mine_ref, peer_ref, g_ref = refs[8:]
    piece = gaps[0].shape[0] // 4
    rows = g_ref.shape[0]

    @pl.when(pl.program_id(0) == 0)
    def _():
        for k, _, part, ref, start in gap_places(gaps, 1):
            to = ids_ref[0] ^ ids_ref[1] ^ k
            place = (to & 1) * (rows // 2) + (to >> 1) * (2 * piece) + part * piece
            g_ref[pl.ds(pl.multiple_of(place, piece), piece), :] = ref[start : start + piece, :]

    out = nt(g_ref[...], w_ref[...]).astype(BF16)
    mine_ref[...] = out[: rows // 2]
    peer_ref[...] = out[rows // 2 :]


def values_partial(ids, gaps, weight, after, tile=512):
    rows, width = 4 * gaps[0].shape[0], gaps[0].shape[1]
    feats = weight.shape[0]
    return call(
        LONG,
        with_unread(values_kernel, len(after)),
        (feats // tile,),
        [shape(rows // 2, feats)] * 2,
        [unread()] * len(after)
        + [smem()]
        + [whole(g) for g in gaps]
        + [pl.BlockSpec((tile, width), lambda j: (j, 0))],
        [pl.BlockSpec((rows // 2, tile), lambda j: (0, j))] * 2,
        [pltpu.VMEM((rows, width), BF16)],
        *after,
        ids,
        *gaps,
        weight,
    )


def turn_kernel(ids_ref, near_ref, pair_ref, far_ref, far_pair_ref, out_ref):
    rows = near_ref.shape[0] // 4
    for half, refs in enumerate(((near_ref, pair_ref), (far_ref, far_pair_ref))):
        for flip, ref in enumerate(refs):
            for z in range(4):
                block = half * 8 + (ids_ref[1] ^ (z * 2 + flip))
                at = pl.multiple_of(block * rows, rows)
                out_ref[:, pl.ds(at, rows)] = ref[z * rows : (z + 1) * rows, :].T


def turned(ids, near, pair, far, far_pair, after):
    rows, feats = near.shape
    return call(
        LONG,
        with_unread(turn_kernel, len(after)),
        (1,),
        shape(feats, 4 * rows),
        [unread()] * len(after) + [smem()] + [whole(near)] * 4,
        pl.BlockSpec((feats, 4 * rows), lambda j: (0, 0)),
        [],
        *after,
        ids,
        near,
        pair,
        far,
        far_pair,
    )


def weight_kernel(ids_ref, *refs):
    gaps = refs[:8]
    v_ref, out_ref, g_ref = refs[8:]
    piece = gaps[0].shape[0] // 4

    @pl.when(pl.program_id(0) == 0)
    def _():
        for k, half, part, ref, start in gap_places(gaps, 2):
            place = half * (g_ref.shape[0] // 2) + (ids_ref[0] ^ k) * (2 * piece) + part * piece
            g_ref[pl.ds(pl.multiple_of(place, piece), piece), :] = ref[start : start + piece, :]

    out_ref[...] = nn(v_ref[...], g_ref[...])


def weight_sums(ids, gaps, values, after, tile=512):
    feats, rows = values.shape
    width = gaps[0].shape[1]
    return call(
        LONG,
        with_unread(weight_kernel, len(after)),
        (feats // tile,),
        shape(feats, width, F32),
        [unread()] * len(after)
        + [smem()]
        + [whole(g) for g in gaps]
        + [pl.BlockSpec((tile, rows), lambda j: (j, 0))],
        pl.BlockSpec((tile, width), lambda j: (j, 0)),
        [pltpu.VMEM((rows, width), BF16)],
        *after,
        ids,
        *gaps,
        values,
    )


def add(*terms):
    total = terms[0].astype(F32)
    for term in terms[1:]:
        total = total + term.astype(F32)
    return total


def join_kernel(*refs):
    rows = refs[0].shape[0]
    for k, ref in enumerate(refs[:-1]):
        refs[-1][k * rows : (k + 1) * rows, :] = ref[...]


def joined(arrays, after=(), micros=LONG):
    rows, width = arrays[0].shape
    tile = width // 2
    return call(
        micros,
        with_unread(join_kernel, len(after)),
        (2,),
        shape(rows * len(arrays), width),
        [unread()] * len(after) + [pl.BlockSpec((rows, tile), lambda j: (0, j))] * len(arrays),
        pl.BlockSpec((rows * len(arrays), tile), lambda j: (0, j)),
        [],
        *after,
        *arrays,
    )


def place_kernel(ids_ref, keep_ref, come_ref, out_ref):
    rows = keep_ref.shape[0]
    for away, ref in enumerate((keep_ref, come_ref)):
        out_ref[pl.ds(pl.multiple_of((ids_ref[2] ^ away) * rows, rows), rows), :] = ref[...]


def placed(ids, keep, come, after=(), micros=LONG):
    rows, width = keep.shape
    return call(
        micros,
        with_unread(place_kernel, len(after)),
        (1,),
        shape(2 * rows, width),
        [unread()] * len(after) + [smem(), whole(keep), whole(come)],
        pl.BlockSpec((2 * rows, width), lambda j: (0, 0)),
        [],
        *after,
        ids,
        keep,
        come,
    )


def marker_kernel(*refs):
    refs[-1][...] = jnp.zeros(refs[-1].shape, F32)


def marker(*after):
    return call(
        LONG,
        marker_kernel,
        (1,),
        shape(8, 128, F32),
        [unread()] * len(after),
        pl.BlockSpec((8, 128), lambda j: (0, 0)),
        [],
        *after,
    )


def gather_tensor(block, after=()):
    across = [swap(block, Z, k) for k in (1, 3, 2)]
    pair = swap(joined(across, after), CORE, 1)
    return [block, *across, swap(block, CORE, 1), pair]


def per_device(
    teacher_values,
    teacher_weight,
    teacher_stream,
    send_order,
    projection,
    student_values,
    student_weight,
    student_stream,
):
    g = lax.axis_index("grp")
    dp = lax.axis_index("x") * 2 + lax.axis_index("yh")
    t = lax.axis_index("z") * 2 + lax.axis_index("core")
    ids = jnp.stack([dp, t, g]).astype(jnp.int32)

    piece = send_order.shape[1] // 16

    loss_scale = 1.0 / math.sqrt(student_stream.shape[0] * 16)

    across = [swap(student_values, Z, k) for k in (1, 3, 2)]
    mine, peer, picked, owned = first_teacher(
        ids, send_order, teacher_values, teacher_weight, teacher_stream
    )
    near = joined((student_values, across[0], across[2], across[1]))
    early = merged((mine, swap(peer, CORE, 1)), 4, (near,))
    moved = [swap(early[k], Z, k) for k in (1, 3, 2)]
    mine, peer = second_teacher(
        picked, owned, teacher_weight, teacher_stream, piece, (early[0],)
    )
    keep, give = merged((early[0], *moved), 2, (mine,), LONG)
    late = merged((mine, swap(peer, CORE, 1)), 4, (keep,))
    moved = [swap(late[k], Z, k) for k in (1, 3, 2)]
    first = placed(ids, keep, swap(give, GRP, 1), (late[0],), SHORT)
    pair = swap(near, CORE, 1)
    far = swap(near, GRP, 1)
    layer_out = layer(ids, near, pair, student_weight, (first,))
    keep, give = merged((late[0], *moved), 2, (layer_out,), LONG)
    first = gather_tensor(first, (give, far))
    second = placed(ids, keep, swap(give, GRP, 1))
    left = less_target(ids, first, layer_out, projection, 0, 1, F32, (second,))[0]
    second = gather_tensor(second, (left,))
    parts = less_target(ids, second, left, projection, 1, 1, BF16)[0]

    parts = lax.all_to_all(parts.reshape(8, -1, parts.shape[1]), DP, 0, 0, tiled=True)
    total = student_stream.astype(F32) + jnp.sum(parts.astype(F32), axis=0)
    gap = (total * loss_scale).astype(BF16)

    rows = gap.shape[0] // 2
    first, second = gap[:rows], gap[rows:]
    around = joined([first] + [swap(first, Y, k) for k in (1, 2, 3)])
    along = joined([second] + [swap(second, X, k) for k in (1, 2, 3)])
    turn = turned(ids, near, pair, far, swap(far, CORE, 1), (around, along))
    gaps = [around] + [swap(around, X, k) for k in (1, 2, 3)]
    gaps += [along] + [swap(along, Y, k) for k in (1, 2, 3)]

    mine, peer = values_partial(ids, gaps, student_weight, (turn,))
    parts = merged((mine, swap(peer, CORE, 1)), 4, (marker(mine),))
    values_grad = add(parts[0], *[swap(parts[k], Z, k) for k in (1, 3, 2)])
    weight_grad = weight_sums(ids, gaps, turn, (parts[0],))
    return (values_grad, weight_grad)


def solution(mesh):
    fine = Mesh(mesh.devices.reshape(2, 4, 2, 4, 2), ("grp", "x", "yh", "z", "core"))
    tensor = ("z", "core")
    in_specs = (
        P("grp", tensor),
        P(tensor, DP),
        P(("grp",) + tensor, DP),
        P(),
        P(DP, tensor),
        P(("grp",) + tensor, DP),
        P(DP, tensor),
        P(("grp",) + DP, tensor),
    )
    out_specs = (P(("grp",) + tensor, DP), P(DP, tensor))
    return jax.shard_map(
        per_device, mesh=fine, in_specs=in_specs, out_specs=out_specs, check_vma=False
    )
```

time: 541 us -> 230 us (0.43)
  waiting for transfers between devices: 455 us -> 40.4 us
  Pallas kernels: 0 us -> 86.2 us
  starting transfers between devices: 0.33 us -> 56.1 us
  matrix products: 43 us -> 0 us
  blocking collectives: 14.6 us -> 33.6 us
  between operations: 14.2 us -> 0.87 us
    reduce_scatter x4 -> x0, waiting for transfers between devices: 251 us -> none  [the longest x1 87.3 us: project(): lax.psum_scatter(jnp.dot(gathered, projection, preferred_element_type=jnp...]
    psum x1 -> x0, waiting for transfers between devices: 109 us -> none  [per_device(): weight_grad = lax.psum(local_weight, 'grp')]
    all_gather x3 -> x0, waiting for transfers between devices: 94.1 us -> none  [the longest x1 54.4 us: per_device(): gathered_gap = lax.all_gather(gap_rows, 'dp', axis=0, tiled=True)]
    pallas_call x0 -> x21, Pallas kernels: none -> 86.2 us  [call(): pl.pallas_call(body, grid=grid, out_shape=out_shape, in_specs=in_specs, o...]
    ppermute x0 -> x42, starting transfers between devices: none -> 56.1 us  [swap(): return lax.ppermute(array, axes, [(i, i ^ distance) for i in range(size)])]
    dot_general x5 -> x0, matrix products: 43 us -> none  [the longest x1 14.6 us: per_device(): jnp.dot(picked, teacher_weight, preferred_element_type=jnp.float32)]
    ppermute x0 -> x42, waiting for transfers between devices: none -> 40.4 us  [swap(): return lax.ppermute(array, axes, [(i, i ^ distance) for i in range(size)])]
    all_to_all x1, blocking collectives: 14.6 us -> 33.6 us  [per_device(): lax.all_to_all(parts.reshape(8, -1, parts.shape[1]), DP, 0, 0, tiled=True)]
  transfers between devices with their start and end apart: 8 -> 42, of which waited for: 8 -> 14; matrix products, arithmetic and copies ran while one was open for 6% -> 0% of each run, Pallas kernels for 0% -> 30%
where the time goes in v2:
time: 230 us; the launch traced here: 229 us
  Pallas kernels  86.2 us (37%)
  starting transfers between devices  56.1 us (24%)
  waiting for transfers between devices  40.4 us (18%)
  blocking collectives  33.6 us (15%)
  local copies, waits for them, and re-layouts  9.89 us (4%)
    pallas_call x21, Pallas kernels, call(): pl.pallas_call(body, grid=grid, out_shape=out_shape, in_specs=in_specs, o...  86.2 us
    ppermute x42, starting transfers between devices, swap(): return lax.ppermute(array, axes, [(i, i ^ distance) for i in range(size)])  56.1 us
    ppermute x42, waiting for transfers between devices, swap(): return lax.ppermute(array, axes, [(i, i ^ distance) for i in range(size)])  40.4 us
    all_to_all x1, blocking collectives, per_device(): lax.all_to_all(parts.reshape(8, -1, parts.shape[1]), DP, 0, 0, tiled=True)  33.6 us
    unnamed x64, local copies, waits for them, and re-layouts  9.87 us
  transfers between devices with their start and end apart: 42, of which 14 were waited for; matrix products, arithmetic and copies ran while one was open for 0% of the time, Pallas kernels for 30%

profile of v2, /device:TPU:1, one launch (start us, length us, event | category | flops | bytes accessed | tf_op | source)
XLA Modules:
  0.0 229.1 jit_solution(2481705504294859111)
XLA Ops:
  0.6 2.5 %collective-permute-start = (bf16[128,1024]{1,0:T(8,128)(2,1)}, bf16[128,1024]{1,0:T(8,128)(2,1)S(1)}, u32[]{:S(2)}, u32[]{:S(2)}) collective-permute-start(bf16[128,1024]{1,0:T(8,128)(2,1)} %refs_0_.1), channel_id=1, source_target_pairs={{0,2},{2,0},{4,6},{6,4},{1,3},{3,1},{5,7},{7,5},{8,10},{10,8},{12,... | collective-permute-start | bytes 786440 | tf_op jit(solution)/shard_map/ppermute | solution.py:29
  3.2 3.3 %collective-permute-start.1 = (bf16[128,1024]{1,0:T(8,128)(2,1)}, bf16[128,1024]{1,0:T(8,128)(2,1)S(1)}, u32[]{:S(2)}, u32[]{:S(2)}) collective-permute-start(bf16[128,1024]{1,0:T(8,128)(2,1)} %refs_0_.1), channel_id=1, source_target_pairs={{0,4},{2,6},{4,0},{6,2},{1,5},{3,7},{5,1},{7,3},{8,12},{10,14},{12... | collective-permute-start | bytes 786440 | tf_op jit(solution)/shard_map/ppermute | solution.py:29
  7.1 12.5 %shard_map.96 = (bf16[512,1024]{1,0:T(8,128)(2,1)}, bf16[512,1024]{1,0:T(8,128)(2,1)}, bf16[1024,2048]{1,0:T(8,128)(2,1)}, bf16[1024,128]{1,0:T(8,128)(2,1)}) custom-call(s32[3]{0:T(128)} %pad_add_fusion.ids_ref.refs_1_.refs_0_.refs_2_, s32[16,128]{1,0:T(8,128)} %order_ref.1, bf16[1024,2048]{1,0:T(8,128)(2,1)} %x_ref.1, bf16[2048,2048]{1,0:T(8,128)(2,1)} %refs_3_.1, ...), custom_call_target="tpu_custom_call" | custom-call | flops 49999998976 | bytes 1024 | tf_op jit(solution)/shard_map/pallas_call | solution.py:37
  22.3 2.2 shard_map.95.refs_0_.refs_2_.refs_3_
  26.1 2.4 %shard_map.97 = (bf16[128,1024]{1,0:T(8,128)(2,1)}, bf16[128,1024]{1,0:T(8,128)(2,1)}, bf16[128,1024]{1,0:T(8,128)(2,1)}, bf16[128,1024]{1,0:T(8,128)(2,1)}) custom-call(bf16[512,1024]{1,0:T(8,128)(2,1)} %shard_map.95.refs_0_.refs_2_.refs_3_, bf16[512,1024]{1,0:T(8,128)(2,1)} %get-tuple-element.26.refs_1_, bf16[512,1024]{1,0:T(8,128)(2,1)} %copy-done.1), custom_call_target="tpu_custom_call" | custom-call | flops 10000000 | bytes 1024 | tf_op jit(solution)/shard_map/pallas_call | solution.py:37
  28.5 2.4 %collective-permute-start.5 = (bf16[128,1024]{1,0:T(8,128)(2,1)}, bf16[128,1024]{1,0:T(8,128)(2,1)S(1)}, u32[]{:S(2)}, u32[]{:S(2)}) collective-permute-start(bf16[128,1024]{1,0:T(8,128)(2,1)} %get-tuple-element.33), channel_id=1, source_target_pairs={{0,6},{2,4},{4,2},{6,0},{1,7},{3,5},{5,3},{7,1},{8,14},{10,12},{12... | collective-permute-start | bytes 786440 | tf_op jit(solution)/shard_map/ppermute | solution.py:29
  32.0 9.2 %shard_map.98 = (bf16[512,1024]{1,0:T(8,128)(2,1)}, bf16[512,1024]{1,0:T(8,128)(2,1)}) custom-call(bf16[128,1024]{1,0:T(8,128)(2,1)} %get-tuple-element.28.refs_0_.refs_1_, bf16[1024,2048]{1,0:T(8,128)(2,1)} %get-tuple-element.29.refs_1_, bf16[1024,128]{1,0:T(8,128)(2,1)} %get-tuple-element.30.refs_2_, bf16[2048,2048]{1,0:T(8,128)(2,1)} %refs_3_.1, ...), custom_call_target="tpu_custom_call" | custom-call | flops 49999998976 | bytes 1024 | tf_op jit(solution)/shard_map/pallas_call | solution.py:37
  44.5 2.1 shard_map.99
  48.0 2.4 %shard_map.100 = (bf16[128,1024]{1,0:T(8,128)(2,1)}, bf16[128,1024]{1,0:T(8,128)(2,1)}, bf16[128,1024]{1,0:T(8,128)(2,1)}, bf16[128,1024]{1,0:T(8,128)(2,1)}) custom-call(bf16[64,1024]{1,0:T(8,128)(2,1)} %get-tuple-element.35.refs_0_.refs_2_, bf16[512,1024]{1,0:T(8,128)(2,1)} %get-tuple-element.31.refs_0_.refs_1_, ...), custom_call_target="tpu_custom_call" | custom-call | flops 10000000 | bytes 1024 | tf_op jit(solution)/shard_map/pallas_call | solution.py:37
  50.4 1.7 collective-permute-start.11
  53.7 1.7 shard_map.101.refs_0_.refs_2_
  55.4 5.9 %shard_map.102.refs_0_.refs_8_ = f32[1024,1024]{1,0:T(8,128)} custom-call(bf16[128,1024]{1,0:T(8,128)(2,1)} %shard_map.101.refs_0_.refs_2_, s32[3]{0:T(128)} %pad_add_fusion.ids_ref.refs_1_.refs_0_.refs_2_, bf16[512,1024]{1,0:T(8,128)(2,1)} %shard_map.95.refs_0_.refs_2_.refs_3_, bf16[512,1024]{1,0:T(8,128)(2,1)} %collective-permute-done.9.refs_3_.refs_4_, ...), custom_call_target="tpu_custom_call" | custom-call | flops 49999998976 | bytes 1024 | tf_op jit(solution)/shard_map/pallas_call | solution.py:37
  61.3 1.7 collective-permute-start.19
  64.5 4.4 %collective-permute-start.21 = (bf16[128,1024]{1,0:T(8,128)(2,1)}, bf16[128,1024]{1,0:T(8,128)(2,1)}, u32[]{:S(2)}, u32[]{:S(2)}) collective-permute-start(bf16[128,1024]{1,0:T(8,128)(2,1)} %shard_map.101.refs_0_.refs_2_), channel_id=1, source_target_pairs={{0,1},{1,0},{2,3},{3,2},{4,5},{5,4},{6,7},{7,6},{8,9},{9,8},{10,11... | collective-permute-start | bytes 786440 | tf_op jit(solution)/shard_map/ppermute | solution.py:29
  68.8 2.0 shard_map.103
  70.8 2.1 collective-permute-done.22.refs_1_.refs_5_
  75.8 2.0 shard_map.105
  77.8 4.2 %collective-permute-start.23 = (bf16[384,1024]{1,0:T(8,128)(2,1)}, bf16[384,1024]{1,0:T(8,128)(2,1)S(1)}, u32[]{:S(2)}, u32[]{:S(2)}) collective-permute-start(bf16[384,1024]{1,0:T(8,128)(2,1)} %shard_map.105), channel_id=1, source_target_pairs={{0,1},{1,0},{2,3},{3,2},{4,5},{5,4},{6,7},{7,6},{8,9},{9,8},{10,11... | collective-permute-start | bytes 2359304 | tf_op jit(solution)/shard_map/ppermute | solution.py:29
  82.6 1.7 shard_map.104.refs_0_.refs_1_
  85.7 1.9 collective-permute-start.16
  88.6 6.5 %shard_map.106.refs_0_.refs_7_ = f32[1024,1024]{1,0:T(8,128)} custom-call(bf16[128,1024]{1,0:T(8,128)(2,1)} %shard_map.104.refs_0_.refs_1_, s32[3]{0:T(128)} %pad_add_fusion.ids_ref.refs_1_.refs_0_.refs_2_, bf16[128,1024]{1,0:T(8,128)(2,1)} %shard_map.101.refs_0_.refs_2_, bf16[128,1024]{1,0:T(8,128)(2,1)} %copy-done.12, bf16[128,1024]{1,0:T(8,128)(2,1)} %copy-done.13, ...), custom_call_target="tpu_custom_call" | custom-call | flops 49999998976 | bytes 1024 | tf_op jit(solution)/shard_map/pallas_call | solution.py:37
  95.2 4.0 %collective-permute-done.16.refs_3_.refs_4_ = bf16[128,1024]{1,0:T(8,128)(2,1)S(1)} collective-permute-done((bf16[128,1024]{1,0:T(8,128)(2,1)}, bf16[128,1024]{1,0:T(8,128)(2,1)S(1)}, u32[]{:S(2)}, u32[]{:S(2)}) %collective-permute-start.16) | collective-permute-done | bytes 262176 | tf_op jit(solution)/shard_map/ppermute | solution.py:29
  99.9 2.0 shard_map.107
  101.9 1.6 collective-permute-start.24
  103.6 2.2 collective-permute-done.17.refs_5_
  107.5 6.2 %shard_map.108 = bf16[1024,1024]{1,0:T(8,128)(2,1)} custom-call(s32[3]{0:T(128)} %pad_add_fusion.ids_ref.refs_1_.refs_0_.refs_2_, bf16[128,1024]{1,0:T(8,128)(2,1)} %shard_map.104.refs_0_.refs_1_, bf16[128,1024]{1,0:T(8,128)(2,1)} %copy-done.19, bf16[128,1024]{1,0:T(8,128)(2,1)} %copy-done.20, bf16[128,1024]{1,0:T(8,128)(2,1)} %copy-done.21, ...), custom_call_target="tpu_custom_call" | custom-call | flops 49999998976 | bytes 1024 | tf_op jit(solution)/shard_map/pallas_call | solution.py:37
  113.6 33.6 %all_to_all.5 = bf16[8,128,1024]{2,1,0:T(8,128)(2,1)S(1)} all-to-all(bf16[8,128,1024]{2,1,0:T(8,128)(2,1)} %bitcast.4), channel_id=1, replica_groups=mesh['grp'=2,'x'=4,'yh'=2,'z'=4,'core'=2] {'x','yh'}, dimensions={0} | all-to-all | bytes 4194304 | tf_op jit(solution)/shard_map/all_to_all | solution.py:519
  147.8 2.1 collective-permute-start.29
  149.9 1.7 collective-permute-start.30
  151.6 3.1 %collective-permute-start.31 = (bf16[512,1024]{1,0:T(8,128)(2,1)}, bf16[512,1024]{1,0:T(8,128)(2,1)S(1)}, u32[]{:S(2)}, u32[]{:S(2)}) collective-permute-start(bf16[512,1024]{1,0:T(8,128)(2,1)} %collective-permute-done.22.refs_1_.refs_5_), channel_id=1, source_target_pairs={{0,1},{1,0},{2,3},{3,2},{4,5},{5,4},{6,7},{7,6},{8,9},{9,8},{10,11... | collective-permute-start | bytes 3145736 | tf_op jit(solution)/shard_map/ppermute | solution.py:29
  156.1 1.9 collective-permute-start.27
  158.7 1.8 shard_map.110.refs_1_.refs_6_
  162.6 1.9 collective-permute-start.37
  164.6 1.8 shard_map.109.refs_0_.refs_2_
  166.4 1.9 collective-permute-start.33
  168.3 6.4 %collective-permute-done.35.refs_7_ = bf16[256,1024]{1,0:T(8,128)(2,1)S(1)} collective-permute-done((bf16[256,1024]{1,0:T(8,128)(2,1)}, bf16[256,1024]{1,0:T(8,128)(2,1)S(1)}, u32[]{:S(2)}, u32[]{:S(2)}) %collective-permute-start.35) | collective-permute-done | bytes 524320 | tf_op jit(solution)/shard_map/ppermute | solution.py:29
  174.8 5.7 %shard_map.111.refs_0_.refs_10_ = bf16[1024,2048]{1,0:T(8,128)(2,1)} custom-call(bf16[256,1024]{1,0:T(8,128)(2,1)} %shard_map.109.refs_0_.refs_2_, bf16[256,1024]{1,0:T(8,128)(2,1)} %shard_map.110.refs_1_.refs_6_, s32[3]{0:T(128)} %pad_add_fusion.ids_ref.refs_1_.refs_0_.refs_2_, bf16[512,1024]{1,0:T(8,128)(2,1)} %shard_map.95.refs_0_.refs_2_.refs_3_, ...), custom_call_target="tpu_custom_call" | custom-call | flops 49999998976 | bytes 1024 | tf_op jit(solution)/shard_map/pallas_call | solution.py:37
  180.4 3.4 %collective-permute-done.36.refs_8_ = bf16[256,1024]{1,0:T(8,128)(2,1)} collective-permute-done((bf16[256,1024]{1,0:T(8,128)(2,1)}, bf16[256,1024]{1,0:T(8,128)(2,1)}, u32[]{:S(2)}, u32[]{:S(2)}) %collective-permute-start.36) | collective-permute-done | bytes 524320 | tf_op jit(solution)/shard_map/ppermute | solution.py:29
  183.9 3.5 %collective-permute-done.37.refs_9_ = bf16[256,1024]{1,0:T(8,128)(2,1)} collective-permute-done((bf16[256,1024]{1,0:T(8,128)(2,1)}, bf16[256,1024]{1,0:T(8,128)(2,1)}, u32[]{:S(2)}, u32[]{:S(2)}) %collective-permute-start.37) | collective-permute-done | bytes 524320 | tf_op jit(solution)/shard_map/ppermute | solution.py:29
  187.4 2.4 %collective-permute-done.33.refs_4_ = bf16[256,1024]{1,0:T(8,128)(2,1)} collective-permute-done((bf16[256,1024]{1,0:T(8,128)(2,1)}, bf16[256,1024]{1,0:T(8,128)(2,1)}, u32[]{:S(2)}, u32[]{:S(2)}) %collective-permute-start.33) | collective-permute-done | bytes 524320 | tf_op jit(solution)/shard_map/ppermute | solution.py:29
  189.8 9.5 %collective-permute-done.34.refs_5_ = bf16[256,1024]{1,0:T(8,128)(2,1)} collective-permute-done((bf16[256,1024]{1,0:T(8,128)(2,1)}, bf16[256,1024]{1,0:T(8,128)(2,1)}, u32[]{:S(2)}, u32[]{:S(2)}) %collective-permute-start.34) | collective-permute-done | bytes 524320 | tf_op jit(solution)/shard_map/ppermute | solution.py:29
  199.3 6.1 %shard_map.112 = (bf16[512,1024]{1,0:T(8,128)(2,1)}, bf16[512,1024]{1,0:T(8,128)(2,1)}) custom-call(bf16[1024,2048]{1,0:T(8,128)(2,1)} %shard_map.111.refs_0_.refs_10_, s32[3]{0:T(128)} %pad_add_fusion.ids_ref.refs_1_.refs_0_.refs_2_, bf16[256,1024]{1,0:T(8,128)(2,1)} %shard_map.109.refs_0_.refs_2_, bf16[256,1024]{1,0:T(8,128)(2,1)} %collective-permute-done.32.refs_3_, ...), custom_call_target="tpu_custom_call" | custom-call | flops 49999998976 | bytes 1024 | tf_op jit(solution)/shard_map/pallas_call | solution.py:37
  205.4 2.4 %collective-permute-start.38 = (bf16[512,1024]{1,0:T(8,128)(2,1)}, bf16[512,1024]{1,0:T(8,128)(2,1)S(1)}, u32[]{:S(2)}, u32[]{:S(2)}) collective-permute-start(bf16[512,1024]{1,0:T(8,128)(2,1)} %get-tuple-element.45), channel_id=1, source_target_pairs={{0,1},{1,0},{2,3},{3,2},{4,5},{5,4},{6,7},{7,6},{8,9},{9,8},{10,11... | collective-permute-start | bytes 3145736 | tf_op jit(solution)/shard_map/ppermute | solution.py:29
  208.4 1.9 collective-permute-done.38.refs_2_
  211.3 2.4 %shard_map.114 = (bf16[128,1024]{1,0:T(8,128)(2,1)}, bf16[128,1024]{1,0:T(8,128)(2,1)}, bf16[128,1024]{1,0:T(8,128)(2,1)}, bf16[128,1024]{1,0:T(8,128)(2,1)}) custom-call(f32[8,128]{1,0:T(8,128)} %shard_map.113.refs_0_, bf16[512,1024]{1,0:T(8,128)(2,1)} %get-tuple-element.44.refs_0_.refs_1_, bf16[512,1024]{1,0:T(8,128)(2,1)} %copy-done.2), custom_call_target="tpu_custom_call" | custom-call | flops 10000000 | bytes 1024 | tf_op jit(solution)/shard_map/pallas_call | solution.py:37
  215.2 1.7 collective-permute-start.41
  216.9 9.1 %shard_map.115 = f32[1024,1024]{1,0:T(8,128)} custom-call(bf16[128,1024]{1,0:T(8,128)(2,1)} %get-tuple-element.46.refs_0_, s32[3]{0:T(128)} %pad_add_fusion.ids_ref.refs_1_.refs_0_.refs_2_, bf16[256,1024]{1,0:T(8,128)(2,1)} %shard_map.109.refs_0_.refs_2_, bf16[256,1024]{1,0:T(8,128)(2,1)} %collective-permute-done.32.refs_3_, ...), custom_call_target="tpu_custom_call" | custom-call | flops 49999998976 | bytes 1024 | tf_op jit(solution)/shard_map/pallas_call | solution.py:37
  226.1 2.0 collective-permute-done.41
  (127 shorter events, 31.0 us)
Async XLA Ops:
  0.6 20.2 %collective-permute-start = (bf16[128,1024]{1,0:T(8,128)(2,1)}, bf16[128,1024]{1,0:T(8,128)(2,1)S(1)}, u32[]{:S(2)}, u32[]{:S(2)}) collective-permute-start(bf16[128,1024]{1,0:T(8,128)(2,1)} %refs_0_.1), channel_id=1, source_target_pairs={{0,2},{2,0},{4,6},{6,4},{1,3},{3,1},{5,7},{7,5},{8,10},{10,8},{12,... | collective-permute-start | bytes 786440 | tf_op jit(solution)/shard_map/ppermute | solution.py:29
  3.2 17.7 %collective-permute-start.1 = (bf16[128,1024]{1,0:T(8,128)(2,1)}, bf16[128,1024]{1,0:T(8,128)(2,1)S(1)}, u32[]{:S(2)}, u32[]{:S(2)}) collective-permute-start(bf16[128,1024]{1,0:T(8,128)(2,1)} %refs_0_.1), channel_id=1, source_target_pairs={{0,4},{2,6},{4,0},{6,2},{1,5},{3,7},{5,1},{7,3},{8,12},{10,14},{12... | collective-permute-start | bytes 786440 | tf_op jit(solution)/shard_map/ppermute | solution.py:29
  6.5 14.4 %collective-permute-start.2 = (bf16[128,1024]{1,0:T(8,128)(2,1)}, bf16[128,1024]{1,0:T(8,128)(2,1)S(1)}, u32[]{:S(2)}, u32[]{:S(2)}) collective-permute-start(bf16[128,1024]{1,0:T(8,128)(2,1)} %refs_0_.1), channel_id=1, source_target_pairs={{0,6},{2,4},{4,2},{6,0},{1,7},{3,5},{5,3},{7,1},{8,14},{10,12},{12... | collective-permute-start | bytes 786440 | tf_op jit(solution)/shard_map/ppermute | solution.py:29
  19.6 5.6 %collective-permute-start.3 = (bf16[512,1024]{1,0:T(8,128)(2,1)}, bf16[512,1024]{1,0:T(8,128)(2,1)S(1)}, u32[]{:S(2)}, u32[]{:S(2)}) collective-permute-start(bf16[512,1024]{1,0:T(8,128)(2,1)} %get-tuple-element.27), channel_id=1, source_target_pairs={{0,1},{1,0},{2,3},{3,2},{4,5},{5,4},{6,7},{7,6},{8,9},{9,8},{10,11... | collective-permute-start | bytes 3145736 | tf_op jit(solution)/shard_map/ppermute | solution.py:29
  24.5 30.8 %collective-permute-start.9 = (bf16[512,1024]{1,0:T(8,128)(2,1)}, bf16[512,1024]{1,0:T(8,128)(2,1)}, u32[]{:S(2)}, u32[]{:S(2)}) collective-permute-start(bf16[512,1024]{1,0:T(8,128)(2,1)} %shard_map.95.refs_0_.refs_2_.refs_3_), channel_id=1, source_target_pairs={{0,1},{1,0},{2,3},{3,2},{4,5},{5,4},{6,7},{7,6},{8,9},{9,8},{10,11... | collective-permute-start | bytes 3145736 | tf_op jit(solution)/shard_map/ppermute | solution.py:29
  28.5 13.7 %collective-permute-start.4 = (bf16[128,1024]{1,0:T(8,128)(2,1)}, bf16[128,1024]{1,0:T(8,128)(2,1)S(1)}, u32[]{:S(2)}, u32[]{:S(2)}) collective-permute-start(bf16[128,1024]{1,0:T(8,128)(2,1)} %get-tuple-element.32), channel_id=1, source_target_pairs={{0,2},{2,0},{4,6},{6,4},{1,3},{3,1},{5,7},{7,5},{8,10},{10,8},{12,... | collective-permute-start | bytes 786440 | tf_op jit(solution)/shard_map/ppermute | solution.py:29
  28.5 13.7 %collective-permute-start.5 = (bf16[128,1024]{1,0:T(8,128)(2,1)}, bf16[128,1024]{1,0:T(8,128)(2,1)S(1)}, u32[]{:S(2)}, u32[]{:S(2)}) collective-permute-start(bf16[128,1024]{1,0:T(8,128)(2,1)} %get-tuple-element.33), channel_id=1, source_target_pairs={{0,6},{2,4},{4,2},{6,0},{1,7},{3,5},{5,3},{7,1},{8,14},{10,12},{12... | collective-permute-start | bytes 786440 | tf_op jit(solution)/shard_map/ppermute | solution.py:29
  30.9 12.8 %collective-permute-start.6 = (bf16[128,1024]{1,0:T(8,128)(2,1)}, bf16[128,1024]{1,0:T(8,128)(2,1)S(1)}, u32[]{:S(2)}, u32[]{:S(2)}) collective-permute-start(bf16[128,1024]{1,0:T(8,128)(2,1)} %get-tuple-element.34), channel_id=1, source_target_pairs={{0,4},{2,6},{4,0},{6,2},{1,5},{3,7},{5,1},{7,3},{8,12},{10,14},{12... | collective-permute-start | bytes 786440 | tf_op jit(solution)/shard_map/ppermute | solution.py:29
  41.2 6.8 %collective-permute-start.7 = (bf16[512,1024]{1,0:T(8,128)(2,1)}, bf16[512,1024]{1,0:T(8,128)(2,1)}, u32[]{:S(2)}, u32[]{:S(2)}) collective-permute-start(bf16[512,1024]{1,0:T(8,128)(2,1)} %get-tuple-element.36), channel_id=1, source_target_pairs={{0,1},{1,0},{2,3},{3,2},{4,5},{5,4},{6,7},{7,6},{8,9},{9,8},{10,11... | collective-permute-start | bytes 3145736 | tf_op jit(solution)/shard_map/ppermute | solution.py:29
  46.5 5.6 %collective-permute-start.8 = (bf16[64,1024]{1,0:T(8,128)(2,1)}, bf16[64,1024]{1,0:T(8,128)(2,1)S(1)}, u32[]{:S(2)}, u32[]{:S(2)}) collective-permute-start(bf16[64,1024]{1,0:T(8,128)(2,1)} %get-tuple-element.38), channel_id=1, source_target_pairs={{0,64},{64,0},{1,65},{65,1},{2,66},{66,2},{3,67},{67,3},{4,68},{68... | collective-permute-start | bytes 393224 | tf_op jit(solution)/shard_map/ppermute | solution.py:29
  47.8 25.1 %collective-permute-start.22 = (bf16[512,1024]{1,0:T(8,128)(2,1)S(1)}, bf16[512,1024]{1,0:T(8,128)(2,1)}, u32[]{:S(2)}, u32[]{:S(2)}) collective-permute-start(bf16[512,1024]{1,0:T(8,128)(2,1)S(1)} %copy-done), channel_id=1, source_target_pairs={{0,64},{64,0},{1,65},{65,1},{2,66},{66,2},{3,67},{67,3},{4,68},{68... | collective-permute-start | bytes 3145736 | tf_op jit(solution)/shard_map/ppermute | solution.py:29
  50.4 10.9 %collective-permute-start.10 = (bf16[128,1024]{1,0:T(8,128)(2,1)}, bf16[128,1024]{1,0:T(8,128)(2,1)}, u32[]{:S(2)}, u32[]{:S(2)}) collective-permute-start(bf16[128,1024]{1,0:T(8,128)(2,1)} %get-tuple-element.39), channel_id=1, source_target_pairs={{0,2},{2,0},{4,6},{6,4},{1,3},{3,1},{5,7},{7,5},{8,10},{10,8},{12,... | collective-permute-start | bytes 786440 | tf_op jit(solution)/shard_map/ppermute | solution.py:29
  50.4 12.6 %collective-permute-start.11 = (bf16[128,1024]{1,0:T(8,128)(2,1)}, bf16[128,1024]{1,0:T(8,128)(2,1)}, u32[]{:S(2)}, u32[]{:S(2)}) collective-permute-start(bf16[128,1024]{1,0:T(8,128)(2,1)} %get-tuple-element.40), channel_id=1, source_target_pairs={{0,6},{2,4},{4,2},{6,0},{1,7},{3,5},{5,3},{7,1},{8,14},{10,12},{12... | collective-permute-start | bytes 786440 | tf_op jit(solution)/shard_map/ppermute | solution.py:29
  52.1 12.3 %collective-permute-start.12 = (bf16[128,1024]{1,0:T(8,128)(2,1)}, bf16[128,1024]{1,0:T(8,128)(2,1)}, u32[]{:S(2)}, u32[]{:S(2)}) collective-permute-start(bf16[128,1024]{1,0:T(8,128)(2,1)} %get-tuple-element.41), channel_id=1, source_target_pairs={{0,4},{2,6},{4,0},{6,2},{1,5},{3,7},{5,1},{7,3},{8,12},{10,14},{12... | collective-permute-start | bytes 786440 | tf_op jit(solution)/shard_map/ppermute | solution.py:29
  55.4 18.9 %collective-permute-start.18 = (bf16[128,1024]{1,0:T(8,128)(2,1)}, bf16[128,1024]{1,0:T(8,128)(2,1)S(1)}, u32[]{:S(2)}, u32[]{:S(2)}) collective-permute-start(bf16[128,1024]{1,0:T(8,128)(2,1)} %shard_map.101.refs_0_.refs_2_), channel_id=1, source_target_pairs={{0,2},{2,0},{4,6},{6,4},{1,3},{3,1},{5,7},{7,5},{8,10},{10,8},{12,... | collective-permute-start | bytes 786440 | tf_op jit(solution)/shard_map/ppermute | solution.py:29
  61.3 13.0 %collective-permute-start.19 = (bf16[128,1024]{1,0:T(8,128)(2,1)}, bf16[128,1024]{1,0:T(8,128)(2,1)S(1)}, u32[]{:S(2)}, u32[]{:S(2)}) collective-permute-start(bf16[128,1024]{1,0:T(8,128)(2,1)} %shard_map.101.refs_0_.refs_2_), channel_id=1, source_target_pairs={{0,6},{2,4},{4,2},{6,0},{1,7},{3,5},{5,3},{7,1},{8,14},{10,12},{12... | collective-permute-start | bytes 786440 | tf_op jit(solution)/shard_map/ppermute | solution.py:29
  63.0 11.8 %collective-permute-start.20 = (bf16[128,1024]{1,0:T(8,128)(2,1)}, bf16[128,1024]{1,0:T(8,128)(2,1)S(1)}, u32[]{:S(2)}, u32[]{:S(2)}) collective-permute-start(bf16[128,1024]{1,0:T(8,128)(2,1)} %shard_map.101.refs_0_.refs_2_), channel_id=1, source_target_pairs={{0,4},{2,6},{4,0},{6,2},{1,5},{3,7},{5,1},{7,3},{8,12},{10,14},{12... | collective-permute-start | bytes 786440 | tf_op jit(solution)/shard_map/ppermute | solution.py:29
  64.5 23.1 %collective-permute-start.21 = (bf16[128,1024]{1,0:T(8,128)(2,1)}, bf16[128,1024]{1,0:T(8,128)(2,1)}, u32[]{:S(2)}, u32[]{:S(2)}) collective-permute-start(bf16[128,1024]{1,0:T(8,128)(2,1)} %shard_map.101.refs_0_.refs_2_), channel_id=1, source_target_pairs={{0,1},{1,0},{2,3},{3,2},{4,5},{5,4},{6,7},{7,6},{8,9},{9,8},{10,11... | collective-permute-start | bytes 786440 | tf_op jit(solution)/shard_map/ppermute | solution.py:29
  73.0 9.0 %collective-permute-start.13 = (bf16[64,1024]{1,0:T(8,128)(2,1)}, bf16[64,1024]{1,0:T(8,128)(2,1)S(1)}, u32[]{:S(2)}, u32[]{:S(2)}) collective-permute-start(bf16[64,1024]{1,0:T(8,128)(2,1)} %get-tuple-element.43.refs_0_), channel_id=1, source_target_pairs={{0,64},{64,0},{1,65},{65,1},{2,66},{66,2},{3,67},{67,3},{4,68},{68... | collective-permute-start | bytes 393224 | tf_op jit(solution)/shard_map/ppermute | solution.py:29
  77.8 9.8 %collective-permute-start.23 = (bf16[384,1024]{1,0:T(8,128)(2,1)}, bf16[384,1024]{1,0:T(8,128)(2,1)S(1)}, u32[]{:S(2)}, u32[]{:S(2)}) collective-permute-start(bf16[384,1024]{1,0:T(8,128)(2,1)} %shard_map.105), channel_id=1, source_target_pairs={{0,1},{1,0},{2,3},{3,2},{4,5},{5,4},{6,7},{7,6},{8,9},{9,8},{10,11... | collective-permute-start | bytes 2359304 | tf_op jit(solution)/shard_map/ppermute | solution.py:29
  84.3 10.8 %collective-permute-start.14 = (bf16[128,1024]{1,0:T(8,128)(2,1)}, bf16[128,1024]{1,0:T(8,128)(2,1)S(1)}, u32[]{:S(2)}, u32[]{:S(2)}) collective-permute-start(bf16[128,1024]{1,0:T(8,128)(2,1)} %shard_map.104.refs_0_.refs_1_), channel_id=1, source_target_pairs={{0,2},{2,0},{4,6},{6,4},{1,3},{3,1},{5,7},{7,5},{8,10},{10,8},{12,... | collective-permute-start | bytes 786440 | tf_op jit(solution)/shard_map/ppermute | solution.py:29
  84.3 10.8 %collective-permute-start.15 = (bf16[128,1024]{1,0:T(8,128)(2,1)}, bf16[128,1024]{1,0:T(8,128)(2,1)S(1)}, u32[]{:S(2)}, u32[]{:S(2)}) collective-permute-start(bf16[128,1024]{1,0:T(8,128)(2,1)} %shard_map.104.refs_0_.refs_1_), channel_id=1, source_target_pairs={{0,6},{2,4},{4,2},{6,0},{1,7},{3,5},{5,3},{7,1},{8,14},{10,12},{12... | collective-permute-start | bytes 786440 | tf_op jit(solution)/shard_map/ppermute | solution.py:29
  85.7 13.5 %collective-permute-start.16 = (bf16[128,1024]{1,0:T(8,128)(2,1)}, bf16[128,1024]{1,0:T(8,128)(2,1)S(1)}, u32[]{:S(2)}, u32[]{:S(2)}) collective-permute-start(bf16[128,1024]{1,0:T(8,128)(2,1)} %shard_map.104.refs_0_.refs_1_), channel_id=1, source_target_pairs={{0,4},{2,6},{4,0},{6,2},{1,5},{3,7},{5,1},{7,3},{8,12},{10,14},{12... | collective-permute-start | bytes 786440 | tf_op jit(solution)/shard_map/ppermute | solution.py:29
  95.1 8.4 %copy-start.18 = (bf16[128,1024]{1,0:T(8,128)(2,1)S(1)}, bf16[128,1024]{1,0:T(8,128)(2,1)}, u32[]{:S(2)}) copy-start(bf16[128,1024]{1,0:T(8,128)(2,1)} %shard_map.104.refs_0_.refs_1_) | copy-start | bytes 786436
  101.9 4.0 %collective-permute-start.24 = (bf16[384,1024]{1,0:T(8,128)(2,1)}, bf16[384,1024]{1,0:T(8,128)(2,1)S(1)}, u32[]{:S(2)}, u32[]{:S(2)}) collective-permute-start(bf16[384,1024]{1,0:T(8,128)(2,1)} %shard_map.107), channel_id=1, source_target_pairs={{0,1},{1,0},{2,3},{3,2},{4,5},{5,4},{6,7},{7,6},{8,9},{9,8},{10,11... | collective-permute-start | bytes 2359304 | tf_op jit(solution)/shard_map/ppermute | solution.py:29
  103.5 2.3 collective-permute-start.17
  113.6 33.9 %copy-start.3 = (bf16[128,1024]{1,0:T(8,128)(2,1)S(1)}, bf16[128,1024]{1,0:T(8,128)(2,1)}, u32[]{:S(2)}) copy-start(bf16[128,1024]{1,0:T(8,128)(2,1)} %param.15) | copy-start | bytes 786436
  147.7 10.3 %copy-start.6 = (bf16[64,1024]{1,0:T(8,128)(2,1)}, bf16[64,1024]{1,0:T(8,128)(2,1)S(1)}, u32[]{:S(2)}) copy-start(bf16[64,1024]{1,0:T(8,128)(2,1)S(1)} %get-tuple-element.50.refs_0_) | copy-start | bytes 393220
  147.7 12.8 %copy-start.5 = (bf16[64,1024]{1,0:T(8,128)(2,1)}, bf16[64,1024]{1,0:T(8,128)(2,1)S(1)}, u32[]{:S(2)}) copy-start(bf16[64,1024]{1,0:T(8,128)(2,1)S(1)} %get-tuple-element.51.refs_0_) | copy-start | bytes 393220
  147.7 8.0 %collective-permute-start.28 = (bf16[64,1024]{1,0:T(8,128)(2,1)S(1)}, bf16[64,1024]{1,0:T(8,128)(2,1)S(1)}, u32[]{:S(2)}, u32[]{:S(2)}) collective-permute-start(bf16[64,1024]{1,0:T(8,128)(2,1)S(1)} %get-tuple-element.50.refs_0_), channel_id=1, source_target_pairs={{0,16},{16,0},{32,48},{48,32},{1,17},{17,1},{33,49},{49,33},{2,18}... | collective-permute-start | bytes 393224 | tf_op jit(solution)/shard_map/ppermute | solution.py:29
  147.8 8.3 %collective-permute-start.29 = (bf16[64,1024]{1,0:T(8,128)(2,1)S(1)}, bf16[64,1024]{1,0:T(8,128)(2,1)S(1)}, u32[]{:S(2)}, u32[]{:S(2)}) collective-permute-start(bf16[64,1024]{1,0:T(8,128)(2,1)S(1)} %get-tuple-element.50.refs_0_), channel_id=1, source_target_pairs={{0,32},{16,48},{32,0},{48,16},{1,33},{17,49},{33,1},{49,17},{2,34}... | collective-permute-start | bytes 393224 | tf_op jit(solution)/shard_map/ppermute | solution.py:29
  149.9 8.1 %collective-permute-start.30 = (bf16[64,1024]{1,0:T(8,128)(2,1)S(1)}, bf16[64,1024]{1,0:T(8,128)(2,1)S(1)}, u32[]{:S(2)}, u32[]{:S(2)}) collective-permute-start(bf16[64,1024]{1,0:T(8,128)(2,1)S(1)} %get-tuple-element.50.refs_0_), channel_id=1, source_target_pairs={{0,48},{16,32},{32,16},{48,0},{1,49},{17,33},{33,17},{49,1},{2,50}... | collective-permute-start | bytes 393224 | tf_op jit(solution)/shard_map/ppermute | solution.py:29
  151.6 14.7 %collective-permute-start.31 = (bf16[512,1024]{1,0:T(8,128)(2,1)}, bf16[512,1024]{1,0:T(8,128)(2,1)S(1)}, u32[]{:S(2)}, u32[]{:S(2)}) collective-permute-start(bf16[512,1024]{1,0:T(8,128)(2,1)} %collective-permute-done.22.refs_1_.refs_5_), channel_id=1, source_target_pairs={{0,1},{1,0},{2,3},{3,2},{4,5},{5,4},{6,7},{7,6},{8,9},{9,8},{10,11... | collective-permute-start | bytes 3145736 | tf_op jit(solution)/shard_map/ppermute | solution.py:29
  154.7 7.1 %collective-permute-start.25 = (bf16[64,1024]{1,0:T(8,128)(2,1)S(1)}, bf16[64,1024]{1,0:T(8,128)(2,1)S(1)}, u32[]{:S(2)}, u32[]{:S(2)}) collective-permute-start(bf16[64,1024]{1,0:T(8,128)(2,1)S(1)} %get-tuple-element.51.refs_0_), channel_id=1, source_target_pairs={{0,8},{8,0},{64,72},{72,64},{1,9},{9,1},{65,73},{73,65},{2,10},{10... | collective-permute-start | bytes 393224 | tf_op jit(solution)/shard_map/ppermute | solution.py:29
  155.7 7.0 %collective-permute-start.26 = (bf16[64,1024]{1,0:T(8,128)(2,1)S(1)}, bf16[64,1024]{1,0:T(8,128)(2,1)S(1)}, u32[]{:S(2)}, u32[]{:S(2)}) collective-permute-start(bf16[64,1024]{1,0:T(8,128)(2,1)S(1)} %get-tuple-element.51.refs_0_), channel_id=1, source_target_pairs={{0,64},{8,72},{64,0},{72,8},{1,65},{9,73},{65,1},{73,9},{2,66},{10... | collective-permute-start | bytes 393224 | tf_op jit(solution)/shard_map/ppermute | solution.py:29
  156.1 8.5 %collective-permute-start.27 = (bf16[64,1024]{1,0:T(8,128)(2,1)S(1)}, bf16[64,1024]{1,0:T(8,128)(2,1)}, u32[]{:S(2)}, u32[]{:S(2)}) collective-permute-start(bf16[64,1024]{1,0:T(8,128)(2,1)S(1)} %get-tuple-element.51.refs_0_), channel_id=1, source_target_pairs={{0,72},{8,64},{64,8},{72,0},{1,73},{9,65},{65,9},{73,1},{2,74},{10... | collective-permute-start | bytes 393224 | tf_op jit(solution)/shard_map/ppermute | solution.py:29
  160.5 14.2 %collective-permute-start.35 = (bf16[256,1024]{1,0:T(8,128)(2,1)}, bf16[256,1024]{1,0:T(8,128)(2,1)S(1)}, u32[]{:S(2)}, u32[]{:S(2)}) collective-permute-start(bf16[256,1024]{1,0:T(8,128)(2,1)} %shard_map.110.refs_1_.refs_6_), channel_id=1, source_target_pairs={{0,8},{8,0},{64,72},{72,64},{1,9},{9,1},{65,73},{73,65},{2,10},{10... | collective-permute-start | bytes 1572872 | tf_op jit(solution)/shard_map/ppermute | solution.py:29
  161.9 22.0 %collective-permute-start.36 = (bf16[256,1024]{1,0:T(8,128)(2,1)}, bf16[256,1024]{1,0:T(8,128)(2,1)}, u32[]{:S(2)}, u32[]{:S(2)}) collective-permute-start(bf16[256,1024]{1,0:T(8,128)(2,1)} %shard_map.110.refs_1_.refs_6_), channel_id=1, source_target_pairs={{0,64},{8,72},{64,0},{72,8},{1,65},{9,73},{65,1},{73,9},{2,66},{10... | collective-permute-start | bytes 1572872 | tf_op jit(solution)/shard_map/ppermute | solution.py:29
  162.6 24.8 %collective-permute-start.37 = (bf16[256,1024]{1,0:T(8,128)(2,1)}, bf16[256,1024]{1,0:T(8,128)(2,1)}, u32[]{:S(2)}, u32[]{:S(2)}) collective-permute-start(bf16[256,1024]{1,0:T(8,128)(2,1)} %shard_map.110.refs_1_.refs_6_), channel_id=1, source_target_pairs={{0,72},{8,64},{64,8},{72,0},{1,73},{9,65},{65,9},{73,1},{2,74},{10... | collective-permute-start | bytes 1572872 | tf_op jit(solution)/shard_map/ppermute | solution.py:29
  166.4 21.0 %collective-permute-start.32 = (bf16[256,1024]{1,0:T(8,128)(2,1)}, bf16[256,1024]{1,0:T(8,128)(2,1)}, u32[]{:S(2)}, u32[]{:S(2)}) collective-permute-start(bf16[256,1024]{1,0:T(8,128)(2,1)} %shard_map.109.refs_0_.refs_2_), channel_id=1, source_target_pairs={{0,16},{16,0},{32,48},{48,32},{1,17},{17,1},{33,49},{49,33},{2,18}... | collective-permute-start | bytes 1572872 | tf_op jit(solution)/shard_map/ppermute | solution.py:29
  166.4 8.4 %copy-start.8 = (bf16[512,1024]{1,0:T(8,128)(2,1)}, bf16[512,1024]{1,0:T(8,128)(2,1)S(1)}, u32[]{:S(2)}) copy-start(bf16[512,1024]{1,0:T(8,128)(2,1)S(1)} %collective-permute-done.31.refs_6_) | copy-start | bytes 3145732
  166.4 23.4 %collective-permute-start.33 = (bf16[256,1024]{1,0:T(8,128)(2,1)}, bf16[256,1024]{1,0:T(8,128)(2,1)}, u32[]{:S(2)}, u32[]{:S(2)}) collective-permute-start(bf16[256,1024]{1,0:T(8,128)(2,1)} %shard_map.109.refs_0_.refs_2_), channel_id=1, source_target_pairs={{0,32},{16,48},{32,0},{48,16},{1,33},{17,49},{33,1},{49,17},{2,34}... | collective-permute-start | bytes 1572872 | tf_op jit(solution)/shard_map/ppermute | solution.py:29
  174.8 24.5 %collective-permute-start.34 = (bf16[256,1024]{1,0:T(8,128)(2,1)}, bf16[256,1024]{1,0:T(8,128)(2,1)}, u32[]{:S(2)}, u32[]{:S(2)}) collective-permute-start(bf16[256,1024]{1,0:T(8,128)(2,1)} %shard_map.109.refs_0_.refs_2_), channel_id=1, source_target_pairs={{0,48},{16,32},{32,16},{48,0},{1,49},{17,33},{33,17},{49,1},{2,50}... | collective-permute-start | bytes 1572872 | tf_op jit(solution)/shard_map/ppermute | solution.py:29
  205.4 4.9 %collective-permute-start.38 = (bf16[512,1024]{1,0:T(8,128)(2,1)}, bf16[512,1024]{1,0:T(8,128)(2,1)S(1)}, u32[]{:S(2)}, u32[]{:S(2)}) collective-permute-start(bf16[512,1024]{1,0:T(8,128)(2,1)} %get-tuple-element.45), channel_id=1, source_target_pairs={{0,1},{1,0},{2,3},{3,2},{4,5},{5,4},{6,7},{7,6},{8,9},{9,8},{10,11... | collective-permute-start | bytes 3145736 | tf_op jit(solution)/shard_map/ppermute | solution.py:29
  213.7 12.4 %collective-permute-start.39 = (bf16[128,1024]{1,0:T(8,128)(2,1)}, bf16[128,1024]{1,0:T(8,128)(2,1)S(1)}, u32[]{:S(2)}, u32[]{:S(2)}) collective-permute-start(bf16[128,1024]{1,0:T(8,128)(2,1)} %get-tuple-element.47), channel_id=1, source_target_pairs={{0,2},{2,0},{4,6},{6,4},{1,3},{3,1},{5,7},{7,5},{8,10},{10,8},{12,... | collective-permute-start | bytes 786440 | tf_op jit(solution)/shard_map/ppermute | solution.py:29
  213.9 12.1 %collective-permute-start.40 = (bf16[128,1024]{1,0:T(8,128)(2,1)}, bf16[128,1024]{1,0:T(8,128)(2,1)S(1)}, u32[]{:S(2)}, u32[]{:S(2)}) collective-permute-start(bf16[128,1024]{1,0:T(8,128)(2,1)} %get-tuple-element.48), channel_id=1, source_target_pairs={{0,6},{2,4},{4,2},{6,0},{1,7},{3,5},{5,3},{7,1},{8,14},{10,12},{12... | collective-permute-start | bytes 786440 | tf_op jit(solution)/shard_map/ppermute | solution.py:29
  215.2 12.9 %collective-permute-start.41 = (bf16[128,1024]{1,0:T(8,128)(2,1)}, bf16[128,1024]{1,0:T(8,128)(2,1)S(1)}, u32[]{:S(2)}, u32[]{:S(2)}) collective-permute-start(bf16[128,1024]{1,0:T(8,128)(2,1)} %get-tuple-element.49), channel_id=1, source_target_pairs={{0,4},{2,6},{4,0},{6,2},{1,5},{3,7},{5,1},{7,3},{8,12},{10,14},{12... | collective-permute-start | bytes 786440 | tf_op jit(solution)/shard_map/ppermute | solution.py:29
  216.9 11.2 %copy-start.4 = (bf16[128,1024]{1,0:T(8,128)(2,1)S(1)}, bf16[128,1024]{1,0:T(8,128)(2,1)}, u32[]{:S(2)}) copy-start(bf16[128,1024]{1,0:T(8,128)(2,1)} %get-tuple-element.46.refs_0_) | copy-start | bytes 786436
  (26 other events, 42.5 us)

commit v3 on v2

--- a/solution.py
+++ b/solution.py
@@ -80,105 +80,61 @@
     return jnp.where(hits, 1.0, 0.0).astype(BF16)
 
 
-def pick_rows(piece, ids_ref, order_ref, x_ref, a_ref, o_ref, pick_ref):
-    rows, size = pick_ref.shape[0], o_ref.shape[1]
+def teacher_kernel(piece, ids_ref, order_ref, x_ref, w_ref, s_ref, mine_ref, peer_ref, pick_ref, out_ref):
+    parts, rows = pick_ref.shape[:2]
+    size = s_ref.shape[0]
+    group = piece * SPAN
     t, g = ids_ref[1], ids_ref[2]
-    to = lax.broadcasted_iota(jnp.int32, (rows, rows), 0)
-    at = lax.broadcasted_iota(jnp.int32, (rows, rows), 1)
-    far = to // (piece * SPAN)
-    owner = ((far % 2) ^ g) * 8 + (t ^ (((far // 2) % 4) * 2 + far // 8))
-    wanted = one_hot(at == ((to // piece) % SPAN) * size + owner * piece + to % piece)
-    line = lax.broadcasted_iota(jnp.int32, (size, size), 0)
-
-    def part(k, _):
-        for b in range(SPAN):
-            order = order_ref[pl.ds(g * 8 + k * SPAN + b, 1), :]
-            columns = slice(b * size, (b + 1) * size)
-            pick_ref[:, columns] = nt(wanted[:, columns], one_hot(line == order)).astype(BF16)
-        here = pl.ds(pl.multiple_of(k * rows, rows), rows)
-        a_ref[here, :] = nn(pick_ref[...], x_ref[here, :]).astype(BF16)
-        mine = t - k * SPAN
-        inside = jnp.logical_and(mine >= 0, mine < SPAN).astype(F32)
-        start = pl.multiple_of(jnp.clip(mine, 0, SPAN - 1) * size, size)
-        o_ref[here, :] = (pick_ref[:, pl.ds(start, size)].astype(F32) * inside).astype(BF16)
-        return 0
-
-    lax.fori_loop(0, x_ref.shape[0] // rows, part, 0)
-
-
-def teacher_tile(piece, a_ref, o_ref, w_ref, s_ref, mine_ref, peer_ref):
-    group = piece * SPAN
-    parts = a_ref.shape[0] // (16 * group)
-    out = (nn(a_ref[...], w_ref[...]) + nn(o_ref[...], s_ref[...])).astype(BF16)
-    for k in range(parts):
-        for far in range(16):
-            start = (k * 16 + far) * group
-            to = ((far % 8) * parts + k) * group
-            (mine_ref, peer_ref)[far // 8][to : to + group, :] = out[start : start + group]
-
-
-def first_teacher_kernel(piece, ids_ref, order_ref, x_ref, w_ref, s_ref, *rest):
-    mine_ref, peer_ref, a_ref, o_ref, pick_ref = rest
 
     @pl.when(pl.program_id(0) == 0)
     def _():
-        pick_rows(piece, ids_ref, order_ref, x_ref, a_ref, o_ref, pick_ref)
-
-    teacher_tile(piece, a_ref, o_ref, w_ref, s_ref, mine_ref, peer_ref)
-
-
-def second_teacher_kernel(piece, a_ref, o_ref, w_ref, s_ref, mine_ref, peer_ref):
-    teacher_tile(piece, a_ref, o_ref, w_ref, s_ref, mine_ref, peer_ref)
-
-
-def first_teacher(ids, order, values, weight, stream, tile=512):
+        to = lax.broadcasted_iota(jnp.int32, (rows, rows), 0)
+        at = lax.broadcasted_iota(jnp.int32, (rows, rows), 1)
+        far = to // group
+        owner = ((far % 2) ^ g) * 8 + (t ^ (((far // 2) % 4) * 2 + far // 8))
+        wanted = one_hot(at == ((to // piece) % SPAN) * size + owner * piece + to % piece)
+        line = lax.broadcasted_iota(jnp.int32, (size, size), 0)
+        for k in range(parts):
+            for b in range(SPAN):
+                order = order_ref[pl.ds(g * 8 + k * SPAN + b, 1), :]
+                columns = slice(b * size, (b + 1) * size)
+                pick_ref[k, :, columns] = nt(wanted[:, columns], one_hot(line == order)).astype(BF16)
+
+    out_ref[...] = nn(x_ref[...], w_ref[...])
+    own = pl.ds(pl.multiple_of(t * size, size), size)
+    out_ref[own, :] = out_ref[own, :] + s_ref[...].astype(F32)
+    for k in range(parts):
+        part = out_ref[k * rows : (k + 1) * rows, :].astype(BF16)
+        part = nn(pick_ref[k], part).astype(BF16)
+        for far in range(16):
+            to = ((far % 8) * parts + k) * group
+            (mine_ref, peer_ref)[far // 8][to : to + group, :] = part[far * group : (far + 1) * group]
+
+
+def teacher(ids, order, values, weight, stream, half, after=(), tile=512):
     rows, depth = values.shape
     width, size = weight.shape[1] // 2, stream.shape[0]
-    piece = order.shape[1] // 16
-    return call(
-        LONG,
-        functools.partial(first_teacher_kernel, piece),
-        (width // tile,),
-        [shape(rows // 2, width)] * 2 + [shape(rows, depth), shape(rows, size)],
-        [
-            smem(),
-            whole(order),
-            whole(values),
-            pl.BlockSpec((depth, tile), lambda j: (0, j)),
-            pl.BlockSpec((size, tile), lambda j: (0, j)),
-        ],
-        [pl.BlockSpec((rows // 2, tile), lambda j: (0, j))] * 2
-        + [pl.BlockSpec((rows, depth), lambda j: (0, 0)), pl.BlockSpec((rows, size), lambda j: (0, 0))],
-        [pltpu.VMEM((SPAN * size, SPAN * size), BF16)],
-        ids,
-        order,
-        values,
-        weight,
-        stream,
-    )
-
-
-def second_teacher(picked, owned, weight, stream, piece, after, tile=512):
-    rows, depth = picked.shape
-    width, size = weight.shape[1] // 2, stream.shape[0]
-    skip = width // tile
-    return call(
-        LONG,
-        with_unread(functools.partial(second_teacher_kernel, piece), len(after)),
+    skip = half * (width // tile)
+    side = SPAN * size
+    return call(
+        LONG,
+        with_unread(functools.partial(teacher_kernel, order.shape[1] // 16), len(after)),
         (width // tile,),
         [shape(rows // 2, width)] * 2,
         [unread()] * len(after)
         + [
-            whole(picked),
-            whole(owned),
+            smem(),
+            whole(order),
+            whole(values),
             pl.BlockSpec((depth, tile), lambda j: (0, j + skip)),
             pl.BlockSpec((size, tile), lambda j: (0, j + skip)),
         ],
         [pl.BlockSpec((rows // 2, tile), lambda j: (0, j))] * 2,
-        [],
-        *after,
-        picked,
-        owned,
+        [pltpu.VMEM((rows // side, side, side), BF16), pltpu.VMEM((rows, tile), F32)],
+        *after,
+        ids,
+        order,
+        values,
         weight,
         stream,
     )
@@ -221,7 +177,7 @@
             start = (k >> 1) * block
             v_ref[pl.ds(pl.multiple_of(place, block), block), :] = ref[start : start + block, :]
 
-    out_ref[...] = nn(v_ref[...], w_ref[...])
+    out_ref[...] = nn(v_ref[...], w_ref[...]).astype(BF16)
 
 
 def layer(ids, near, pair, weight, after, tile=512):
@@ -231,7 +187,7 @@
         LONG,
         with_unread(layer_kernel, len(after)),
         (width // tile,),
-        shape(rows, width, F32),
+        shape(rows, width),
         [unread()] * len(after)
         + [smem(), whole(near), whole(pair), pl.BlockSpec((depth, tile), lambda j: (0, j))],
         pl.BlockSpec((rows, tile), lambda j: (0, j)),
@@ -244,43 +200,39 @@
     )
 
 
-def target_kernel(ids_ref, *refs):
-    hidden = refs[:6]
-    l_ref, p_ref = refs[6:8]
-    outs, h_ref = refs[8:-1], refs[-1]
+def target_kernel(places, ids_ref, *refs):
+    count = 1 + max(k for _, k, _ in places)
+    hidden = refs[:count]
+    l_ref, p_ref, out_ref, h_ref = refs[count:]
     piece = hidden[0].shape[0]
-    blocks = [(0, 0, 0), (2, 1, 0), (6, 2, 0), (4, 3, 0), (1, 4, 0), (3, 5, 0), (7, 5, 1), (5, 5, 2)]
 
     @pl.when(pl.program_id(0) == 0)
     def _():
-        for far, k, start in blocks:
+        for far, k, start in places:
             at = pl.multiple_of((ids_ref[1] ^ far) * piece, piece)
             h_ref[pl.ds(at, piece), :] = hidden[k][start * piece : (start + 1) * piece, :]
 
-    out = l_ref[...] - nn(h_ref[...], p_ref[...])
-    rows = out.shape[0] // len(outs)
-    for k, to in enumerate(outs):
-        to[...] = out[k * rows : (k + 1) * rows].astype(to.dtype)
-
-
-def less_target(ids, hidden, left, projection, half, outs, kind, after=(), tile=512):
-    piece, deep = hidden[0].shape
-    width = projection.shape[1]
-    rows = 8 * piece
-    return call(
-        LONG,
-        with_unread(target_kernel, len(after)),
+    out_ref[...] = (l_ref[...].astype(F32) - nn(h_ref[...], p_ref[...])).astype(BF16)
+
+
+def less_target(ids, hidden, left, projection, half, after=(), tile=512):
+    arrays, places = hidden
+    piece, deep = arrays[0].shape
+    rows, width = left.shape
+    return call(
+        LONG,
+        with_unread(functools.partial(target_kernel, places), len(after)),
         (width // tile,),
-        [shape(rows // outs, width, kind)] * outs,
+        shape(rows, width),
         [unread()] * len(after)
         + [smem()]
-        + [whole(h) for h in hidden]
+        + [whole(h) for h in arrays]
         + [pl.BlockSpec((rows, tile), lambda j: (0, j)), pl.BlockSpec((deep, tile), lambda j: (half, j))],
-        [pl.BlockSpec((rows // outs, tile), lambda j: (0, j))] * outs,
+        pl.BlockSpec((rows, tile), lambda j: (0, j)),
         [pltpu.VMEM((rows, deep), BF16)],
         *after,
         ids,
-        *hidden,
+        *arrays,
         left,
         projection,
     )
@@ -289,15 +241,22 @@
 def gap_places(gaps, halves):
     piece = gaps[0].shape[0] // 4
     for half in range(halves):
-        for e in range(4):
-            for n in range(2):
-                yield 2 * e + n, half, 0, gaps[e], (2 * half + n) * piece
-                yield 2 * e + n, half, 1, gaps[4 + 2 * half + n], e * piece
+        for n in range(2):
+            by_x = ((0, 0), (1, 0), (2 + half, 0), (4, 0))
+            for e, (array, _) in enumerate(by_x):
+                start = n if e == 2 else 2 * half + n
+                yield 2 * e + n, half, 0, gaps[array], start * piece
+            for e in range(4):
+                if (half, n) == (0, 1):
+                    array, start = 6 + e // 2, e % 2
+                else:
+                    array, start = {(0, 0): 5, (1, 0): 8, (1, 1): 9}[half, n], e
+                yield 2 * e + n, half, 1, gaps[array], start * piece
 
 
 def values_kernel(ids_ref, *refs):
-    gaps = refs[:8]
-    w_ref, mine_ref, peer_ref, g_ref = refs[8:]
+    gaps = refs[:10]
+    w_ref, mine_ref, peer_ref, g_ref = refs[10:]
     piece = gaps[0].shape[0] // 4
     rows = g_ref.shape[0]
 
@@ -364,8 +323,8 @@
 
 
 def weight_kernel(ids_ref, *refs):
-    gaps = refs[:8]
-    v_ref, out_ref, g_ref = refs[8:]
+    gaps = refs[:10]
+    v_ref, out_ref, g_ref = refs[10:]
     piece = gaps[0].shape[0] // 4
 
     @pl.when(pl.program_id(0) == 0)
@@ -406,21 +365,23 @@
 
 
 def join_kernel(*refs):
-    rows = refs[0].shape[0]
-    for k, ref in enumerate(refs[:-1]):
-        refs[-1][k * rows : (k + 1) * rows, :] = ref[...]
+    start = 0
+    for ref in refs[:-1]:
+        refs[-1][start : start + ref.shape[0], :] = ref[...]
+        start += ref.shape[0]
 
 
 def joined(arrays, after=(), micros=LONG):
-    rows, width = arrays[0].shape
+    rows, width = sum(array.shape[0] for array in arrays), arrays[0].shape[1]
     tile = width // 2
     return call(
         micros,
         with_unread(join_kernel, len(after)),
         (2,),
-        shape(rows * len(arrays), width),
-        [unread()] * len(after) + [pl.BlockSpec((rows, tile), lambda j: (0, j))] * len(arrays),
-        pl.BlockSpec((rows * len(arrays), tile), lambda j: (0, j)),
+        shape(rows, width),
+        [unread()] * len(after)
+        + [pl.BlockSpec((array.shape[0], tile), lambda j: (0, j)) for array in arrays],
+        pl.BlockSpec((rows, tile), lambda j: (0, j)),
         [],
         *after,
         *arrays,
@@ -467,10 +428,47 @@
     )
 
 
+def halve_kernel(a_ref, b_ref, out_a_ref, out_b_ref):
+    out_a_ref[...] = a_ref[...]
+    out_b_ref[...] = b_ref[...]
+
+
+def halved(a, b, after=(), micros=SHORT):
+    rows, width = a.shape[0] // 2, a.shape[1]
+    first, last = (pl.BlockSpec((rows, width), lambda j, k=k: (k, 0)) for k in (0, 1))
+    return call(
+        micros,
+        with_unread(halve_kernel, len(after)),
+        (1,),
+        [shape(rows, width)] * 2,
+        [unread()] * len(after) + [first, last],
+        [first, first],
+        [],
+        *after,
+        a,
+        b,
+    )
+
+
+def near_ring(block, axes, one, three):
+    return swap(block, axes, one), swap(block, axes, three)
+
+
+def far_ring(halves, axes, one, three):
+    return swap(halves[0], axes, three), swap(halves[1], axes, one)
+
+
 def gather_tensor(block, after=()):
     across = [swap(block, Z, k) for k in (1, 3, 2)]
-    pair = swap(joined(across, after), CORE, 1)
-    return [block, *across, swap(block, CORE, 1), pair]
+    arrays = [block, *across, swap(block, CORE, 1)]
+    places = [(0, 0, 0), (2, 1, 0), (6, 2, 0), (4, 3, 0), (1, 4, 0)]
+    if after:
+        arrays.append(swap(joined(across, after), CORE, 1))
+        places += [(3, 5, 0), (7, 5, 1), (5, 5, 2)]
+    else:
+        arrays += [swap(piece, CORE, 1) for piece in across]
+        places += [(3, 5, 0), (7, 6, 0), (5, 7, 0)]
+    return arrays, places
 
 
 def per_device(
@@ -488,21 +486,17 @@
     t = lax.axis_index("z") * 2 + lax.axis_index("core")
     ids = jnp.stack([dp, t, g]).astype(jnp.int32)
 
-    piece = send_order.shape[1] // 16
-
     loss_scale = 1.0 / math.sqrt(student_stream.shape[0] * 16)
 
-    across = [swap(student_values, Z, k) for k in (1, 3, 2)]
-    mine, peer, picked, owned = first_teacher(
-        ids, send_order, teacher_values, teacher_weight, teacher_stream
-    )
-    near = joined((student_values, across[0], across[2], across[1]))
-    early = merged((mine, swap(peer, CORE, 1)), 4, (near,))
+    across = near_ring(student_values, Z, 1, 3)
+    taught = (ids, send_order, teacher_values, teacher_weight, teacher_stream)
+    mine, peer = teacher(*taught, 0)
+    halves = halved(*across, (mine,), LONG)
+    early = merged((mine, swap(peer, CORE, 1)), 4, halves[:1])
     moved = [swap(early[k], Z, k) for k in (1, 3, 2)]
-    mine, peer = second_teacher(
-        picked, owned, teacher_weight, teacher_stream, piece, (early[0],)
-    )
-    keep, give = merged((early[0], *moved), 2, (mine,), LONG)
+    mine, peer = teacher(*taught, 1, (early[0],))
+    near = joined((student_values, across[0], *far_ring(halves, Z, 1, 3), across[1]), (mine,), SHORT)
+    keep, give = merged((early[0], *moved), 2, (near,), LONG)
     late = merged((mine, swap(peer, CORE, 1)), 4, (keep,))
     moved = [swap(late[k], Z, k) for k in (1, 3, 2)]
     first = placed(ids, keep, swap(give, GRP, 1), (late[0],), SHORT)
@@ -510,11 +504,13 @@
     far = swap(near, GRP, 1)
     layer_out = layer(ids, near, pair, student_weight, (first,))
     keep, give = merged((late[0], *moved), 2, (layer_out,), LONG)
-    first = gather_tensor(first, (give, far))
+    first = gather_tensor(first)
     second = placed(ids, keep, swap(give, GRP, 1))
-    left = less_target(ids, first, layer_out, projection, 0, 1, F32, (second,))[0]
-    second = gather_tensor(second, (left,))
-    parts = less_target(ids, second, left, projection, 1, 1, BF16)[0]
+    far_pair = swap(far, CORE, 1)
+    left = less_target(ids, first, layer_out, projection, 0, (second, far))
+    turn = turned(ids, near, pair, far, far_pair, (left,))
+    second = gather_tensor(second, (left, turn))
+    parts = less_target(ids, second, left, projection, 1)
 
     parts = lax.all_to_all(parts.reshape(8, -1, parts.shape[1]), DP, 0, 0, tiled=True)
     total = student_stream.astype(F32) + jnp.sum(parts.astype(F32), axis=0)
@@ -523,12 +519,17 @@
     rows = gap.shape[0] // 2
     first, second = gap[:rows], gap[rows:]
     around = joined([first] + [swap(first, Y, k) for k in (1, 2, 3)])
-    along = joined([second] + [swap(second, X, k) for k in (1, 2, 3)])
-    turn = turned(ids, near, pair, far, swap(far, CORE, 1), (around, along))
-    gaps = [around] + [swap(around, X, k) for k in (1, 2, 3)]
-    gaps += [along] + [swap(along, Y, k) for k in (1, 2, 3)]
-
-    mine, peer = values_partial(ids, gaps, student_weight, (turn,))
+    along = joined([second] + [swap(second, X, k) for k in (1, 2, 3)], (around,))
+    around = joined([first] + [swap(first, Y, k) for k in (1, 2, 3)])
+    along = joined([second] + [swap(second, X, k) for k in (1, 2, 3)], (around,))
+    near_x = near_ring(around, X, 1, 3)
+    near_y = near_ring(along, Y, 2, 3)
+    halves_x = halved(*near_x)
+    far_x = far_ring(halves_x, X, 1, 3)
+    far_y = far_ring(halved(*near_y, halves_x[:1]), Y, 2, 3)
+    gaps = [around, near_x[0], *far_x, near_x[1], along, *far_y, *near_y]
+
+    mine, peer = values_partial(ids, gaps, student_weight, ())
     parts = merged((mine, swap(peer, CORE, 1)), 4, (marker(mine),))
     values_grad = add(parts[0], *[swap(parts[k], Z, k) for k in (1, 3, 2)])
     weight_grad = weight_sums(ids, gaps, turn, (parts[0],))

time: 230 us -> 217 us (0.943)
  waiting for transfers between devices: 40.4 us -> 29.3 us
  starting transfers between devices: 56.1 us -> 50.4 us
  local copies, waits for them, and re-layouts: 9.89 us -> 13.6 us
    ppermute x42 -> x47, waiting for transfers between devices: 40.4 us -> 29.3 us  [swap(): return lax.ppermute(array, axes, [(i, i ^ distance) for i in range(size)])]
    ppermute x42 -> x47, starting transfers between devices: 56.1 us -> 50.4 us  [swap(): return lax.ppermute(array, axes, [(i, i ^ distance) for i in range(size)])]
    unnamed x64 -> x78, local copies, waits for them, and re-layouts: 9.87 us -> 13.6 us
    pallas_call x21 -> x23, Pallas kernels: 86.2 us -> 86.2 us  [call(): pl.pallas_call(body, grid=grid, out_shape=out_shape, in_specs=in_specs, o...]
  transfers between devices with their start and end apart: 42 -> 47, of which waited for: 14 -> 11; matrix products, arithmetic and copies ran while one was open for 0% -> 0% of each run, Pallas kernels for 30% -> 32%
where the time goes in v3:
time: 217 us; the launch traced here: 216 us
  Pallas kernels  86.2 us (40%)
  starting transfers between devices  50.4 us (23%)
  blocking collectives  33.6 us (15%)
  waiting for transfers between devices  29.3 us (14%)
  local copies, waits for them, and re-layouts  13.6 us (6%)
    pallas_call x23, Pallas kernels, call(): pl.pallas_call(body, grid=grid, out_shape=out_shape, in_specs=in_specs, o...  86.2 us
    ppermute x47, starting transfers between devices, swap(): return lax.ppermute(array, axes, [(i, i ^ distance) for i in range(size)])  50.4 us
    all_to_all x1, blocking collectives, per_device(): lax.all_to_all(parts.reshape(8, -1, parts.shape[1]), DP, 0, 0, tiled=True)  33.6 us
    ppermute x47, waiting for transfers between devices, swap(): return lax.ppermute(array, axes, [(i, i ^ distance) for i in range(size)])  29.3 us
    unnamed x78, local copies, waits for them, and re-layouts  13.6 us
  transfers between devices with their start and end apart: 47, of which 11 were waited for; matrix products, arithmetic and copies ran while one was open for 0% of the time, Pallas kernels for 32%

profile of v3, /device:TPU:1, one launch (start us, length us, event | category | flops | bytes accessed | tf_op | source)
XLA Modules:
  0.0 216.1 jit_solution(432832063937138122)
XLA Ops:
  0.6 2.5 %collective-permute-start = (bf16[128,1024]{1,0:T(8,128)(2,1)}, bf16[128,1024]{1,0:T(8,128)(2,1)S(1)}, u32[]{:S(2)}, u32[]{:S(2)}) collective-permute-start(bf16[128,1024]{1,0:T(8,128)(2,1)} %refs_1_.3), channel_id=1, source_target_pairs={{0,2},{2,0},{4,6},{6,4},{1,3},{3,1},{5,7},{7,5},{8,10},{10,8},{12,... | collective-permute-start | bytes 786440 | tf_op jit(solution)/shard_map/ppermute | solution.py:29
  3.2 2.2 %collective-permute-start.1 = (bf16[128,1024]{1,0:T(8,128)(2,1)}, bf16[128,1024]{1,0:T(8,128)(2,1)S(1)}, u32[]{:S(2)}, u32[]{:S(2)}) collective-permute-start(bf16[128,1024]{1,0:T(8,128)(2,1)} %refs_1_.3), channel_id=1, source_target_pairs={{0,6},{2,4},{4,2},{6,0},{1,7},{3,5},{5,3},{7,1},{8,14},{10,12},{12... | collective-permute-start | bytes 786440 | tf_op jit(solution)/shard_map/ppermute | solution.py:29
  6.1 9.9 %shard_map.95 = (bf16[512,1024]{1,0:T(8,128)(2,1)}, bf16[512,1024]{1,0:T(8,128)(2,1)}) custom-call(s32[3]{0:T(128)} %pad_add_fusion.refs_0_.refs_1_.refs_2_, s32[16,128]{1,0:T(8,128)} %refs_2_.3, bf16[1024,2048]{1,0:T(8,128)(2,1)} %refs_3_.3, bf16[2048,2048]{1,0:T(8,128)(2,1)} %refs_4_.4, bf16[128,2048]{1,0:T(8,128)(2,1)} %refs_5_.1), custom_call_target="tpu_custom_call" | custom-call | flops 49999998976 | bytes 1024 | tf_op jit(solution)/shard_map/pallas_call | solution.py:37
  18.0 1.7 shard_map.96
  21.4 2.4 %shard_map.97 = (bf16[128,1024]{1,0:T(8,128)(2,1)}, bf16[128,1024]{1,0:T(8,128)(2,1)}, bf16[128,1024]{1,0:T(8,128)(2,1)}, bf16[128,1024]{1,0:T(8,128)(2,1)}) custom-call(bf16[64,1024]{1,0:T(8,128)(2,1)} %get-tuple-element.31.refs_0_, bf16[512,1024]{1,0:T(8,128)(2,1)} %get-tuple-element.30.refs_0_.refs_1_, bf16[512,1024]{1,0:T(8,128)(2,1)} %copy-done.1), custom_call_target="tpu_custom_call" | custom-call | flops 10000000 | bytes 1024 | tf_op jit(solution)/shard_map/pallas_call | solution.py:37
  25.0 2.2 %collective-permute-start.6 = (bf16[128,1024]{1,0:T(8,128)(2,1)}, bf16[128,1024]{1,0:T(8,128)(2,1)S(1)}, u32[]{:S(2)}, u32[]{:S(2)}) collective-permute-start(bf16[128,1024]{1,0:T(8,128)(2,1)} %get-tuple-element.37), channel_id=1, source_target_pairs={{0,6},{2,4},{4,2},{6,0},{1,7},{3,5},{5,3},{7,1},{8,14},{10,12},{12... | collective-permute-start | bytes 786440 | tf_op jit(solution)/shard_map/ppermute | solution.py:29
  27.2 9.9 %shard_map.98 = (bf16[512,1024]{1,0:T(8,128)(2,1)}, bf16[512,1024]{1,0:T(8,128)(2,1)}) custom-call(bf16[128,1024]{1,0:T(8,128)(2,1)} %get-tuple-element.33.refs_0_.refs_1_, s32[3]{0:T(128)} %pad_add_fusion.refs_0_.refs_1_.refs_2_, s32[16,128]{1,0:T(8,128)} %refs_2_.3, bf16[1024,2048]{1,0:T(8,128)(2,1)} %refs_3_.3, bf16[2048,2048]{1,0:T(8,128)(2,1)} %refs_4_.4, ...), custom_call_target="tpu_custom_call" | custom-call | flops 49999998976 | bytes 1024 | tf_op jit(solution)/shard_map/pallas_call | solution.py:37
  39.0 2.2 %shard_map.99.refs_0_.refs_2_ = bf16[512,1024]{1,0:T(8,128)(2,1)} custom-call(bf16[512,1024]{1,0:T(8,128)(2,1)} %get-tuple-element.34.refs_0_.refs_1_, bf16[128,1024]{1,0:T(8,128)(2,1)} %refs_1_.3, bf16[128,1024]{1,0:T(8,128)(2,1)} %copy-done.6, bf16[64,1024]{1,0:T(8,128)(2,1)} %copy-done.11, bf16[64,1024]{1,0:T(8,128)(2,1)} %copy-done.12, ...), custom_call_target="tpu_custom_call" | custom-call | flops 10000000 | bytes 1024 | tf_op jit(solution)/shard_map/pallas_call | solution.py:37
  42.7 2.0 shard_map.100
  44.7 1.3 collective-permute-start.9
  46.2 2.4 %shard_map.101 = (bf16[128,1024]{1,0:T(8,128)(2,1)}, bf16[128,1024]{1,0:T(8,128)(2,1)}, bf16[128,1024]{1,0:T(8,128)(2,1)}, bf16[128,1024]{1,0:T(8,128)(2,1)}) custom-call(bf16[64,1024]{1,0:T(8,128)(2,1)} %get-tuple-element.39.refs_0_.refs_2_, bf16[512,1024]{1,0:T(8,128)(2,1)} %get-tuple-element.34.refs_0_.refs_1_, ...), custom_call_target="tpu_custom_call" | custom-call | flops 10000000 | bytes 1024 | tf_op jit(solution)/shard_map/pallas_call | solution.py:37
  49.9 2.2 %collective-permute-start.12 = (bf16[128,1024]{1,0:T(8,128)(2,1)}, bf16[128,1024]{1,0:T(8,128)(2,1)}, u32[]{:S(2)}, u32[]{:S(2)}) collective-permute-start(bf16[128,1024]{1,0:T(8,128)(2,1)} %get-tuple-element.44), channel_id=1, source_target_pairs={{0,6},{2,4},{4,2},{6,0},{1,7},{3,5},{5,3},{7,1},{8,14},{10,12},{12... | collective-permute-start | bytes 786440 | tf_op jit(solution)/shard_map/ppermute | solution.py:29
  52.8 1.7 shard_map.102.refs_0_.refs_3_
  54.8 5.5 %shard_map.103.refs_0_.refs_11_ = bf16[1024,1024]{1,0:T(8,128)(2,1)} custom-call(bf16[128,1024]{1,0:T(8,128)(2,1)} %shard_map.102.refs_0_.refs_3_, s32[3]{0:T(128)} %pad_add_fusion.refs_0_.refs_1_.refs_2_, bf16[512,1024]{1,0:T(8,128)(2,1)} %shard_map.99.refs_0_.refs_2_, bf16[512,1024]{1,0:T(8,128)(2,1)} %collective-permute-done.10.refs_3_, ...), custom_call_target="tpu_custom_call" | custom-call | flops 49999998976 | bytes 1024 | tf_op jit(solution)/shard_map/pallas_call | solution.py:37
  60.3 2.3 %collective-permute-start.21 = (bf16[128,1024]{1,0:T(8,128)(2,1)S(1)}, bf16[128,1024]{1,0:T(8,128)(2,1)S(1)}, u32[]{:S(2)}, u32[]{:S(2)}) collective-permute-start(bf16[128,1024]{1,0:T(8,128)(2,1)S(1)} %copy-done.9), channel_id=1, source_target_pairs={{0,6},{2,4},{4,2},{6,0},{1,7},{3,5},{5,3},{7,1},{8,14},{10,12},{12... | collective-permute-start | bytes 786440 | tf_op jit(solution)/shard_map/ppermute | solution.py:29
  63.3 2.0 shard_map.104
  65.3 1.3 collective-permute-start.14
  66.6 5.5 %collective-permute-done.19.refs_1_.refs_4_ = bf16[512,1024]{1,0:T(8,128)(2,1)} collective-permute-done((bf16[512,1024]{1,0:T(8,128)(2,1)S(1)}, bf16[512,1024]{1,0:T(8,128)(2,1)}, u32[]{:S(2)}, u32[]{:S(2)}) %collective-permute-start.19) | collective-permute-done | bytes 1048608 | tf_op jit(solution)/shard_map/ppermute | solution.py:29
  72.1 2.3 %collective-permute-start.23 = (bf16[128,1024]{1,0:T(8,128)(2,1)S(1)}, bf16[128,1024]{1,0:T(8,128)(2,1)}, u32[]{:S(2)}, u32[]{:S(2)}) collective-permute-start(bf16[128,1024]{1,0:T(8,128)(2,1)S(1)} %copy-done.9), channel_id=1, source_target_pairs={{0,1},{1,0},{2,3},{3,2},{4,5},{5,4},{6,7},{7,6},{8,9},{9,8},{10,11... | collective-permute-start | bytes 786440 | tf_op jit(solution)/shard_map/ppermute | solution.py:29
  74.5 2.5 %collective-permute-start.24 = (bf16[128,1024]{1,0:T(8,128)(2,1)S(1)}, bf16[128,1024]{1,0:T(8,128)(2,1)}, u32[]{:S(2)}, u32[]{:S(2)}) collective-permute-start(bf16[128,1024]{1,0:T(8,128)(2,1)S(1)} %collective-permute-done.20.refs_4_), channel_id=1, source_target_pairs={{0,1},{1,0},{2,3},{3,2},{4,5},{5,4},{6,7},{7,6},{8,9},{9,8},{10,11... | collective-permute-start | bytes 786440 | tf_op jit(solution)/shard_map/ppermute | solution.py:29
  77.9 1.7 shard_map.105.refs_0_.refs_1_
  79.9 2.0 collective-permute-start.16
  83.1 5.9 %shard_map.106.refs_0_.refs_7_ = bf16[1024,1024]{1,0:T(8,128)(2,1)} custom-call(bf16[128,1024]{1,0:T(8,128)(2,1)} %shard_map.105.refs_0_.refs_1_, bf16[512,1024]{1,0:T(8,128)(2,1)} %collective-permute-done.19.refs_1_.refs_4_, s32[3]{0:T(128)} %pad_add_fusion.refs_0_.refs_1_.refs_2_, bf16[128,1024]{1,0:T(8,128)(2,1)} %shard_map.102.refs_0_.refs_3_, ...), custom_call_target="tpu_custom_call" | custom-call | flops 49999998976 | bytes 1024 | tf_op jit(solution)/shard_map/pallas_call | solution.py:37
  90.0 5.5 %shard_map.107.refs_1_.refs_12_ = bf16[1024,2048]{1,0:T(8,128)(2,1)} custom-call(bf16[1024,1024]{1,0:T(8,128)(2,1)} %shard_map.106.refs_0_.refs_7_, s32[3]{0:T(128)} %pad_add_fusion.refs_0_.refs_1_.refs_2_, bf16[512,1024]{1,0:T(8,128)(2,1)} %shard_map.99.refs_0_.refs_2_, bf16[512,1024]{1,0:T(8,128)(2,1)} %collective-permute-done.10.refs_3_, ...), custom_call_target="tpu_custom_call" | custom-call | flops 49999998976 | bytes 1024 | tf_op jit(solution)/shard_map/pallas_call | solution.py:37
  97.0 2.0 shard_map.108
  100.0 2.2 %collective-permute-done.18.refs_5_ = bf16[128,1024]{1,0:T(8,128)(2,1)S(1)} collective-permute-done((bf16[128,1024]{1,0:T(8,128)(2,1)S(1)}, bf16[128,1024]{1,0:T(8,128)(2,1)S(1)}, u32[]{:S(2)}, u32[]{:S(2)}) %collective-permute-start.18) | collective-permute-done | bytes 262176 | tf_op jit(solution)/shard_map/ppermute | solution.py:29
  103.9 5.9 %shard_map.109 = bf16[1024,1024]{1,0:T(8,128)(2,1)} custom-call(s32[3]{0:T(128)} %pad_add_fusion.refs_0_.refs_1_.refs_2_, bf16[128,1024]{1,0:T(8,128)(2,1)} %shard_map.105.refs_0_.refs_1_, bf16[128,1024]{1,0:T(8,128)(2,1)} %copy-done.24, bf16[128,1024]{1,0:T(8,128)(2,1)} %copy-done.26, bf16[128,1024]{1,0:T(8,128)(2,1)} %copy-done.28, ...), custom_call_target="tpu_custom_call" | custom-call | flops 49999998976 | bytes 1024 | tf_op jit(solution)/shard_map/pallas_call | solution.py:37
  109.7 33.6 %all_to_all.5 = bf16[8,128,1024]{2,1,0:T(8,128)(2,1)S(1)} all-to-all(bf16[8,128,1024]{2,1,0:T(8,128)(2,1)} %bitcast.4), channel_id=1, replica_groups=mesh['grp'=2,'x'=4,'yh'=2,'z'=4,'core'=2] {'x','yh'}, dimensions={0} | all-to-all | bytes 4194304 | tf_op jit(solution)/shard_map/all_to_all | solution.py:515
  143.8 1.7 collective-permute-start.29
  147.1 2.1 collective-permute-start.37
  149.3 1.7 collective-permute-start.38
  151.0 1.8 collective-permute-done.31.refs_3_
  153.5 1.8 shard_map.110.refs_0_.refs_1_.refs_2_
  157.7 1.8 shard_map.112.refs_6_.refs_7_
  161.4 4.7 %collective-permute-done.32.refs_0_.refs_2_.refs_3_ = bf16[256,1024]{1,0:T(8,128)(2,1)S(1)} collective-permute-done((bf16[256,1024]{1,0:T(8,128)(2,1)}, bf16[256,1024]{1,0:T(8,128)(2,1)S(1)}, u32[]{:S(2)}, u32[]{:S(2)}) %collective-permute-start.32) | collective-permute-done | bytes 524320 | tf_op jit(solution)/shard_map/ppermute | solution.py:29
  166.1 1.9 collective-permute-done.33.refs_1_.refs_5_.refs_6_
  168.8 1.8 shard_map.111
  171.3 1.8 collective-permute-done.40.refs_2_.refs_10_.refs_11_
  173.1 1.9 shard_map.113
  175.8 1.5 collective-permute-done.34.refs_3_.refs_4_
  177.3 4.3 %collective-permute-done.41.refs_7_.refs_8_ = bf16[128,1024]{1,0:T(8,128)(2,1)S(1)} collective-permute-done((bf16[128,1024]{1,0:T(8,128)(2,1)}, bf16[128,1024]{1,0:T(8,128)(2,1)S(1)}, u32[]{:S(2)}, u32[]{:S(2)}) %collective-permute-start.41) | collective-permute-done | bytes 262176 | tf_op jit(solution)/shard_map/ppermute | solution.py:29
  183.0 6.1 %shard_map.114 = (bf16[512,1024]{1,0:T(8,128)(2,1)}, bf16[512,1024]{1,0:T(8,128)(2,1)}) custom-call(s32[3]{0:T(128)} %pad_add_fusion.refs_0_.refs_1_.refs_2_, bf16[256,1024]{1,0:T(8,128)(2,1)} %shard_map.110.refs_0_.refs_1_.refs_2_, bf16[256,1024]{1,0:T(8,128)(2,1)} %copy-done.3, bf16[128,1024]{1,0:T(8,128)(2,1)} %copy-done.20, ...), custom_call_target="tpu_custom_call" | custom-call | flops 49999998976 | bytes 1024 | tf_op jit(solution)/shard_map/pallas_call | solution.py:37
  189.2 4.5 %collective-permute-start.43 = (bf16[512,1024]{1,0:T(8,128)(2,1)}, bf16[512,1024]{1,0:T(8,128)(2,1)S(1)}, u32[]{:S(2)}, u32[]{:S(2)}) collective-permute-start(bf16[512,1024]{1,0:T(8,128)(2,1)} %get-tuple-element.53), channel_id=1, source_target_pairs={{0,1},{1,0},{2,3},{3,2},{4,5},{5,4},{6,7},{7,6},{8,9},{9,8},{10,11... | collective-permute-start | bytes 3145736 | tf_op jit(solution)/shard_map/ppermute | solution.py:29
  194.2 1.9 collective-permute-done.43.refs_2_
  197.2 2.4 %shard_map.116 = (bf16[128,1024]{1,0:T(8,128)(2,1)}, bf16[128,1024]{1,0:T(8,128)(2,1)}, bf16[128,1024]{1,0:T(8,128)(2,1)}, bf16[128,1024]{1,0:T(8,128)(2,1)}) custom-call(f32[8,128]{1,0:T(8,128)} %shard_map.115.refs_0_, bf16[512,1024]{1,0:T(8,128)(2,1)} %get-tuple-element.52.refs_0_.refs_1_, bf16[512,1024]{1,0:T(8,128)(2,1)} %copy-done.2), custom_call_target="tpu_custom_call" | custom-call | flops 10000000 | bytes 1024 | tf_op jit(solution)/shard_map/pallas_call | solution.py:37
  199.5 1.9 collective-permute-start.46
  202.3 9.1 %shard_map.117 = f32[1024,1024]{1,0:T(8,128)} custom-call(bf16[128,1024]{1,0:T(8,128)(2,1)} %get-tuple-element.54.refs_0_, s32[3]{0:T(128)} %pad_add_fusion.refs_0_.refs_1_.refs_2_, bf16[256,1024]{1,0:T(8,128)(2,1)} %shard_map.110.refs_0_.refs_1_.refs_2_, bf16[256,1024]{1,0:T(8,128)(2,1)} %copy-done.3, bf16[128,1024]{1,0:T(8,128)(2,1)} %copy-done.20, ...), custom_call_target="tpu_custom_call" | custom-call | flops 49999998976 | bytes 1024 | tf_op jit(solution)/shard_map/pallas_call | solution.py:37
  211.5 3.7 %collective-permute-done.45 = bf16[128,1024]{1,0:T(8,128)(2,1)S(1)} collective-permute-done((bf16[128,1024]{1,0:T(8,128)(2,1)}, bf16[128,1024]{1,0:T(8,128)(2,1)S(1)}, u32[]{:S(2)}, u32[]{:S(2)}) %collective-permute-start.45) | collective-permute-done | bytes 262176 | tf_op jit(solution)/shard_map/ppermute | solution.py:29
  (153 shorter events, 33.9 us)
Async XLA Ops:
  0.6 16.6 %collective-permute-start = (bf16[128,1024]{1,0:T(8,128)(2,1)}, bf16[128,1024]{1,0:T(8,128)(2,1)S(1)}, u32[]{:S(2)}, u32[]{:S(2)}) collective-permute-start(bf16[128,1024]{1,0:T(8,128)(2,1)} %refs_1_.3), channel_id=1, source_target_pairs={{0,2},{2,0},{4,6},{6,4},{1,3},{3,1},{5,7},{7,5},{8,10},{10,8},{12,... | collective-permute-start | bytes 786440 | tf_op jit(solution)/shard_map/ppermute | solution.py:29
  3.2 14.0 %collective-permute-start.1 = (bf16[128,1024]{1,0:T(8,128)(2,1)}, bf16[128,1024]{1,0:T(8,128)(2,1)S(1)}, u32[]{:S(2)}, u32[]{:S(2)}) collective-permute-start(bf16[128,1024]{1,0:T(8,128)(2,1)} %refs_1_.3), channel_id=1, source_target_pairs={{0,6},{2,4},{4,2},{6,0},{1,7},{3,5},{5,3},{7,1},{8,14},{10,12},{12... | collective-permute-start | bytes 786440 | tf_op jit(solution)/shard_map/ppermute | solution.py:29
  16.0 4.5 %collective-permute-start.2 = (bf16[512,1024]{1,0:T(8,128)(2,1)}, bf16[512,1024]{1,0:T(8,128)(2,1)S(1)}, u32[]{:S(2)}, u32[]{:S(2)}) collective-permute-start(bf16[512,1024]{1,0:T(8,128)(2,1)} %get-tuple-element.32), channel_id=1, source_target_pairs={{0,1},{1,0},{2,3},{3,2},{4,5},{5,4},{6,7},{7,6},{8,9},{9,8},{10,11... | collective-permute-start | bytes 3145736 | tf_op jit(solution)/shard_map/ppermute | solution.py:29
  19.7 17.4 %collective-permute-start.3 = (bf16[64,1024]{1,0:T(8,128)(2,1)}, bf16[64,1024]{1,0:T(8,128)(2,1)S(1)}, u32[]{:S(2)}, u32[]{:S(2)}) collective-permute-start(bf16[64,1024]{1,0:T(8,128)(2,1)} %get-tuple-element.31.refs_0_), channel_id=1, source_target_pairs={{0,6},{2,4},{4,2},{6,0},{1,7},{3,5},{5,3},{7,1},{8,14},{10,12},{12... | collective-permute-start | bytes 393224 | tf_op jit(solution)/shard_map/ppermute | solution.py:29
  20.1 18.2 %collective-permute-start.4 = (bf16[64,1024]{1,0:T(8,128)(2,1)}, bf16[64,1024]{1,0:T(8,128)(2,1)S(1)}, u32[]{:S(2)}, u32[]{:S(2)}) collective-permute-start(bf16[64,1024]{1,0:T(8,128)(2,1)} %get-tuple-element.35), channel_id=1, source_target_pairs={{0,2},{2,0},{4,6},{6,4},{1,3},{3,1},{5,7},{7,5},{8,10},{10,8},{12,... | collective-permute-start | bytes 393224 | tf_op jit(solution)/shard_map/ppermute | solution.py:29
  23.8 17.5 %collective-permute-start.5 = (bf16[128,1024]{1,0:T(8,128)(2,1)}, bf16[128,1024]{1,0:T(8,128)(2,1)S(1)}, u32[]{:S(2)}, u32[]{:S(2)}) collective-permute-start(bf16[128,1024]{1,0:T(8,128)(2,1)} %get-tuple-element.36), channel_id=1, source_target_pairs={{0,2},{2,0},{4,6},{6,4},{1,3},{3,1},{5,7},{7,5},{8,10},{10,8},{12,... | collective-permute-start | bytes 786440 | tf_op jit(solution)/shard_map/ppermute | solution.py:29
  25.0 16.3 %collective-permute-start.6 = (bf16[128,1024]{1,0:T(8,128)(2,1)}, bf16[128,1024]{1,0:T(8,128)(2,1)S(1)}, u32[]{:S(2)}, u32[]{:S(2)}) collective-permute-start(bf16[128,1024]{1,0:T(8,128)(2,1)} %get-tuple-element.37), channel_id=1, source_target_pairs={{0,6},{2,4},{4,2},{6,0},{1,7},{3,5},{5,3},{7,1},{8,14},{10,12},{12... | collective-permute-start | bytes 786440 | tf_op jit(solution)/shard_map/ppermute | solution.py:29
  27.2 14.1 %collective-permute-start.7 = (bf16[128,1024]{1,0:T(8,128)(2,1)}, bf16[128,1024]{1,0:T(8,128)(2,1)S(1)}, u32[]{:S(2)}, u32[]{:S(2)}) collective-permute-start(bf16[128,1024]{1,0:T(8,128)(2,1)} %get-tuple-element.38), channel_id=1, source_target_pairs={{0,4},{2,6},{4,0},{6,2},{1,5},{3,7},{5,1},{7,3},{8,12},{10,14},{12... | collective-permute-start | bytes 786440 | tf_op jit(solution)/shard_map/ppermute | solution.py:29
  37.1 9.1 %collective-permute-start.8 = (bf16[512,1024]{1,0:T(8,128)(2,1)}, bf16[512,1024]{1,0:T(8,128)(2,1)}, u32[]{:S(2)}, u32[]{:S(2)}) collective-permute-start(bf16[512,1024]{1,0:T(8,128)(2,1)} %get-tuple-element.40), channel_id=1, source_target_pairs={{0,1},{1,0},{2,3},{3,2},{4,5},{5,4},{6,7},{7,6},{8,9},{9,8},{10,11... | collective-permute-start | bytes 3145736 | tf_op jit(solution)/shard_map/ppermute | solution.py:29
  41.2 13.2 %collective-permute-start.10 = (bf16[512,1024]{1,0:T(8,128)(2,1)}, bf16[512,1024]{1,0:T(8,128)(2,1)}, u32[]{:S(2)}, u32[]{:S(2)}) collective-permute-start(bf16[512,1024]{1,0:T(8,128)(2,1)} %shard_map.99.refs_0_.refs_2_), channel_id=1, source_target_pairs={{0,1},{1,0},{2,3},{3,2},{4,5},{5,4},{6,7},{7,6},{8,9},{9,8},{10,11... | collective-permute-start | bytes 3145736 | tf_op jit(solution)/shard_map/ppermute | solution.py:29
  44.7 7.4 %collective-permute-start.9 = (bf16[64,1024]{1,0:T(8,128)(2,1)}, bf16[64,1024]{1,0:T(8,128)(2,1)S(1)}, u32[]{:S(2)}, u32[]{:S(2)}) collective-permute-start(bf16[64,1024]{1,0:T(8,128)(2,1)} %get-tuple-element.42), channel_id=1, source_target_pairs={{0,64},{64,0},{1,65},{65,1},{2,66},{66,2},{3,67},{67,3},{4,68},{68... | collective-permute-start | bytes 393224 | tf_op jit(solution)/shard_map/ppermute | solution.py:29
  46.0 26.1 %collective-permute-start.19 = (bf16[512,1024]{1,0:T(8,128)(2,1)S(1)}, bf16[512,1024]{1,0:T(8,128)(2,1)}, u32[]{:S(2)}, u32[]{:S(2)}) collective-permute-start(bf16[512,1024]{1,0:T(8,128)(2,1)S(1)} %copy-done), channel_id=1, source_target_pairs={{0,64},{64,0},{1,65},{65,1},{2,66},{66,2},{3,67},{67,3},{4,68},{68... | collective-permute-start | bytes 3145736 | tf_op jit(solution)/shard_map/ppermute | solution.py:29
  48.6 11.7 %collective-permute-start.11 = (bf16[128,1024]{1,0:T(8,128)(2,1)}, bf16[128,1024]{1,0:T(8,128)(2,1)}, u32[]{:S(2)}, u32[]{:S(2)}) collective-permute-start(bf16[128,1024]{1,0:T(8,128)(2,1)} %get-tuple-element.43), channel_id=1, source_target_pairs={{0,2},{2,0},{4,6},{6,4},{1,3},{3,1},{5,7},{7,5},{8,10},{10,8},{12,... | collective-permute-start | bytes 786440 | tf_op jit(solution)/shard_map/ppermute | solution.py:29
  49.9 12.8 %collective-permute-start.12 = (bf16[128,1024]{1,0:T(8,128)(2,1)}, bf16[128,1024]{1,0:T(8,128)(2,1)}, u32[]{:S(2)}, u32[]{:S(2)}) collective-permute-start(bf16[128,1024]{1,0:T(8,128)(2,1)} %get-tuple-element.44), channel_id=1, source_target_pairs={{0,6},{2,4},{4,2},{6,0},{1,7},{3,5},{5,3},{7,1},{8,14},{10,12},{12... | collective-permute-start | bytes 786440 | tf_op jit(solution)/shard_map/ppermute | solution.py:29
  52.1 11.2 %collective-permute-start.13 = (bf16[128,1024]{1,0:T(8,128)(2,1)}, bf16[128,1024]{1,0:T(8,128)(2,1)}, u32[]{:S(2)}, u32[]{:S(2)}) collective-permute-start(bf16[128,1024]{1,0:T(8,128)(2,1)} %get-tuple-element.45), channel_id=1, source_target_pairs={{0,4},{2,6},{4,0},{6,2},{1,5},{3,7},{5,1},{7,3},{8,12},{10,14},{12... | collective-permute-start | bytes 786440 | tf_op jit(solution)/shard_map/ppermute | solution.py:29
  54.5 19.9 %collective-permute-start.20 = (bf16[128,1024]{1,0:T(8,128)(2,1)}, bf16[128,1024]{1,0:T(8,128)(2,1)S(1)}, u32[]{:S(2)}, u32[]{:S(2)}) collective-permute-start(bf16[128,1024]{1,0:T(8,128)(2,1)} %shard_map.102.refs_0_.refs_3_), channel_id=1, source_target_pairs={{0,2},{2,0},{4,6},{6,4},{1,3},{3,1},{5,7},{7,5},{8,10},{10,8},{12,... | collective-permute-start | bytes 786440 | tf_op jit(solution)/shard_map/ppermute | solution.py:29
  60.3 14.1 %collective-permute-start.21 = (bf16[128,1024]{1,0:T(8,128)(2,1)S(1)}, bf16[128,1024]{1,0:T(8,128)(2,1)S(1)}, u32[]{:S(2)}, u32[]{:S(2)}) collective-permute-start(bf16[128,1024]{1,0:T(8,128)(2,1)S(1)} %copy-done.9), channel_id=1, source_target_pairs={{0,6},{2,4},{4,2},{6,0},{1,7},{3,5},{5,3},{7,1},{8,14},{10,12},{12... | collective-permute-start | bytes 786440 | tf_op jit(solution)/shard_map/ppermute | solution.py:29
  62.7 14.3 %collective-permute-start.22 = (bf16[128,1024]{1,0:T(8,128)(2,1)S(1)}, bf16[128,1024]{1,0:T(8,128)(2,1)}, u32[]{:S(2)}, u32[]{:S(2)}) collective-permute-start(bf16[128,1024]{1,0:T(8,128)(2,1)S(1)} %copy-done.9), channel_id=1, source_target_pairs={{0,4},{2,6},{4,0},{6,2},{1,5},{3,7},{5,1},{7,3},{8,12},{10,14},{12... | collective-permute-start | bytes 786440 | tf_op jit(solution)/shard_map/ppermute | solution.py:29
  65.3 11.9 %collective-permute-start.14 = (bf16[64,1024]{1,0:T(8,128)(2,1)}, bf16[64,1024]{1,0:T(8,128)(2,1)S(1)}, u32[]{:S(2)}, u32[]{:S(2)}) collective-permute-start(bf16[64,1024]{1,0:T(8,128)(2,1)} %get-tuple-element.47), channel_id=1, source_target_pairs={{0,64},{64,0},{1,65},{65,1},{2,66},{66,2},{3,67},{67,3},{4,68},{68... | collective-permute-start | bytes 393224 | tf_op jit(solution)/shard_map/ppermute | solution.py:29
  72.1 7.5 %collective-permute-start.23 = (bf16[128,1024]{1,0:T(8,128)(2,1)S(1)}, bf16[128,1024]{1,0:T(8,128)(2,1)}, u32[]{:S(2)}, u32[]{:S(2)}) collective-permute-start(bf16[128,1024]{1,0:T(8,128)(2,1)S(1)} %copy-done.9), channel_id=1, source_target_pairs={{0,1},{1,0},{2,3},{3,2},{4,5},{5,4},{6,7},{7,6},{8,9},{9,8},{10,11... | collective-permute-start | bytes 786440 | tf_op jit(solution)/shard_map/ppermute | solution.py:29
  74.4 14.6 %collective-permute-start.27 = (bf16[512,1024]{1,0:T(8,128)(2,1)}, bf16[512,1024]{1,0:T(8,128)(2,1)S(1)}, u32[]{:S(2)}, u32[]{:S(2)}) collective-permute-start(bf16[512,1024]{1,0:T(8,128)(2,1)} %collective-permute-done.19.refs_1_.refs_4_), channel_id=1, source_target_pairs={{0,1},{1,0},{2,3},{3,2},{4,5},{5,4},{6,7},{7,6},{8,9},{9,8},{10,11... | collective-permute-start | bytes 3145736 | tf_op jit(solution)/shard_map/ppermute | solution.py:29
  74.5 5.5 %collective-permute-start.24 = (bf16[128,1024]{1,0:T(8,128)(2,1)S(1)}, bf16[128,1024]{1,0:T(8,128)(2,1)}, u32[]{:S(2)}, u32[]{:S(2)}) collective-permute-start(bf16[128,1024]{1,0:T(8,128)(2,1)S(1)} %collective-permute-done.20.refs_4_), channel_id=1, source_target_pairs={{0,1},{1,0},{2,3},{3,2},{4,5},{5,4},{6,7},{7,6},{8,9},{9,8},{10,11... | collective-permute-start | bytes 786440 | tf_op jit(solution)/shard_map/ppermute | solution.py:29
  76.9 5.0 %collective-permute-start.25 = (bf16[128,1024]{1,0:T(8,128)(2,1)S(1)}, bf16[128,1024]{1,0:T(8,128)(2,1)}, u32[]{:S(2)}, u32[]{:S(2)}) collective-permute-start(bf16[128,1024]{1,0:T(8,128)(2,1)S(1)} %collective-permute-done.21.refs_5_), channel_id=1, source_target_pairs={{0,1},{1,0},{2,3},{3,2},{4,5},{5,4},{6,7},{7,6},{8,9},{9,8},{10,11... | collective-permute-start | bytes 786440 | tf_op jit(solution)/shard_map/ppermute | solution.py:29
  77.2 5.9 %collective-permute-start.26 = (bf16[128,1024]{1,0:T(8,128)(2,1)}, bf16[128,1024]{1,0:T(8,128)(2,1)}, u32[]{:S(2)}, u32[]{:S(2)}) collective-permute-start(bf16[128,1024]{1,0:T(8,128)(2,1)} %collective-permute-done.22.refs_6_), channel_id=1, source_target_pairs={{0,1},{1,0},{2,3},{3,2},{4,5},{5,4},{6,7},{7,6},{8,9},{9,8},{10,11... | collective-permute-start | bytes 786440 | tf_op jit(solution)/shard_map/ppermute | solution.py:29
  79.6 15.9 %collective-permute-start.15 = (bf16[128,1024]{1,0:T(8,128)(2,1)}, bf16[128,1024]{1,0:T(8,128)(2,1)S(1)}, u32[]{:S(2)}, u32[]{:S(2)}) collective-permute-start(bf16[128,1024]{1,0:T(8,128)(2,1)} %shard_map.105.refs_0_.refs_1_), channel_id=1, source_target_pairs={{0,2},{2,0},{4,6},{6,4},{1,3},{3,1},{5,7},{7,5},{8,10},{10,8},{12,... | collective-permute-start | bytes 786440 | tf_op jit(solution)/shard_map/ppermute | solution.py:29
  79.9 15.6 %collective-permute-start.16 = (bf16[128,1024]{1,0:T(8,128)(2,1)}, bf16[128,1024]{1,0:T(8,128)(2,1)S(1)}, u32[]{:S(2)}, u32[]{:S(2)}) collective-permute-start(bf16[128,1024]{1,0:T(8,128)(2,1)} %shard_map.105.refs_0_.refs_1_), channel_id=1, source_target_pairs={{0,6},{2,4},{4,2},{6,0},{1,7},{3,5},{5,3},{7,1},{8,14},{10,12},{12... | collective-permute-start | bytes 786440 | tf_op jit(solution)/shard_map/ppermute | solution.py:29
  81.9 13.6 %collective-permute-start.17 = (bf16[128,1024]{1,0:T(8,128)(2,1)}, bf16[128,1024]{1,0:T(8,128)(2,1)S(1)}, u32[]{:S(2)}, u32[]{:S(2)}) collective-permute-start(bf16[128,1024]{1,0:T(8,128)(2,1)} %shard_map.105.refs_0_.refs_1_), channel_id=1, source_target_pairs={{0,4},{2,6},{4,0},{6,2},{1,5},{3,7},{5,1},{7,3},{8,12},{10,14},{12... | collective-permute-start | bytes 786440 | tf_op jit(solution)/shard_map/ppermute | solution.py:29
  99.0 3.3 %collective-permute-start.28 = (bf16[384,1024]{1,0:T(8,128)(2,1)}, bf16[384,1024]{1,0:T(8,128)(2,1)S(1)}, u32[]{:S(2)}, u32[]{:S(2)}) collective-permute-start(bf16[384,1024]{1,0:T(8,128)(2,1)} %shard_map.108), channel_id=1, source_target_pairs={{0,1},{1,0},{2,3},{3,2},{4,5},{5,4},{6,7},{7,6},{8,9},{9,8},{10,11... | collective-permute-start | bytes 2359304 | tf_op jit(solution)/shard_map/ppermute | solution.py:29
  99.9 2.3 %collective-permute-start.18 = (bf16[128,1024]{1,0:T(8,128)(2,1)S(1)}, bf16[128,1024]{1,0:T(8,128)(2,1)S(1)}, u32[]{:S(2)}, u32[]{:S(2)}) collective-permute-start(bf16[128,1024]{1,0:T(8,128)(2,1)S(1)} %copy-done.22), channel_id=1, source_target_pairs={{0,1},{1,0},{2,3},{3,2},{4,5},{5,4},{6,7},{7,6},{8,9},{9,8},{10,11... | collective-permute-start | bytes 786440 | tf_op jit(solution)/shard_map/ppermute | solution.py:29
  109.7 34.0 %copy-start.8 = (bf16[128,1024]{1,0:T(8,128)(2,1)S(1)}, bf16[128,1024]{1,0:T(8,128)(2,1)}, u32[]{:S(2)}) copy-start(bf16[128,1024]{1,0:T(8,128)(2,1)} %param.15) | copy-start | bytes 786436
  143.8 5.5 %collective-permute-start.29 = (bf16[64,1024]{1,0:T(8,128)(2,1)S(1)}, bf16[64,1024]{1,0:T(8,128)(2,1)S(1)}, u32[]{:S(2)}, u32[]{:S(2)}) collective-permute-start(bf16[64,1024]{1,0:T(8,128)(2,1)S(1)} %get-tuple-element.59.refs_0_), channel_id=1, source_target_pairs={{0,8},{8,0},{64,72},{72,64},{1,9},{9,1},{65,73},{73,65},{2,10},{10... | collective-permute-start | bytes 393224 | tf_op jit(solution)/shard_map/ppermute | solution.py:29
  145.5 5.5 %collective-permute-start.30 = (bf16[64,1024]{1,0:T(8,128)(2,1)S(1)}, bf16[64,1024]{1,0:T(8,128)(2,1)S(1)}, u32[]{:S(2)}, u32[]{:S(2)}) collective-permute-start(bf16[64,1024]{1,0:T(8,128)(2,1)S(1)} %get-tuple-element.59.refs_0_), channel_id=1, source_target_pairs={{0,64},{8,72},{64,0},{72,8},{1,65},{9,73},{65,1},{73,9},{2,66},{10... | collective-permute-start | bytes 393224 | tf_op jit(solution)/shard_map/ppermute | solution.py:29
  145.9 6.9 %collective-permute-start.31 = (bf16[64,1024]{1,0:T(8,128)(2,1)S(1)}, bf16[64,1024]{1,0:T(8,128)(2,1)S(1)}, u32[]{:S(2)}, u32[]{:S(2)}) collective-permute-start(bf16[64,1024]{1,0:T(8,128)(2,1)S(1)} %get-tuple-element.59.refs_0_), channel_id=1, source_target_pairs={{0,72},{8,64},{64,8},{72,0},{1,73},{9,65},{65,9},{73,1},{2,74},{10... | collective-permute-start | bytes 393224 | tf_op jit(solution)/shard_map/ppermute | solution.py:29
  147.1 9.2 %collective-permute-start.36 = (bf16[64,1024]{1,0:T(8,128)(2,1)S(1)}, bf16[64,1024]{1,0:T(8,128)(2,1)S(1)}, u32[]{:S(2)}, u32[]{:S(2)}) collective-permute-start(bf16[64,1024]{1,0:T(8,128)(2,1)S(1)} %get-tuple-element.58.refs_1_), channel_id=1, source_target_pairs={{0,16},{16,0},{32,48},{48,32},{1,17},{17,1},{33,49},{49,33},{2,18}... | collective-permute-start | bytes 393224 | tf_op jit(solution)/shard_map/ppermute | solution.py:29
  147.1 9.2 %collective-permute-start.37 = (bf16[64,1024]{1,0:T(8,128)(2,1)S(1)}, bf16[64,1024]{1,0:T(8,128)(2,1)S(1)}, u32[]{:S(2)}, u32[]{:S(2)}) collective-permute-start(bf16[64,1024]{1,0:T(8,128)(2,1)S(1)} %get-tuple-element.58.refs_1_), channel_id=1, source_target_pairs={{0,32},{16,48},{32,0},{48,16},{1,33},{17,49},{33,1},{49,17},{2,34}... | collective-permute-start | bytes 393224 | tf_op jit(solution)/shard_map/ppermute | solution.py:29
  149.3 7.1 %collective-permute-start.38 = (bf16[64,1024]{1,0:T(8,128)(2,1)S(1)}, bf16[64,1024]{1,0:T(8,128)(2,1)S(1)}, u32[]{:S(2)}, u32[]{:S(2)}) collective-permute-start(bf16[64,1024]{1,0:T(8,128)(2,1)S(1)} %get-tuple-element.58.refs_1_), channel_id=1, source_target_pairs={{0,48},{16,32},{32,16},{48,0},{1,49},{17,33},{33,17},{49,1},{2,50}... | collective-permute-start | bytes 393224 | tf_op jit(solution)/shard_map/ppermute | solution.py:29
  155.2 10.9 %collective-permute-start.32 = (bf16[256,1024]{1,0:T(8,128)(2,1)}, bf16[256,1024]{1,0:T(8,128)(2,1)S(1)}, u32[]{:S(2)}, u32[]{:S(2)}) collective-permute-start(bf16[256,1024]{1,0:T(8,128)(2,1)} %shard_map.110.refs_0_.refs_1_.refs_2_), channel_id=1, source_target_pairs={{0,16},{16,0},{32,48},{48,32},{1,17},{17,1},{33,49},{49,33},{2,18}... | collective-permute-start | bytes 1572872 | tf_op jit(solution)/shard_map/ppermute | solution.py:29
  155.6 12.4 %collective-permute-start.33 = (bf16[256,1024]{1,0:T(8,128)(2,1)}, bf16[256,1024]{1,0:T(8,128)(2,1)S(1)}, u32[]{:S(2)}, u32[]{:S(2)}) collective-permute-start(bf16[256,1024]{1,0:T(8,128)(2,1)} %shard_map.110.refs_0_.refs_1_.refs_2_), channel_id=1, source_target_pairs={{0,48},{16,32},{32,16},{48,0},{1,49},{17,33},{33,17},{49,1},{2,50}... | collective-permute-start | bytes 1572872 | tf_op jit(solution)/shard_map/ppermute | solution.py:29
  159.5 11.8 %collective-permute-start.39 = (bf16[256,1024]{1,0:T(8,128)(2,1)}, bf16[256,1024]{1,0:T(8,128)(2,1)S(1)}, u32[]{:S(2)}, u32[]{:S(2)}) collective-permute-start(bf16[256,1024]{1,0:T(8,128)(2,1)} %shard_map.112.refs_6_.refs_7_), channel_id=1, source_target_pairs={{0,64},{8,72},{64,0},{72,8},{1,65},{9,73},{65,1},{73,9},{2,66},{10... | collective-permute-start | bytes 1572872 | tf_op jit(solution)/shard_map/ppermute | solution.py:29
  160.6 12.5 %collective-permute-start.40 = (bf16[256,1024]{1,0:T(8,128)(2,1)}, bf16[256,1024]{1,0:T(8,128)(2,1)}, u32[]{:S(2)}, u32[]{:S(2)}) collective-permute-start(bf16[256,1024]{1,0:T(8,128)(2,1)} %shard_map.112.refs_6_.refs_7_), channel_id=1, source_target_pairs={{0,72},{8,64},{64,8},{72,0},{1,73},{9,65},{65,9},{73,1},{2,74},{10... | collective-permute-start | bytes 1572872 | tf_op jit(solution)/shard_map/ppermute | solution.py:29
  170.6 6.6 %collective-permute-start.34 = (bf16[128,1024]{1,0:T(8,128)(2,1)}, bf16[128,1024]{1,0:T(8,128)(2,1)S(1)}, u32[]{:S(2)}, u32[]{:S(2)}) collective-permute-start(bf16[128,1024]{1,0:T(8,128)(2,1)} %get-tuple-element.48.refs_0_), channel_id=1, source_target_pairs={{0,48},{16,32},{32,16},{48,0},{1,49},{17,33},{33,17},{49,1},{2,50}... | collective-permute-start | bytes 786440 | tf_op jit(solution)/shard_map/ppermute | solution.py:29
  171.2 6.0 %collective-permute-start.35 = (bf16[128,1024]{1,0:T(8,128)(2,1)}, bf16[128,1024]{1,0:T(8,128)(2,1)S(1)}, u32[]{:S(2)}, u32[]{:S(2)}) collective-permute-start(bf16[128,1024]{1,0:T(8,128)(2,1)} %get-tuple-element.49), channel_id=1, source_target_pairs={{0,16},{16,0},{32,48},{48,32},{1,17},{17,1},{33,49},{49,33},{2,18}... | collective-permute-start | bytes 786440 | tf_op jit(solution)/shard_map/ppermute | solution.py:29
  174.9 6.6 %collective-permute-start.41 = (bf16[128,1024]{1,0:T(8,128)(2,1)}, bf16[128,1024]{1,0:T(8,128)(2,1)S(1)}, u32[]{:S(2)}, u32[]{:S(2)}) collective-permute-start(bf16[128,1024]{1,0:T(8,128)(2,1)} %get-tuple-element.50), channel_id=1, source_target_pairs={{0,72},{8,64},{64,8},{72,0},{1,73},{9,65},{65,9},{73,1},{2,74},{10... | collective-permute-start | bytes 786440 | tf_op jit(solution)/shard_map/ppermute | solution.py:29
  175.2 6.4 %collective-permute-start.42 = (bf16[128,1024]{1,0:T(8,128)(2,1)}, bf16[128,1024]{1,0:T(8,128)(2,1)S(1)}, u32[]{:S(2)}, u32[]{:S(2)}) collective-permute-start(bf16[128,1024]{1,0:T(8,128)(2,1)} %get-tuple-element.51), channel_id=1, source_target_pairs={{0,64},{8,72},{64,0},{72,8},{1,65},{9,73},{65,1},{73,9},{2,66},{10... | collective-permute-start | bytes 786440 | tf_op jit(solution)/shard_map/ppermute | solution.py:29
  189.2 7.0 %collective-permute-start.43 = (bf16[512,1024]{1,0:T(8,128)(2,1)}, bf16[512,1024]{1,0:T(8,128)(2,1)S(1)}, u32[]{:S(2)}, u32[]{:S(2)}) collective-permute-start(bf16[512,1024]{1,0:T(8,128)(2,1)} %get-tuple-element.53), channel_id=1, source_target_pairs={{0,1},{1,0},{2,3},{3,2},{4,5},{5,4},{6,7},{7,6},{8,9},{9,8},{10,11... | collective-permute-start | bytes 3145736 | tf_op jit(solution)/shard_map/ppermute | solution.py:29
  199.5 11.9 %collective-permute-start.46 = (bf16[128,1024]{1,0:T(8,128)(2,1)}, bf16[128,1024]{1,0:T(8,128)(2,1)S(1)}, u32[]{:S(2)}, u32[]{:S(2)}) collective-permute-start(bf16[128,1024]{1,0:T(8,128)(2,1)} %get-tuple-element.57), channel_id=1, source_target_pairs={{0,4},{2,6},{4,0},{6,2},{1,5},{3,7},{5,1},{7,3},{8,12},{10,14},{12... | collective-permute-start | bytes 786440 | tf_op jit(solution)/shard_map/ppermute | solution.py:29
  201.5 13.6 %collective-permute-start.45 = (bf16[128,1024]{1,0:T(8,128)(2,1)}, bf16[128,1024]{1,0:T(8,128)(2,1)S(1)}, u32[]{:S(2)}, u32[]{:S(2)}) collective-permute-start(bf16[128,1024]{1,0:T(8,128)(2,1)} %get-tuple-element.56), channel_id=1, source_target_pairs={{0,6},{2,4},{4,2},{6,0},{1,7},{3,5},{5,3},{7,1},{8,14},{10,12},{12... | collective-permute-start | bytes 786440 | tf_op jit(solution)/shard_map/ppermute | solution.py:29
  202.2 12.9 %collective-permute-start.44 = (bf16[128,1024]{1,0:T(8,128)(2,1)}, bf16[128,1024]{1,0:T(8,128)(2,1)S(1)}, u32[]{:S(2)}, u32[]{:S(2)}) collective-permute-start(bf16[128,1024]{1,0:T(8,128)(2,1)} %get-tuple-element.55), channel_id=1, source_target_pairs={{0,2},{2,0},{4,6},{6,4},{1,3},{3,1},{5,7},{7,5},{8,10},{10,8},{12,... | collective-permute-start | bytes 786440 | tf_op jit(solution)/shard_map/ppermute | solution.py:29
  (38 other events, 94.9 us)

commit v4 on v3

--- a/solution.py
+++ b/solution.py
@@ -238,31 +238,31 @@
     )
 
 
-def gap_places(gaps, halves):
-    piece = gaps[0].shape[0] // 4
-    for half in range(halves):
-        for n in range(2):
-            by_x = ((0, 0), (1, 0), (2 + half, 0), (4, 0))
-            for e, (array, _) in enumerate(by_x):
-                start = n if e == 2 else 2 * half + n
-                yield 2 * e + n, half, 0, gaps[array], start * piece
-            for e in range(4):
-                if (half, n) == (0, 1):
-                    array, start = 6 + e // 2, e % 2
-                else:
-                    array, start = {(0, 0): 5, (1, 0): 8, (1, 1): 9}[half, n], e
-                yield 2 * e + n, half, 1, gaps[array], start * piece
+def own_places(own_x, near_x, far_x, next_x, own_y, far_y):
+    piece = own_x.shape[0] // 4
+    for n in range(2):
+        for e, ref in enumerate((own_x, near_x, far_x, next_x)):
+            yield 2 * e + n, 0, ref, n * piece
+            yield 2 * e + n, 1, (own_y, far_y)[n], e * piece
+
+
+def other_places(own_x, near_x, far_x, next_x, near_y, next_y):
+    piece = own_x.shape[0] // 4
+    for n in range(2):
+        for e, ref in enumerate((own_x, near_x, far_x, next_x)):
+            yield 2 * e + n, 0, ref, (n if e == 2 else 2 + n) * piece
+            yield 2 * e + n, 1, (near_y, next_y)[n], e * piece
 
 
 def values_kernel(ids_ref, *refs):
-    gaps = refs[:10]
-    w_ref, mine_ref, peer_ref, g_ref = refs[10:]
+    gaps = refs[:6]
+    w_ref, mine_ref, peer_ref, g_ref = refs[6:]
     piece = gaps[0].shape[0] // 4
     rows = g_ref.shape[0]
 
     @pl.when(pl.program_id(0) == 0)
     def _():
-        for k, _, part, ref, start in gap_places(gaps, 1):
+        for k, part, ref, start in own_places(*gaps):
             to = ids_ref[0] ^ ids_ref[1] ^ k
             place = (to & 1) * (rows // 2) + (to >> 1) * (2 * piece) + part * piece
             g_ref[pl.ds(pl.multiple_of(place, piece), piece), :] = ref[start : start + piece, :]
@@ -323,15 +323,18 @@
 
 
 def weight_kernel(ids_ref, *refs):
-    gaps = refs[:10]
-    v_ref, out_ref, g_ref = refs[10:]
+    gaps = refs[:9]
+    v_ref, out_ref, g_ref = refs[9:]
     piece = gaps[0].shape[0] // 4
 
     @pl.when(pl.program_id(0) == 0)
     def _():
-        for k, half, part, ref, start in gap_places(gaps, 2):
-            place = half * (g_ref.shape[0] // 2) + (ids_ref[0] ^ k) * (2 * piece) + part * piece
-            g_ref[pl.ds(pl.multiple_of(place, piece), piece), :] = ref[start : start + piece, :]
+        own = own_places(*gaps[:3], *gaps[4:7])
+        other = other_places(*gaps[:2], *gaps[3:5], *gaps[7:])
+        for half, places in enumerate((own, other)):
+            for k, part, ref, start in places:
+                place = half * (g_ref.shape[0] // 2) + (ids_ref[0] ^ k) * (2 * piece) + part * piece
+                g_ref[pl.ds(pl.multiple_of(place, piece), piece), :] = ref[start : start + piece, :]
 
     out_ref[...] = nn(v_ref[...], g_ref[...])
 
@@ -456,6 +459,11 @@
 
 def far_ring(halves, axes, one, three):
     return swap(halves[0], axes, three), swap(halves[1], axes, one)
+
+
+def split(a, b):
+    rows = a.shape[0] // 2
+    return a[:rows], b[rows:]
 
 
 def gather_tensor(block, after=()):
@@ -520,16 +528,13 @@
     first, second = gap[:rows], gap[rows:]
     around = joined([first] + [swap(first, Y, k) for k in (1, 2, 3)])
     along = joined([second] + [swap(second, X, k) for k in (1, 2, 3)], (around,))
-    around = joined([first] + [swap(first, Y, k) for k in (1, 2, 3)])
-    along = joined([second] + [swap(second, X, k) for k in (1, 2, 3)], (around,))
     near_x = near_ring(around, X, 1, 3)
-    near_y = near_ring(along, Y, 2, 3)
-    halves_x = halved(*near_x)
-    far_x = far_ring(halves_x, X, 1, 3)
-    far_y = far_ring(halved(*near_y, halves_x[:1]), Y, 2, 3)
-    gaps = [around, near_x[0], *far_x, near_x[1], along, *far_y, *near_y]
-
-    mine, peer = values_partial(ids, gaps, student_weight, ())
+    own_y = swap(along, Y, 1)
+    far_x = far_ring(split(*near_x), X, 1, 3)
+    gaps = [around, near_x[0], *far_x, near_x[1], along, own_y]
+    gaps += [swap(along, Y, 2), swap(along, Y, 3)]
+
+    mine, peer = values_partial(ids, gaps[:3] + gaps[4:7], student_weight, ())
     parts = merged((mine, swap(peer, CORE, 1)), 4, (marker(mine),))
     values_grad = add(parts[0], *[swap(parts[k], Z, k) for k in (1, 3, 2)])
     weight_grad = weight_sums(ids, gaps, turn, (parts[0],))

time: 217 us -> 209 us (0.963)
  waiting for transfers between devices: 29.3 us -> 24.6 us
  Pallas kernels: 86.2 us -> 82.2 us
  starting transfers between devices: 50.4 us -> 53.4 us
  local copies, waits for them, and re-layouts: 13.6 us -> 11.4 us
    ppermute x47 -> x46, waiting for transfers between devices: 29.3 us -> 24.6 us  [swap(): return lax.ppermute(array, axes, [(i, i ^ distance) for i in range(size)])]
    pallas_call x23 -> x21, Pallas kernels: 86.2 us -> 82.2 us  [call(): pl.pallas_call(body, grid=grid, out_shape=out_shape, in_specs=in_specs, o...]
    ppermute x47 -> x46, starting transfers between devices: 50.4 us -> 53.4 us  [swap(): return lax.ppermute(array, axes, [(i, i ^ distance) for i in range(size)])]
    unnamed x78 -> x70, local copies, waits for them, and re-layouts: 13.6 us -> 11.3 us
  transfers between devices with their start and end apart: 47 -> 46, of which waited for: 11 -> 10; matrix products, arithmetic and copies ran while one was open for 0% -> 0% of each run, Pallas kernels for 32% -> 36%
where the time goes in v4:
time: 209 us; the launch traced here: 208 us
  Pallas kernels  82.2 us (39%)
  starting transfers between devices  53.4 us (26%)
  blocking collectives  33.6 us (16%)
  waiting for transfers between devices  24.6 us (12%)
  local copies, waits for them, and re-layouts  11.4 us (5%)
    pallas_call x21, Pallas kernels, call(): pl.pallas_call(body, grid=grid, out_shape=out_shape, in_specs=in_specs, o...  82.2 us
    ppermute x46, starting transfers between devices, swap(): return lax.ppermute(array, axes, [(i, i ^ distance) for i in range(size)])  53.4 us
    all_to_all x1, blocking collectives, per_device(): lax.all_to_all(parts.reshape(8, -1, parts.shape[1]), DP, 0, 0, tiled=True)  33.6 us
    ppermute x46, waiting for transfers between devices, swap(): return lax.ppermute(array, axes, [(i, i ^ distance) for i in range(size)])  24.6 us
    unnamed x70, local copies, waits for them, and re-layouts  11.3 us
  transfers between devices with their start and end apart: 46, of which 10 were waited for; matrix products, arithmetic and copies ran while one was open for 0% of the time, Pallas kernels for 36%

profile of v4, /device:TPU:1, one launch (start us, length us, event | category | flops | bytes accessed | tf_op | source)
XLA Modules:
  0.0 208.1 jit_solution(9827062772102862610)
XLA Ops:
  0.6 2.5 %collective-permute-start = (bf16[128,1024]{1,0:T(8,128)(2,1)}, bf16[128,1024]{1,0:T(8,128)(2,1)S(1)}, u32[]{:S(2)}, u32[]{:S(2)}) collective-permute-start(bf16[128,1024]{1,0:T(8,128)(2,1)} %refs_1_.3), channel_id=1, source_target_pairs={{0,2},{2,0},{4,6},{6,4},{1,3},{3,1},{5,7},{7,5},{8,10},{10,8},{12,... | collective-permute-start | bytes 786440 | tf_op jit(solution)/shard_map/ppermute | solution.py:29
  3.2 2.2 %collective-permute-start.1 = (bf16[128,1024]{1,0:T(8,128)(2,1)}, bf16[128,1024]{1,0:T(8,128)(2,1)S(1)}, u32[]{:S(2)}, u32[]{:S(2)}) collective-permute-start(bf16[128,1024]{1,0:T(8,128)(2,1)} %refs_1_.3), channel_id=1, source_target_pairs={{0,6},{2,4},{4,2},{6,0},{1,7},{3,5},{5,3},{7,1},{8,14},{10,12},{12... | collective-permute-start | bytes 786440 | tf_op jit(solution)/shard_map/ppermute | solution.py:29
  6.1 9.9 %shard_map.95 = (bf16[512,1024]{1,0:T(8,128)(2,1)}, bf16[512,1024]{1,0:T(8,128)(2,1)}) custom-call(s32[3]{0:T(128)} %pad_add_fusion.refs_0_.refs_1_.refs_2_, s32[16,128]{1,0:T(8,128)} %refs_2_.3, bf16[1024,2048]{1,0:T(8,128)(2,1)} %refs_3_.3, bf16[2048,2048]{1,0:T(8,128)(2,1)} %refs_4_.4, bf16[128,2048]{1,0:T(8,128)(2,1)} %refs_5_.1), custom_call_target="tpu_custom_call" | custom-call | flops 49999998976 | bytes 1024 | tf_op jit(solution)/shard_map/pallas_call | solution.py:37
  16.0 1.2 collective-permute-start.2
  18.0 1.7 shard_map.96
  21.4 2.4 %shard_map.97 = (bf16[128,1024]{1,0:T(8,128)(2,1)}, bf16[128,1024]{1,0:T(8,128)(2,1)}, bf16[128,1024]{1,0:T(8,128)(2,1)}, bf16[128,1024]{1,0:T(8,128)(2,1)}) custom-call(bf16[64,1024]{1,0:T(8,128)(2,1)} %get-tuple-element.27.refs_0_, bf16[512,1024]{1,0:T(8,128)(2,1)} %get-tuple-element.26.refs_0_.refs_1_, bf16[512,1024]{1,0:T(8,128)(2,1)} %copy-done.1), custom_call_target="tpu_custom_call" | custom-call | flops 10000000 | bytes 1024 | tf_op jit(solution)/shard_map/pallas_call | solution.py:37
  25.0 2.3 %collective-permute-start.6 = (bf16[128,1024]{1,0:T(8,128)(2,1)}, bf16[128,1024]{1,0:T(8,128)(2,1)S(1)}, u32[]{:S(2)}, u32[]{:S(2)}) collective-permute-start(bf16[128,1024]{1,0:T(8,128)(2,1)} %get-tuple-element.33), channel_id=1, source_target_pairs={{0,6},{2,4},{4,2},{6,0},{1,7},{3,5},{5,3},{7,1},{8,14},{10,12},{12... | collective-permute-start | bytes 786440 | tf_op jit(solution)/shard_map/ppermute | solution.py:29
  27.2 9.9 %shard_map.98 = (bf16[512,1024]{1,0:T(8,128)(2,1)}, bf16[512,1024]{1,0:T(8,128)(2,1)}) custom-call(bf16[128,1024]{1,0:T(8,128)(2,1)} %get-tuple-element.29.refs_0_.refs_1_, s32[3]{0:T(128)} %pad_add_fusion.refs_0_.refs_1_.refs_2_, s32[16,128]{1,0:T(8,128)} %refs_2_.3, bf16[1024,2048]{1,0:T(8,128)(2,1)} %refs_3_.3, bf16[2048,2048]{1,0:T(8,128)(2,1)} %refs_4_.4, ...), custom_call_target="tpu_custom_call" | custom-call | flops 49999998976 | bytes 1024 | tf_op jit(solution)/shard_map/pallas_call | solution.py:37
  39.0 2.2 %shard_map.99.refs_0_.refs_2_ = bf16[512,1024]{1,0:T(8,128)(2,1)} custom-call(bf16[512,1024]{1,0:T(8,128)(2,1)} %get-tuple-element.30.refs_0_.refs_1_, bf16[128,1024]{1,0:T(8,128)(2,1)} %refs_1_.3, bf16[128,1024]{1,0:T(8,128)(2,1)} %copy-done.3, bf16[64,1024]{1,0:T(8,128)(2,1)} %copy-done.8, bf16[64,1024]{1,0:T(8,128)(2,1)} %copy-done.9, ...), custom_call_target="tpu_custom_call" | custom-call | flops 10000000 | bytes 1024 | tf_op jit(solution)/shard_map/pallas_call | solution.py:37
  42.7 2.0 shard_map.100
  44.7 1.3 collective-permute-start.9
  46.2 2.4 %shard_map.101 = (bf16[128,1024]{1,0:T(8,128)(2,1)}, bf16[128,1024]{1,0:T(8,128)(2,1)}, bf16[128,1024]{1,0:T(8,128)(2,1)}, bf16[128,1024]{1,0:T(8,128)(2,1)}) custom-call(bf16[64,1024]{1,0:T(8,128)(2,1)} %get-tuple-element.35.refs_0_.refs_2_, bf16[512,1024]{1,0:T(8,128)(2,1)} %get-tuple-element.30.refs_0_.refs_1_, ...), custom_call_target="tpu_custom_call" | custom-call | flops 10000000 | bytes 1024 | tf_op jit(solution)/shard_map/pallas_call | solution.py:37
  48.6 1.3 collective-permute-start.11
  49.8 2.3 %collective-permute-start.12 = (bf16[128,1024]{1,0:T(8,128)(2,1)}, bf16[128,1024]{1,0:T(8,128)(2,1)}, u32[]{:S(2)}, u32[]{:S(2)}) collective-permute-start(bf16[128,1024]{1,0:T(8,128)(2,1)} %get-tuple-element.40), channel_id=1, source_target_pairs={{0,6},{2,4},{4,2},{6,0},{1,7},{3,5},{5,3},{7,1},{8,14},{10,12},{12... | collective-permute-start | bytes 786440 | tf_op jit(solution)/shard_map/ppermute | solution.py:29
  52.8 1.7 shard_map.102.refs_0_.refs_3_
  54.8 5.5 %shard_map.103.refs_0_.refs_11_ = bf16[1024,1024]{1,0:T(8,128)(2,1)} custom-call(bf16[128,1024]{1,0:T(8,128)(2,1)} %shard_map.102.refs_0_.refs_3_, s32[3]{0:T(128)} %pad_add_fusion.refs_0_.refs_1_.refs_2_, bf16[512,1024]{1,0:T(8,128)(2,1)} %shard_map.99.refs_0_.refs_2_, bf16[512,1024]{1,0:T(8,128)(2,1)} %collective-permute-done.10.refs_3_, ...), custom_call_target="tpu_custom_call" | custom-call | flops 49999998976 | bytes 1024 | tf_op jit(solution)/shard_map/pallas_call | solution.py:37
  60.3 2.3 %collective-permute-start.21 = (bf16[128,1024]{1,0:T(8,128)(2,1)S(1)}, bf16[128,1024]{1,0:T(8,128)(2,1)S(1)}, u32[]{:S(2)}, u32[]{:S(2)}) collective-permute-start(bf16[128,1024]{1,0:T(8,128)(2,1)S(1)} %copy-done.6), channel_id=1, source_target_pairs={{0,6},{2,4},{4,2},{6,0},{1,7},{3,5},{5,3},{7,1},{8,14},{10,12},{12... | collective-permute-start | bytes 786440 | tf_op jit(solution)/shard_map/ppermute | solution.py:29
  63.3 2.0 shard_map.104
  65.3 1.3 collective-permute-start.14
  66.6 5.5 %collective-permute-done.19.refs_1_.refs_4_ = bf16[512,1024]{1,0:T(8,128)(2,1)} collective-permute-done((bf16[512,1024]{1,0:T(8,128)(2,1)S(1)}, bf16[512,1024]{1,0:T(8,128)(2,1)}, u32[]{:S(2)}, u32[]{:S(2)}) %collective-permute-start.19) | collective-permute-done | bytes 1048608 | tf_op jit(solution)/shard_map/ppermute | solution.py:29
  72.1 2.3 %collective-permute-start.23 = (bf16[128,1024]{1,0:T(8,128)(2,1)S(1)}, bf16[128,1024]{1,0:T(8,128)(2,1)}, u32[]{:S(2)}, u32[]{:S(2)}) collective-permute-start(bf16[128,1024]{1,0:T(8,128)(2,1)S(1)} %copy-done.6), channel_id=1, source_target_pairs={{0,1},{1,0},{2,3},{3,2},{4,5},{5,4},{6,7},{7,6},{8,9},{9,8},{10,11... | collective-permute-start | bytes 786440 | tf_op jit(solution)/shard_map/ppermute | solution.py:29
  74.5 2.4 %collective-permute-start.24 = (bf16[128,1024]{1,0:T(8,128)(2,1)S(1)}, bf16[128,1024]{1,0:T(8,128)(2,1)}, u32[]{:S(2)}, u32[]{:S(2)}) collective-permute-start(bf16[128,1024]{1,0:T(8,128)(2,1)S(1)} %collective-permute-done.20.refs_4_), channel_id=1, source_target_pairs={{0,1},{1,0},{2,3},{3,2},{4,5},{5,4},{6,7},{7,6},{8,9},{9,8},{10,11... | collective-permute-start | bytes 786440 | tf_op jit(solution)/shard_map/ppermute | solution.py:29
  77.8 1.7 shard_map.105.refs_0_.refs_1_
  79.9 2.0 collective-permute-start.16
  83.1 5.9 %shard_map.106.refs_0_.refs_7_ = bf16[1024,1024]{1,0:T(8,128)(2,1)} custom-call(bf16[128,1024]{1,0:T(8,128)(2,1)} %shard_map.105.refs_0_.refs_1_, bf16[512,1024]{1,0:T(8,128)(2,1)} %collective-permute-done.19.refs_1_.refs_4_, s32[3]{0:T(128)} %pad_add_fusion.refs_0_.refs_1_.refs_2_, bf16[128,1024]{1,0:T(8,128)(2,1)} %shard_map.102.refs_0_.refs_3_, ...), custom_call_target="tpu_custom_call" | custom-call | flops 49999998976 | bytes 1024 | tf_op jit(solution)/shard_map/pallas_call | solution.py:37
  90.0 5.5 %shard_map.107.refs_1_.refs_11_ = bf16[1024,2048]{1,0:T(8,128)(2,1)} custom-call(bf16[1024,1024]{1,0:T(8,128)(2,1)} %shard_map.106.refs_0_.refs_7_, s32[3]{0:T(128)} %pad_add_fusion.refs_0_.refs_1_.refs_2_, bf16[512,1024]{1,0:T(8,128)(2,1)} %shard_map.99.refs_0_.refs_2_, bf16[512,1024]{1,0:T(8,128)(2,1)} %collective-permute-done.10.refs_3_, ...), custom_call_target="tpu_custom_call" | custom-call | flops 49999998976 | bytes 1024 | tf_op jit(solution)/shard_map/pallas_call | solution.py:37
  97.1 2.0 shard_map.108
  100.1 2.2 %collective-permute-done.18.refs_5_ = bf16[128,1024]{1,0:T(8,128)(2,1)S(1)} collective-permute-done((bf16[128,1024]{1,0:T(8,128)(2,1)S(1)}, bf16[128,1024]{1,0:T(8,128)(2,1)S(1)}, u32[]{:S(2)}, u32[]{:S(2)}) %collective-permute-start.18) | collective-permute-done | bytes 262176 | tf_op jit(solution)/shard_map/ppermute | solution.py:29
  103.9 5.9 %shard_map.109 = bf16[1024,1024]{1,0:T(8,128)(2,1)} custom-call(s32[3]{0:T(128)} %pad_add_fusion.refs_0_.refs_1_.refs_2_, bf16[128,1024]{1,0:T(8,128)(2,1)} %shard_map.105.refs_0_.refs_1_, bf16[128,1024]{1,0:T(8,128)(2,1)} %copy-done.21, bf16[128,1024]{1,0:T(8,128)(2,1)} %copy-done.22, bf16[128,1024]{1,0:T(8,128)(2,1)} %copy-done.24, ...), custom_call_target="tpu_custom_call" | custom-call | flops 49999998976 | bytes 1024 | tf_op jit(solution)/shard_map/pallas_call | solution.py:37
  109.8 33.6 %all_to_all.5 = bf16[8,128,1024]{2,1,0:T(8,128)(2,1)S(1)} all-to-all(bf16[8,128,1024]{2,1,0:T(8,128)(2,1)} %bitcast.4), channel_id=1, replica_groups=mesh['grp'=2,'x'=4,'yh'=2,'z'=4,'core'=2] {'x','yh'}, dimensions={0} | all-to-all | bytes 4194304 | tf_op jit(solution)/shard_map/all_to_all | solution.py:523
  143.9 1.7 collective-permute-start.29
  147.2 2.1 %collective-permute-start.36 = (bf16[64,1024]{1,0:T(8,128)(2,1)S(1)}, bf16[64,1024]{1,0:T(8,128)(2,1)S(1)}, u32[]{:S(2)}, u32[]{:S(2)}) collective-permute-start(bf16[64,1024]{1,0:T(8,128)(2,1)S(1)} %get-tuple-element.50.refs_1_), channel_id=1, source_target_pairs={{0,32},{16,48},{32,0},{48,16},{1,33},{17,49},{33,1},{49,17},{2,34}... | collective-permute-start | bytes 393224 | tf_op jit(solution)/shard_map/ppermute | solution.py:29
  149.4 1.7 collective-permute-start.37
  151.1 1.8 collective-permute-done.31.refs_3_
  153.6 1.8 shard_map.110.refs_0_.refs_1_.refs_2_
  157.8 1.8 shard_map.111.refs_5_.refs_7_
  159.6 1.7 collective-permute-start.38
  161.3 4.9 %collective-permute-done.32.refs_2_.refs_3_ = bf16[256,1024]{1,0:T(8,128)(2,1)S(1)} collective-permute-done((bf16[256,1024]{1,0:T(8,128)(2,1)}, bf16[256,1024]{1,0:T(8,128)(2,1)S(1)}, u32[]{:S(2)}, u32[]{:S(2)}) %collective-permute-start.32) | collective-permute-done | bytes 524320 | tf_op jit(solution)/shard_map/ppermute | solution.py:29
  168.0 1.5 collective-permute-start.43
  169.5 2.4 %collective-permute-done.38.refs_6_.refs_8_ = bf16[256,1024]{1,0:T(8,128)(2,1)S(1)} collective-permute-done((bf16[256,1024]{1,0:T(8,128)(2,1)}, bf16[256,1024]{1,0:T(8,128)(2,1)S(1)}, u32[]{:S(2)}, u32[]{:S(2)}) %collective-permute-start.38) | collective-permute-done | bytes 524320 | tf_op jit(solution)/shard_map/ppermute | solution.py:29
  171.9 2.0 collective-permute-done.33.refs_3_.refs_4_
  173.9 5.8 %shard_map.112 = (bf16[512,1024]{1,0:T(8,128)(2,1)}, bf16[512,1024]{1,0:T(8,128)(2,1)}) custom-call(s32[3]{0:T(128)} %pad_add_fusion.refs_0_.refs_1_.refs_2_, bf16[256,1024]{1,0:T(8,128)(2,1)} %shard_map.110.refs_0_.refs_1_.refs_2_, bf16[256,1024]{1,0:T(8,128)(2,1)} %copy-done.10, bf16[128,1024]{1,0:T(8,128)(2,1)} %collective-permute-done.33.refs_3_.refs_4_, ...), custom_call_target="tpu_custom_call" | custom-call | flops 49999998976 | bytes 1024 | tf_op jit(solution)/shard_map/pallas_call | solution.py:37
  179.6 6.0 %collective-permute-start.39 = (bf16[512,1024]{1,0:T(8,128)(2,1)}, bf16[512,1024]{1,0:T(8,128)(2,1)S(1)}, u32[]{:S(2)}, u32[]{:S(2)}) collective-permute-start(bf16[512,1024]{1,0:T(8,128)(2,1)} %get-tuple-element.45), channel_id=1, source_target_pairs={{0,1},{1,0},{2,3},{3,2},{4,5},{5,4},{6,7},{7,6},{8,9},{9,8},{10,11... | collective-permute-start | bytes 3145736 | tf_op jit(solution)/shard_map/ppermute | solution.py:29
  186.3 1.9 collective-permute-done.39.refs_2_
  189.2 2.4 %shard_map.114 = (bf16[128,1024]{1,0:T(8,128)(2,1)}, bf16[128,1024]{1,0:T(8,128)(2,1)}, bf16[128,1024]{1,0:T(8,128)(2,1)}, bf16[128,1024]{1,0:T(8,128)(2,1)}) custom-call(f32[8,128]{1,0:T(8,128)} %shard_map.113.refs_0_, bf16[512,1024]{1,0:T(8,128)(2,1)} %get-tuple-element.44.refs_0_.refs_1_, bf16[512,1024]{1,0:T(8,128)(2,1)} %copy-done.2), custom_call_target="tpu_custom_call" | custom-call | flops 10000000 | bytes 1024 | tf_op jit(solution)/shard_map/pallas_call | solution.py:37
  191.6 1.9 collective-permute-start.42
  194.3 9.2 %shard_map.115 = f32[1024,1024]{1,0:T(8,128)} custom-call(bf16[128,1024]{1,0:T(8,128)(2,1)} %get-tuple-element.46.refs_0_, s32[3]{0:T(128)} %pad_add_fusion.refs_0_.refs_1_.refs_2_, bf16[256,1024]{1,0:T(8,128)(2,1)} %shard_map.110.refs_0_.refs_1_.refs_2_, bf16[256,1024]{1,0:T(8,128)(2,1)} %copy-done.10, ...), custom_call_target="tpu_custom_call" | custom-call | flops 49999998976 | bytes 1024 | tf_op jit(solution)/shard_map/pallas_call | solution.py:37
  203.5 3.6 %collective-permute-done.41 = bf16[128,1024]{1,0:T(8,128)(2,1)S(1)} collective-permute-done((bf16[128,1024]{1,0:T(8,128)(2,1)}, bf16[128,1024]{1,0:T(8,128)(2,1)S(1)}, u32[]{:S(2)}, u32[]{:S(2)}) %collective-permute-start.41) | collective-permute-done | bytes 262176 | tf_op jit(solution)/shard_map/ppermute | solution.py:29
  (143 shorter events, 27.6 us)
Async XLA Ops:
  0.6 16.6 %collective-permute-start = (bf16[128,1024]{1,0:T(8,128)(2,1)}, bf16[128,1024]{1,0:T(8,128)(2,1)S(1)}, u32[]{:S(2)}, u32[]{:S(2)}) collective-permute-start(bf16[128,1024]{1,0:T(8,128)(2,1)} %refs_1_.3), channel_id=1, source_target_pairs={{0,2},{2,0},{4,6},{6,4},{1,3},{3,1},{5,7},{7,5},{8,10},{10,8},{12,... | collective-permute-start | bytes 786440 | tf_op jit(solution)/shard_map/ppermute | solution.py:29
  3.2 14.1 %collective-permute-start.1 = (bf16[128,1024]{1,0:T(8,128)(2,1)}, bf16[128,1024]{1,0:T(8,128)(2,1)S(1)}, u32[]{:S(2)}, u32[]{:S(2)}) collective-permute-start(bf16[128,1024]{1,0:T(8,128)(2,1)} %refs_1_.3), channel_id=1, source_target_pairs={{0,6},{2,4},{4,2},{6,0},{1,7},{3,5},{5,3},{7,1},{8,14},{10,12},{12... | collective-permute-start | bytes 786440 | tf_op jit(solution)/shard_map/ppermute | solution.py:29
  16.0 4.5 %collective-permute-start.2 = (bf16[512,1024]{1,0:T(8,128)(2,1)}, bf16[512,1024]{1,0:T(8,128)(2,1)S(1)}, u32[]{:S(2)}, u32[]{:S(2)}) collective-permute-start(bf16[512,1024]{1,0:T(8,128)(2,1)} %get-tuple-element.28), channel_id=1, source_target_pairs={{0,1},{1,0},{2,3},{3,2},{4,5},{5,4},{6,7},{7,6},{8,9},{9,8},{10,11... | collective-permute-start | bytes 3145736 | tf_op jit(solution)/shard_map/ppermute | solution.py:29
  19.7 17.4 %collective-permute-start.3 = (bf16[64,1024]{1,0:T(8,128)(2,1)}, bf16[64,1024]{1,0:T(8,128)(2,1)S(1)}, u32[]{:S(2)}, u32[]{:S(2)}) collective-permute-start(bf16[64,1024]{1,0:T(8,128)(2,1)} %get-tuple-element.27.refs_0_), channel_id=1, source_target_pairs={{0,6},{2,4},{4,2},{6,0},{1,7},{3,5},{5,3},{7,1},{8,14},{10,12},{12... | collective-permute-start | bytes 393224 | tf_op jit(solution)/shard_map/ppermute | solution.py:29
  20.1 18.2 %collective-permute-start.4 = (bf16[64,1024]{1,0:T(8,128)(2,1)}, bf16[64,1024]{1,0:T(8,128)(2,1)S(1)}, u32[]{:S(2)}, u32[]{:S(2)}) collective-permute-start(bf16[64,1024]{1,0:T(8,128)(2,1)} %get-tuple-element.31), channel_id=1, source_target_pairs={{0,2},{2,0},{4,6},{6,4},{1,3},{3,1},{5,7},{7,5},{8,10},{10,8},{12,... | collective-permute-start | bytes 393224 | tf_op jit(solution)/shard_map/ppermute | solution.py:29
  23.8 17.4 %collective-permute-start.5 = (bf16[128,1024]{1,0:T(8,128)(2,1)}, bf16[128,1024]{1,0:T(8,128)(2,1)S(1)}, u32[]{:S(2)}, u32[]{:S(2)}) collective-permute-start(bf16[128,1024]{1,0:T(8,128)(2,1)} %get-tuple-element.32), channel_id=1, source_target_pairs={{0,2},{2,0},{4,6},{6,4},{1,3},{3,1},{5,7},{7,5},{8,10},{10,8},{12,... | collective-permute-start | bytes 786440 | tf_op jit(solution)/shard_map/ppermute | solution.py:29
  25.0 16.3 %collective-permute-start.6 = (bf16[128,1024]{1,0:T(8,128)(2,1)}, bf16[128,1024]{1,0:T(8,128)(2,1)S(1)}, u32[]{:S(2)}, u32[]{:S(2)}) collective-permute-start(bf16[128,1024]{1,0:T(8,128)(2,1)} %get-tuple-element.33), channel_id=1, source_target_pairs={{0,6},{2,4},{4,2},{6,0},{1,7},{3,5},{5,3},{7,1},{8,14},{10,12},{12... | collective-permute-start | bytes 786440 | tf_op jit(solution)/shard_map/ppermute | solution.py:29
  27.2 14.1 %collective-permute-start.7 = (bf16[128,1024]{1,0:T(8,128)(2,1)}, bf16[128,1024]{1,0:T(8,128)(2,1)S(1)}, u32[]{:S(2)}, u32[]{:S(2)}) collective-permute-start(bf16[128,1024]{1,0:T(8,128)(2,1)} %get-tuple-element.34), channel_id=1, source_target_pairs={{0,4},{2,6},{4,0},{6,2},{1,5},{3,7},{5,1},{7,3},{8,12},{10,14},{12... | collective-permute-start | bytes 786440 | tf_op jit(solution)/shard_map/ppermute | solution.py:29
  37.1 9.1 %collective-permute-start.8 = (bf16[512,1024]{1,0:T(8,128)(2,1)}, bf16[512,1024]{1,0:T(8,128)(2,1)}, u32[]{:S(2)}, u32[]{:S(2)}) collective-permute-start(bf16[512,1024]{1,0:T(8,128)(2,1)} %get-tuple-element.36), channel_id=1, source_target_pairs={{0,1},{1,0},{2,3},{3,2},{4,5},{5,4},{6,7},{7,6},{8,9},{9,8},{10,11... | collective-permute-start | bytes 3145736 | tf_op jit(solution)/shard_map/ppermute | solution.py:29
  41.2 13.2 %collective-permute-start.10 = (bf16[512,1024]{1,0:T(8,128)(2,1)}, bf16[512,1024]{1,0:T(8,128)(2,1)}, u32[]{:S(2)}, u32[]{:S(2)}) collective-permute-start(bf16[512,1024]{1,0:T(8,128)(2,1)} %shard_map.99.refs_0_.refs_2_), channel_id=1, source_target_pairs={{0,1},{1,0},{2,3},{3,2},{4,5},{5,4},{6,7},{7,6},{8,9},{9,8},{10,11... | collective-permute-start | bytes 3145736 | tf_op jit(solution)/shard_map/ppermute | solution.py:29
  44.7 7.4 %collective-permute-start.9 = (bf16[64,1024]{1,0:T(8,128)(2,1)}, bf16[64,1024]{1,0:T(8,128)(2,1)S(1)}, u32[]{:S(2)}, u32[]{:S(2)}) collective-permute-start(bf16[64,1024]{1,0:T(8,128)(2,1)} %get-tuple-element.38), channel_id=1, source_target_pairs={{0,64},{64,0},{1,65},{65,1},{2,66},{66,2},{3,67},{67,3},{4,68},{68... | collective-permute-start | bytes 393224 | tf_op jit(solution)/shard_map/ppermute | solution.py:29
  46.0 26.1 %collective-permute-start.19 = (bf16[512,1024]{1,0:T(8,128)(2,1)S(1)}, bf16[512,1024]{1,0:T(8,128)(2,1)}, u32[]{:S(2)}, u32[]{:S(2)}) collective-permute-start(bf16[512,1024]{1,0:T(8,128)(2,1)S(1)} %copy-done), channel_id=1, source_target_pairs={{0,64},{64,0},{1,65},{65,1},{2,66},{66,2},{3,67},{67,3},{4,68},{68... | collective-permute-start | bytes 3145736 | tf_op jit(solution)/shard_map/ppermute | solution.py:29
  48.6 11.7 %collective-permute-start.11 = (bf16[128,1024]{1,0:T(8,128)(2,1)}, bf16[128,1024]{1,0:T(8,128)(2,1)}, u32[]{:S(2)}, u32[]{:S(2)}) collective-permute-start(bf16[128,1024]{1,0:T(8,128)(2,1)} %get-tuple-element.39), channel_id=1, source_target_pairs={{0,2},{2,0},{4,6},{6,4},{1,3},{3,1},{5,7},{7,5},{8,10},{10,8},{12,... | collective-permute-start | bytes 786440 | tf_op jit(solution)/shard_map/ppermute | solution.py:29
  49.8 12.8 %collective-permute-start.12 = (bf16[128,1024]{1,0:T(8,128)(2,1)}, bf16[128,1024]{1,0:T(8,128)(2,1)}, u32[]{:S(2)}, u32[]{:S(2)}) collective-permute-start(bf16[128,1024]{1,0:T(8,128)(2,1)} %get-tuple-element.40), channel_id=1, source_target_pairs={{0,6},{2,4},{4,2},{6,0},{1,7},{3,5},{5,3},{7,1},{8,14},{10,12},{12... | collective-permute-start | bytes 786440 | tf_op jit(solution)/shard_map/ppermute | solution.py:29
  52.1 11.2 %collective-permute-start.13 = (bf16[128,1024]{1,0:T(8,128)(2,1)}, bf16[128,1024]{1,0:T(8,128)(2,1)}, u32[]{:S(2)}, u32[]{:S(2)}) collective-permute-start(bf16[128,1024]{1,0:T(8,128)(2,1)} %get-tuple-element.41), channel_id=1, source_target_pairs={{0,4},{2,6},{4,0},{6,2},{1,5},{3,7},{5,1},{7,3},{8,12},{10,14},{12... | collective-permute-start | bytes 786440 | tf_op jit(solution)/shard_map/ppermute | solution.py:29
  54.5 19.9 %collective-permute-start.20 = (bf16[128,1024]{1,0:T(8,128)(2,1)}, bf16[128,1024]{1,0:T(8,128)(2,1)S(1)}, u32[]{:S(2)}, u32[]{:S(2)}) collective-permute-start(bf16[128,1024]{1,0:T(8,128)(2,1)} %shard_map.102.refs_0_.refs_3_), channel_id=1, source_target_pairs={{0,2},{2,0},{4,6},{6,4},{1,3},{3,1},{5,7},{7,5},{8,10},{10,8},{12,... | collective-permute-start | bytes 786440 | tf_op jit(solution)/shard_map/ppermute | solution.py:29
  60.3 14.1 %collective-permute-start.21 = (bf16[128,1024]{1,0:T(8,128)(2,1)S(1)}, bf16[128,1024]{1,0:T(8,128)(2,1)S(1)}, u32[]{:S(2)}, u32[]{:S(2)}) collective-permute-start(bf16[128,1024]{1,0:T(8,128)(2,1)S(1)} %copy-done.6), channel_id=1, source_target_pairs={{0,6},{2,4},{4,2},{6,0},{1,7},{3,5},{5,3},{7,1},{8,14},{10,12},{12... | collective-permute-start | bytes 786440 | tf_op jit(solution)/shard_map/ppermute | solution.py:29
  62.7 14.3 %collective-permute-start.22 = (bf16[128,1024]{1,0:T(8,128)(2,1)S(1)}, bf16[128,1024]{1,0:T(8,128)(2,1)}, u32[]{:S(2)}, u32[]{:S(2)}) collective-permute-start(bf16[128,1024]{1,0:T(8,128)(2,1)S(1)} %copy-done.6), channel_id=1, source_target_pairs={{0,4},{2,6},{4,0},{6,2},{1,5},{3,7},{5,1},{7,3},{8,12},{10,14},{12... | collective-permute-start | bytes 786440 | tf_op jit(solution)/shard_map/ppermute | solution.py:29
  65.3 11.9 %collective-permute-start.14 = (bf16[64,1024]{1,0:T(8,128)(2,1)}, bf16[64,1024]{1,0:T(8,128)(2,1)S(1)}, u32[]{:S(2)}, u32[]{:S(2)}) collective-permute-start(bf16[64,1024]{1,0:T(8,128)(2,1)} %get-tuple-element.43), channel_id=1, source_target_pairs={{0,64},{64,0},{1,65},{65,1},{2,66},{66,2},{3,67},{67,3},{4,68},{68... | collective-permute-start | bytes 393224 | tf_op jit(solution)/shard_map/ppermute | solution.py:29
  72.1 7.4 %collective-permute-start.23 = (bf16[128,1024]{1,0:T(8,128)(2,1)S(1)}, bf16[128,1024]{1,0:T(8,128)(2,1)}, u32[]{:S(2)}, u32[]{:S(2)}) collective-permute-start(bf16[128,1024]{1,0:T(8,128)(2,1)S(1)} %copy-done.6), channel_id=1, source_target_pairs={{0,1},{1,0},{2,3},{3,2},{4,5},{5,4},{6,7},{7,6},{8,9},{9,8},{10,11... | collective-permute-start | bytes 786440 | tf_op jit(solution)/shard_map/ppermute | solution.py:29
  74.4 14.7 %collective-permute-start.27 = (bf16[512,1024]{1,0:T(8,128)(2,1)}, bf16[512,1024]{1,0:T(8,128)(2,1)S(1)}, u32[]{:S(2)}, u32[]{:S(2)}) collective-permute-start(bf16[512,1024]{1,0:T(8,128)(2,1)} %collective-permute-done.19.refs_1_.refs_4_), channel_id=1, source_target_pairs={{0,1},{1,0},{2,3},{3,2},{4,5},{5,4},{6,7},{7,6},{8,9},{9,8},{10,11... | collective-permute-start | bytes 3145736 | tf_op jit(solution)/shard_map/ppermute | solution.py:29
  74.5 5.5 %collective-permute-start.24 = (bf16[128,1024]{1,0:T(8,128)(2,1)S(1)}, bf16[128,1024]{1,0:T(8,128)(2,1)}, u32[]{:S(2)}, u32[]{:S(2)}) collective-permute-start(bf16[128,1024]{1,0:T(8,128)(2,1)S(1)} %collective-permute-done.20.refs_4_), channel_id=1, source_target_pairs={{0,1},{1,0},{2,3},{3,2},{4,5},{5,4},{6,7},{7,6},{8,9},{9,8},{10,11... | collective-permute-start | bytes 786440 | tf_op jit(solution)/shard_map/ppermute | solution.py:29
  76.9 5.0 %collective-permute-start.25 = (bf16[128,1024]{1,0:T(8,128)(2,1)S(1)}, bf16[128,1024]{1,0:T(8,128)(2,1)}, u32[]{:S(2)}, u32[]{:S(2)}) collective-permute-start(bf16[128,1024]{1,0:T(8,128)(2,1)S(1)} %collective-permute-done.21.refs_5_), channel_id=1, source_target_pairs={{0,1},{1,0},{2,3},{3,2},{4,5},{5,4},{6,7},{7,6},{8,9},{9,8},{10,11... | collective-permute-start | bytes 786440 | tf_op jit(solution)/shard_map/ppermute | solution.py:29
  77.2 5.9 %collective-permute-start.26 = (bf16[128,1024]{1,0:T(8,128)(2,1)}, bf16[128,1024]{1,0:T(8,128)(2,1)}, u32[]{:S(2)}, u32[]{:S(2)}) collective-permute-start(bf16[128,1024]{1,0:T(8,128)(2,1)} %collective-permute-done.22.refs_6_), channel_id=1, source_target_pairs={{0,1},{1,0},{2,3},{3,2},{4,5},{5,4},{6,7},{7,6},{8,9},{9,8},{10,11... | collective-permute-start | bytes 786440 | tf_op jit(solution)/shard_map/ppermute | solution.py:29
  79.6 16.0 %collective-permute-start.15 = (bf16[128,1024]{1,0:T(8,128)(2,1)}, bf16[128,1024]{1,0:T(8,128)(2,1)S(1)}, u32[]{:S(2)}, u32[]{:S(2)}) collective-permute-start(bf16[128,1024]{1,0:T(8,128)(2,1)} %shard_map.105.refs_0_.refs_1_), channel_id=1, source_target_pairs={{0,2},{2,0},{4,6},{6,4},{1,3},{3,1},{5,7},{7,5},{8,10},{10,8},{12,... | collective-permute-start | bytes 786440 | tf_op jit(solution)/shard_map/ppermute | solution.py:29
  79.9 15.6 %collective-permute-start.16 = (bf16[128,1024]{1,0:T(8,128)(2,1)}, bf16[128,1024]{1,0:T(8,128)(2,1)S(1)}, u32[]{:S(2)}, u32[]{:S(2)}) collective-permute-start(bf16[128,1024]{1,0:T(8,128)(2,1)} %shard_map.105.refs_0_.refs_1_), channel_id=1, source_target_pairs={{0,6},{2,4},{4,2},{6,0},{1,7},{3,5},{5,3},{7,1},{8,14},{10,12},{12... | collective-permute-start | bytes 786440 | tf_op jit(solution)/shard_map/ppermute | solution.py:29
  81.9 13.7 %collective-permute-start.17 = (bf16[128,1024]{1,0:T(8,128)(2,1)}, bf16[128,1024]{1,0:T(8,128)(2,1)S(1)}, u32[]{:S(2)}, u32[]{:S(2)}) collective-permute-start(bf16[128,1024]{1,0:T(8,128)(2,1)} %shard_map.105.refs_0_.refs_1_), channel_id=1, source_target_pairs={{0,4},{2,6},{4,0},{6,2},{1,5},{3,7},{5,1},{7,3},{8,12},{10,14},{12... | collective-permute-start | bytes 786440 | tf_op jit(solution)/shard_map/ppermute | solution.py:29
  99.1 3.3 %collective-permute-start.28 = (bf16[384,1024]{1,0:T(8,128)(2,1)}, bf16[384,1024]{1,0:T(8,128)(2,1)S(1)}, u32[]{:S(2)}, u32[]{:S(2)}) collective-permute-start(bf16[384,1024]{1,0:T(8,128)(2,1)} %shard_map.108), channel_id=1, source_target_pairs={{0,1},{1,0},{2,3},{3,2},{4,5},{5,4},{6,7},{7,6},{8,9},{9,8},{10,11... | collective-permute-start | bytes 2359304 | tf_op jit(solution)/shard_map/ppermute | solution.py:29
  100.0 2.3 %collective-permute-start.18 = (bf16[128,1024]{1,0:T(8,128)(2,1)S(1)}, bf16[128,1024]{1,0:T(8,128)(2,1)S(1)}, u32[]{:S(2)}, u32[]{:S(2)}) collective-permute-start(bf16[128,1024]{1,0:T(8,128)(2,1)S(1)} %copy-done.20), channel_id=1, source_target_pairs={{0,1},{1,0},{2,3},{3,2},{4,5},{5,4},{6,7},{7,6},{8,9},{9,8},{10,11... | collective-permute-start | bytes 786440 | tf_op jit(solution)/shard_map/ppermute | solution.py:29
  109.8 34.0 %copy-start.5 = (bf16[128,1024]{1,0:T(8,128)(2,1)S(1)}, bf16[128,1024]{1,0:T(8,128)(2,1)}, u32[]{:S(2)}) copy-start(bf16[128,1024]{1,0:T(8,128)(2,1)} %param.15) | copy-start | bytes 786436
  143.9 5.5 %collective-permute-start.29 = (bf16[64,1024]{1,0:T(8,128)(2,1)S(1)}, bf16[64,1024]{1,0:T(8,128)(2,1)S(1)}, u32[]{:S(2)}, u32[]{:S(2)}) collective-permute-start(bf16[64,1024]{1,0:T(8,128)(2,1)S(1)} %get-tuple-element.51.refs_0_), channel_id=1, source_target_pairs={{0,8},{8,0},{64,72},{72,64},{1,9},{9,1},{65,73},{73,65},{2,10},{10... | collective-permute-start | bytes 393224 | tf_op jit(solution)/shard_map/ppermute | solution.py:29
  145.6 5.5 %collective-permute-start.30 = (bf16[64,1024]{1,0:T(8,128)(2,1)S(1)}, bf16[64,1024]{1,0:T(8,128)(2,1)S(1)}, u32[]{:S(2)}, u32[]{:S(2)}) collective-permute-start(bf16[64,1024]{1,0:T(8,128)(2,1)S(1)} %get-tuple-element.51.refs_0_), channel_id=1, source_target_pairs={{0,64},{8,72},{64,0},{72,8},{1,65},{9,73},{65,1},{73,9},{2,66},{10... | collective-permute-start | bytes 393224 | tf_op jit(solution)/shard_map/ppermute | solution.py:29
  146.0 6.9 %collective-permute-start.31 = (bf16[64,1024]{1,0:T(8,128)(2,1)S(1)}, bf16[64,1024]{1,0:T(8,128)(2,1)S(1)}, u32[]{:S(2)}, u32[]{:S(2)}) collective-permute-start(bf16[64,1024]{1,0:T(8,128)(2,1)S(1)} %get-tuple-element.51.refs_0_), channel_id=1, source_target_pairs={{0,72},{8,64},{64,8},{72,0},{1,73},{9,65},{65,9},{73,1},{2,74},{10... | collective-permute-start | bytes 393224 | tf_op jit(solution)/shard_map/ppermute | solution.py:29
  147.2 9.2 %collective-permute-start.35 = (bf16[64,1024]{1,0:T(8,128)(2,1)S(1)}, bf16[64,1024]{1,0:T(8,128)(2,1)S(1)}, u32[]{:S(2)}, u32[]{:S(2)}) collective-permute-start(bf16[64,1024]{1,0:T(8,128)(2,1)S(1)} %get-tuple-element.50.refs_1_), channel_id=1, source_target_pairs={{0,16},{16,0},{32,48},{48,32},{1,17},{17,1},{33,49},{49,33},{2,18}... | collective-permute-start | bytes 393224 | tf_op jit(solution)/shard_map/ppermute | solution.py:29
  147.2 9.2 %collective-permute-start.36 = (bf16[64,1024]{1,0:T(8,128)(2,1)S(1)}, bf16[64,1024]{1,0:T(8,128)(2,1)S(1)}, u32[]{:S(2)}, u32[]{:S(2)}) collective-permute-start(bf16[64,1024]{1,0:T(8,128)(2,1)S(1)} %get-tuple-element.50.refs_1_), channel_id=1, source_target_pairs={{0,32},{16,48},{32,0},{48,16},{1,33},{17,49},{33,1},{49,17},{2,34}... | collective-permute-start | bytes 393224 | tf_op jit(solution)/shard_map/ppermute | solution.py:29
  149.4 7.1 %collective-permute-start.37 = (bf16[64,1024]{1,0:T(8,128)(2,1)S(1)}, bf16[64,1024]{1,0:T(8,128)(2,1)S(1)}, u32[]{:S(2)}, u32[]{:S(2)}) collective-permute-start(bf16[64,1024]{1,0:T(8,128)(2,1)S(1)} %get-tuple-element.50.refs_1_), channel_id=1, source_target_pairs={{0,48},{16,32},{32,16},{48,0},{1,49},{17,33},{33,17},{49,1},{2,50}... | collective-permute-start | bytes 393224 | tf_op jit(solution)/shard_map/ppermute | solution.py:29
  155.3 10.9 %collective-permute-start.32 = (bf16[256,1024]{1,0:T(8,128)(2,1)}, bf16[256,1024]{1,0:T(8,128)(2,1)S(1)}, u32[]{:S(2)}, u32[]{:S(2)}) collective-permute-start(bf16[256,1024]{1,0:T(8,128)(2,1)} %shard_map.110.refs_0_.refs_1_.refs_2_), channel_id=1, source_target_pairs={{0,16},{16,0},{32,48},{48,32},{1,17},{17,1},{33,49},{49,33},{2,18}... | collective-permute-start | bytes 1572872 | tf_op jit(solution)/shard_map/ppermute | solution.py:29
  155.7 12.3 %collective-permute-start.34 = (bf16[256,1024]{1,0:T(8,128)(2,1)}, bf16[256,1024]{1,0:T(8,128)(2,1)S(1)}, u32[]{:S(2)}, u32[]{:S(2)}) collective-permute-start(bf16[256,1024]{1,0:T(8,128)(2,1)} %shard_map.110.refs_0_.refs_1_.refs_2_), channel_id=1, source_target_pairs={{0,48},{16,32},{32,16},{48,0},{1,49},{17,33},{33,17},{49,1},{2,50}... | collective-permute-start | bytes 1572872 | tf_op jit(solution)/shard_map/ppermute | solution.py:29
  159.6 12.2 %collective-permute-start.38 = (bf16[256,1024]{1,0:T(8,128)(2,1)}, bf16[256,1024]{1,0:T(8,128)(2,1)S(1)}, u32[]{:S(2)}, u32[]{:S(2)}) collective-permute-start(bf16[256,1024]{1,0:T(8,128)(2,1)} %shard_map.111.refs_5_.refs_7_), channel_id=1, source_target_pairs={{0,8},{8,0},{64,72},{72,64},{1,9},{9,1},{65,73},{73,65},{2,10},{10... | collective-permute-start | bytes 1572872 | tf_op jit(solution)/shard_map/ppermute | solution.py:29
  166.2 7.6 %collective-permute-start.33 = (bf16[128,1024]{1,0:T(8,128)(2,1)S(1)}, bf16[128,1024]{1,0:T(8,128)(2,1)}, u32[]{:S(2)}, u32[]{:S(2)}) collective-permute-start(bf16[128,1024]{1,0:T(8,128)(2,1)S(1)} %slice.17), channel_id=1, source_target_pairs={{0,48},{16,32},{32,16},{48,0},{1,49},{17,33},{33,17},{49,1},{2,50}... | collective-permute-start | bytes 786440 | tf_op jit(solution)/shard_map/ppermute | solution.py:29
  167.1 27.2 %collective-permute-start.44 = (bf16[256,1024]{1,0:T(8,128)(2,1)}, bf16[256,1024]{1,0:T(8,128)(2,1)}, u32[]{:S(2)}, u32[]{:S(2)}) collective-permute-start(bf16[256,1024]{1,0:T(8,128)(2,1)} %shard_map.111.refs_5_.refs_7_), channel_id=1, source_target_pairs={{0,64},{8,72},{64,0},{72,8},{1,65},{9,73},{65,1},{73,9},{2,66},{10... | collective-permute-start | bytes 1572872 | tf_op jit(solution)/shard_map/ppermute | solution.py:29
  167.6 26.7 %collective-permute-start.45 = (bf16[256,1024]{1,0:T(8,128)(2,1)}, bf16[256,1024]{1,0:T(8,128)(2,1)}, u32[]{:S(2)}, u32[]{:S(2)}) collective-permute-start(bf16[256,1024]{1,0:T(8,128)(2,1)} %shard_map.111.refs_5_.refs_7_), channel_id=1, source_target_pairs={{0,72},{8,64},{64,8},{72,0},{1,73},{9,65},{65,9},{73,1},{2,74},{10... | collective-permute-start | bytes 1572872 | tf_op jit(solution)/shard_map/ppermute | solution.py:29
  168.0 26.3 %collective-permute-start.43 = (bf16[128,1024]{1,0:T(8,128)(2,1)S(1)}, bf16[128,1024]{1,0:T(8,128)(2,1)}, u32[]{:S(2)}, u32[]{:S(2)}) collective-permute-start(bf16[128,1024]{1,0:T(8,128)(2,1)S(1)} %slice.19), channel_id=1, source_target_pairs={{0,16},{16,0},{32,48},{48,32},{1,17},{17,1},{33,49},{49,33},{2,18}... | collective-permute-start | bytes 786440 | tf_op jit(solution)/shard_map/ppermute | solution.py:29
  179.6 8.5 %collective-permute-start.39 = (bf16[512,1024]{1,0:T(8,128)(2,1)}, bf16[512,1024]{1,0:T(8,128)(2,1)S(1)}, u32[]{:S(2)}, u32[]{:S(2)}) collective-permute-start(bf16[512,1024]{1,0:T(8,128)(2,1)} %get-tuple-element.45), channel_id=1, source_target_pairs={{0,1},{1,0},{2,3},{3,2},{4,5},{5,4},{6,7},{7,6},{8,9},{9,8},{10,11... | collective-permute-start | bytes 3145736 | tf_op jit(solution)/shard_map/ppermute | solution.py:29
  191.6 11.9 %collective-permute-start.42 = (bf16[128,1024]{1,0:T(8,128)(2,1)}, bf16[128,1024]{1,0:T(8,128)(2,1)S(1)}, u32[]{:S(2)}, u32[]{:S(2)}) collective-permute-start(bf16[128,1024]{1,0:T(8,128)(2,1)} %get-tuple-element.49), channel_id=1, source_target_pairs={{0,4},{2,6},{4,0},{6,2},{1,5},{3,7},{5,1},{7,3},{8,12},{10,14},{12... | collective-permute-start | bytes 786440 | tf_op jit(solution)/shard_map/ppermute | solution.py:29
  193.5 13.6 %collective-permute-start.41 = (bf16[128,1024]{1,0:T(8,128)(2,1)}, bf16[128,1024]{1,0:T(8,128)(2,1)S(1)}, u32[]{:S(2)}, u32[]{:S(2)}) collective-permute-start(bf16[128,1024]{1,0:T(8,128)(2,1)} %get-tuple-element.48), channel_id=1, source_target_pairs={{0,6},{2,4},{4,2},{6,0},{1,7},{3,5},{5,3},{7,1},{8,14},{10,12},{12... | collective-permute-start | bytes 786440 | tf_op jit(solution)/shard_map/ppermute | solution.py:29
  194.3 12.9 %collective-permute-start.40 = (bf16[128,1024]{1,0:T(8,128)(2,1)}, bf16[128,1024]{1,0:T(8,128)(2,1)S(1)}, u32[]{:S(2)}, u32[]{:S(2)}) collective-permute-start(bf16[128,1024]{1,0:T(8,128)(2,1)} %get-tuple-element.47), channel_id=1, source_target_pairs={{0,2},{2,0},{4,6},{6,4},{1,3},{3,1},{5,7},{7,5},{8,10},{10,8},{12,... | collective-permute-start | bytes 786440 | tf_op jit(solution)/shard_map/ppermute | solution.py:29
  194.3 12.8 %copy-start.7 = (bf16[128,1024]{1,0:T(8,128)(2,1)S(1)}, bf16[128,1024]{1,0:T(8,128)(2,1)}, u32[]{:S(2)}) copy-start(bf16[128,1024]{1,0:T(8,128)(2,1)} %get-tuple-element.46.refs_0_) | copy-start | bytes 786436
  (33 other events, 83.0 us)

commit v5 on v4

--- a/solution.py
+++ b/solution.py
@@ -74,6 +74,10 @@
 
 def with_unread(body, count):
     return lambda *refs: body(*refs[count:])
+
+
+def tn(a, b):
+    return lax.dot_general(a, b, (((0,), (0,)), ((), ())), preferred_element_type=F32)
 
 
 def one_hot(hits):
@@ -238,6 +242,70 @@
     )
 
 
+def some_target_kernel(fars, ids_ref, *refs):
+    hidden = refs[:4]
+    l_ref, p_ref = refs[4:6]
+    out_ref, h_ref, stage_ref, sems = refs[-4:]
+    piece, tile = hidden[0].shape[0], p_ref.shape[1]
+    steps = stage_ref.shape[0]
+    places = [pl.ds(pl.multiple_of((ids_ref[1] ^ far) * piece, piece), piece) for far in fars]
+
+    @pl.when(pl.program_id(0) == 0)
+    def _():
+        for k in range(4):
+            h_ref[k * piece : (k + 1) * piece, :] = hidden[k][...]
+
+    out = nn(h_ref[...], p_ref[...])
+
+    def copies(j):
+        for k in range(4):
+            yield pltpu.make_async_copy(
+                stage_ref.at[j, pl.ds(k * piece, piece)],
+                out_ref.at[places[k], pl.ds(j * tile, tile)],
+                sems.at[j, k],
+            )
+
+    for j in range(steps):
+
+        @pl.when(pl.program_id(0) == j)
+        def _():
+            for k in range(4):
+                rows = slice(k * piece, (k + 1) * piece)
+                part = l_ref[places[k], :].astype(F32) - out[rows]
+                stage_ref[j, rows, :] = part.astype(BF16)
+            for copy in copies(j):
+                copy.start()
+            if j == steps - 1:
+                for i in range(steps):
+                    for copy in copies(i):
+                        copy.wait()
+
+
+def some_less_target(ids, fars, hidden, left, projection, half, into=(), after=(), tile=512):
+    piece, deep = hidden[0].shape
+    rows, width = left.shape
+    steps = width // tile
+    return pl.pallas_call(
+        with_unread(functools.partial(some_target_kernel, fars), len(after)),
+        grid=(steps,),
+        out_shape=shape(rows, width),
+        in_specs=[unread()] * len(after)
+        + [smem()]
+        + [whole(h) for h in hidden]
+        + [pl.BlockSpec((rows, tile), lambda j: (0, j)), pl.BlockSpec((deep, tile), lambda j: (half, j))]
+        + [unread()] * len(into),
+        out_specs=unread(),
+        scratch_shapes=[
+            pltpu.VMEM((4 * piece, deep), BF16),
+            pltpu.VMEM((steps, 4 * piece, tile), BF16),
+            pltpu.SemaphoreType.DMA((steps, 4)),
+        ],
+        input_output_aliases={len(after) + 7: 0} if into else {},
+        compiler_params=params(),
+        cost_estimate=pl.CostEstimate(flops=int(LONG * 1e9), bytes_accessed=1024, transcendentals=0),
+    )(*after, ids, *hidden, left, projection, *into)
+
+
 def own_places(own_x, near_x, far_x, next_x, own_y, far_y):
     piece = own_x.shape[0] // 4
     for n in range(2):
@@ -293,39 +361,11 @@
     )
 
 
-def turn_kernel(ids_ref, near_ref, pair_ref, far_ref, far_pair_ref, out_ref):
-    rows = near_ref.shape[0] // 4
-    for half, refs in enumerate(((near_ref, pair_ref), (far_ref, far_pair_ref))):
-        for flip, ref in enumerate(refs):
-            for z in range(4):
-                block = half * 8 + (ids_ref[1] ^ (z * 2 + flip))
-                at = pl.multiple_of(block * rows, rows)
-                out_ref[:, pl.ds(at, rows)] = ref[z * rows : (z + 1) * rows, :].T
-
-
-def turned(ids, near, pair, far, far_pair, after):
-    rows, feats = near.shape
-    return call(
-        LONG,
-        with_unread(turn_kernel, len(after)),
-        (1,),
-        shape(feats, 4 * rows),
-        [unread()] * len(after) + [smem()] + [whole(near)] * 4,
-        pl.BlockSpec((feats, 4 * rows), lambda j: (0, 0)),
-        [],
-        *after,
-        ids,
-        near,
-        pair,
-        far,
-        far_pair,
-    )
-
-
 def weight_kernel(ids_ref, *refs):
-    gaps = refs[:9]
-    v_ref, out_ref, g_ref = refs[9:]
+    gaps, values = refs[:9], refs[9:13]
+    out_ref, g_ref = refs[13:]
     piece = gaps[0].shape[0] // 4
+    rows = g_ref.shape[0] // 4
 
     @pl.when(pl.program_id(0) == 0)
     def _():
@@ -333,14 +373,18 @@
         other = other_places(*gaps[:2], *gaps[3:5], *gaps[7:])
         for half, places in enumerate((own, other)):
             for k, part, ref, start in places:
-                place = half * (g_ref.shape[0] // 2) + (ids_ref[0] ^ k) * (2 * piece) + part * piece
+                far = ids_ref[0] ^ ids_ref[1] ^ k
+                place = (2 * half + (far & 1)) * rows + (far >> 1) * (2 * piece) + part * piece
                 g_ref[pl.ds(pl.multiple_of(place, piece), piece), :] = ref[start : start + piece, :]
 
-    out_ref[...] = nn(v_ref[...], g_ref[...])
+    total = tn(values[0][...], g_ref[:rows])
+    for k in range(1, 4):
+        total = total + tn(values[k][...], g_ref[k * rows : (k + 1) * rows])
+    out_ref[...] = total
 
 
 def weight_sums(ids, gaps, values, after, tile=512):
-    feats, rows = values.shape
+    rows, feats = values[0].shape
     width = gaps[0].shape[1]
     return call(
         LONG,
@@ -350,13 +394,13 @@
         [unread()] * len(after)
         + [smem()]
         + [whole(g) for g in gaps]
-        + [pl.BlockSpec((tile, rows), lambda j: (j, 0))],
+        + [pl.BlockSpec((rows, tile), lambda j: (0, j))] * 4,
         pl.BlockSpec((tile, width), lambda j: (j, 0)),
-        [pltpu.VMEM((rows, width), BF16)],
+        [pltpu.VMEM((4 * rows, width), BF16)],
         *after,
         ids,
         *gaps,
-        values,
+        *values,
     )
 
 
@@ -516,9 +560,10 @@
     second = placed(ids, keep, swap(give, GRP, 1))
     far_pair = swap(far, CORE, 1)
     left = less_target(ids, first, layer_out, projection, 0, (second, far))
-    turn = turned(ids, near, pair, far, far_pair, (left,))
-    second = gather_tensor(second, (left, turn))
-    parts = less_target(ids, second, left, projection, 1)
+    blocks = [second, *[swap(second, Z, k) for k in (1, 3, 2)]]
+    pairs = [swap(block, CORE, 1) for block in blocks]
+    parts = some_less_target(ids, (0, 2, 6, 4), blocks, left, projection, 1, (), (marker(left, far_pair),))
+    parts = some_less_target(ids, (1, 3, 7, 5), pairs, left, projection, 1, (parts,))
 
     parts = lax.all_to_all(parts.reshape(8, -1, parts.shape[1]), DP, 0, 0, tiled=True)
     total = student_stream.astype(F32) + jnp.sum(parts.astype(F32), axis=0)
@@ -537,7 +582,7 @@
     mine, peer = values_partial(ids, gaps[:3] + gaps[4:7], student_weight, ())
     parts = merged((mine, swap(peer, CORE, 1)), 4, (marker(mine),))
     values_grad = add(parts[0], *[swap(parts[k], Z, k) for k in (1, 3, 2)])
-    weight_grad = weight_sums(ids, gaps, turn, (parts[0],))
+    weight_grad = weight_sums(ids, gaps, (near, pair, far, far_pair), (parts[0],))
     return (values_grad, weight_grad)
 
 

time: 209 us -> 207 us (level)
  Pallas kernels: 82.2 us -> 78.5 us
  starting transfers between devices: 53.4 us -> 56.7 us
  local copies, waits for them, and re-layouts: 11.4 us -> 8.83 us
    pallas_call x21 -> x19, Pallas kernels: 82.2 us -> 69.6 us  [call(): pl.pallas_call(body, grid=grid, out_shape=out_shape, in_specs=in_specs, o...]
    pallas_call x0 -> x2, Pallas kernels: none -> 8.89 us  [some_less_target(): pl.pallas_call(with_unread(functools.partial(some_target_kernel, fars), l...]
    ppermute x46 -> x48, starting transfers between devices: 53.4 us -> 56.7 us  [swap(): return lax.ppermute(array, axes, [(i, i ^ distance) for i in range(size)])]
    unnamed x70 -> x64, local copies, waits for them, and re-layouts: 11.3 us -> 8.77 us
    ppermute x46 -> x48, waiting for transfers between devices: 24.6 us -> 24.7 us  [swap(): return lax.ppermute(array, axes, [(i, i ^ distance) for i in range(size)])]
  transfers between devices with their start and end apart: 46 -> 48, of which waited for: 10 -> 9; matrix products, arithmetic and copies ran while one was open for 0% -> 0% of each run, Pallas kernels for 36% -> 36%
where the time goes in v5:
time: 207 us; the launch traced here: 206 us
  Pallas kernels  78.5 us (38%)
  starting transfers between devices  56.7 us (27%)
  blocking collectives  34.5 us (17%)
  waiting for transfers between devices  24.7 us (12%)
  local copies, waits for them, and re-layouts  8.83 us (4%)
    pallas_call x19, Pallas kernels, call(): pl.pallas_call(body, grid=grid, out_shape=out_shape, in_specs=in_specs, o...  69.6 us
    ppermute x48, starting transfers between devices, swap(): return lax.ppermute(array, axes, [(i, i ^ distance) for i in range(size)])  56.7 us
    all_to_all x1, blocking collectives, per_device(): lax.all_to_all(parts.reshape(8, -1, parts.shape[1]), DP, 0, 0, tiled=True)  34.5 us
    ppermute x48, waiting for transfers between devices, swap(): return lax.ppermute(array, axes, [(i, i ^ distance) for i in range(size)])  24.7 us
    pallas_call x2, Pallas kernels, some_less_target(): pl.pallas_call(with_unread(functools.partial(some_target_kernel, fars), l...  8.89 us
    unnamed x64, local copies, waits for them, and re-layouts  8.77 us
  transfers between devices with their start and end apart: 48, of which 9 were waited for; matrix products, arithmetic and copies ran while one was open for 0% of the time, Pallas kernels for 36%

profile of v5, /device:TPU:1, one launch (start us, length us, event | category | flops | bytes accessed | tf_op | source)
XLA Modules:
  0.0 206.0 jit_solution(12725179084277212915)
XLA Ops:
  0.6 2.5 %collective-permute-start = (bf16[128,1024]{1,0:T(8,128)(2,1)}, bf16[128,1024]{1,0:T(8,128)(2,1)S(1)}, u32[]{:S(2)}, u32[]{:S(2)}) collective-permute-start(bf16[128,1024]{1,0:T(8,128)(2,1)} %refs_1_.3), channel_id=1, source_target_pairs={{0,2},{2,0},{4,6},{6,4},{1,3},{3,1},{5,7},{7,5},{8,10},{10,8},{12,... | collective-permute-start | bytes 786440 | tf_op jit(solution)/shard_map/ppermute | solution.py:29
  3.2 2.2 %collective-permute-start.1 = (bf16[128,1024]{1,0:T(8,128)(2,1)}, bf16[128,1024]{1,0:T(8,128)(2,1)S(1)}, u32[]{:S(2)}, u32[]{:S(2)}) collective-permute-start(bf16[128,1024]{1,0:T(8,128)(2,1)} %refs_1_.3), channel_id=1, source_target_pairs={{0,6},{2,4},{4,2},{6,0},{1,7},{3,5},{5,3},{7,1},{8,14},{10,12},{12... | collective-permute-start | bytes 786440 | tf_op jit(solution)/shard_map/ppermute | solution.py:29
  6.0 9.9 %shard_map.95 = (bf16[512,1024]{1,0:T(8,128)(2,1)}, bf16[512,1024]{1,0:T(8,128)(2,1)}) custom-call(s32[3]{0:T(128)} %pad_add_fusion.refs_0_.refs_1_.refs_2_, s32[16,128]{1,0:T(8,128)} %refs_2_.3, bf16[1024,2048]{1,0:T(8,128)(2,1)} %refs_3_.3, bf16[2048,2048]{1,0:T(8,128)(2,1)} %refs_4_.4, bf16[128,2048]{1,0:T(8,128)(2,1)} %refs_5_.1), custom_call_target="tpu_custom_call" | custom-call | flops 49999998976 | bytes 1024 | tf_op jit(solution)/shard_map/pallas_call | solution.py:37
  15.9 1.2 collective-permute-start.2
  18.0 1.7 shard_map.96
  21.4 2.5 %shard_map.97 = (bf16[128,1024]{1,0:T(8,128)(2,1)}, bf16[128,1024]{1,0:T(8,128)(2,1)}, bf16[128,1024]{1,0:T(8,128)(2,1)}, bf16[128,1024]{1,0:T(8,128)(2,1)}) custom-call(bf16[64,1024]{1,0:T(8,128)(2,1)} %get-tuple-element.27.refs_0_, bf16[512,1024]{1,0:T(8,128)(2,1)} %get-tuple-element.26.refs_0_.refs_1_, bf16[512,1024]{1,0:T(8,128)(2,1)} %copy-done.1), custom_call_target="tpu_custom_call" | custom-call | flops 10000000 | bytes 1024 | tf_op jit(solution)/shard_map/pallas_call | solution.py:37
  23.8 1.2 collective-permute-start.5
  25.0 2.2 %collective-permute-start.6 = (bf16[128,1024]{1,0:T(8,128)(2,1)}, bf16[128,1024]{1,0:T(8,128)(2,1)S(1)}, u32[]{:S(2)}, u32[]{:S(2)}) collective-permute-start(bf16[128,1024]{1,0:T(8,128)(2,1)} %get-tuple-element.33), channel_id=1, source_target_pairs={{0,6},{2,4},{4,2},{6,0},{1,7},{3,5},{5,3},{7,1},{8,14},{10,12},{12... | collective-permute-start | bytes 786440 | tf_op jit(solution)/shard_map/ppermute | solution.py:29
  27.3 9.9 %shard_map.98 = (bf16[512,1024]{1,0:T(8,128)(2,1)}, bf16[512,1024]{1,0:T(8,128)(2,1)}) custom-call(bf16[128,1024]{1,0:T(8,128)(2,1)} %get-tuple-element.29.refs_0_.refs_1_, s32[3]{0:T(128)} %pad_add_fusion.refs_0_.refs_1_.refs_2_, s32[16,128]{1,0:T(8,128)} %refs_2_.3, bf16[1024,2048]{1,0:T(8,128)(2,1)} %refs_3_.3, bf16[2048,2048]{1,0:T(8,128)(2,1)} %refs_4_.4, ...), custom_call_target="tpu_custom_call" | custom-call | flops 49999998976 | bytes 1024 | tf_op jit(solution)/shard_map/pallas_call | solution.py:37
  37.2 1.2 collective-permute-start.8
  39.0 2.1 %shard_map.99.refs_0_.refs_2_.refs_11_ = bf16[512,1024]{1,0:T(8,128)(2,1)} custom-call(bf16[512,1024]{1,0:T(8,128)(2,1)} %get-tuple-element.30.refs_0_.refs_1_, bf16[128,1024]{1,0:T(8,128)(2,1)} %refs_1_.3, bf16[128,1024]{1,0:T(8,128)(2,1)} %copy-done.3, bf16[64,1024]{1,0:T(8,128)(2,1)} %copy-done.8, bf16[64,1024]{1,0:T(8,128)(2,1)} %copy-done.9, ...), custom_call_target="tpu_custom_call" | custom-call | flops 10000000 | bytes 1024 | tf_op jit(solution)/shard_map/pallas_call | solution.py:37
  42.7 2.0 shard_map.100
  44.7 1.3 collective-permute-start.9
  46.1 2.4 %shard_map.101 = (bf16[128,1024]{1,0:T(8,128)(2,1)}, bf16[128,1024]{1,0:T(8,128)(2,1)}, bf16[128,1024]{1,0:T(8,128)(2,1)}, bf16[128,1024]{1,0:T(8,128)(2,1)}) custom-call(bf16[64,1024]{1,0:T(8,128)(2,1)} %get-tuple-element.35.refs_0_.refs_2_, bf16[512,1024]{1,0:T(8,128)(2,1)} %get-tuple-element.30.refs_0_.refs_1_, ...), custom_call_target="tpu_custom_call" | custom-call | flops 10000000 | bytes 1024 | tf_op jit(solution)/shard_map/pallas_call | solution.py:37
  48.5 1.3 collective-permute-start.11
  49.8 2.2 %collective-permute-start.12 = (bf16[128,1024]{1,0:T(8,128)(2,1)}, bf16[128,1024]{1,0:T(8,128)(2,1)}, u32[]{:S(2)}, u32[]{:S(2)}) collective-permute-start(bf16[128,1024]{1,0:T(8,128)(2,1)} %get-tuple-element.40), channel_id=1, source_target_pairs={{0,6},{2,4},{4,2},{6,0},{1,7},{3,5},{5,3},{7,1},{8,14},{10,12},{12... | collective-permute-start | bytes 786440 | tf_op jit(solution)/shard_map/ppermute | solution.py:29
  52.7 1.7 shard_map.102.refs_0_.refs_3_
  54.8 5.5 %shard_map.103.refs_0_.refs_11_ = bf16[1024,1024]{1,0:T(8,128)(2,1)} custom-call(bf16[128,1024]{1,0:T(8,128)(2,1)} %shard_map.102.refs_0_.refs_3_, s32[3]{0:T(128)} %pad_add_fusion.refs_0_.refs_1_.refs_2_, bf16[512,1024]{1,0:T(8,128)(2,1)} %shard_map.99.refs_0_.refs_2_.refs_11_, bf16[512,1024]{1,0:T(8,128)(2,1)} %collective-permute-done.10.refs_3_.refs_12_, ...), custom_call_target="tpu_custom_call" | custom-call | flops 49999998976 | bytes 1024 | tf_op jit(solution)/shard_map/pallas_call | solution.py:37
  60.3 2.3 %collective-permute-start.24 = (bf16[128,1024]{1,0:T(8,128)(2,1)S(1)}, bf16[128,1024]{1,0:T(8,128)(2,1)S(1)}, u32[]{:S(2)}, u32[]{:S(2)}) collective-permute-start(bf16[128,1024]{1,0:T(8,128)(2,1)S(1)} %copy-done.6), channel_id=1, source_target_pairs={{0,6},{2,4},{4,2},{6,0},{1,7},{3,5},{5,3},{7,1},{8,14},{10,12},{12... | collective-permute-start | bytes 786440 | tf_op jit(solution)/shard_map/ppermute | solution.py:29
  63.2 2.0 shard_map.104
  65.2 1.3 collective-permute-start.14
  66.5 5.5 %collective-permute-done.22.refs_1_.refs_13_ = bf16[512,1024]{1,0:T(8,128)(2,1)} collective-permute-done((bf16[512,1024]{1,0:T(8,128)(2,1)S(1)}, bf16[512,1024]{1,0:T(8,128)(2,1)}, u32[]{:S(2)}, u32[]{:S(2)}) %collective-permute-start.22) | collective-permute-done | bytes 1048608 | tf_op jit(solution)/shard_map/ppermute | solution.py:29
  72.0 2.3 %collective-permute-start.26 = (bf16[128,1024]{1,0:T(8,128)(2,1)S(1)}, bf16[128,1024]{1,0:T(8,128)(2,1)}, u32[]{:S(2)}, u32[]{:S(2)}) collective-permute-start(bf16[128,1024]{1,0:T(8,128)(2,1)S(1)} %copy-done.6), channel_id=1, source_target_pairs={{0,1},{1,0},{2,3},{3,2},{4,5},{5,4},{6,7},{7,6},{8,9},{9,8},{10,11... | collective-permute-start | bytes 786440 | tf_op jit(solution)/shard_map/ppermute | solution.py:29
  74.4 2.5 %collective-permute-start.27 = (bf16[128,1024]{1,0:T(8,128)(2,1)S(1)}, bf16[128,1024]{1,0:T(8,128)(2,1)}, u32[]{:S(2)}, u32[]{:S(2)}) collective-permute-start(bf16[128,1024]{1,0:T(8,128)(2,1)S(1)} %collective-permute-done.23.refs_4_), channel_id=1, source_target_pairs={{0,1},{1,0},{2,3},{3,2},{4,5},{5,4},{6,7},{7,6},{8,9},{9,8},{10,11... | collective-permute-start | bytes 786440 | tf_op jit(solution)/shard_map/ppermute | solution.py:29
  77.8 1.7 shard_map.105.refs_0_.refs_2_
  80.1 2.0 collective-permute-start.18
  82.1 1.2 collective-permute-start.20
  83.2 5.9 %shard_map.106.refs_0_.refs_6_.refs_5_ = bf16[1024,1024]{1,0:T(8,128)(2,1)} custom-call(bf16[128,1024]{1,0:T(8,128)(2,1)} %shard_map.105.refs_0_.refs_2_, bf16[512,1024]{1,0:T(8,128)(2,1)} %collective-permute-done.22.refs_1_.refs_13_, s32[3]{0:T(128)} %pad_add_fusion.refs_0_.refs_1_.refs_2_, bf16[128,1024]{1,0:T(8,128)(2,1)} %shard_map.102.refs_0_.refs_3_, ...), custom_call_target="tpu_custom_call" | custom-call | flops 49999998976 | bytes 1024 | tf_op jit(solution)/shard_map/pallas_call | solution.py:37
  90.2 4.4 %collective-permute-start.19 = (bf16[128,1024]{1,0:T(8,128)(2,1)S(1)}, bf16[128,1024]{1,0:T(8,128)(2,1)}, u32[]{:S(2)}, u32[]{:S(2)}) collective-permute-start(bf16[128,1024]{1,0:T(8,128)(2,1)S(1)} %collective-permute-done.18.refs_4_), channel_id=1, source_target_pairs={{0,1},{1,0},{2,3},{3,2},{4,5},{5,4},{6,7},{7,6},{8,9},{9,8},{10,11... | collective-permute-start | bytes 786440 | tf_op jit(solution)/shard_map/ppermute | solution.py:29
  95.2 1.1 collective-permute-start.21
  97.8 4.4 %shard_map.108.refs_7_ = bf16[1024,1024]{1,0:T(8,128)(2,1)} custom-call(f32[8,128]{1,0:T(8,128)} %shard_map.107.refs_0_, s32[3]{0:T(128)} %pad_add_fusion.refs_0_.refs_1_.refs_2_, bf16[128,1024]{1,0:T(8,128)(2,1)} %shard_map.105.refs_0_.refs_2_, bf16[128,1024]{1,0:T(8,128)(2,1)} %copy-done.19, bf16[128,1024]{1,0:T(8,128)(2,1)} %copy-done.20, ...), custom_call_target="tpu_custom_call" | custom-call | flops 49999998976 | bytes 1024 | tf_op jit(solution)/shard_map/pallas_call | solution.py:288
  102.3 4.5 %shard_map.109 = bf16[1024,1024]{1,0:T(8,128)(2,1)} custom-call(s32[3]{0:T(128)} %pad_add_fusion.refs_0_.refs_1_.refs_2_, bf16[128,1024]{1,0:T(8,128)(2,1)} %collective-permute-done.15.refs_1_, bf16[128,1024]{1,0:T(8,128)(2,1)} %collective-permute-done.17.refs_2_, bf16[128,1024]{1,0:T(8,128)(2,1)} %collective-permute-done.19.refs_3_, ...), custom_call_target="tpu_custom_call", output_to_operand_aliasing={{}: (7, {})} | custom-call | flops 49999998976 | bytes 1024 | tf_op jit(solution)/shard_map/pallas_call | solution.py:288
  106.8 34.5 %all_to_all.5 = bf16[8,128,1024]{2,1,0:T(8,128)(2,1)S(1)} all-to-all(bf16[8,128,1024]{2,1,0:T(8,128)(2,1)} %bitcast.4), channel_id=1, replica_groups=mesh['grp'=2,'x'=4,'yh'=2,'z'=4,'core'=2] {'x','yh'}, dimensions={0} | all-to-all | bytes 4194304 | tf_op jit(solution)/shard_map/all_to_all | solution.py:568
  143.8 1.9 collective-permute-start.33
  145.6 1.5 collective-permute-start.38
  147.7 1.8 collective-permute-start.39
  149.5 1.5 collective-permute-done.33.refs_3_
  151.7 1.8 shard_map.110.refs_0_.refs_1_.refs_2_
  155.8 1.8 shard_map.111.refs_5_.refs_7_
  158.6 6.5 %collective-permute-done.34.refs_2_.refs_3_ = bf16[256,1024]{1,0:T(8,128)(2,1)S(1)} collective-permute-done((bf16[256,1024]{1,0:T(8,128)(2,1)}, bf16[256,1024]{1,0:T(8,128)(2,1)S(1)}, u32[]{:S(2)}, u32[]{:S(2)}) %collective-permute-start.34) | collective-permute-done | bytes 524320 | tf_op jit(solution)/shard_map/ppermute | solution.py:29
  167.6 1.9 collective-permute-done.40.refs_6_.refs_8_
  169.5 2.5 %collective-permute-done.35.refs_3_.refs_4_ = bf16[128,1024]{1,0:T(8,128)(2,1)} collective-permute-done((bf16[128,1024]{1,0:T(8,128)(2,1)S(1)}, bf16[128,1024]{1,0:T(8,128)(2,1)}, u32[]{:S(2)}, u32[]{:S(2)}) %collective-permute-start.35) | collective-permute-done | bytes 262176 | tf_op jit(solution)/shard_map/ppermute | solution.py:29
  172.0 5.8 %shard_map.112 = (bf16[512,1024]{1,0:T(8,128)(2,1)}, bf16[512,1024]{1,0:T(8,128)(2,1)}) custom-call(s32[3]{0:T(128)} %pad_add_fusion.refs_0_.refs_1_.refs_2_, bf16[256,1024]{1,0:T(8,128)(2,1)} %shard_map.110.refs_0_.refs_1_.refs_2_, bf16[256,1024]{1,0:T(8,128)(2,1)} %copy-done.10, bf16[128,1024]{1,0:T(8,128)(2,1)} %collective-permute-done.35.refs_3_.refs_4_, ...), custom_call_target="tpu_custom_call" | custom-call | flops 49999998976 | bytes 1024 | tf_op jit(solution)/shard_map/pallas_call | solution.py:37
  177.8 5.9 %collective-permute-start.41 = (bf16[512,1024]{1,0:T(8,128)(2,1)}, bf16[512,1024]{1,0:T(8,128)(2,1)S(1)}, u32[]{:S(2)}, u32[]{:S(2)}) collective-permute-start(bf16[512,1024]{1,0:T(8,128)(2,1)} %get-tuple-element.45), channel_id=1, source_target_pairs={{0,1},{1,0},{2,3},{3,2},{4,5},{5,4},{6,7},{7,6},{8,9},{9,8},{10,11... | collective-permute-start | bytes 3145736 | tf_op jit(solution)/shard_map/ppermute | solution.py:29
  184.2 1.9 collective-permute-done.41.refs_2_
  187.1 2.4 %shard_map.114 = (bf16[128,1024]{1,0:T(8,128)(2,1)}, bf16[128,1024]{1,0:T(8,128)(2,1)}, bf16[128,1024]{1,0:T(8,128)(2,1)}, bf16[128,1024]{1,0:T(8,128)(2,1)}) custom-call(f32[8,128]{1,0:T(8,128)} %shard_map.113.refs_0_, bf16[512,1024]{1,0:T(8,128)(2,1)} %get-tuple-element.44.refs_0_.refs_1_, bf16[512,1024]{1,0:T(8,128)(2,1)} %copy-done.2), custom_call_target="tpu_custom_call" | custom-call | flops 10000000 | bytes 1024 | tf_op jit(solution)/shard_map/pallas_call | solution.py:37
  192.2 9.4 %shard_map.115 = f32[1024,1024]{1,0:T(8,128)} custom-call(bf16[128,1024]{1,0:T(8,128)(2,1)} %get-tuple-element.46.refs_0_, s32[3]{0:T(128)} %pad_add_fusion.refs_0_.refs_1_.refs_2_, bf16[256,1024]{1,0:T(8,128)(2,1)} %shard_map.110.refs_0_.refs_1_.refs_2_, bf16[256,1024]{1,0:T(8,128)(2,1)} %copy-done.10, ...), custom_call_target="tpu_custom_call" | custom-call | flops 49999998976 | bytes 1024 | tf_op jit(solution)/shard_map/pallas_call | solution.py:37
  201.6 3.5 %collective-permute-done.43 = bf16[128,1024]{1,0:T(8,128)(2,1)S(1)} collective-permute-done((bf16[128,1024]{1,0:T(8,128)(2,1)}, bf16[128,1024]{1,0:T(8,128)(2,1)S(1)}, u32[]{:S(2)}, u32[]{:S(2)}) %collective-permute-start.43) | collective-permute-done | bytes 262176 | tf_op jit(solution)/shard_map/ppermute | solution.py:29
  (141 shorter events, 26.6 us)
Async XLA Ops:
  0.6 16.5 %collective-permute-start = (bf16[128,1024]{1,0:T(8,128)(2,1)}, bf16[128,1024]{1,0:T(8,128)(2,1)S(1)}, u32[]{:S(2)}, u32[]{:S(2)}) collective-permute-start(bf16[128,1024]{1,0:T(8,128)(2,1)} %refs_1_.3), channel_id=1, source_target_pairs={{0,2},{2,0},{4,6},{6,4},{1,3},{3,1},{5,7},{7,5},{8,10},{10,8},{12,... | collective-permute-start | bytes 786440 | tf_op jit(solution)/shard_map/ppermute | solution.py:29
  3.2 14.0 %collective-permute-start.1 = (bf16[128,1024]{1,0:T(8,128)(2,1)}, bf16[128,1024]{1,0:T(8,128)(2,1)S(1)}, u32[]{:S(2)}, u32[]{:S(2)}) collective-permute-start(bf16[128,1024]{1,0:T(8,128)(2,1)} %refs_1_.3), channel_id=1, source_target_pairs={{0,6},{2,4},{4,2},{6,0},{1,7},{3,5},{5,3},{7,1},{8,14},{10,12},{12... | collective-permute-start | bytes 786440 | tf_op jit(solution)/shard_map/ppermute | solution.py:29
  15.9 4.5 %collective-permute-start.2 = (bf16[512,1024]{1,0:T(8,128)(2,1)}, bf16[512,1024]{1,0:T(8,128)(2,1)S(1)}, u32[]{:S(2)}, u32[]{:S(2)}) collective-permute-start(bf16[512,1024]{1,0:T(8,128)(2,1)} %get-tuple-element.28), channel_id=1, source_target_pairs={{0,1},{1,0},{2,3},{3,2},{4,5},{5,4},{6,7},{7,6},{8,9},{9,8},{10,11... | collective-permute-start | bytes 3145736 | tf_op jit(solution)/shard_map/ppermute | solution.py:29
  19.7 17.5 %collective-permute-start.3 = (bf16[64,1024]{1,0:T(8,128)(2,1)}, bf16[64,1024]{1,0:T(8,128)(2,1)S(1)}, u32[]{:S(2)}, u32[]{:S(2)}) collective-permute-start(bf16[64,1024]{1,0:T(8,128)(2,1)} %get-tuple-element.27.refs_0_), channel_id=1, source_target_pairs={{0,6},{2,4},{4,2},{6,0},{1,7},{3,5},{5,3},{7,1},{8,14},{10,12},{12... | collective-permute-start | bytes 393224 | tf_op jit(solution)/shard_map/ppermute | solution.py:29
  20.1 18.3 %collective-permute-start.4 = (bf16[64,1024]{1,0:T(8,128)(2,1)}, bf16[64,1024]{1,0:T(8,128)(2,1)S(1)}, u32[]{:S(2)}, u32[]{:S(2)}) collective-permute-start(bf16[64,1024]{1,0:T(8,128)(2,1)} %get-tuple-element.31), channel_id=1, source_target_pairs={{0,2},{2,0},{4,6},{6,4},{1,3},{3,1},{5,7},{7,5},{8,10},{10,8},{12,... | collective-permute-start | bytes 393224 | tf_op jit(solution)/shard_map/ppermute | solution.py:29
  23.8 17.3 %collective-permute-start.5 = (bf16[128,1024]{1,0:T(8,128)(2,1)}, bf16[128,1024]{1,0:T(8,128)(2,1)S(1)}, u32[]{:S(2)}, u32[]{:S(2)}) collective-permute-start(bf16[128,1024]{1,0:T(8,128)(2,1)} %get-tuple-element.32), channel_id=1, source_target_pairs={{0,2},{2,0},{4,6},{6,4},{1,3},{3,1},{5,7},{7,5},{8,10},{10,8},{12,... | collective-permute-start | bytes 786440 | tf_op jit(solution)/shard_map/ppermute | solution.py:29
  25.0 16.2 %collective-permute-start.6 = (bf16[128,1024]{1,0:T(8,128)(2,1)}, bf16[128,1024]{1,0:T(8,128)(2,1)S(1)}, u32[]{:S(2)}, u32[]{:S(2)}) collective-permute-start(bf16[128,1024]{1,0:T(8,128)(2,1)} %get-tuple-element.33), channel_id=1, source_target_pairs={{0,6},{2,4},{4,2},{6,0},{1,7},{3,5},{5,3},{7,1},{8,14},{10,12},{12... | collective-permute-start | bytes 786440 | tf_op jit(solution)/shard_map/ppermute | solution.py:29
  27.2 14.0 %collective-permute-start.7 = (bf16[128,1024]{1,0:T(8,128)(2,1)}, bf16[128,1024]{1,0:T(8,128)(2,1)S(1)}, u32[]{:S(2)}, u32[]{:S(2)}) collective-permute-start(bf16[128,1024]{1,0:T(8,128)(2,1)} %get-tuple-element.34), channel_id=1, source_target_pairs={{0,4},{2,6},{4,0},{6,2},{1,5},{3,7},{5,1},{7,3},{8,12},{10,14},{12... | collective-permute-start | bytes 786440 | tf_op jit(solution)/shard_map/ppermute | solution.py:29
  37.2 9.0 %collective-permute-start.8 = (bf16[512,1024]{1,0:T(8,128)(2,1)}, bf16[512,1024]{1,0:T(8,128)(2,1)}, u32[]{:S(2)}, u32[]{:S(2)}) collective-permute-start(bf16[512,1024]{1,0:T(8,128)(2,1)} %get-tuple-element.36), channel_id=1, source_target_pairs={{0,1},{1,0},{2,3},{3,2},{4,5},{5,4},{6,7},{7,6},{8,9},{9,8},{10,11... | collective-permute-start | bytes 3145736 | tf_op jit(solution)/shard_map/ppermute | solution.py:29
  41.2 13.2 %collective-permute-start.10 = (bf16[512,1024]{1,0:T(8,128)(2,1)}, bf16[512,1024]{1,0:T(8,128)(2,1)}, u32[]{:S(2)}, u32[]{:S(2)}) collective-permute-start(bf16[512,1024]{1,0:T(8,128)(2,1)} %shard_map.99.refs_0_.refs_2_.refs_11_), channel_id=1, source_target_pairs={{0,1},{1,0},{2,3},{3,2},{4,5},{5,4},{6,7},{7,6},{8,9},{9,8},{10,11... | collective-permute-start | bytes 3145736 | tf_op jit(solution)/shard_map/ppermute | solution.py:29
  44.7 7.4 %collective-permute-start.9 = (bf16[64,1024]{1,0:T(8,128)(2,1)}, bf16[64,1024]{1,0:T(8,128)(2,1)S(1)}, u32[]{:S(2)}, u32[]{:S(2)}) collective-permute-start(bf16[64,1024]{1,0:T(8,128)(2,1)} %get-tuple-element.38), channel_id=1, source_target_pairs={{0,64},{64,0},{1,65},{65,1},{2,66},{66,2},{3,67},{67,3},{4,68},{68... | collective-permute-start | bytes 393224 | tf_op jit(solution)/shard_map/ppermute | solution.py:29
  46.0 26.1 %collective-permute-start.22 = (bf16[512,1024]{1,0:T(8,128)(2,1)S(1)}, bf16[512,1024]{1,0:T(8,128)(2,1)}, u32[]{:S(2)}, u32[]{:S(2)}) collective-permute-start(bf16[512,1024]{1,0:T(8,128)(2,1)S(1)} %copy-done), channel_id=1, source_target_pairs={{0,64},{64,0},{1,65},{65,1},{2,66},{66,2},{3,67},{67,3},{4,68},{68... | collective-permute-start | bytes 3145736 | tf_op jit(solution)/shard_map/ppermute | solution.py:29
  48.5 11.8 %collective-permute-start.11 = (bf16[128,1024]{1,0:T(8,128)(2,1)}, bf16[128,1024]{1,0:T(8,128)(2,1)}, u32[]{:S(2)}, u32[]{:S(2)}) collective-permute-start(bf16[128,1024]{1,0:T(8,128)(2,1)} %get-tuple-element.39), channel_id=1, source_target_pairs={{0,2},{2,0},{4,6},{6,4},{1,3},{3,1},{5,7},{7,5},{8,10},{10,8},{12,... | collective-permute-start | bytes 786440 | tf_op jit(solution)/shard_map/ppermute | solution.py:29
  49.8 12.8 %collective-permute-start.12 = (bf16[128,1024]{1,0:T(8,128)(2,1)}, bf16[128,1024]{1,0:T(8,128)(2,1)}, u32[]{:S(2)}, u32[]{:S(2)}) collective-permute-start(bf16[128,1024]{1,0:T(8,128)(2,1)} %get-tuple-element.40), channel_id=1, source_target_pairs={{0,6},{2,4},{4,2},{6,0},{1,7},{3,5},{5,3},{7,1},{8,14},{10,12},{12... | collective-permute-start | bytes 786440 | tf_op jit(solution)/shard_map/ppermute | solution.py:29
  52.0 11.2 %collective-permute-start.13 = (bf16[128,1024]{1,0:T(8,128)(2,1)}, bf16[128,1024]{1,0:T(8,128)(2,1)}, u32[]{:S(2)}, u32[]{:S(2)}) collective-permute-start(bf16[128,1024]{1,0:T(8,128)(2,1)} %get-tuple-element.41), channel_id=1, source_target_pairs={{0,4},{2,6},{4,0},{6,2},{1,5},{3,7},{5,1},{7,3},{8,12},{10,14},{12... | collective-permute-start | bytes 786440 | tf_op jit(solution)/shard_map/ppermute | solution.py:29
  54.4 19.9 %collective-permute-start.23 = (bf16[128,1024]{1,0:T(8,128)(2,1)}, bf16[128,1024]{1,0:T(8,128)(2,1)S(1)}, u32[]{:S(2)}, u32[]{:S(2)}) collective-permute-start(bf16[128,1024]{1,0:T(8,128)(2,1)} %shard_map.102.refs_0_.refs_3_), channel_id=1, source_target_pairs={{0,2},{2,0},{4,6},{6,4},{1,3},{3,1},{5,7},{7,5},{8,10},{10,8},{12,... | collective-permute-start | bytes 786440 | tf_op jit(solution)/shard_map/ppermute | solution.py:29
  60.3 14.1 %collective-permute-start.24 = (bf16[128,1024]{1,0:T(8,128)(2,1)S(1)}, bf16[128,1024]{1,0:T(8,128)(2,1)S(1)}, u32[]{:S(2)}, u32[]{:S(2)}) collective-permute-start(bf16[128,1024]{1,0:T(8,128)(2,1)S(1)} %copy-done.6), channel_id=1, source_target_pairs={{0,6},{2,4},{4,2},{6,0},{1,7},{3,5},{5,3},{7,1},{8,14},{10,12},{12... | collective-permute-start | bytes 786440 | tf_op jit(solution)/shard_map/ppermute | solution.py:29
  62.6 14.3 %collective-permute-start.25 = (bf16[128,1024]{1,0:T(8,128)(2,1)S(1)}, bf16[128,1024]{1,0:T(8,128)(2,1)}, u32[]{:S(2)}, u32[]{:S(2)}) collective-permute-start(bf16[128,1024]{1,0:T(8,128)(2,1)S(1)} %copy-done.6), channel_id=1, source_target_pairs={{0,4},{2,6},{4,0},{6,2},{1,5},{3,7},{5,1},{7,3},{8,12},{10,14},{12... | collective-permute-start | bytes 786440 | tf_op jit(solution)/shard_map/ppermute | solution.py:29
  65.2 11.9 %collective-permute-start.14 = (bf16[64,1024]{1,0:T(8,128)(2,1)}, bf16[64,1024]{1,0:T(8,128)(2,1)S(1)}, u32[]{:S(2)}, u32[]{:S(2)}) collective-permute-start(bf16[64,1024]{1,0:T(8,128)(2,1)} %get-tuple-element.43), channel_id=1, source_target_pairs={{0,64},{64,0},{1,65},{65,1},{2,66},{66,2},{3,67},{67,3},{4,68},{68... | collective-permute-start | bytes 393224 | tf_op jit(solution)/shard_map/ppermute | solution.py:29
  72.0 7.5 %collective-permute-start.26 = (bf16[128,1024]{1,0:T(8,128)(2,1)S(1)}, bf16[128,1024]{1,0:T(8,128)(2,1)}, u32[]{:S(2)}, u32[]{:S(2)}) collective-permute-start(bf16[128,1024]{1,0:T(8,128)(2,1)S(1)} %copy-done.6), channel_id=1, source_target_pairs={{0,1},{1,0},{2,3},{3,2},{4,5},{5,4},{6,7},{7,6},{8,9},{9,8},{10,11... | collective-permute-start | bytes 786440 | tf_op jit(solution)/shard_map/ppermute | solution.py:29
  74.3 21.9 %collective-permute-start.30 = (bf16[512,1024]{1,0:T(8,128)(2,1)}, bf16[512,1024]{1,0:T(8,128)(2,1)S(1)}, u32[]{:S(2)}, u32[]{:S(2)}) collective-permute-start(bf16[512,1024]{1,0:T(8,128)(2,1)} %collective-permute-done.22.refs_1_.refs_13_), channel_id=1, source_target_pairs={{0,1},{1,0},{2,3},{3,2},{4,5},{5,4},{6,7},{7,6},{8,9},{9,8},{10,11... | collective-permute-start | bytes 3145736 | tf_op jit(solution)/shard_map/ppermute | solution.py:29
  74.4 5.4 %collective-permute-start.27 = (bf16[128,1024]{1,0:T(8,128)(2,1)S(1)}, bf16[128,1024]{1,0:T(8,128)(2,1)}, u32[]{:S(2)}, u32[]{:S(2)}) collective-permute-start(bf16[128,1024]{1,0:T(8,128)(2,1)S(1)} %collective-permute-done.23.refs_4_), channel_id=1, source_target_pairs={{0,1},{1,0},{2,3},{3,2},{4,5},{5,4},{6,7},{7,6},{8,9},{9,8},{10,11... | collective-permute-start | bytes 786440 | tf_op jit(solution)/shard_map/ppermute | solution.py:29
  76.9 3.2 %collective-permute-start.28 = (bf16[128,1024]{1,0:T(8,128)(2,1)S(1)}, bf16[128,1024]{1,0:T(8,128)(2,1)}, u32[]{:S(2)}, u32[]{:S(2)}) collective-permute-start(bf16[128,1024]{1,0:T(8,128)(2,1)S(1)} %collective-permute-done.24.refs_5_), channel_id=1, source_target_pairs={{0,1},{1,0},{2,3},{3,2},{4,5},{5,4},{6,7},{7,6},{8,9},{9,8},{10,11... | collective-permute-start | bytes 786440 | tf_op jit(solution)/shard_map/ppermute | solution.py:29
  77.1 4.9 %collective-permute-start.29 = (bf16[128,1024]{1,0:T(8,128)(2,1)}, bf16[128,1024]{1,0:T(8,128)(2,1)}, u32[]{:S(2)}, u32[]{:S(2)}) collective-permute-start(bf16[128,1024]{1,0:T(8,128)(2,1)} %collective-permute-done.25.refs_6_), channel_id=1, source_target_pairs={{0,1},{1,0},{2,3},{3,2},{4,5},{5,4},{6,7},{7,6},{8,9},{9,8},{10,11... | collective-permute-start | bytes 786440 | tf_op jit(solution)/shard_map/ppermute | solution.py:29
  79.5 22.8 %collective-permute-start.15 = (bf16[128,1024]{1,0:T(8,128)(2,1)}, bf16[128,1024]{1,0:T(8,128)(2,1)}, u32[]{:S(2)}, u32[]{:S(2)}) collective-permute-start(bf16[128,1024]{1,0:T(8,128)(2,1)} %shard_map.105.refs_0_.refs_2_), channel_id=1, source_target_pairs={{0,1},{1,0},{2,3},{3,2},{4,5},{5,4},{6,7},{7,6},{8,9},{9,8},{10,11... | collective-permute-start | bytes 786440 | tf_op jit(solution)/shard_map/ppermute | solution.py:29
  79.8 9.3 %collective-permute-start.16 = (bf16[128,1024]{1,0:T(8,128)(2,1)}, bf16[128,1024]{1,0:T(8,128)(2,1)S(1)}, u32[]{:S(2)}, u32[]{:S(2)}) collective-permute-start(bf16[128,1024]{1,0:T(8,128)(2,1)} %shard_map.105.refs_0_.refs_2_), channel_id=1, source_target_pairs={{0,2},{2,0},{4,6},{6,4},{1,3},{3,1},{5,7},{7,5},{8,10},{10,8},{12,... | collective-permute-start | bytes 786440 | tf_op jit(solution)/shard_map/ppermute | solution.py:29
  80.1 10.0 %collective-permute-start.18 = (bf16[128,1024]{1,0:T(8,128)(2,1)}, bf16[128,1024]{1,0:T(8,128)(2,1)S(1)}, u32[]{:S(2)}, u32[]{:S(2)}) collective-permute-start(bf16[128,1024]{1,0:T(8,128)(2,1)} %shard_map.105.refs_0_.refs_2_), channel_id=1, source_target_pairs={{0,6},{2,4},{4,2},{6,0},{1,7},{3,5},{5,3},{7,1},{8,14},{10,12},{12... | collective-permute-start | bytes 786440 | tf_op jit(solution)/shard_map/ppermute | solution.py:29
  82.1 13.1 %collective-permute-start.20 = (bf16[128,1024]{1,0:T(8,128)(2,1)}, bf16[128,1024]{1,0:T(8,128)(2,1)S(1)}, u32[]{:S(2)}, u32[]{:S(2)}) collective-permute-start(bf16[128,1024]{1,0:T(8,128)(2,1)} %shard_map.105.refs_0_.refs_2_), channel_id=1, source_target_pairs={{0,4},{2,6},{4,0},{6,2},{1,5},{3,7},{5,1},{7,3},{8,12},{10,14},{12... | collective-permute-start | bytes 786440 | tf_op jit(solution)/shard_map/ppermute | solution.py:29
  89.1 13.1 %collective-permute-start.17 = (bf16[128,1024]{1,0:T(8,128)(2,1)S(1)}, bf16[128,1024]{1,0:T(8,128)(2,1)}, u32[]{:S(2)}, u32[]{:S(2)}) collective-permute-start(bf16[128,1024]{1,0:T(8,128)(2,1)S(1)} %collective-permute-done.16.refs_3_), channel_id=1, source_target_pairs={{0,1},{1,0},{2,3},{3,2},{4,5},{5,4},{6,7},{7,6},{8,9},{9,8},{10,11... | collective-permute-start | bytes 786440 | tf_op jit(solution)/shard_map/ppermute | solution.py:29
  90.2 12.1 %collective-permute-start.19 = (bf16[128,1024]{1,0:T(8,128)(2,1)S(1)}, bf16[128,1024]{1,0:T(8,128)(2,1)}, u32[]{:S(2)}, u32[]{:S(2)}) collective-permute-start(bf16[128,1024]{1,0:T(8,128)(2,1)S(1)} %collective-permute-done.18.refs_4_), channel_id=1, source_target_pairs={{0,1},{1,0},{2,3},{3,2},{4,5},{5,4},{6,7},{7,6},{8,9},{9,8},{10,11... | collective-permute-start | bytes 786440 | tf_op jit(solution)/shard_map/ppermute | solution.py:29
  95.2 7.1 %collective-permute-start.21 = (bf16[128,1024]{1,0:T(8,128)(2,1)S(1)}, bf16[128,1024]{1,0:T(8,128)(2,1)}, u32[]{:S(2)}, u32[]{:S(2)}) collective-permute-start(bf16[128,1024]{1,0:T(8,128)(2,1)S(1)} %collective-permute-done.20.refs_5_), channel_id=1, source_target_pairs={{0,1},{1,0},{2,3},{3,2},{4,5},{5,4},{6,7},{7,6},{8,9},{9,8},{10,11... | collective-permute-start | bytes 786440 | tf_op jit(solution)/shard_map/ppermute | solution.py:29
  142.3 5.4 %collective-permute-start.31 = (bf16[64,1024]{1,0:T(8,128)(2,1)S(1)}, bf16[64,1024]{1,0:T(8,128)(2,1)S(1)}, u32[]{:S(2)}, u32[]{:S(2)}) collective-permute-start(bf16[64,1024]{1,0:T(8,128)(2,1)S(1)} %get-tuple-element.51.refs_0_), channel_id=1, source_target_pairs={{0,8},{8,0},{64,72},{72,64},{1,9},{9,1},{65,73},{73,65},{2,10},{10... | collective-permute-start | bytes 393224 | tf_op jit(solution)/shard_map/ppermute | solution.py:29
  143.4 6.1 %collective-permute-start.32 = (bf16[64,1024]{1,0:T(8,128)(2,1)S(1)}, bf16[64,1024]{1,0:T(8,128)(2,1)S(1)}, u32[]{:S(2)}, u32[]{:S(2)}) collective-permute-start(bf16[64,1024]{1,0:T(8,128)(2,1)S(1)} %get-tuple-element.51.refs_0_), channel_id=1, source_target_pairs={{0,64},{8,72},{64,0},{72,8},{1,65},{9,73},{65,1},{73,9},{2,66},{10... | collective-permute-start | bytes 393224 | tf_op jit(solution)/shard_map/ppermute | solution.py:29
  143.8 7.2 %collective-permute-start.33 = (bf16[64,1024]{1,0:T(8,128)(2,1)S(1)}, bf16[64,1024]{1,0:T(8,128)(2,1)S(1)}, u32[]{:S(2)}, u32[]{:S(2)}) collective-permute-start(bf16[64,1024]{1,0:T(8,128)(2,1)S(1)} %get-tuple-element.51.refs_0_), channel_id=1, source_target_pairs={{0,72},{8,64},{64,8},{72,0},{1,73},{9,65},{65,9},{73,1},{2,74},{10... | collective-permute-start | bytes 393224 | tf_op jit(solution)/shard_map/ppermute | solution.py:29
  145.6 8.8 %collective-permute-start.37 = (bf16[64,1024]{1,0:T(8,128)(2,1)S(1)}, bf16[64,1024]{1,0:T(8,128)(2,1)S(1)}, u32[]{:S(2)}, u32[]{:S(2)}) collective-permute-start(bf16[64,1024]{1,0:T(8,128)(2,1)S(1)} %get-tuple-element.50.refs_1_), channel_id=1, source_target_pairs={{0,16},{16,0},{32,48},{48,32},{1,17},{17,1},{33,49},{49,33},{2,18}... | collective-permute-start | bytes 393224 | tf_op jit(solution)/shard_map/ppermute | solution.py:29
  145.6 8.8 %collective-permute-start.38 = (bf16[64,1024]{1,0:T(8,128)(2,1)S(1)}, bf16[64,1024]{1,0:T(8,128)(2,1)S(1)}, u32[]{:S(2)}, u32[]{:S(2)}) collective-permute-start(bf16[64,1024]{1,0:T(8,128)(2,1)S(1)} %get-tuple-element.50.refs_1_), channel_id=1, source_target_pairs={{0,32},{16,48},{32,0},{48,16},{1,33},{17,49},{33,1},{49,17},{2,34}... | collective-permute-start | bytes 393224 | tf_op jit(solution)/shard_map/ppermute | solution.py:29
  147.7 6.7 %collective-permute-start.39 = (bf16[64,1024]{1,0:T(8,128)(2,1)S(1)}, bf16[64,1024]{1,0:T(8,128)(2,1)S(1)}, u32[]{:S(2)}, u32[]{:S(2)}) collective-permute-start(bf16[64,1024]{1,0:T(8,128)(2,1)S(1)} %get-tuple-element.50.refs_1_), channel_id=1, source_target_pairs={{0,48},{16,32},{32,16},{48,0},{1,49},{17,33},{33,17},{49,1},{2,50}... | collective-permute-start | bytes 393224 | tf_op jit(solution)/shard_map/ppermute | solution.py:29
  153.5 11.6 %collective-permute-start.34 = (bf16[256,1024]{1,0:T(8,128)(2,1)}, bf16[256,1024]{1,0:T(8,128)(2,1)S(1)}, u32[]{:S(2)}, u32[]{:S(2)}) collective-permute-start(bf16[256,1024]{1,0:T(8,128)(2,1)} %shard_map.110.refs_0_.refs_1_.refs_2_), channel_id=1, source_target_pairs={{0,16},{16,0},{32,48},{48,32},{1,17},{17,1},{33,49},{49,33},{2,18}... | collective-permute-start | bytes 1572872 | tf_op jit(solution)/shard_map/ppermute | solution.py:29
  153.8 13.4 %collective-permute-start.36 = (bf16[256,1024]{1,0:T(8,128)(2,1)}, bf16[256,1024]{1,0:T(8,128)(2,1)S(1)}, u32[]{:S(2)}, u32[]{:S(2)}) collective-permute-start(bf16[256,1024]{1,0:T(8,128)(2,1)} %shard_map.110.refs_0_.refs_1_.refs_2_), channel_id=1, source_target_pairs={{0,48},{16,32},{32,16},{48,0},{1,49},{17,33},{33,17},{49,1},{2,50}... | collective-permute-start | bytes 1572872 | tf_op jit(solution)/shard_map/ppermute | solution.py:29
  157.6 11.9 %collective-permute-start.40 = (bf16[256,1024]{1,0:T(8,128)(2,1)}, bf16[256,1024]{1,0:T(8,128)(2,1)S(1)}, u32[]{:S(2)}, u32[]{:S(2)}) collective-permute-start(bf16[256,1024]{1,0:T(8,128)(2,1)} %shard_map.111.refs_5_.refs_7_), channel_id=1, source_target_pairs={{0,8},{8,0},{64,72},{72,64},{1,9},{9,1},{65,73},{73,65},{2,10},{10... | collective-permute-start | bytes 1572872 | tf_op jit(solution)/shard_map/ppermute | solution.py:29
  165.1 6.9 %collective-permute-start.35 = (bf16[128,1024]{1,0:T(8,128)(2,1)S(1)}, bf16[128,1024]{1,0:T(8,128)(2,1)}, u32[]{:S(2)}, u32[]{:S(2)}) collective-permute-start(bf16[128,1024]{1,0:T(8,128)(2,1)S(1)} %slice.17), channel_id=1, source_target_pairs={{0,48},{16,32},{32,16},{48,0},{1,49},{17,33},{33,17},{49,1},{2,50}... | collective-permute-start | bytes 786440 | tf_op jit(solution)/shard_map/ppermute | solution.py:29
  165.2 26.0 %collective-permute-start.46 = (bf16[256,1024]{1,0:T(8,128)(2,1)}, bf16[256,1024]{1,0:T(8,128)(2,1)}, u32[]{:S(2)}, u32[]{:S(2)}) collective-permute-start(bf16[256,1024]{1,0:T(8,128)(2,1)} %shard_map.111.refs_5_.refs_7_), channel_id=1, source_target_pairs={{0,64},{8,72},{64,0},{72,8},{1,65},{9,73},{65,1},{73,9},{2,66},{10... | collective-permute-start | bytes 1572872 | tf_op jit(solution)/shard_map/ppermute | solution.py:29
  166.2 26.0 %collective-permute-start.47 = (bf16[256,1024]{1,0:T(8,128)(2,1)}, bf16[256,1024]{1,0:T(8,128)(2,1)}, u32[]{:S(2)}, u32[]{:S(2)}) collective-permute-start(bf16[256,1024]{1,0:T(8,128)(2,1)} %shard_map.111.refs_5_.refs_7_), channel_id=1, source_target_pairs={{0,72},{8,64},{64,8},{72,0},{1,73},{9,65},{65,9},{73,1},{2,74},{10... | collective-permute-start | bytes 1572872 | tf_op jit(solution)/shard_map/ppermute | solution.py:29
  167.3 24.9 %collective-permute-start.45 = (bf16[128,1024]{1,0:T(8,128)(2,1)S(1)}, bf16[128,1024]{1,0:T(8,128)(2,1)}, u32[]{:S(2)}, u32[]{:S(2)}) collective-permute-start(bf16[128,1024]{1,0:T(8,128)(2,1)S(1)} %slice.19), channel_id=1, source_target_pairs={{0,16},{16,0},{32,48},{48,32},{1,17},{17,1},{33,49},{49,33},{2,18}... | collective-permute-start | bytes 786440 | tf_op jit(solution)/shard_map/ppermute | solution.py:29
  177.8 8.4 %collective-permute-start.41 = (bf16[512,1024]{1,0:T(8,128)(2,1)}, bf16[512,1024]{1,0:T(8,128)(2,1)S(1)}, u32[]{:S(2)}, u32[]{:S(2)}) collective-permute-start(bf16[512,1024]{1,0:T(8,128)(2,1)} %get-tuple-element.45), channel_id=1, source_target_pairs={{0,1},{1,0},{2,3},{3,2},{4,5},{5,4},{6,7},{7,6},{8,9},{9,8},{10,11... | collective-permute-start | bytes 3145736 | tf_op jit(solution)/shard_map/ppermute | solution.py:29
  189.5 12.1 %collective-permute-start.44 = (bf16[128,1024]{1,0:T(8,128)(2,1)}, bf16[128,1024]{1,0:T(8,128)(2,1)S(1)}, u32[]{:S(2)}, u32[]{:S(2)}) collective-permute-start(bf16[128,1024]{1,0:T(8,128)(2,1)} %get-tuple-element.49), channel_id=1, source_target_pairs={{0,4},{2,6},{4,0},{6,2},{1,5},{3,7},{5,1},{7,3},{8,12},{10,14},{12... | collective-permute-start | bytes 786440 | tf_op jit(solution)/shard_map/ppermute | solution.py:29
  190.5 14.6 %collective-permute-start.43 = (bf16[128,1024]{1,0:T(8,128)(2,1)}, bf16[128,1024]{1,0:T(8,128)(2,1)S(1)}, u32[]{:S(2)}, u32[]{:S(2)}) collective-permute-start(bf16[128,1024]{1,0:T(8,128)(2,1)} %get-tuple-element.48), channel_id=1, source_target_pairs={{0,6},{2,4},{4,2},{6,0},{1,7},{3,5},{5,3},{7,1},{8,14},{10,12},{12... | collective-permute-start | bytes 786440 | tf_op jit(solution)/shard_map/ppermute | solution.py:29
  191.2 13.9 %collective-permute-start.42 = (bf16[128,1024]{1,0:T(8,128)(2,1)}, bf16[128,1024]{1,0:T(8,128)(2,1)S(1)}, u32[]{:S(2)}, u32[]{:S(2)}) collective-permute-start(bf16[128,1024]{1,0:T(8,128)(2,1)} %get-tuple-element.47), channel_id=1, source_target_pairs={{0,2},{2,0},{4,6},{6,4},{1,3},{3,1},{5,7},{7,5},{8,10},{10,8},{12,... | collective-permute-start | bytes 786440 | tf_op jit(solution)/shard_map/ppermute | solution.py:29
  (32 other events, 105.1 us)

commit v6 on v5

--- a/solution.py
+++ b/solution.py
@@ -322,37 +322,38 @@
             yield 2 * e + n, 1, (near_y, next_y)[n], e * piece
 
 
-def values_kernel(ids_ref, *refs):
+def values_kernel(which, ids_ref, *refs):
     gaps = refs[:6]
-    w_ref, mine_ref, peer_ref, g_ref = refs[6:]
+    w_ref, out_ref, g_ref = refs[6:]
     piece = gaps[0].shape[0] // 4
-    rows = g_ref.shape[0]
-
-    @pl.when(pl.program_id(0) == 0)
-    def _():
-        for k, part, ref, start in own_places(*gaps):
-            to = ids_ref[0] ^ ids_ref[1] ^ k
-            place = (to & 1) * (rows // 2) + (to >> 1) * (2 * piece) + part * piece
-            g_ref[pl.ds(pl.multiple_of(place, piece), piece), :] = ref[start : start + piece, :]
-
-    out = nt(g_ref[...], w_ref[...]).astype(BF16)
-    mine_ref[...] = out[: rows // 2]
-    peer_ref[...] = out[rows // 2 :]
-
-
-def values_partial(ids, gaps, weight, after, tile=512):
-    rows, width = 4 * gaps[0].shape[0], gaps[0].shape[1]
+    distance = ids_ref[0] ^ ids_ref[1]
+
+    for odd in range(2):
+
+        @pl.when(jnp.logical_and(pl.program_id(0) == 0, ((distance & 1) ^ odd) == which))
+        def _():
+            for k, part, ref, start in own_places(*gaps):
+                if k & 1 == odd:
+                    place = ((distance ^ k) >> 1) * (2 * piece) + part * piece
+                    at = pl.multiple_of(place, piece)
+                    g_ref[pl.ds(at, piece), :] = ref[start : start + piece, :]
+
+    out_ref[...] = nt(g_ref[...], w_ref[...]).astype(BF16)
+
+
+def values_partial(ids, gaps, weight, which, after=(), tile=512):
+    rows, width = 2 * gaps[0].shape[0], gaps[0].shape[1]
     feats = weight.shape[0]
     return call(
         LONG,
-        with_unread(values_kernel, len(after)),
+        with_unread(functools.partial(values_kernel, which), len(after)),
         (feats // tile,),
-        [shape(rows // 2, feats)] * 2,
+        shape(rows, feats),
         [unread()] * len(after)
         + [smem()]
         + [whole(g) for g in gaps]
         + [pl.BlockSpec((tile, width), lambda j: (j, 0))],
-        [pl.BlockSpec((rows // 2, tile), lambda j: (0, j))] * 2,
+        pl.BlockSpec((rows, tile), lambda j: (0, j)),
         [pltpu.VMEM((rows, width), BF16)],
         *after,
         ids,
@@ -579,8 +580,10 @@
     gaps = [around, near_x[0], *far_x, near_x[1], along, own_y]
     gaps += [swap(along, Y, 2), swap(along, Y, 3)]
 
-    mine, peer = values_partial(ids, gaps[:3] + gaps[4:7], student_weight, ())
-    parts = merged((mine, swap(peer, CORE, 1)), 4, (marker(mine),))
+    near_gaps = gaps[:3] + gaps[4:7]
+    peer = values_partial(ids, near_gaps, student_weight, 1)
+    mine = values_partial(ids, near_gaps, student_weight, 0, (peer,))
+    parts = merged((mine, swap(peer, CORE, 1)), 4)
     values_grad = add(parts[0], *[swap(parts[k], Z, k) for k in (1, 3, 2)])
     weight_grad = weight_sums(ids, gaps, (near, pair, far, far_pair), (parts[0],))
     return (values_grad, weight_grad)

time: 207 us -> 208 us (level)
  Pallas kernels: 78.5 us -> 81.3 us
    pallas_call x19, Pallas kernels: 69.6 us -> 72.4 us  [call(): pl.pallas_call(body, grid=grid, out_shape=out_shape, in_specs=in_specs, o...]
  transfers between devices with their start and end apart: 48 -> 48, of which waited for: 9 -> 8; matrix products, arithmetic and copies ran while one was open for 0% -> 0% of each run, Pallas kernels for 36% -> 37%
where the time goes in v6:
time: 208 us; the launch traced here: 207 us
  Pallas kernels  81.3 us (39%)
  starting transfers between devices  56.6 us (27%)
  blocking collectives  34.5 us (17%)
  waiting for transfers between devices  22.9 us (11%)
  local copies, waits for them, and re-layouts  8.88 us (4%)
    pallas_call x19, Pallas kernels, call(): pl.pallas_call(body, grid=grid, out_shape=out_shape, in_specs=in_specs, o...  72.4 us
    ppermute x48, starting transfers between devices, swap(): return lax.ppermute(array, axes, [(i, i ^ distance) for i in range(size)])  56.6 us
    all_to_all x1, blocking collectives, per_device(): lax.all_to_all(parts.reshape(8, -1, parts.shape[1]), DP, 0, 0, tiled=True)  34.5 us
    ppermute x48, waiting for transfers between devices, swap(): return lax.ppermute(array, axes, [(i, i ^ distance) for i in range(size)])  22.9 us
    pallas_call x2, Pallas kernels, some_less_target(): pl.pallas_call(with_unread(functools.partial(some_target_kernel, fars), l...  8.92 us
    unnamed x64, local copies, waits for them, and re-layouts  8.82 us
  transfers between devices with their start and end apart: 48, of which 8 were waited for; matrix products, arithmetic and copies ran while one was open for 0% of the time, Pallas kernels for 37%

profile of v6, /device:TPU:1, one launch (start us, length us, event | category | flops | bytes accessed | tf_op | source)
XLA Modules:
  0.0 207.0 jit_solution(13589069208346736626)
XLA Ops:
  0.6 2.5 %collective-permute-start = (bf16[128,1024]{1,0:T(8,128)(2,1)}, bf16[128,1024]{1,0:T(8,128)(2,1)S(1)}, u32[]{:S(2)}, u32[]{:S(2)}) collective-permute-start(bf16[128,1024]{1,0:T(8,128)(2,1)} %refs_1_.3), channel_id=1, source_target_pairs={{0,2},{2,0},{4,6},{6,4},{1,3},{3,1},{5,7},{7,5},{8,10},{10,8},{12,... | collective-permute-start | bytes 786440 | tf_op jit(solution)/shard_map/ppermute | solution.py:29
  3.2 2.2 %collective-permute-start.1 = (bf16[128,1024]{1,0:T(8,128)(2,1)}, bf16[128,1024]{1,0:T(8,128)(2,1)S(1)}, u32[]{:S(2)}, u32[]{:S(2)}) collective-permute-start(bf16[128,1024]{1,0:T(8,128)(2,1)} %refs_1_.3), channel_id=1, source_target_pairs={{0,6},{2,4},{4,2},{6,0},{1,7},{3,5},{5,3},{7,1},{8,14},{10,12},{12... | collective-permute-start | bytes 786440 | tf_op jit(solution)/shard_map/ppermute | solution.py:29
  6.1 9.9 %shard_map.95 = (bf16[512,1024]{1,0:T(8,128)(2,1)}, bf16[512,1024]{1,0:T(8,128)(2,1)}) custom-call(s32[3]{0:T(128)} %pad_add_fusion.refs_0_.refs_1_.refs_2_, s32[16,128]{1,0:T(8,128)} %refs_2_.3, bf16[1024,2048]{1,0:T(8,128)(2,1)} %refs_3_.3, bf16[2048,2048]{1,0:T(8,128)(2,1)} %refs_4_.4, bf16[128,2048]{1,0:T(8,128)(2,1)} %refs_5_.1), custom_call_target="tpu_custom_call" | custom-call | flops 49999998976 | bytes 1024 | tf_op jit(solution)/shard_map/pallas_call | solution.py:37
  16.0 1.2 collective-permute-start.2
  18.0 1.7 shard_map.96
  21.4 2.5 %shard_map.97 = (bf16[128,1024]{1,0:T(8,128)(2,1)}, bf16[128,1024]{1,0:T(8,128)(2,1)}, bf16[128,1024]{1,0:T(8,128)(2,1)}, bf16[128,1024]{1,0:T(8,128)(2,1)}) custom-call(bf16[64,1024]{1,0:T(8,128)(2,1)} %get-tuple-element.25.refs_0_, bf16[512,1024]{1,0:T(8,128)(2,1)} %get-tuple-element.24.refs_0_.refs_1_, bf16[512,1024]{1,0:T(8,128)(2,1)} %copy-done.1), custom_call_target="tpu_custom_call" | custom-call | flops 10000000 | bytes 1024 | tf_op jit(solution)/shard_map/pallas_call | solution.py:37
  23.9 1.2 collective-permute-start.5
  25.1 2.2 %collective-permute-start.6 = (bf16[128,1024]{1,0:T(8,128)(2,1)}, bf16[128,1024]{1,0:T(8,128)(2,1)S(1)}, u32[]{:S(2)}, u32[]{:S(2)}) collective-permute-start(bf16[128,1024]{1,0:T(8,128)(2,1)} %get-tuple-element.31), channel_id=1, source_target_pairs={{0,6},{2,4},{4,2},{6,0},{1,7},{3,5},{5,3},{7,1},{8,14},{10,12},{12... | collective-permute-start | bytes 786440 | tf_op jit(solution)/shard_map/ppermute | solution.py:29
  27.3 9.9 %shard_map.98 = (bf16[512,1024]{1,0:T(8,128)(2,1)}, bf16[512,1024]{1,0:T(8,128)(2,1)}) custom-call(bf16[128,1024]{1,0:T(8,128)(2,1)} %get-tuple-element.27.refs_0_.refs_1_, s32[3]{0:T(128)} %pad_add_fusion.refs_0_.refs_1_.refs_2_, s32[16,128]{1,0:T(8,128)} %refs_2_.3, bf16[1024,2048]{1,0:T(8,128)(2,1)} %refs_3_.3, bf16[2048,2048]{1,0:T(8,128)(2,1)} %refs_4_.4, ...), custom_call_target="tpu_custom_call" | custom-call | flops 49999998976 | bytes 1024 | tf_op jit(solution)/shard_map/pallas_call | solution.py:37
  37.2 1.2 collective-permute-start.8
  39.1 2.1 %shard_map.99.refs_0_.refs_2_.refs_11_ = bf16[512,1024]{1,0:T(8,128)(2,1)} custom-call(bf16[512,1024]{1,0:T(8,128)(2,1)} %get-tuple-element.28.refs_0_.refs_1_, bf16[128,1024]{1,0:T(8,128)(2,1)} %refs_1_.3, bf16[128,1024]{1,0:T(8,128)(2,1)} %copy-done.3, bf16[64,1024]{1,0:T(8,128)(2,1)} %copy-done.8, bf16[64,1024]{1,0:T(8,128)(2,1)} %copy-done.9, ...), custom_call_target="tpu_custom_call" | custom-call | flops 10000000 | bytes 1024 | tf_op jit(solution)/shard_map/pallas_call | solution.py:37
  42.7 2.0 shard_map.100
  44.7 1.3 collective-permute-start.9
  46.2 2.4 %shard_map.101 = (bf16[128,1024]{1,0:T(8,128)(2,1)}, bf16[128,1024]{1,0:T(8,128)(2,1)}, bf16[128,1024]{1,0:T(8,128)(2,1)}, bf16[128,1024]{1,0:T(8,128)(2,1)}) custom-call(bf16[64,1024]{1,0:T(8,128)(2,1)} %get-tuple-element.33.refs_0_.refs_2_, bf16[512,1024]{1,0:T(8,128)(2,1)} %get-tuple-element.28.refs_0_.refs_1_, ...), custom_call_target="tpu_custom_call" | custom-call | flops 10000000 | bytes 1024 | tf_op jit(solution)/shard_map/pallas_call | solution.py:37
  48.6 1.3 collective-permute-start.11
  49.9 2.2 %collective-permute-start.12 = (bf16[128,1024]{1,0:T(8,128)(2,1)}, bf16[128,1024]{1,0:T(8,128)(2,1)}, u32[]{:S(2)}, u32[]{:S(2)}) collective-permute-start(bf16[128,1024]{1,0:T(8,128)(2,1)} %get-tuple-element.38), channel_id=1, source_target_pairs={{0,6},{2,4},{4,2},{6,0},{1,7},{3,5},{5,3},{7,1},{8,14},{10,12},{12... | collective-permute-start | bytes 786440 | tf_op jit(solution)/shard_map/ppermute | solution.py:29
  52.8 1.7 shard_map.102.refs_0_.refs_3_
  54.8 5.5 %shard_map.103.refs_0_.refs_11_ = bf16[1024,1024]{1,0:T(8,128)(2,1)} custom-call(bf16[128,1024]{1,0:T(8,128)(2,1)} %shard_map.102.refs_0_.refs_3_, s32[3]{0:T(128)} %pad_add_fusion.refs_0_.refs_1_.refs_2_, bf16[512,1024]{1,0:T(8,128)(2,1)} %shard_map.99.refs_0_.refs_2_.refs_11_, bf16[512,1024]{1,0:T(8,128)(2,1)} %collective-permute-done.10.refs_3_.refs_12_, ...), custom_call_target="tpu_custom_call" | custom-call | flops 49999998976 | bytes 1024 | tf_op jit(solution)/shard_map/pallas_call | solution.py:37
  60.4 2.3 %collective-permute-start.24 = (bf16[128,1024]{1,0:T(8,128)(2,1)S(1)}, bf16[128,1024]{1,0:T(8,128)(2,1)S(1)}, u32[]{:S(2)}, u32[]{:S(2)}) collective-permute-start(bf16[128,1024]{1,0:T(8,128)(2,1)S(1)} %copy-done.6), channel_id=1, source_target_pairs={{0,6},{2,4},{4,2},{6,0},{1,7},{3,5},{5,3},{7,1},{8,14},{10,12},{12... | collective-permute-start | bytes 786440 | tf_op jit(solution)/shard_map/ppermute | solution.py:29
  63.3 2.0 shard_map.104
  65.3 1.3 collective-permute-start.14
  66.7 5.4 %collective-permute-done.22.refs_1_.refs_13_ = bf16[512,1024]{1,0:T(8,128)(2,1)} collective-permute-done((bf16[512,1024]{1,0:T(8,128)(2,1)S(1)}, bf16[512,1024]{1,0:T(8,128)(2,1)}, u32[]{:S(2)}, u32[]{:S(2)}) %collective-permute-start.22) | collective-permute-done | bytes 1048608 | tf_op jit(solution)/shard_map/ppermute | solution.py:29
  72.1 2.3 %collective-permute-start.26 = (bf16[128,1024]{1,0:T(8,128)(2,1)S(1)}, bf16[128,1024]{1,0:T(8,128)(2,1)}, u32[]{:S(2)}, u32[]{:S(2)}) collective-permute-start(bf16[128,1024]{1,0:T(8,128)(2,1)S(1)} %copy-done.6), channel_id=1, source_target_pairs={{0,1},{1,0},{2,3},{3,2},{4,5},{5,4},{6,7},{7,6},{8,9},{9,8},{10,11... | collective-permute-start | bytes 786440 | tf_op jit(solution)/shard_map/ppermute | solution.py:29
  74.5 2.5 %collective-permute-start.27 = (bf16[128,1024]{1,0:T(8,128)(2,1)S(1)}, bf16[128,1024]{1,0:T(8,128)(2,1)}, u32[]{:S(2)}, u32[]{:S(2)}) collective-permute-start(bf16[128,1024]{1,0:T(8,128)(2,1)S(1)} %collective-permute-done.23.refs_4_), channel_id=1, source_target_pairs={{0,1},{1,0},{2,3},{3,2},{4,5},{5,4},{6,7},{7,6},{8,9},{9,8},{10,11... | collective-permute-start | bytes 786440 | tf_op jit(solution)/shard_map/ppermute | solution.py:29
  77.8 1.7 shard_map.105.refs_0_.refs_2_
  80.2 2.0 collective-permute-start.18
  82.1 1.2 collective-permute-start.20
  83.3 5.9 %shard_map.106.refs_0_.refs_6_.refs_5_ = bf16[1024,1024]{1,0:T(8,128)(2,1)} custom-call(bf16[128,1024]{1,0:T(8,128)(2,1)} %shard_map.105.refs_0_.refs_2_, bf16[512,1024]{1,0:T(8,128)(2,1)} %collective-permute-done.22.refs_1_.refs_13_, s32[3]{0:T(128)} %pad_add_fusion.refs_0_.refs_1_.refs_2_, bf16[128,1024]{1,0:T(8,128)(2,1)} %shard_map.102.refs_0_.refs_3_, ...), custom_call_target="tpu_custom_call" | custom-call | flops 49999998976 | bytes 1024 | tf_op jit(solution)/shard_map/pallas_call | solution.py:37
  90.2 4.4 %collective-permute-start.19 = (bf16[128,1024]{1,0:T(8,128)(2,1)S(1)}, bf16[128,1024]{1,0:T(8,128)(2,1)}, u32[]{:S(2)}, u32[]{:S(2)}) collective-permute-start(bf16[128,1024]{1,0:T(8,128)(2,1)S(1)} %collective-permute-done.18.refs_4_), channel_id=1, source_target_pairs={{0,1},{1,0},{2,3},{3,2},{4,5},{5,4},{6,7},{7,6},{8,9},{9,8},{10,11... | collective-permute-start | bytes 786440 | tf_op jit(solution)/shard_map/ppermute | solution.py:29
  95.2 1.1 collective-permute-start.21
  97.9 4.4 %shard_map.108.refs_7_ = bf16[1024,1024]{1,0:T(8,128)(2,1)} custom-call(f32[8,128]{1,0:T(8,128)} %shard_map.107.refs_0_, s32[3]{0:T(128)} %pad_add_fusion.refs_0_.refs_1_.refs_2_, bf16[128,1024]{1,0:T(8,128)(2,1)} %shard_map.105.refs_0_.refs_2_, bf16[128,1024]{1,0:T(8,128)(2,1)} %copy-done.19, bf16[128,1024]{1,0:T(8,128)(2,1)} %copy-done.20, ...), custom_call_target="tpu_custom_call" | custom-call | flops 49999998976 | bytes 1024 | tf_op jit(solution)/shard_map/pallas_call | solution.py:288
  102.4 4.5 %shard_map.109 = bf16[1024,1024]{1,0:T(8,128)(2,1)} custom-call(s32[3]{0:T(128)} %pad_add_fusion.refs_0_.refs_1_.refs_2_, bf16[128,1024]{1,0:T(8,128)(2,1)} %collective-permute-done.15.refs_1_, bf16[128,1024]{1,0:T(8,128)(2,1)} %collective-permute-done.17.refs_2_, bf16[128,1024]{1,0:T(8,128)(2,1)} %collective-permute-done.19.refs_3_, ...), custom_call_target="tpu_custom_call", output_to_operand_aliasing={{}: (7, {})} | custom-call | flops 49999998976 | bytes 1024 | tf_op jit(solution)/shard_map/pallas_call | solution.py:288
  106.9 34.5 %all_to_all.5 = bf16[8,128,1024]{2,1,0:T(8,128)(2,1)S(1)} all-to-all(bf16[8,128,1024]{2,1,0:T(8,128)(2,1)} %bitcast.4), channel_id=1, replica_groups=mesh['grp'=2,'x'=4,'yh'=2,'z'=4,'core'=2] {'x','yh'}, dimensions={0} | all-to-all | bytes 4194304 | tf_op jit(solution)/shard_map/all_to_all | solution.py:569
  143.9 1.9 collective-permute-start.33
  145.8 1.5 collective-permute-start.38
  147.9 1.8 collective-permute-start.39
  149.6 1.5 collective-permute-done.33.refs_3_
  151.9 1.8 shard_map.110.refs_0_.refs_1_.refs_2_
  155.9 1.8 shard_map.111.refs_5_.refs_6_.refs_7_
  158.7 6.6 %collective-permute-done.34.refs_2_.refs_3_ = bf16[256,1024]{1,0:T(8,128)(2,1)S(1)} collective-permute-done((bf16[256,1024]{1,0:T(8,128)(2,1)}, bf16[256,1024]{1,0:T(8,128)(2,1)S(1)}, u32[]{:S(2)}, u32[]{:S(2)}) %collective-permute-start.34) | collective-permute-done | bytes 524320 | tf_op jit(solution)/shard_map/ppermute | solution.py:29
  167.7 1.9 collective-permute-done.40.refs_6_.refs_7_.refs_8_
  169.6 2.5 %collective-permute-done.35.refs_3_.refs_4_ = bf16[128,1024]{1,0:T(8,128)(2,1)} collective-permute-done((bf16[128,1024]{1,0:T(8,128)(2,1)S(1)}, bf16[128,1024]{1,0:T(8,128)(2,1)}, u32[]{:S(2)}, u32[]{:S(2)}) %collective-permute-start.35) | collective-permute-done | bytes 262176 | tf_op jit(solution)/shard_map/ppermute | solution.py:29
  172.1 4.5 %shard_map.112.refs_0_ = bf16[512,1024]{1,0:T(8,128)(2,1)} custom-call(s32[3]{0:T(128)} %pad_add_fusion.refs_0_.refs_1_.refs_2_, bf16[256,1024]{1,0:T(8,128)(2,1)} %shard_map.110.refs_0_.refs_1_.refs_2_, bf16[256,1024]{1,0:T(8,128)(2,1)} %copy-done.10, bf16[128,1024]{1,0:T(8,128)(2,1)} %collective-permute-done.35.refs_3_.refs_4_, ...), custom_call_target="tpu_custom_call" | custom-call | flops 49999998976 | bytes 1024 | tf_op jit(solution)/shard_map/pallas_call | solution.py:37
  176.7 5.8 %collective-permute-start.41 = (bf16[512,1024]{1,0:T(8,128)(2,1)}, bf16[512,1024]{1,0:T(8,128)(2,1)S(1)}, u32[]{:S(2)}, u32[]{:S(2)}) collective-permute-start(bf16[512,1024]{1,0:T(8,128)(2,1)} %shard_map.112.refs_0_), channel_id=1, source_target_pairs={{0,1},{1,0},{2,3},{3,2},{4,5},{5,4},{6,7},{7,6},{8,9},{9,8},{10,11... | collective-permute-start | bytes 3145736 | tf_op jit(solution)/shard_map/ppermute | solution.py:29
  182.5 4.6 %shard_map.113.refs_0_ = bf16[512,1024]{1,0:T(8,128)(2,1)} custom-call(bf16[512,1024]{1,0:T(8,128)(2,1)} %shard_map.112.refs_0_, s32[3]{0:T(128)} %pad_add_fusion.refs_0_.refs_1_.refs_2_, bf16[256,1024]{1,0:T(8,128)(2,1)} %shard_map.110.refs_0_.refs_1_.refs_2_, bf16[256,1024]{1,0:T(8,128)(2,1)} %copy-done.10, ...), custom_call_target="tpu_custom_call" | custom-call | flops 49999998976 | bytes 1024 | tf_op jit(solution)/shard_map/pallas_call | solution.py:37
  188.1 2.4 %shard_map.114 = (bf16[128,1024]{1,0:T(8,128)(2,1)}, bf16[128,1024]{1,0:T(8,128)(2,1)}, bf16[128,1024]{1,0:T(8,128)(2,1)}, bf16[128,1024]{1,0:T(8,128)(2,1)}) custom-call(bf16[512,1024]{1,0:T(8,128)(2,1)} %shard_map.113.refs_0_, bf16[512,1024]{1,0:T(8,128)(2,1)} %copy-done.2), custom_call_target="tpu_custom_call" | custom-call | flops 10000000 | bytes 1024 | tf_op jit(solution)/shard_map/pallas_call | solution.py:37
  193.2 9.4 %shard_map.115 = f32[1024,1024]{1,0:T(8,128)} custom-call(bf16[128,1024]{1,0:T(8,128)(2,1)} %get-tuple-element.42.refs_0_, s32[3]{0:T(128)} %pad_add_fusion.refs_0_.refs_1_.refs_2_, bf16[256,1024]{1,0:T(8,128)(2,1)} %shard_map.110.refs_0_.refs_1_.refs_2_, bf16[256,1024]{1,0:T(8,128)(2,1)} %copy-done.10, ...), custom_call_target="tpu_custom_call" | custom-call | flops 49999998976 | bytes 1024 | tf_op jit(solution)/shard_map/pallas_call | solution.py:37
  202.5 3.5 %collective-permute-done.43 = bf16[128,1024]{1,0:T(8,128)(2,1)S(1)} collective-permute-done((bf16[128,1024]{1,0:T(8,128)(2,1)}, bf16[128,1024]{1,0:T(8,128)(2,1)S(1)}, u32[]{:S(2)}, u32[]{:S(2)}) %collective-permute-start.43) | collective-permute-done | bytes 262176 | tf_op jit(solution)/shard_map/ppermute | solution.py:29
  (141 shorter events, 26.0 us)
Async XLA Ops:
  0.6 16.6 %collective-permute-start = (bf16[128,1024]{1,0:T(8,128)(2,1)}, bf16[128,1024]{1,0:T(8,128)(2,1)S(1)}, u32[]{:S(2)}, u32[]{:S(2)}) collective-permute-start(bf16[128,1024]{1,0:T(8,128)(2,1)} %refs_1_.3), channel_id=1, source_target_pairs={{0,2},{2,0},{4,6},{6,4},{1,3},{3,1},{5,7},{7,5},{8,10},{10,8},{12,... | collective-permute-start | bytes 786440 | tf_op jit(solution)/shard_map/ppermute | solution.py:29
  3.2 14.0 %collective-permute-start.1 = (bf16[128,1024]{1,0:T(8,128)(2,1)}, bf16[128,1024]{1,0:T(8,128)(2,1)S(1)}, u32[]{:S(2)}, u32[]{:S(2)}) collective-permute-start(bf16[128,1024]{1,0:T(8,128)(2,1)} %refs_1_.3), channel_id=1, source_target_pairs={{0,6},{2,4},{4,2},{6,0},{1,7},{3,5},{5,3},{7,1},{8,14},{10,12},{12... | collective-permute-start | bytes 786440 | tf_op jit(solution)/shard_map/ppermute | solution.py:29
  16.0 4.5 %collective-permute-start.2 = (bf16[512,1024]{1,0:T(8,128)(2,1)}, bf16[512,1024]{1,0:T(8,128)(2,1)S(1)}, u32[]{:S(2)}, u32[]{:S(2)}) collective-permute-start(bf16[512,1024]{1,0:T(8,128)(2,1)} %get-tuple-element.26), channel_id=1, source_target_pairs={{0,1},{1,0},{2,3},{3,2},{4,5},{5,4},{6,7},{7,6},{8,9},{9,8},{10,11... | collective-permute-start | bytes 3145736 | tf_op jit(solution)/shard_map/ppermute | solution.py:29
  19.7 17.5 %collective-permute-start.3 = (bf16[64,1024]{1,0:T(8,128)(2,1)}, bf16[64,1024]{1,0:T(8,128)(2,1)S(1)}, u32[]{:S(2)}, u32[]{:S(2)}) collective-permute-start(bf16[64,1024]{1,0:T(8,128)(2,1)} %get-tuple-element.25.refs_0_), channel_id=1, source_target_pairs={{0,6},{2,4},{4,2},{6,0},{1,7},{3,5},{5,3},{7,1},{8,14},{10,12},{12... | collective-permute-start | bytes 393224 | tf_op jit(solution)/shard_map/ppermute | solution.py:29
  20.1 18.3 %collective-permute-start.4 = (bf16[64,1024]{1,0:T(8,128)(2,1)}, bf16[64,1024]{1,0:T(8,128)(2,1)S(1)}, u32[]{:S(2)}, u32[]{:S(2)}) collective-permute-start(bf16[64,1024]{1,0:T(8,128)(2,1)} %get-tuple-element.29), channel_id=1, source_target_pairs={{0,2},{2,0},{4,6},{6,4},{1,3},{3,1},{5,7},{7,5},{8,10},{10,8},{12,... | collective-permute-start | bytes 393224 | tf_op jit(solution)/shard_map/ppermute | solution.py:29
  23.9 17.3 %collective-permute-start.5 = (bf16[128,1024]{1,0:T(8,128)(2,1)}, bf16[128,1024]{1,0:T(8,128)(2,1)S(1)}, u32[]{:S(2)}, u32[]{:S(2)}) collective-permute-start(bf16[128,1024]{1,0:T(8,128)(2,1)} %get-tuple-element.30), channel_id=1, source_target_pairs={{0,2},{2,0},{4,6},{6,4},{1,3},{3,1},{5,7},{7,5},{8,10},{10,8},{12,... | collective-permute-start | bytes 786440 | tf_op jit(solution)/shard_map/ppermute | solution.py:29
  25.1 16.2 %collective-permute-start.6 = (bf16[128,1024]{1,0:T(8,128)(2,1)}, bf16[128,1024]{1,0:T(8,128)(2,1)S(1)}, u32[]{:S(2)}, u32[]{:S(2)}) collective-permute-start(bf16[128,1024]{1,0:T(8,128)(2,1)} %get-tuple-element.31), channel_id=1, source_target_pairs={{0,6},{2,4},{4,2},{6,0},{1,7},{3,5},{5,3},{7,1},{8,14},{10,12},{12... | collective-permute-start | bytes 786440 | tf_op jit(solution)/shard_map/ppermute | solution.py:29
  27.3 14.0 %collective-permute-start.7 = (bf16[128,1024]{1,0:T(8,128)(2,1)}, bf16[128,1024]{1,0:T(8,128)(2,1)S(1)}, u32[]{:S(2)}, u32[]{:S(2)}) collective-permute-start(bf16[128,1024]{1,0:T(8,128)(2,1)} %get-tuple-element.32), channel_id=1, source_target_pairs={{0,4},{2,6},{4,0},{6,2},{1,5},{3,7},{5,1},{7,3},{8,12},{10,14},{12... | collective-permute-start | bytes 786440 | tf_op jit(solution)/shard_map/ppermute | solution.py:29
  37.2 9.0 %collective-permute-start.8 = (bf16[512,1024]{1,0:T(8,128)(2,1)}, bf16[512,1024]{1,0:T(8,128)(2,1)}, u32[]{:S(2)}, u32[]{:S(2)}) collective-permute-start(bf16[512,1024]{1,0:T(8,128)(2,1)} %get-tuple-element.34), channel_id=1, source_target_pairs={{0,1},{1,0},{2,3},{3,2},{4,5},{5,4},{6,7},{7,6},{8,9},{9,8},{10,11... | collective-permute-start | bytes 3145736 | tf_op jit(solution)/shard_map/ppermute | solution.py:29
  41.2 13.3 %collective-permute-start.10 = (bf16[512,1024]{1,0:T(8,128)(2,1)}, bf16[512,1024]{1,0:T(8,128)(2,1)}, u32[]{:S(2)}, u32[]{:S(2)}) collective-permute-start(bf16[512,1024]{1,0:T(8,128)(2,1)} %shard_map.99.refs_0_.refs_2_.refs_11_), channel_id=1, source_target_pairs={{0,1},{1,0},{2,3},{3,2},{4,5},{5,4},{6,7},{7,6},{8,9},{9,8},{10,11... | collective-permute-start | bytes 3145736 | tf_op jit(solution)/shard_map/ppermute | solution.py:29
  44.7 7.4 %collective-permute-start.9 = (bf16[64,1024]{1,0:T(8,128)(2,1)}, bf16[64,1024]{1,0:T(8,128)(2,1)S(1)}, u32[]{:S(2)}, u32[]{:S(2)}) collective-permute-start(bf16[64,1024]{1,0:T(8,128)(2,1)} %get-tuple-element.36), channel_id=1, source_target_pairs={{0,64},{64,0},{1,65},{65,1},{2,66},{66,2},{3,67},{67,3},{4,68},{68... | collective-permute-start | bytes 393224 | tf_op jit(solution)/shard_map/ppermute | solution.py:29
  46.0 26.1 %collective-permute-start.22 = (bf16[512,1024]{1,0:T(8,128)(2,1)S(1)}, bf16[512,1024]{1,0:T(8,128)(2,1)}, u32[]{:S(2)}, u32[]{:S(2)}) collective-permute-start(bf16[512,1024]{1,0:T(8,128)(2,1)S(1)} %copy-done), channel_id=1, source_target_pairs={{0,64},{64,0},{1,65},{65,1},{2,66},{66,2},{3,67},{67,3},{4,68},{68... | collective-permute-start | bytes 3145736 | tf_op jit(solution)/shard_map/ppermute | solution.py:29
  48.6 11.8 %collective-permute-start.11 = (bf16[128,1024]{1,0:T(8,128)(2,1)}, bf16[128,1024]{1,0:T(8,128)(2,1)}, u32[]{:S(2)}, u32[]{:S(2)}) collective-permute-start(bf16[128,1024]{1,0:T(8,128)(2,1)} %get-tuple-element.37), channel_id=1, source_target_pairs={{0,2},{2,0},{4,6},{6,4},{1,3},{3,1},{5,7},{7,5},{8,10},{10,8},{12,... | collective-permute-start | bytes 786440 | tf_op jit(solution)/shard_map/ppermute | solution.py:29
  49.9 12.8 %collective-permute-start.12 = (bf16[128,1024]{1,0:T(8,128)(2,1)}, bf16[128,1024]{1,0:T(8,128)(2,1)}, u32[]{:S(2)}, u32[]{:S(2)}) collective-permute-start(bf16[128,1024]{1,0:T(8,128)(2,1)} %get-tuple-element.38), channel_id=1, source_target_pairs={{0,6},{2,4},{4,2},{6,0},{1,7},{3,5},{5,3},{7,1},{8,14},{10,12},{12... | collective-permute-start | bytes 786440 | tf_op jit(solution)/shard_map/ppermute | solution.py:29
  52.1 11.2 %collective-permute-start.13 = (bf16[128,1024]{1,0:T(8,128)(2,1)}, bf16[128,1024]{1,0:T(8,128)(2,1)}, u32[]{:S(2)}, u32[]{:S(2)}) collective-permute-start(bf16[128,1024]{1,0:T(8,128)(2,1)} %get-tuple-element.39), channel_id=1, source_target_pairs={{0,4},{2,6},{4,0},{6,2},{1,5},{3,7},{5,1},{7,3},{8,12},{10,14},{12... | collective-permute-start | bytes 786440 | tf_op jit(solution)/shard_map/ppermute | solution.py:29
  54.5 19.9 %collective-permute-start.23 = (bf16[128,1024]{1,0:T(8,128)(2,1)}, bf16[128,1024]{1,0:T(8,128)(2,1)S(1)}, u32[]{:S(2)}, u32[]{:S(2)}) collective-permute-start(bf16[128,1024]{1,0:T(8,128)(2,1)} %shard_map.102.refs_0_.refs_3_), channel_id=1, source_target_pairs={{0,2},{2,0},{4,6},{6,4},{1,3},{3,1},{5,7},{7,5},{8,10},{10,8},{12,... | collective-permute-start | bytes 786440 | tf_op jit(solution)/shard_map/ppermute | solution.py:29
  60.4 14.1 %collective-permute-start.24 = (bf16[128,1024]{1,0:T(8,128)(2,1)S(1)}, bf16[128,1024]{1,0:T(8,128)(2,1)S(1)}, u32[]{:S(2)}, u32[]{:S(2)}) collective-permute-start(bf16[128,1024]{1,0:T(8,128)(2,1)S(1)} %copy-done.6), channel_id=1, source_target_pairs={{0,6},{2,4},{4,2},{6,0},{1,7},{3,5},{5,3},{7,1},{8,14},{10,12},{12... | collective-permute-start | bytes 786440 | tf_op jit(solution)/shard_map/ppermute | solution.py:29
  62.7 14.3 %collective-permute-start.25 = (bf16[128,1024]{1,0:T(8,128)(2,1)S(1)}, bf16[128,1024]{1,0:T(8,128)(2,1)}, u32[]{:S(2)}, u32[]{:S(2)}) collective-permute-start(bf16[128,1024]{1,0:T(8,128)(2,1)S(1)} %copy-done.6), channel_id=1, source_target_pairs={{0,4},{2,6},{4,0},{6,2},{1,5},{3,7},{5,1},{7,3},{8,12},{10,14},{12... | collective-permute-start | bytes 786440 | tf_op jit(solution)/shard_map/ppermute | solution.py:29
  65.3 11.9 %collective-permute-start.14 = (bf16[64,1024]{1,0:T(8,128)(2,1)}, bf16[64,1024]{1,0:T(8,128)(2,1)S(1)}, u32[]{:S(2)}, u32[]{:S(2)}) collective-permute-start(bf16[64,1024]{1,0:T(8,128)(2,1)} %get-tuple-element.41), channel_id=1, source_target_pairs={{0,64},{64,0},{1,65},{65,1},{2,66},{66,2},{3,67},{67,3},{4,68},{68... | collective-permute-start | bytes 393224 | tf_op jit(solution)/shard_map/ppermute | solution.py:29
  72.1 7.5 %collective-permute-start.26 = (bf16[128,1024]{1,0:T(8,128)(2,1)S(1)}, bf16[128,1024]{1,0:T(8,128)(2,1)}, u32[]{:S(2)}, u32[]{:S(2)}) collective-permute-start(bf16[128,1024]{1,0:T(8,128)(2,1)S(1)} %copy-done.6), channel_id=1, source_target_pairs={{0,1},{1,0},{2,3},{3,2},{4,5},{5,4},{6,7},{7,6},{8,9},{9,8},{10,11... | collective-permute-start | bytes 786440 | tf_op jit(solution)/shard_map/ppermute | solution.py:29
  74.4 22.0 %collective-permute-start.30 = (bf16[512,1024]{1,0:T(8,128)(2,1)}, bf16[512,1024]{1,0:T(8,128)(2,1)S(1)}, u32[]{:S(2)}, u32[]{:S(2)}) collective-permute-start(bf16[512,1024]{1,0:T(8,128)(2,1)} %collective-permute-done.22.refs_1_.refs_13_), channel_id=1, source_target_pairs={{0,1},{1,0},{2,3},{3,2},{4,5},{5,4},{6,7},{7,6},{8,9},{9,8},{10,11... | collective-permute-start | bytes 3145736 | tf_op jit(solution)/shard_map/ppermute | solution.py:29
  74.5 5.4 %collective-permute-start.27 = (bf16[128,1024]{1,0:T(8,128)(2,1)S(1)}, bf16[128,1024]{1,0:T(8,128)(2,1)}, u32[]{:S(2)}, u32[]{:S(2)}) collective-permute-start(bf16[128,1024]{1,0:T(8,128)(2,1)S(1)} %collective-permute-done.23.refs_4_), channel_id=1, source_target_pairs={{0,1},{1,0},{2,3},{3,2},{4,5},{5,4},{6,7},{7,6},{8,9},{9,8},{10,11... | collective-permute-start | bytes 786440 | tf_op jit(solution)/shard_map/ppermute | solution.py:29
  76.9 3.2 %collective-permute-start.28 = (bf16[128,1024]{1,0:T(8,128)(2,1)S(1)}, bf16[128,1024]{1,0:T(8,128)(2,1)}, u32[]{:S(2)}, u32[]{:S(2)}) collective-permute-start(bf16[128,1024]{1,0:T(8,128)(2,1)S(1)} %collective-permute-done.24.refs_5_), channel_id=1, source_target_pairs={{0,1},{1,0},{2,3},{3,2},{4,5},{5,4},{6,7},{7,6},{8,9},{9,8},{10,11... | collective-permute-start | bytes 786440 | tf_op jit(solution)/shard_map/ppermute | solution.py:29
  77.2 4.9 %collective-permute-start.29 = (bf16[128,1024]{1,0:T(8,128)(2,1)}, bf16[128,1024]{1,0:T(8,128)(2,1)}, u32[]{:S(2)}, u32[]{:S(2)}) collective-permute-start(bf16[128,1024]{1,0:T(8,128)(2,1)} %collective-permute-done.25.refs_6_), channel_id=1, source_target_pairs={{0,1},{1,0},{2,3},{3,2},{4,5},{5,4},{6,7},{7,6},{8,9},{9,8},{10,11... | collective-permute-start | bytes 786440 | tf_op jit(solution)/shard_map/ppermute | solution.py:29
  79.6 22.8 %collective-permute-start.15 = (bf16[128,1024]{1,0:T(8,128)(2,1)}, bf16[128,1024]{1,0:T(8,128)(2,1)}, u32[]{:S(2)}, u32[]{:S(2)}) collective-permute-start(bf16[128,1024]{1,0:T(8,128)(2,1)} %shard_map.105.refs_0_.refs_2_), channel_id=1, source_target_pairs={{0,1},{1,0},{2,3},{3,2},{4,5},{5,4},{6,7},{7,6},{8,9},{9,8},{10,11... | collective-permute-start | bytes 786440 | tf_op jit(solution)/shard_map/ppermute | solution.py:29
  79.9 9.3 %collective-permute-start.16 = (bf16[128,1024]{1,0:T(8,128)(2,1)}, bf16[128,1024]{1,0:T(8,128)(2,1)S(1)}, u32[]{:S(2)}, u32[]{:S(2)}) collective-permute-start(bf16[128,1024]{1,0:T(8,128)(2,1)} %shard_map.105.refs_0_.refs_2_), channel_id=1, source_target_pairs={{0,2},{2,0},{4,6},{6,4},{1,3},{3,1},{5,7},{7,5},{8,10},{10,8},{12,... | collective-permute-start | bytes 786440 | tf_op jit(solution)/shard_map/ppermute | solution.py:29
  80.2 10.1 %collective-permute-start.18 = (bf16[128,1024]{1,0:T(8,128)(2,1)}, bf16[128,1024]{1,0:T(8,128)(2,1)S(1)}, u32[]{:S(2)}, u32[]{:S(2)}) collective-permute-start(bf16[128,1024]{1,0:T(8,128)(2,1)} %shard_map.105.refs_0_.refs_2_), channel_id=1, source_target_pairs={{0,6},{2,4},{4,2},{6,0},{1,7},{3,5},{5,3},{7,1},{8,14},{10,12},{12... | collective-permute-start | bytes 786440 | tf_op jit(solution)/shard_map/ppermute | solution.py:29
  82.1 13.1 %collective-permute-start.20 = (bf16[128,1024]{1,0:T(8,128)(2,1)}, bf16[128,1024]{1,0:T(8,128)(2,1)S(1)}, u32[]{:S(2)}, u32[]{:S(2)}) collective-permute-start(bf16[128,1024]{1,0:T(8,128)(2,1)} %shard_map.105.refs_0_.refs_2_), channel_id=1, source_target_pairs={{0,4},{2,6},{4,0},{6,2},{1,5},{3,7},{5,1},{7,3},{8,12},{10,14},{12... | collective-permute-start | bytes 786440 | tf_op jit(solution)/shard_map/ppermute | solution.py:29
  89.2 13.1 %collective-permute-start.17 = (bf16[128,1024]{1,0:T(8,128)(2,1)S(1)}, bf16[128,1024]{1,0:T(8,128)(2,1)}, u32[]{:S(2)}, u32[]{:S(2)}) collective-permute-start(bf16[128,1024]{1,0:T(8,128)(2,1)S(1)} %collective-permute-done.16.refs_3_), channel_id=1, source_target_pairs={{0,1},{1,0},{2,3},{3,2},{4,5},{5,4},{6,7},{7,6},{8,9},{9,8},{10,11... | collective-permute-start | bytes 786440 | tf_op jit(solution)/shard_map/ppermute | solution.py:29
  90.2 12.1 %collective-permute-start.19 = (bf16[128,1024]{1,0:T(8,128)(2,1)S(1)}, bf16[128,1024]{1,0:T(8,128)(2,1)}, u32[]{:S(2)}, u32[]{:S(2)}) collective-permute-start(bf16[128,1024]{1,0:T(8,128)(2,1)S(1)} %collective-permute-done.18.refs_4_), channel_id=1, source_target_pairs={{0,1},{1,0},{2,3},{3,2},{4,5},{5,4},{6,7},{7,6},{8,9},{9,8},{10,11... | collective-permute-start | bytes 786440 | tf_op jit(solution)/shard_map/ppermute | solution.py:29
  95.2 7.1 %collective-permute-start.21 = (bf16[128,1024]{1,0:T(8,128)(2,1)S(1)}, bf16[128,1024]{1,0:T(8,128)(2,1)}, u32[]{:S(2)}, u32[]{:S(2)}) collective-permute-start(bf16[128,1024]{1,0:T(8,128)(2,1)S(1)} %collective-permute-done.20.refs_5_), channel_id=1, source_target_pairs={{0,1},{1,0},{2,3},{3,2},{4,5},{5,4},{6,7},{7,6},{8,9},{9,8},{10,11... | collective-permute-start | bytes 786440 | tf_op jit(solution)/shard_map/ppermute | solution.py:29
  142.4 5.4 %collective-permute-start.31 = (bf16[64,1024]{1,0:T(8,128)(2,1)S(1)}, bf16[64,1024]{1,0:T(8,128)(2,1)S(1)}, u32[]{:S(2)}, u32[]{:S(2)}) collective-permute-start(bf16[64,1024]{1,0:T(8,128)(2,1)S(1)} %get-tuple-element.47.refs_0_), channel_id=1, source_target_pairs={{0,8},{8,0},{64,72},{72,64},{1,9},{9,1},{65,73},{73,65},{2,10},{10... | collective-permute-start | bytes 393224 | tf_op jit(solution)/shard_map/ppermute | solution.py:29
  143.5 6.1 %collective-permute-start.32 = (bf16[64,1024]{1,0:T(8,128)(2,1)S(1)}, bf16[64,1024]{1,0:T(8,128)(2,1)S(1)}, u32[]{:S(2)}, u32[]{:S(2)}) collective-permute-start(bf16[64,1024]{1,0:T(8,128)(2,1)S(1)} %get-tuple-element.47.refs_0_), channel_id=1, source_target_pairs={{0,64},{8,72},{64,0},{72,8},{1,65},{9,73},{65,1},{73,9},{2,66},{10... | collective-permute-start | bytes 393224 | tf_op jit(solution)/shard_map/ppermute | solution.py:29
  143.9 7.3 %collective-permute-start.33 = (bf16[64,1024]{1,0:T(8,128)(2,1)S(1)}, bf16[64,1024]{1,0:T(8,128)(2,1)S(1)}, u32[]{:S(2)}, u32[]{:S(2)}) collective-permute-start(bf16[64,1024]{1,0:T(8,128)(2,1)S(1)} %get-tuple-element.47.refs_0_), channel_id=1, source_target_pairs={{0,72},{8,64},{64,8},{72,0},{1,73},{9,65},{65,9},{73,1},{2,74},{10... | collective-permute-start | bytes 393224 | tf_op jit(solution)/shard_map/ppermute | solution.py:29
  145.8 8.8 %collective-permute-start.37 = (bf16[64,1024]{1,0:T(8,128)(2,1)S(1)}, bf16[64,1024]{1,0:T(8,128)(2,1)S(1)}, u32[]{:S(2)}, u32[]{:S(2)}) collective-permute-start(bf16[64,1024]{1,0:T(8,128)(2,1)S(1)} %get-tuple-element.46.refs_1_), channel_id=1, source_target_pairs={{0,16},{16,0},{32,48},{48,32},{1,17},{17,1},{33,49},{49,33},{2,18}... | collective-permute-start | bytes 393224 | tf_op jit(solution)/shard_map/ppermute | solution.py:29
  145.8 8.8 %collective-permute-start.38 = (bf16[64,1024]{1,0:T(8,128)(2,1)S(1)}, bf16[64,1024]{1,0:T(8,128)(2,1)S(1)}, u32[]{:S(2)}, u32[]{:S(2)}) collective-permute-start(bf16[64,1024]{1,0:T(8,128)(2,1)S(1)} %get-tuple-element.46.refs_1_), channel_id=1, source_target_pairs={{0,32},{16,48},{32,0},{48,16},{1,33},{17,49},{33,1},{49,17},{2,34}... | collective-permute-start | bytes 393224 | tf_op jit(solution)/shard_map/ppermute | solution.py:29
  147.9 6.7 %collective-permute-start.39 = (bf16[64,1024]{1,0:T(8,128)(2,1)S(1)}, bf16[64,1024]{1,0:T(8,128)(2,1)S(1)}, u32[]{:S(2)}, u32[]{:S(2)}) collective-permute-start(bf16[64,1024]{1,0:T(8,128)(2,1)S(1)} %get-tuple-element.46.refs_1_), channel_id=1, source_target_pairs={{0,48},{16,32},{32,16},{48,0},{1,49},{17,33},{33,17},{49,1},{2,50}... | collective-permute-start | bytes 393224 | tf_op jit(solution)/shard_map/ppermute | solution.py:29
  153.7 11.7 %collective-permute-start.34 = (bf16[256,1024]{1,0:T(8,128)(2,1)}, bf16[256,1024]{1,0:T(8,128)(2,1)S(1)}, u32[]{:S(2)}, u32[]{:S(2)}) collective-permute-start(bf16[256,1024]{1,0:T(8,128)(2,1)} %shard_map.110.refs_0_.refs_1_.refs_2_), channel_id=1, source_target_pairs={{0,16},{16,0},{32,48},{48,32},{1,17},{17,1},{33,49},{49,33},{2,18}... | collective-permute-start | bytes 1572872 | tf_op jit(solution)/shard_map/ppermute | solution.py:29
  153.9 13.4 %collective-permute-start.36 = (bf16[256,1024]{1,0:T(8,128)(2,1)}, bf16[256,1024]{1,0:T(8,128)(2,1)S(1)}, u32[]{:S(2)}, u32[]{:S(2)}) collective-permute-start(bf16[256,1024]{1,0:T(8,128)(2,1)} %shard_map.110.refs_0_.refs_1_.refs_2_), channel_id=1, source_target_pairs={{0,48},{16,32},{32,16},{48,0},{1,49},{17,33},{33,17},{49,1},{2,50}... | collective-permute-start | bytes 1572872 | tf_op jit(solution)/shard_map/ppermute | solution.py:29
  157.7 11.9 %collective-permute-start.40 = (bf16[256,1024]{1,0:T(8,128)(2,1)}, bf16[256,1024]{1,0:T(8,128)(2,1)S(1)}, u32[]{:S(2)}, u32[]{:S(2)}) collective-permute-start(bf16[256,1024]{1,0:T(8,128)(2,1)} %shard_map.111.refs_5_.refs_6_.refs_7_), channel_id=1, source_target_pairs={{0,8},{8,0},{64,72},{72,64},{1,9},{9,1},{65,73},{73,65},{2,10},{10... | collective-permute-start | bytes 1572872 | tf_op jit(solution)/shard_map/ppermute | solution.py:29
  165.3 6.8 %collective-permute-start.35 = (bf16[128,1024]{1,0:T(8,128)(2,1)S(1)}, bf16[128,1024]{1,0:T(8,128)(2,1)}, u32[]{:S(2)}, u32[]{:S(2)}) collective-permute-start(bf16[128,1024]{1,0:T(8,128)(2,1)S(1)} %slice.17), channel_id=1, source_target_pairs={{0,48},{16,32},{32,16},{48,0},{1,49},{17,33},{33,17},{49,1},{2,50}... | collective-permute-start | bytes 786440 | tf_op jit(solution)/shard_map/ppermute | solution.py:29
  165.4 26.7 %collective-permute-start.46 = (bf16[256,1024]{1,0:T(8,128)(2,1)}, bf16[256,1024]{1,0:T(8,128)(2,1)}, u32[]{:S(2)}, u32[]{:S(2)}) collective-permute-start(bf16[256,1024]{1,0:T(8,128)(2,1)} %shard_map.111.refs_5_.refs_6_.refs_7_), channel_id=1, source_target_pairs={{0,64},{8,72},{64,0},{72,8},{1,65},{9,73},{65,1},{73,9},{2,66},{10... | collective-permute-start | bytes 1572872 | tf_op jit(solution)/shard_map/ppermute | solution.py:29
  166.4 26.7 %collective-permute-start.47 = (bf16[256,1024]{1,0:T(8,128)(2,1)}, bf16[256,1024]{1,0:T(8,128)(2,1)}, u32[]{:S(2)}, u32[]{:S(2)}) collective-permute-start(bf16[256,1024]{1,0:T(8,128)(2,1)} %shard_map.111.refs_5_.refs_6_.refs_7_), channel_id=1, source_target_pairs={{0,72},{8,64},{64,8},{72,0},{1,73},{9,65},{65,9},{73,1},{2,74},{10... | collective-permute-start | bytes 1572872 | tf_op jit(solution)/shard_map/ppermute | solution.py:29
  167.4 25.7 %collective-permute-start.45 = (bf16[128,1024]{1,0:T(8,128)(2,1)S(1)}, bf16[128,1024]{1,0:T(8,128)(2,1)}, u32[]{:S(2)}, u32[]{:S(2)}) collective-permute-start(bf16[128,1024]{1,0:T(8,128)(2,1)S(1)} %slice.19), channel_id=1, source_target_pairs={{0,16},{16,0},{32,48},{48,32},{1,17},{17,1},{33,49},{49,33},{2,18}... | collective-permute-start | bytes 786440 | tf_op jit(solution)/shard_map/ppermute | solution.py:29
  176.7 10.4 %collective-permute-start.41 = (bf16[512,1024]{1,0:T(8,128)(2,1)}, bf16[512,1024]{1,0:T(8,128)(2,1)S(1)}, u32[]{:S(2)}, u32[]{:S(2)}) collective-permute-start(bf16[512,1024]{1,0:T(8,128)(2,1)} %shard_map.112.refs_0_), channel_id=1, source_target_pairs={{0,1},{1,0},{2,3},{3,2},{4,5},{5,4},{6,7},{7,6},{8,9},{9,8},{10,11... | collective-permute-start | bytes 3145736 | tf_op jit(solution)/shard_map/ppermute | solution.py:29
  190.5 12.0 %collective-permute-start.44 = (bf16[128,1024]{1,0:T(8,128)(2,1)}, bf16[128,1024]{1,0:T(8,128)(2,1)S(1)}, u32[]{:S(2)}, u32[]{:S(2)}) collective-permute-start(bf16[128,1024]{1,0:T(8,128)(2,1)} %get-tuple-element.45), channel_id=1, source_target_pairs={{0,4},{2,6},{4,0},{6,2},{1,5},{3,7},{5,1},{7,3},{8,12},{10,14},{12... | collective-permute-start | bytes 786440 | tf_op jit(solution)/shard_map/ppermute | solution.py:29
  191.5 14.6 %collective-permute-start.43 = (bf16[128,1024]{1,0:T(8,128)(2,1)}, bf16[128,1024]{1,0:T(8,128)(2,1)S(1)}, u32[]{:S(2)}, u32[]{:S(2)}) collective-permute-start(bf16[128,1024]{1,0:T(8,128)(2,1)} %get-tuple-element.44), channel_id=1, source_target_pairs={{0,6},{2,4},{4,2},{6,0},{1,7},{3,5},{5,3},{7,1},{8,14},{10,12},{12... | collective-permute-start | bytes 786440 | tf_op jit(solution)/shard_map/ppermute | solution.py:29
  192.1 14.0 %collective-permute-start.42 = (bf16[128,1024]{1,0:T(8,128)(2,1)}, bf16[128,1024]{1,0:T(8,128)(2,1)S(1)}, u32[]{:S(2)}, u32[]{:S(2)}) collective-permute-start(bf16[128,1024]{1,0:T(8,128)(2,1)} %get-tuple-element.43), channel_id=1, source_target_pairs={{0,2},{2,0},{4,6},{6,4},{1,3},{3,1},{5,7},{7,5},{8,10},{10,8},{12,... | collective-permute-start | bytes 786440 | tf_op jit(solution)/shard_map/ppermute | solution.py:29
  (32 other events, 105.3 us)

commit v7 on v5

--- a/solution.py
+++ b/solution.py
@@ -27,6 +27,11 @@
     names = axes if isinstance(axes, tuple) else (axes,)
     size = math.prod(SIZES[name] for name in names)
     return lax.ppermute(array, axes, [(i, i ^ distance) for i in range(size)])
+
+
+def z_swaps(part):
+    two = swap(part(2), Z, 2)
+    return [swap(part(1), Z, 1), swap(part(3), Z, 3), two]
 
 
 def params():
@@ -511,7 +516,7 @@
 
 
 def gather_tensor(block, after=()):
-    across = [swap(block, Z, k) for k in (1, 3, 2)]
+    across = z_swaps(lambda k: block)
     arrays = [block, *across, swap(block, CORE, 1)]
     places = [(0, 0, 0), (2, 1, 0), (6, 2, 0), (4, 3, 0), (1, 4, 0)]
     if after:
@@ -545,12 +550,12 @@
     mine, peer = teacher(*taught, 0)
     halves = halved(*across, (mine,), LONG)
     early = merged((mine, swap(peer, CORE, 1)), 4, halves[:1])
-    moved = [swap(early[k], Z, k) for k in (1, 3, 2)]
+    moved = z_swaps(lambda k: early[k])
     mine, peer = teacher(*taught, 1, (early[0],))
     near = joined((student_values, across[0], *far_ring(halves, Z, 1, 3), across[1]), (mine,), SHORT)
     keep, give = merged((early[0], *moved), 2, (near,), LONG)
     late = merged((mine, swap(peer, CORE, 1)), 4, (keep,))
-    moved = [swap(late[k], Z, k) for k in (1, 3, 2)]
+    moved = z_swaps(lambda k: late[k])
     first = placed(ids, keep, swap(give, GRP, 1), (late[0],), SHORT)
     pair = swap(near, CORE, 1)
     far = swap(near, GRP, 1)
@@ -560,7 +565,7 @@
     second = placed(ids, keep, swap(give, GRP, 1))
     far_pair = swap(far, CORE, 1)
     left = less_target(ids, first, layer_out, projection, 0, (second, far))
-    blocks = [second, *[swap(second, Z, k) for k in (1, 3, 2)]]
+    blocks = [second, *z_swaps(lambda k: second)]
     pairs = [swap(block, CORE, 1) for block in blocks]
     parts = some_less_target(ids, (0, 2, 6, 4), blocks, left, projection, 1, (), (marker(left, far_pair),))
     parts = some_less_target(ids, (1, 3, 7, 5), pairs, left, projection, 1, (parts,))
@@ -581,7 +586,7 @@
 
     mine, peer = values_partial(ids, gaps[:3] + gaps[4:7], student_weight, ())
     parts = merged((mine, swap(peer, CORE, 1)), 4, (marker(mine),))
-    values_grad = add(parts[0], *[swap(parts[k], Z, k) for k in (1, 3, 2)])
+    values_grad = add(parts[0], *z_swaps(lambda k: parts[k]))
     weight_grad = weight_sums(ids, gaps, (near, pair, far, far_pair), (parts[0],))
     return (values_grad, weight_grad)
 

time: 207 us -> 207 us (level)
  no operation moved by 1% of the time
where the time goes in v7:
time: 207 us; the launch traced here: 206 us
  Pallas kernels  78.5 us (38%)
  starting transfers between devices  56.7 us (27%)
  blocking collectives  34.5 us (17%)
  waiting for transfers between devices  24.7 us (12%)
  local copies, waits for them, and re-layouts  8.83 us (4%)
    pallas_call x19, Pallas kernels, call(): pl.pallas_call(body, grid=grid, out_shape=out_shape, in_specs=in_specs, o...  69.6 us
    ppermute x48, starting transfers between devices, swap(): return lax.ppermute(array, axes, [(i, i ^ distance) for i in range(size)])  56.7 us
    all_to_all x1, blocking collectives, per_device(): lax.all_to_all(parts.reshape(8, -1, parts.shape[1]), DP, 0, 0, tiled=True)  34.5 us
    ppermute x48, waiting for transfers between devices, swap(): return lax.ppermute(array, axes, [(i, i ^ distance) for i in range(size)])  24.7 us
    pallas_call x2, Pallas kernels, some_less_target(): pl.pallas_call(with_unread(functools.partial(some_target_kernel, fars), l...  8.89 us
    unnamed x64, local copies, waits for them, and re-layouts  8.77 us
  transfers between devices with their start and end apart: 48, of which 9 were waited for; matrix products, arithmetic and copies ran while one was open for 0% of the time, Pallas kernels for 36%

profile of v7, /device:TPU:1, one launch (start us, length us, event | category | flops | bytes accessed | tf_op | source)
XLA Modules:
  0.0 206.0 jit_solution(12725179084277212915)
XLA Ops:
  0.6 2.5 %collective-permute-start = (bf16[128,1024]{1,0:T(8,128)(2,1)}, bf16[128,1024]{1,0:T(8,128)(2,1)S(1)}, u32[]{:S(2)}, u32[]{:S(2)}) collective-permute-start(bf16[128,1024]{1,0:T(8,128)(2,1)} %refs_1_.3), channel_id=1, source_target_pairs={{0,2},{2,0},{4,6},{6,4},{1,3},{3,1},{5,7},{7,5},{8,10},{10,8},{12,... | collective-permute-start | bytes 786440 | tf_op jit(solution)/shard_map/ppermute | solution.py:29
  3.2 2.2 %collective-permute-start.1 = (bf16[128,1024]{1,0:T(8,128)(2,1)}, bf16[128,1024]{1,0:T(8,128)(2,1)S(1)}, u32[]{:S(2)}, u32[]{:S(2)}) collective-permute-start(bf16[128,1024]{1,0:T(8,128)(2,1)} %refs_1_.3), channel_id=1, source_target_pairs={{0,6},{2,4},{4,2},{6,0},{1,7},{3,5},{5,3},{7,1},{8,14},{10,12},{12... | collective-permute-start | bytes 786440 | tf_op jit(solution)/shard_map/ppermute | solution.py:29
  6.0 9.9 %shard_map.95 = (bf16[512,1024]{1,0:T(8,128)(2,1)}, bf16[512,1024]{1,0:T(8,128)(2,1)}) custom-call(s32[3]{0:T(128)} %pad_add_fusion.refs_0_.refs_1_.refs_2_, s32[16,128]{1,0:T(8,128)} %refs_2_.3, bf16[1024,2048]{1,0:T(8,128)(2,1)} %refs_3_.3, bf16[2048,2048]{1,0:T(8,128)(2,1)} %refs_4_.4, bf16[128,2048]{1,0:T(8,128)(2,1)} %refs_5_.1), custom_call_target="tpu_custom_call" | custom-call | flops 49999998976 | bytes 1024 | tf_op jit(solution)/shard_map/pallas_call | solution.py:42
  15.9 1.2 collective-permute-start.2
  18.0 1.7 shard_map.96
  21.4 2.5 %shard_map.97 = (bf16[128,1024]{1,0:T(8,128)(2,1)}, bf16[128,1024]{1,0:T(8,128)(2,1)}, bf16[128,1024]{1,0:T(8,128)(2,1)}, bf16[128,1024]{1,0:T(8,128)(2,1)}) custom-call(bf16[64,1024]{1,0:T(8,128)(2,1)} %get-tuple-element.27.refs_0_, bf16[512,1024]{1,0:T(8,128)(2,1)} %get-tuple-element.26.refs_0_.refs_1_, bf16[512,1024]{1,0:T(8,128)(2,1)} %copy-done.1), custom_call_target="tpu_custom_call" | custom-call | flops 10000000 | bytes 1024 | tf_op jit(solution)/shard_map/pallas_call | solution.py:42
  23.8 1.2 collective-permute-start.5
  25.0 2.2 %collective-permute-start.6 = (bf16[128,1024]{1,0:T(8,128)(2,1)}, bf16[128,1024]{1,0:T(8,128)(2,1)S(1)}, u32[]{:S(2)}, u32[]{:S(2)}) collective-permute-start(bf16[128,1024]{1,0:T(8,128)(2,1)} %get-tuple-element.33), channel_id=1, source_target_pairs={{0,6},{2,4},{4,2},{6,0},{1,7},{3,5},{5,3},{7,1},{8,14},{10,12},{12... | collective-permute-start | bytes 786440 | tf_op jit(solution)/shard_map/ppermute | solution.py:29
  27.3 9.9 %shard_map.98 = (bf16[512,1024]{1,0:T(8,128)(2,1)}, bf16[512,1024]{1,0:T(8,128)(2,1)}) custom-call(bf16[128,1024]{1,0:T(8,128)(2,1)} %get-tuple-element.29.refs_0_.refs_1_, s32[3]{0:T(128)} %pad_add_fusion.refs_0_.refs_1_.refs_2_, s32[16,128]{1,0:T(8,128)} %refs_2_.3, bf16[1024,2048]{1,0:T(8,128)(2,1)} %refs_3_.3, bf16[2048,2048]{1,0:T(8,128)(2,1)} %refs_4_.4, ...), custom_call_target="tpu_custom_call" | custom-call | flops 49999998976 | bytes 1024 | tf_op jit(solution)/shard_map/pallas_call | solution.py:42
  37.2 1.2 collective-permute-start.8
  39.0 2.1 %shard_map.99.refs_0_.refs_2_.refs_11_ = bf16[512,1024]{1,0:T(8,128)(2,1)} custom-call(bf16[512,1024]{1,0:T(8,128)(2,1)} %get-tuple-element.30.refs_0_.refs_1_, bf16[128,1024]{1,0:T(8,128)(2,1)} %refs_1_.3, bf16[128,1024]{1,0:T(8,128)(2,1)} %copy-done.3, bf16[64,1024]{1,0:T(8,128)(2,1)} %copy-done.8, bf16[64,1024]{1,0:T(8,128)(2,1)} %copy-done.9, ...), custom_call_target="tpu_custom_call" | custom-call | flops 10000000 | bytes 1024 | tf_op jit(solution)/shard_map/pallas_call | solution.py:42
  42.7 2.0 shard_map.100
  44.7 1.3 collective-permute-start.9
  46.1 2.4 %shard_map.101 = (bf16[128,1024]{1,0:T(8,128)(2,1)}, bf16[128,1024]{1,0:T(8,128)(2,1)}, bf16[128,1024]{1,0:T(8,128)(2,1)}, bf16[128,1024]{1,0:T(8,128)(2,1)}) custom-call(bf16[64,1024]{1,0:T(8,128)(2,1)} %get-tuple-element.35.refs_0_.refs_2_, bf16[512,1024]{1,0:T(8,128)(2,1)} %get-tuple-element.30.refs_0_.refs_1_, ...), custom_call_target="tpu_custom_call" | custom-call | flops 10000000 | bytes 1024 | tf_op jit(solution)/shard_map/pallas_call | solution.py:42
  48.5 1.3 collective-permute-start.11
  49.8 2.2 %collective-permute-start.12 = (bf16[128,1024]{1,0:T(8,128)(2,1)}, bf16[128,1024]{1,0:T(8,128)(2,1)}, u32[]{:S(2)}, u32[]{:S(2)}) collective-permute-start(bf16[128,1024]{1,0:T(8,128)(2,1)} %get-tuple-element.40), channel_id=1, source_target_pairs={{0,6},{2,4},{4,2},{6,0},{1,7},{3,5},{5,3},{7,1},{8,14},{10,12},{12... | collective-permute-start | bytes 786440 | tf_op jit(solution)/shard_map/ppermute | solution.py:29
  52.7 1.7 shard_map.102.refs_0_.refs_3_
  54.8 5.5 %shard_map.103.refs_0_.refs_11_ = bf16[1024,1024]{1,0:T(8,128)(2,1)} custom-call(bf16[128,1024]{1,0:T(8,128)(2,1)} %shard_map.102.refs_0_.refs_3_, s32[3]{0:T(128)} %pad_add_fusion.refs_0_.refs_1_.refs_2_, bf16[512,1024]{1,0:T(8,128)(2,1)} %shard_map.99.refs_0_.refs_2_.refs_11_, bf16[512,1024]{1,0:T(8,128)(2,1)} %collective-permute-done.10.refs_3_.refs_12_, ...), custom_call_target="tpu_custom_call" | custom-call | flops 49999998976 | bytes 1024 | tf_op jit(solution)/shard_map/pallas_call | solution.py:42
  60.3 2.3 %collective-permute-start.24 = (bf16[128,1024]{1,0:T(8,128)(2,1)S(1)}, bf16[128,1024]{1,0:T(8,128)(2,1)S(1)}, u32[]{:S(2)}, u32[]{:S(2)}) collective-permute-start(bf16[128,1024]{1,0:T(8,128)(2,1)S(1)} %copy-done.6), channel_id=1, source_target_pairs={{0,6},{2,4},{4,2},{6,0},{1,7},{3,5},{5,3},{7,1},{8,14},{10,12},{12... | collective-permute-start | bytes 786440 | tf_op jit(solution)/shard_map/ppermute | solution.py:29
  63.2 2.0 shard_map.104
  65.2 1.3 collective-permute-start.14
  66.5 5.5 %collective-permute-done.22.refs_1_.refs_13_ = bf16[512,1024]{1,0:T(8,128)(2,1)} collective-permute-done((bf16[512,1024]{1,0:T(8,128)(2,1)S(1)}, bf16[512,1024]{1,0:T(8,128)(2,1)}, u32[]{:S(2)}, u32[]{:S(2)}) %collective-permute-start.22) | collective-permute-done | bytes 1048608 | tf_op jit(solution)/shard_map/ppermute | solution.py:29
  72.0 2.3 %collective-permute-start.26 = (bf16[128,1024]{1,0:T(8,128)(2,1)S(1)}, bf16[128,1024]{1,0:T(8,128)(2,1)}, u32[]{:S(2)}, u32[]{:S(2)}) collective-permute-start(bf16[128,1024]{1,0:T(8,128)(2,1)S(1)} %copy-done.6), channel_id=1, source_target_pairs={{0,1},{1,0},{2,3},{3,2},{4,5},{5,4},{6,7},{7,6},{8,9},{9,8},{10,11... | collective-permute-start | bytes 786440 | tf_op jit(solution)/shard_map/ppermute | solution.py:29
  74.4 2.5 %collective-permute-start.27 = (bf16[128,1024]{1,0:T(8,128)(2,1)S(1)}, bf16[128,1024]{1,0:T(8,128)(2,1)}, u32[]{:S(2)}, u32[]{:S(2)}) collective-permute-start(bf16[128,1024]{1,0:T(8,128)(2,1)S(1)} %collective-permute-done.23.refs_4_), channel_id=1, source_target_pairs={{0,1},{1,0},{2,3},{3,2},{4,5},{5,4},{6,7},{7,6},{8,9},{9,8},{10,11... | collective-permute-start | bytes 786440 | tf_op jit(solution)/shard_map/ppermute | solution.py:29
  77.8 1.7 shard_map.105.refs_0_.refs_2_
  80.1 2.0 collective-permute-start.18
  82.1 1.2 collective-permute-start.20
  83.2 5.9 %shard_map.106.refs_0_.refs_6_.refs_5_ = bf16[1024,1024]{1,0:T(8,128)(2,1)} custom-call(bf16[128,1024]{1,0:T(8,128)(2,1)} %shard_map.105.refs_0_.refs_2_, bf16[512,1024]{1,0:T(8,128)(2,1)} %collective-permute-done.22.refs_1_.refs_13_, s32[3]{0:T(128)} %pad_add_fusion.refs_0_.refs_1_.refs_2_, bf16[128,1024]{1,0:T(8,128)(2,1)} %shard_map.102.refs_0_.refs_3_, ...), custom_call_target="tpu_custom_call" | custom-call | flops 49999998976 | bytes 1024 | tf_op jit(solution)/shard_map/pallas_call | solution.py:42
  90.2 4.4 %collective-permute-start.19 = (bf16[128,1024]{1,0:T(8,128)(2,1)S(1)}, bf16[128,1024]{1,0:T(8,128)(2,1)}, u32[]{:S(2)}, u32[]{:S(2)}) collective-permute-start(bf16[128,1024]{1,0:T(8,128)(2,1)S(1)} %collective-permute-done.18.refs_4_), channel_id=1, source_target_pairs={{0,1},{1,0},{2,3},{3,2},{4,5},{5,4},{6,7},{7,6},{8,9},{9,8},{10,11... | collective-permute-start | bytes 786440 | tf_op jit(solution)/shard_map/ppermute | solution.py:29
  95.2 1.1 collective-permute-start.21
  97.8 4.4 %shard_map.108.refs_7_ = bf16[1024,1024]{1,0:T(8,128)(2,1)} custom-call(f32[8,128]{1,0:T(8,128)} %shard_map.107.refs_0_, s32[3]{0:T(128)} %pad_add_fusion.refs_0_.refs_1_.refs_2_, bf16[128,1024]{1,0:T(8,128)(2,1)} %shard_map.105.refs_0_.refs_2_, bf16[128,1024]{1,0:T(8,128)(2,1)} %copy-done.19, bf16[128,1024]{1,0:T(8,128)(2,1)} %copy-done.20, ...), custom_call_target="tpu_custom_call" | custom-call | flops 49999998976 | bytes 1024 | tf_op jit(solution)/shard_map/pallas_call | solution.py:293
  102.3 4.5 %shard_map.109 = bf16[1024,1024]{1,0:T(8,128)(2,1)} custom-call(s32[3]{0:T(128)} %pad_add_fusion.refs_0_.refs_1_.refs_2_, bf16[128,1024]{1,0:T(8,128)(2,1)} %collective-permute-done.15.refs_1_, bf16[128,1024]{1,0:T(8,128)(2,1)} %collective-permute-done.17.refs_2_, bf16[128,1024]{1,0:T(8,128)(2,1)} %collective-permute-done.19.refs_3_, ...), custom_call_target="tpu_custom_call", output_to_operand_aliasing={{}: (7, {})} | custom-call | flops 49999998976 | bytes 1024 | tf_op jit(solution)/shard_map/pallas_call | solution.py:293
  106.8 34.5 %all_to_all.5 = bf16[8,128,1024]{2,1,0:T(8,128)(2,1)S(1)} all-to-all(bf16[8,128,1024]{2,1,0:T(8,128)(2,1)} %bitcast.4), channel_id=1, replica_groups=mesh['grp'=2,'x'=4,'yh'=2,'z'=4,'core'=2] {'x','yh'}, dimensions={0} | all-to-all | bytes 4194304 | tf_op jit(solution)/shard_map/all_to_all | solution.py:573
  143.8 1.9 collective-permute-start.33
  145.6 1.5 collective-permute-start.38
  147.7 1.8 collective-permute-start.39
  149.5 1.5 collective-permute-done.33.refs_3_
  151.7 1.8 shard_map.110.refs_0_.refs_1_.refs_2_
  155.8 1.8 shard_map.111.refs_5_.refs_7_
  158.6 6.5 %collective-permute-done.34.refs_2_.refs_3_ = bf16[256,1024]{1,0:T(8,128)(2,1)S(1)} collective-permute-done((bf16[256,1024]{1,0:T(8,128)(2,1)}, bf16[256,1024]{1,0:T(8,128)(2,1)S(1)}, u32[]{:S(2)}, u32[]{:S(2)}) %collective-permute-start.34) | collective-permute-done | bytes 524320 | tf_op jit(solution)/shard_map/ppermute | solution.py:29
  167.6 1.9 collective-permute-done.40.refs_6_.refs_8_
  169.5 2.5 %collective-permute-done.35.refs_3_.refs_4_ = bf16[128,1024]{1,0:T(8,128)(2,1)} collective-permute-done((bf16[128,1024]{1,0:T(8,128)(2,1)S(1)}, bf16[128,1024]{1,0:T(8,128)(2,1)}, u32[]{:S(2)}, u32[]{:S(2)}) %collective-permute-start.35) | collective-permute-done | bytes 262176 | tf_op jit(solution)/shard_map/ppermute | solution.py:29
  172.0 5.8 %shard_map.112 = (bf16[512,1024]{1,0:T(8,128)(2,1)}, bf16[512,1024]{1,0:T(8,128)(2,1)}) custom-call(s32[3]{0:T(128)} %pad_add_fusion.refs_0_.refs_1_.refs_2_, bf16[256,1024]{1,0:T(8,128)(2,1)} %shard_map.110.refs_0_.refs_1_.refs_2_, bf16[256,1024]{1,0:T(8,128)(2,1)} %copy-done.10, bf16[128,1024]{1,0:T(8,128)(2,1)} %collective-permute-done.35.refs_3_.refs_4_, ...), custom_call_target="tpu_custom_call" | custom-call | flops 49999998976 | bytes 1024 | tf_op jit(solution)/shard_map/pallas_call | solution.py:42
  177.8 5.9 %collective-permute-start.41 = (bf16[512,1024]{1,0:T(8,128)(2,1)}, bf16[512,1024]{1,0:T(8,128)(2,1)S(1)}, u32[]{:S(2)}, u32[]{:S(2)}) collective-permute-start(bf16[512,1024]{1,0:T(8,128)(2,1)} %get-tuple-element.45), channel_id=1, source_target_pairs={{0,1},{1,0},{2,3},{3,2},{4,5},{5,4},{6,7},{7,6},{8,9},{9,8},{10,11... | collective-permute-start | bytes 3145736 | tf_op jit(solution)/shard_map/ppermute | solution.py:29
  184.2 1.9 collective-permute-done.41.refs_2_
  187.1 2.4 %shard_map.114 = (bf16[128,1024]{1,0:T(8,128)(2,1)}, bf16[128,1024]{1,0:T(8,128)(2,1)}, bf16[128,1024]{1,0:T(8,128)(2,1)}, bf16[128,1024]{1,0:T(8,128)(2,1)}) custom-call(f32[8,128]{1,0:T(8,128)} %shard_map.113.refs_0_, bf16[512,1024]{1,0:T(8,128)(2,1)} %get-tuple-element.44.refs_0_.refs_1_, bf16[512,1024]{1,0:T(8,128)(2,1)} %copy-done.2), custom_call_target="tpu_custom_call" | custom-call | flops 10000000 | bytes 1024 | tf_op jit(solution)/shard_map/pallas_call | solution.py:42
  192.2 9.4 %shard_map.115 = f32[1024,1024]{1,0:T(8,128)} custom-call(bf16[128,1024]{1,0:T(8,128)(2,1)} %get-tuple-element.46.refs_0_, s32[3]{0:T(128)} %pad_add_fusion.refs_0_.refs_1_.refs_2_, bf16[256,1024]{1,0:T(8,128)(2,1)} %shard_map.110.refs_0_.refs_1_.refs_2_, bf16[256,1024]{1,0:T(8,128)(2,1)} %copy-done.10, ...), custom_call_target="tpu_custom_call" | custom-call | flops 49999998976 | bytes 1024 | tf_op jit(solution)/shard_map/pallas_call | solution.py:42
  201.6 3.5 %collective-permute-done.43 = bf16[128,1024]{1,0:T(8,128)(2,1)S(1)} collective-permute-done((bf16[128,1024]{1,0:T(8,128)(2,1)}, bf16[128,1024]{1,0:T(8,128)(2,1)S(1)}, u32[]{:S(2)}, u32[]{:S(2)}) %collective-permute-start.43) | collective-permute-done | bytes 262176 | tf_op jit(solution)/shard_map/ppermute | solution.py:29
  (141 shorter events, 26.6 us)
Async XLA Ops:
  0.6 16.5 %collective-permute-start = (bf16[128,1024]{1,0:T(8,128)(2,1)}, bf16[128,1024]{1,0:T(8,128)(2,1)S(1)}, u32[]{:S(2)}, u32[]{:S(2)}) collective-permute-start(bf16[128,1024]{1,0:T(8,128)(2,1)} %refs_1_.3), channel_id=1, source_target_pairs={{0,2},{2,0},{4,6},{6,4},{1,3},{3,1},{5,7},{7,5},{8,10},{10,8},{12,... | collective-permute-start | bytes 786440 | tf_op jit(solution)/shard_map/ppermute | solution.py:29
  3.2 14.0 %collective-permute-start.1 = (bf16[128,1024]{1,0:T(8,128)(2,1)}, bf16[128,1024]{1,0:T(8,128)(2,1)S(1)}, u32[]{:S(2)}, u32[]{:S(2)}) collective-permute-start(bf16[128,1024]{1,0:T(8,128)(2,1)} %refs_1_.3), channel_id=1, source_target_pairs={{0,6},{2,4},{4,2},{6,0},{1,7},{3,5},{5,3},{7,1},{8,14},{10,12},{12... | collective-permute-start | bytes 786440 | tf_op jit(solution)/shard_map/ppermute | solution.py:29
  15.9 4.5 %collective-permute-start.2 = (bf16[512,1024]{1,0:T(8,128)(2,1)}, bf16[512,1024]{1,0:T(8,128)(2,1)S(1)}, u32[]{:S(2)}, u32[]{:S(2)}) collective-permute-start(bf16[512,1024]{1,0:T(8,128)(2,1)} %get-tuple-element.28), channel_id=1, source_target_pairs={{0,1},{1,0},{2,3},{3,2},{4,5},{5,4},{6,7},{7,6},{8,9},{9,8},{10,11... | collective-permute-start | bytes 3145736 | tf_op jit(solution)/shard_map/ppermute | solution.py:29
  19.7 17.5 %collective-permute-start.3 = (bf16[64,1024]{1,0:T(8,128)(2,1)}, bf16[64,1024]{1,0:T(8,128)(2,1)S(1)}, u32[]{:S(2)}, u32[]{:S(2)}) collective-permute-start(bf16[64,1024]{1,0:T(8,128)(2,1)} %get-tuple-element.27.refs_0_), channel_id=1, source_target_pairs={{0,6},{2,4},{4,2},{6,0},{1,7},{3,5},{5,3},{7,1},{8,14},{10,12},{12... | collective-permute-start | bytes 393224 | tf_op jit(solution)/shard_map/ppermute | solution.py:29
  20.1 18.3 %collective-permute-start.4 = (bf16[64,1024]{1,0:T(8,128)(2,1)}, bf16[64,1024]{1,0:T(8,128)(2,1)S(1)}, u32[]{:S(2)}, u32[]{:S(2)}) collective-permute-start(bf16[64,1024]{1,0:T(8,128)(2,1)} %get-tuple-element.31), channel_id=1, source_target_pairs={{0,2},{2,0},{4,6},{6,4},{1,3},{3,1},{5,7},{7,5},{8,10},{10,8},{12,... | collective-permute-start | bytes 393224 | tf_op jit(solution)/shard_map/ppermute | solution.py:29
  23.8 17.3 %collective-permute-start.5 = (bf16[128,1024]{1,0:T(8,128)(2,1)}, bf16[128,1024]{1,0:T(8,128)(2,1)S(1)}, u32[]{:S(2)}, u32[]{:S(2)}) collective-permute-start(bf16[128,1024]{1,0:T(8,128)(2,1)} %get-tuple-element.32), channel_id=1, source_target_pairs={{0,2},{2,0},{4,6},{6,4},{1,3},{3,1},{5,7},{7,5},{8,10},{10,8},{12,... | collective-permute-start | bytes 786440 | tf_op jit(solution)/shard_map/ppermute | solution.py:29
  25.0 16.2 %collective-permute-start.6 = (bf16[128,1024]{1,0:T(8,128)(2,1)}, bf16[128,1024]{1,0:T(8,128)(2,1)S(1)}, u32[]{:S(2)}, u32[]{:S(2)}) collective-permute-start(bf16[128,1024]{1,0:T(8,128)(2,1)} %get-tuple-element.33), channel_id=1, source_target_pairs={{0,6},{2,4},{4,2},{6,0},{1,7},{3,5},{5,3},{7,1},{8,14},{10,12},{12... | collective-permute-start | bytes 786440 | tf_op jit(solution)/shard_map/ppermute | solution.py:29
  27.2 14.0 %collective-permute-start.7 = (bf16[128,1024]{1,0:T(8,128)(2,1)}, bf16[128,1024]{1,0:T(8,128)(2,1)S(1)}, u32[]{:S(2)}, u32[]{:S(2)}) collective-permute-start(bf16[128,1024]{1,0:T(8,128)(2,1)} %get-tuple-element.34), channel_id=1, source_target_pairs={{0,4},{2,6},{4,0},{6,2},{1,5},{3,7},{5,1},{7,3},{8,12},{10,14},{12... | collective-permute-start | bytes 786440 | tf_op jit(solution)/shard_map/ppermute | solution.py:29
  37.2 9.0 %collective-permute-start.8 = (bf16[512,1024]{1,0:T(8,128)(2,1)}, bf16[512,1024]{1,0:T(8,128)(2,1)}, u32[]{:S(2)}, u32[]{:S(2)}) collective-permute-start(bf16[512,1024]{1,0:T(8,128)(2,1)} %get-tuple-element.36), channel_id=1, source_target_pairs={{0,1},{1,0},{2,3},{3,2},{4,5},{5,4},{6,7},{7,6},{8,9},{9,8},{10,11... | collective-permute-start | bytes 3145736 | tf_op jit(solution)/shard_map/ppermute | solution.py:29
  41.2 13.2 %collective-permute-start.10 = (bf16[512,1024]{1,0:T(8,128)(2,1)}, bf16[512,1024]{1,0:T(8,128)(2,1)}, u32[]{:S(2)}, u32[]{:S(2)}) collective-permute-start(bf16[512,1024]{1,0:T(8,128)(2,1)} %shard_map.99.refs_0_.refs_2_.refs_11_), channel_id=1, source_target_pairs={{0,1},{1,0},{2,3},{3,2},{4,5},{5,4},{6,7},{7,6},{8,9},{9,8},{10,11... | collective-permute-start | bytes 3145736 | tf_op jit(solution)/shard_map/ppermute | solution.py:29
  44.7 7.4 %collective-permute-start.9 = (bf16[64,1024]{1,0:T(8,128)(2,1)}, bf16[64,1024]{1,0:T(8,128)(2,1)S(1)}, u32[]{:S(2)}, u32[]{:S(2)}) collective-permute-start(bf16[64,1024]{1,0:T(8,128)(2,1)} %get-tuple-element.38), channel_id=1, source_target_pairs={{0,64},{64,0},{1,65},{65,1},{2,66},{66,2},{3,67},{67,3},{4,68},{68... | collective-permute-start | bytes 393224 | tf_op jit(solution)/shard_map/ppermute | solution.py:29
  46.0 26.1 %collective-permute-start.22 = (bf16[512,1024]{1,0:T(8,128)(2,1)S(1)}, bf16[512,1024]{1,0:T(8,128)(2,1)}, u32[]{:S(2)}, u32[]{:S(2)}) collective-permute-start(bf16[512,1024]{1,0:T(8,128)(2,1)S(1)} %copy-done), channel_id=1, source_target_pairs={{0,64},{64,0},{1,65},{65,1},{2,66},{66,2},{3,67},{67,3},{4,68},{68... | collective-permute-start | bytes 3145736 | tf_op jit(solution)/shard_map/ppermute | solution.py:29
  48.5 11.8 %collective-permute-start.11 = (bf16[128,1024]{1,0:T(8,128)(2,1)}, bf16[128,1024]{1,0:T(8,128)(2,1)}, u32[]{:S(2)}, u32[]{:S(2)}) collective-permute-start(bf16[128,1024]{1,0:T(8,128)(2,1)} %get-tuple-element.39), channel_id=1, source_target_pairs={{0,2},{2,0},{4,6},{6,4},{1,3},{3,1},{5,7},{7,5},{8,10},{10,8},{12,... | collective-permute-start | bytes 786440 | tf_op jit(solution)/shard_map/ppermute | solution.py:29
  49.8 12.8 %collective-permute-start.12 = (bf16[128,1024]{1,0:T(8,128)(2,1)}, bf16[128,1024]{1,0:T(8,128)(2,1)}, u32[]{:S(2)}, u32[]{:S(2)}) collective-permute-start(bf16[128,1024]{1,0:T(8,128)(2,1)} %get-tuple-element.40), channel_id=1, source_target_pairs={{0,6},{2,4},{4,2},{6,0},{1,7},{3,5},{5,3},{7,1},{8,14},{10,12},{12... | collective-permute-start | bytes 786440 | tf_op jit(solution)/shard_map/ppermute | solution.py:29
  52.0 11.2 %collective-permute-start.13 = (bf16[128,1024]{1,0:T(8,128)(2,1)}, bf16[128,1024]{1,0:T(8,128)(2,1)}, u32[]{:S(2)}, u32[]{:S(2)}) collective-permute-start(bf16[128,1024]{1,0:T(8,128)(2,1)} %get-tuple-element.41), channel_id=1, source_target_pairs={{0,4},{2,6},{4,0},{6,2},{1,5},{3,7},{5,1},{7,3},{8,12},{10,14},{12... | collective-permute-start | bytes 786440 | tf_op jit(solution)/shard_map/ppermute | solution.py:29
  54.4 19.9 %collective-permute-start.23 = (bf16[128,1024]{1,0:T(8,128)(2,1)}, bf16[128,1024]{1,0:T(8,128)(2,1)S(1)}, u32[]{:S(2)}, u32[]{:S(2)}) collective-permute-start(bf16[128,1024]{1,0:T(8,128)(2,1)} %shard_map.102.refs_0_.refs_3_), channel_id=1, source_target_pairs={{0,2},{2,0},{4,6},{6,4},{1,3},{3,1},{5,7},{7,5},{8,10},{10,8},{12,... | collective-permute-start | bytes 786440 | tf_op jit(solution)/shard_map/ppermute | solution.py:29
  60.3 14.1 %collective-permute-start.24 = (bf16[128,1024]{1,0:T(8,128)(2,1)S(1)}, bf16[128,1024]{1,0:T(8,128)(2,1)S(1)}, u32[]{:S(2)}, u32[]{:S(2)}) collective-permute-start(bf16[128,1024]{1,0:T(8,128)(2,1)S(1)} %copy-done.6), channel_id=1, source_target_pairs={{0,6},{2,4},{4,2},{6,0},{1,7},{3,5},{5,3},{7,1},{8,14},{10,12},{12... | collective-permute-start | bytes 786440 | tf_op jit(solution)/shard_map/ppermute | solution.py:29
  62.6 14.3 %collective-permute-start.25 = (bf16[128,1024]{1,0:T(8,128)(2,1)S(1)}, bf16[128,1024]{1,0:T(8,128)(2,1)}, u32[]{:S(2)}, u32[]{:S(2)}) collective-permute-start(bf16[128,1024]{1,0:T(8,128)(2,1)S(1)} %copy-done.6), channel_id=1, source_target_pairs={{0,4},{2,6},{4,0},{6,2},{1,5},{3,7},{5,1},{7,3},{8,12},{10,14},{12... | collective-permute-start | bytes 786440 | tf_op jit(solution)/shard_map/ppermute | solution.py:29
  65.2 11.9 %collective-permute-start.14 = (bf16[64,1024]{1,0:T(8,128)(2,1)}, bf16[64,1024]{1,0:T(8,128)(2,1)S(1)}, u32[]{:S(2)}, u32[]{:S(2)}) collective-permute-start(bf16[64,1024]{1,0:T(8,128)(2,1)} %get-tuple-element.43), channel_id=1, source_target_pairs={{0,64},{64,0},{1,65},{65,1},{2,66},{66,2},{3,67},{67,3},{4,68},{68... | collective-permute-start | bytes 393224 | tf_op jit(solution)/shard_map/ppermute | solution.py:29
  72.0 7.5 %collective-permute-start.26 = (bf16[128,1024]{1,0:T(8,128)(2,1)S(1)}, bf16[128,1024]{1,0:T(8,128)(2,1)}, u32[]{:S(2)}, u32[]{:S(2)}) collective-permute-start(bf16[128,1024]{1,0:T(8,128)(2,1)S(1)} %copy-done.6), channel_id=1, source_target_pairs={{0,1},{1,0},{2,3},{3,2},{4,5},{5,4},{6,7},{7,6},{8,9},{9,8},{10,11... | collective-permute-start | bytes 786440 | tf_op jit(solution)/shard_map/ppermute | solution.py:29
  74.3 21.9 %collective-permute-start.30 = (bf16[512,1024]{1,0:T(8,128)(2,1)}, bf16[512,1024]{1,0:T(8,128)(2,1)S(1)}, u32[]{:S(2)}, u32[]{:S(2)}) collective-permute-start(bf16[512,1024]{1,0:T(8,128)(2,1)} %collective-permute-done.22.refs_1_.refs_13_), channel_id=1, source_target_pairs={{0,1},{1,0},{2,3},{3,2},{4,5},{5,4},{6,7},{7,6},{8,9},{9,8},{10,11... | collective-permute-start | bytes 3145736 | tf_op jit(solution)/shard_map/ppermute | solution.py:29
  74.4 5.4 %collective-permute-start.27 = (bf16[128,1024]{1,0:T(8,128)(2,1)S(1)}, bf16[128,1024]{1,0:T(8,128)(2,1)}, u32[]{:S(2)}, u32[]{:S(2)}) collective-permute-start(bf16[128,1024]{1,0:T(8,128)(2,1)S(1)} %collective-permute-done.23.refs_4_), channel_id=1, source_target_pairs={{0,1},{1,0},{2,3},{3,2},{4,5},{5,4},{6,7},{7,6},{8,9},{9,8},{10,11... | collective-permute-start | bytes 786440 | tf_op jit(solution)/shard_map/ppermute | solution.py:29
  76.9 3.2 %collective-permute-start.28 = (bf16[128,1024]{1,0:T(8,128)(2,1)S(1)}, bf16[128,1024]{1,0:T(8,128)(2,1)}, u32[]{:S(2)}, u32[]{:S(2)}) collective-permute-start(bf16[128,1024]{1,0:T(8,128)(2,1)S(1)} %collective-permute-done.24.refs_5_), channel_id=1, source_target_pairs={{0,1},{1,0},{2,3},{3,2},{4,5},{5,4},{6,7},{7,6},{8,9},{9,8},{10,11... | collective-permute-start | bytes 786440 | tf_op jit(solution)/shard_map/ppermute | solution.py:29
  77.1 4.9 %collective-permute-start.29 = (bf16[128,1024]{1,0:T(8,128)(2,1)}, bf16[128,1024]{1,0:T(8,128)(2,1)}, u32[]{:S(2)}, u32[]{:S(2)}) collective-permute-start(bf16[128,1024]{1,0:T(8,128)(2,1)} %collective-permute-done.25.refs_6_), channel_id=1, source_target_pairs={{0,1},{1,0},{2,3},{3,2},{4,5},{5,4},{6,7},{7,6},{8,9},{9,8},{10,11... | collective-permute-start | bytes 786440 | tf_op jit(solution)/shard_map/ppermute | solution.py:29
  79.5 22.8 %collective-permute-start.15 = (bf16[128,1024]{1,0:T(8,128)(2,1)}, bf16[128,1024]{1,0:T(8,128)(2,1)}, u32[]{:S(2)}, u32[]{:S(2)}) collective-permute-start(bf16[128,1024]{1,0:T(8,128)(2,1)} %shard_map.105.refs_0_.refs_2_), channel_id=1, source_target_pairs={{0,1},{1,0},{2,3},{3,2},{4,5},{5,4},{6,7},{7,6},{8,9},{9,8},{10,11... | collective-permute-start | bytes 786440 | tf_op jit(solution)/shard_map/ppermute | solution.py:29
  79.8 9.3 %collective-permute-start.16 = (bf16[128,1024]{1,0:T(8,128)(2,1)}, bf16[128,1024]{1,0:T(8,128)(2,1)S(1)}, u32[]{:S(2)}, u32[]{:S(2)}) collective-permute-start(bf16[128,1024]{1,0:T(8,128)(2,1)} %shard_map.105.refs_0_.refs_2_), channel_id=1, source_target_pairs={{0,2},{2,0},{4,6},{6,4},{1,3},{3,1},{5,7},{7,5},{8,10},{10,8},{12,... | collective-permute-start | bytes 786440 | tf_op jit(solution)/shard_map/ppermute | solution.py:29
  80.1 10.0 %collective-permute-start.18 = (bf16[128,1024]{1,0:T(8,128)(2,1)}, bf16[128,1024]{1,0:T(8,128)(2,1)S(1)}, u32[]{:S(2)}, u32[]{:S(2)}) collective-permute-start(bf16[128,1024]{1,0:T(8,128)(2,1)} %shard_map.105.refs_0_.refs_2_), channel_id=1, source_target_pairs={{0,6},{2,4},{4,2},{6,0},{1,7},{3,5},{5,3},{7,1},{8,14},{10,12},{12... | collective-permute-start | bytes 786440 | tf_op jit(solution)/shard_map/ppermute | solution.py:29
  82.1 13.1 %collective-permute-start.20 = (bf16[128,1024]{1,0:T(8,128)(2,1)}, bf16[128,1024]{1,0:T(8,128)(2,1)S(1)}, u32[]{:S(2)}, u32[]{:S(2)}) collective-permute-start(bf16[128,1024]{1,0:T(8,128)(2,1)} %shard_map.105.refs_0_.refs_2_), channel_id=1, source_target_pairs={{0,4},{2,6},{4,0},{6,2},{1,5},{3,7},{5,1},{7,3},{8,12},{10,14},{12... | collective-permute-start | bytes 786440 | tf_op jit(solution)/shard_map/ppermute | solution.py:29
  89.1 13.1 %collective-permute-start.17 = (bf16[128,1024]{1,0:T(8,128)(2,1)S(1)}, bf16[128,1024]{1,0:T(8,128)(2,1)}, u32[]{:S(2)}, u32[]{:S(2)}) collective-permute-start(bf16[128,1024]{1,0:T(8,128)(2,1)S(1)} %collective-permute-done.16.refs_3_), channel_id=1, source_target_pairs={{0,1},{1,0},{2,3},{3,2},{4,5},{5,4},{6,7},{7,6},{8,9},{9,8},{10,11... | collective-permute-start | bytes 786440 | tf_op jit(solution)/shard_map/ppermute | solution.py:29
  90.2 12.1 %collective-permute-start.19 = (bf16[128,1024]{1,0:T(8,128)(2,1)S(1)}, bf16[128,1024]{1,0:T(8,128)(2,1)}, u32[]{:S(2)}, u32[]{:S(2)}) collective-permute-start(bf16[128,1024]{1,0:T(8,128)(2,1)S(1)} %collective-permute-done.18.refs_4_), channel_id=1, source_target_pairs={{0,1},{1,0},{2,3},{3,2},{4,5},{5,4},{6,7},{7,6},{8,9},{9,8},{10,11... | collective-permute-start | bytes 786440 | tf_op jit(solution)/shard_map/ppermute | solution.py:29
  95.2 7.1 %collective-permute-start.21 = (bf16[128,1024]{1,0:T(8,128)(2,1)S(1)}, bf16[128,1024]{1,0:T(8,128)(2,1)}, u32[]{:S(2)}, u32[]{:S(2)}) collective-permute-start(bf16[128,1024]{1,0:T(8,128)(2,1)S(1)} %collective-permute-done.20.refs_5_), channel_id=1, source_target_pairs={{0,1},{1,0},{2,3},{3,2},{4,5},{5,4},{6,7},{7,6},{8,9},{9,8},{10,11... | collective-permute-start | bytes 786440 | tf_op jit(solution)/shard_map/ppermute | solution.py:29
  142.3 5.4 %collective-permute-start.31 = (bf16[64,1024]{1,0:T(8,128)(2,1)S(1)}, bf16[64,1024]{1,0:T(8,128)(2,1)S(1)}, u32[]{:S(2)}, u32[]{:S(2)}) collective-permute-start(bf16[64,1024]{1,0:T(8,128)(2,1)S(1)} %get-tuple-element.51.refs_0_), channel_id=1, source_target_pairs={{0,8},{8,0},{64,72},{72,64},{1,9},{9,1},{65,73},{73,65},{2,10},{10... | collective-permute-start | bytes 393224 | tf_op jit(solution)/shard_map/ppermute | solution.py:29
  143.4 6.1 %collective-permute-start.32 = (bf16[64,1024]{1,0:T(8,128)(2,1)S(1)}, bf16[64,1024]{1,0:T(8,128)(2,1)S(1)}, u32[]{:S(2)}, u32[]{:S(2)}) collective-permute-start(bf16[64,1024]{1,0:T(8,128)(2,1)S(1)} %get-tuple-element.51.refs_0_), channel_id=1, source_target_pairs={{0,64},{8,72},{64,0},{72,8},{1,65},{9,73},{65,1},{73,9},{2,66},{10... | collective-permute-start | bytes 393224 | tf_op jit(solution)/shard_map/ppermute | solution.py:29
  143.8 7.2 %collective-permute-start.33 = (bf16[64,1024]{1,0:T(8,128)(2,1)S(1)}, bf16[64,1024]{1,0:T(8,128)(2,1)S(1)}, u32[]{:S(2)}, u32[]{:S(2)}) collective-permute-start(bf16[64,1024]{1,0:T(8,128)(2,1)S(1)} %get-tuple-element.51.refs_0_), channel_id=1, source_target_pairs={{0,72},{8,64},{64,8},{72,0},{1,73},{9,65},{65,9},{73,1},{2,74},{10... | collective-permute-start | bytes 393224 | tf_op jit(solution)/shard_map/ppermute | solution.py:29
  145.6 8.8 %collective-permute-start.37 = (bf16[64,1024]{1,0:T(8,128)(2,1)S(1)}, bf16[64,1024]{1,0:T(8,128)(2,1)S(1)}, u32[]{:S(2)}, u32[]{:S(2)}) collective-permute-start(bf16[64,1024]{1,0:T(8,128)(2,1)S(1)} %get-tuple-element.50.refs_1_), channel_id=1, source_target_pairs={{0,16},{16,0},{32,48},{48,32},{1,17},{17,1},{33,49},{49,33},{2,18}... | collective-permute-start | bytes 393224 | tf_op jit(solution)/shard_map/ppermute | solution.py:29
  145.6 8.8 %collective-permute-start.38 = (bf16[64,1024]{1,0:T(8,128)(2,1)S(1)}, bf16[64,1024]{1,0:T(8,128)(2,1)S(1)}, u32[]{:S(2)}, u32[]{:S(2)}) collective-permute-start(bf16[64,1024]{1,0:T(8,128)(2,1)S(1)} %get-tuple-element.50.refs_1_), channel_id=1, source_target_pairs={{0,32},{16,48},{32,0},{48,16},{1,33},{17,49},{33,1},{49,17},{2,34}... | collective-permute-start | bytes 393224 | tf_op jit(solution)/shard_map/ppermute | solution.py:29
  147.7 6.7 %collective-permute-start.39 = (bf16[64,1024]{1,0:T(8,128)(2,1)S(1)}, bf16[64,1024]{1,0:T(8,128)(2,1)S(1)}, u32[]{:S(2)}, u32[]{:S(2)}) collective-permute-start(bf16[64,1024]{1,0:T(8,128)(2,1)S(1)} %get-tuple-element.50.refs_1_), channel_id=1, source_target_pairs={{0,48},{16,32},{32,16},{48,0},{1,49},{17,33},{33,17},{49,1},{2,50}... | collective-permute-start | bytes 393224 | tf_op jit(solution)/shard_map/ppermute | solution.py:29
  153.5 11.6 %collective-permute-start.34 = (bf16[256,1024]{1,0:T(8,128)(2,1)}, bf16[256,1024]{1,0:T(8,128)(2,1)S(1)}, u32[]{:S(2)}, u32[]{:S(2)}) collective-permute-start(bf16[256,1024]{1,0:T(8,128)(2,1)} %shard_map.110.refs_0_.refs_1_.refs_2_), channel_id=1, source_target_pairs={{0,16},{16,0},{32,48},{48,32},{1,17},{17,1},{33,49},{49,33},{2,18}... | collective-permute-start | bytes 1572872 | tf_op jit(solution)/shard_map/ppermute | solution.py:29
  153.8 13.4 %collective-permute-start.36 = (bf16[256,1024]{1,0:T(8,128)(2,1)}, bf16[256,1024]{1,0:T(8,128)(2,1)S(1)}, u32[]{:S(2)}, u32[]{:S(2)}) collective-permute-start(bf16[256,1024]{1,0:T(8,128)(2,1)} %shard_map.110.refs_0_.refs_1_.refs_2_), channel_id=1, source_target_pairs={{0,48},{16,32},{32,16},{48,0},{1,49},{17,33},{33,17},{49,1},{2,50}... | collective-permute-start | bytes 1572872 | tf_op jit(solution)/shard_map/ppermute | solution.py:29
  157.6 11.9 %collective-permute-start.40 = (bf16[256,1024]{1,0:T(8,128)(2,1)}, bf16[256,1024]{1,0:T(8,128)(2,1)S(1)}, u32[]{:S(2)}, u32[]{:S(2)}) collective-permute-start(bf16[256,1024]{1,0:T(8,128)(2,1)} %shard_map.111.refs_5_.refs_7_), channel_id=1, source_target_pairs={{0,8},{8,0},{64,72},{72,64},{1,9},{9,1},{65,73},{73,65},{2,10},{10... | collective-permute-start | bytes 1572872 | tf_op jit(solution)/shard_map/ppermute | solution.py:29
  165.1 6.9 %collective-permute-start.35 = (bf16[128,1024]{1,0:T(8,128)(2,1)S(1)}, bf16[128,1024]{1,0:T(8,128)(2,1)}, u32[]{:S(2)}, u32[]{:S(2)}) collective-permute-start(bf16[128,1024]{1,0:T(8,128)(2,1)S(1)} %slice.17), channel_id=1, source_target_pairs={{0,48},{16,32},{32,16},{48,0},{1,49},{17,33},{33,17},{49,1},{2,50}... | collective-permute-start | bytes 786440 | tf_op jit(solution)/shard_map/ppermute | solution.py:29
  165.2 26.0 %collective-permute-start.46 = (bf16[256,1024]{1,0:T(8,128)(2,1)}, bf16[256,1024]{1,0:T(8,128)(2,1)}, u32[]{:S(2)}, u32[]{:S(2)}) collective-permute-start(bf16[256,1024]{1,0:T(8,128)(2,1)} %shard_map.111.refs_5_.refs_7_), channel_id=1, source_target_pairs={{0,64},{8,72},{64,0},{72,8},{1,65},{9,73},{65,1},{73,9},{2,66},{10... | collective-permute-start | bytes 1572872 | tf_op jit(solution)/shard_map/ppermute | solution.py:29
  166.2 26.0 %collective-permute-start.47 = (bf16[256,1024]{1,0:T(8,128)(2,1)}, bf16[256,1024]{1,0:T(8,128)(2,1)}, u32[]{:S(2)}, u32[]{:S(2)}) collective-permute-start(bf16[256,1024]{1,0:T(8,128)(2,1)} %shard_map.111.refs_5_.refs_7_), channel_id=1, source_target_pairs={{0,72},{8,64},{64,8},{72,0},{1,73},{9,65},{65,9},{73,1},{2,74},{10... | collective-permute-start | bytes 1572872 | tf_op jit(solution)/shard_map/ppermute | solution.py:29
  167.3 24.9 %collective-permute-start.45 = (bf16[128,1024]{1,0:T(8,128)(2,1)S(1)}, bf16[128,1024]{1,0:T(8,128)(2,1)}, u32[]{:S(2)}, u32[]{:S(2)}) collective-permute-start(bf16[128,1024]{1,0:T(8,128)(2,1)S(1)} %slice.19), channel_id=1, source_target_pairs={{0,16},{16,0},{32,48},{48,32},{1,17},{17,1},{33,49},{49,33},{2,18}... | collective-permute-start | bytes 786440 | tf_op jit(solution)/shard_map/ppermute | solution.py:29
  177.8 8.4 %collective-permute-start.41 = (bf16[512,1024]{1,0:T(8,128)(2,1)}, bf16[512,1024]{1,0:T(8,128)(2,1)S(1)}, u32[]{:S(2)}, u32[]{:S(2)}) collective-permute-start(bf16[512,1024]{1,0:T(8,128)(2,1)} %get-tuple-element.45), channel_id=1, source_target_pairs={{0,1},{1,0},{2,3},{3,2},{4,5},{5,4},{6,7},{7,6},{8,9},{9,8},{10,11... | collective-permute-start | bytes 3145736 | tf_op jit(solution)/shard_map/ppermute | solution.py:29
  189.5 12.1 %collective-permute-start.44 = (bf16[128,1024]{1,0:T(8,128)(2,1)}, bf16[128,1024]{1,0:T(8,128)(2,1)S(1)}, u32[]{:S(2)}, u32[]{:S(2)}) collective-permute-start(bf16[128,1024]{1,0:T(8,128)(2,1)} %get-tuple-element.49), channel_id=1, source_target_pairs={{0,4},{2,6},{4,0},{6,2},{1,5},{3,7},{5,1},{7,3},{8,12},{10,14},{12... | collective-permute-start | bytes 786440 | tf_op jit(solution)/shard_map/ppermute | solution.py:29
  190.5 14.6 %collective-permute-start.43 = (bf16[128,1024]{1,0:T(8,128)(2,1)}, bf16[128,1024]{1,0:T(8,128)(2,1)S(1)}, u32[]{:S(2)}, u32[]{:S(2)}) collective-permute-start(bf16[128,1024]{1,0:T(8,128)(2,1)} %get-tuple-element.48), channel_id=1, source_target_pairs={{0,6},{2,4},{4,2},{6,0},{1,7},{3,5},{5,3},{7,1},{8,14},{10,12},{12... | collective-permute-start | bytes 786440 | tf_op jit(solution)/shard_map/ppermute | solution.py:29
  191.2 13.9 %collective-permute-start.42 = (bf16[128,1024]{1,0:T(8,128)(2,1)}, bf16[128,1024]{1,0:T(8,128)(2,1)S(1)}, u32[]{:S(2)}, u32[]{:S(2)}) collective-permute-start(bf16[128,1024]{1,0:T(8,128)(2,1)} %get-tuple-element.47), channel_id=1, source_target_pairs={{0,2},{2,0},{4,6},{6,4},{1,3},{3,1},{5,7},{7,5},{8,10},{10,8},{12,... | collective-permute-start | bytes 786440 | tf_op jit(solution)/shard_map/ppermute | solution.py:29
  (32 other events, 105.1 us)
